TPU v7x, 32 devices: a whole 2x2x4 slice. The times are simulated.
32 devices in a mesh: dp: 8 (over y, x, core), head: 4 (over z).
Axes of the slice: x: 2, y: 2, z: 4, core: 2. Of those that a mesh axis runs over, the one named last changes fastest.
Arguments:
- tokens_in: bfloat16 [16384, 768], P(('dp', 'head')), may hold values from -6 to 6
- segment: int32 [16, 1024], P('dp'), may hold values from 0 to 7, never falling along the last dimension, each value on 1 to 384 neighbouring positions
- w_qkv: bfloat16 [2, 768, 3, 12, 64], P(None, None, None, 'head'), may hold values from -0.21875 to 0.21875
- qv_bias: bfloat16 [2, 2, 12, 64], P(None, None, 'head'), may hold values from -3 to 3
- w_out: bfloat16 [2, 768, 768], replicated, may hold values from -0.875 to 0.875
- out_bias: bfloat16 [2, 768], replicated, may hold values from -2 to 2
- ln1_gain: bfloat16 [2, 768], replicated, may hold values from 0.25 to 1.75
- ln1_bias: bfloat16 [2, 768], replicated, may hold values from -2 to 2
- w_up: bfloat16 [2, 768, 3072], replicated, may hold values from -0.21875 to 0.21875
- up_bias: bfloat16 [2, 3072], replicated, may hold values from -3 to 3
- w_down: bfloat16 [2, 3072, 768], replicated, may hold values from -0.109375 to 0.109375
- down_bias: bfloat16 [2, 768], replicated, may hold values from -2 to 2
- ln2_gain: bfloat16 [2, 768], replicated, may hold values from 0.25 to 1.75
- ln2_bias: bfloat16 [2, 768], replicated, may hold values from -2 to 2
- cotangent: bfloat16 [16384, 768], P(('dp', 'head')), may hold values from -6 to 6
Outputs:
- output: bfloat16 [16384, 768], P(('dp', 'head'))
- input_grad: float32 [16384, 768], P(('dp', 'head'))
- grad_qkv: float32 [2, 768, 3, 12, 64], P(None, 'dp', None, 'head')
- grad_qv_bias: float32 [2, 2, 12, 64], P(None, None, 'head', 'dp')
- grad_out_w: float32 [2, 768, 768], P(None, ('dp', 'head'))
- grad_out_bias: float32 [2, 768], P(None, ('dp', 'head'))
- grad_ln1_gain: float32 [2, 768], P(None, ('dp', 'head'))
- grad_ln1_bias: float32 [2, 768], P(None, ('dp', 'head'))
- grad_up: float32 [2, 768, 3072], P(None, ('dp', 'head'))
- grad_up_bias: float32 [2, 3072], P(None, ('dp', 'head'))
- grad_down: float32 [2, 3072, 768], P(None, ('dp', 'head'))
- grad_down_bias: float32 [2, 768], P(None, ('dp', 'head'))
- grad_ln2_gain: float32 [2, 768], P(None, ('dp', 'head'))
- grad_ln2_bias: float32 [2, 768], P(None, ('dp', 'head'))
Inputs may be any that keep to these rules, and one draw needn't show every extreme that they name: Along each packed row segment numbers start at 0 and never fall; each of the 8 numbers holds 1 to 384 tokens of the row, some row has one of exactly 384.
All inputs are finite; a program needn't handle non-finite values.
Results may differ from a plain program's by a relative error of at most 0.028.
Values may be sent and summed in bfloat16 or wider, within the bound.
No kernel may reach another device: no remote copies, remote signals or barrier semaphores. Data moves between devices by JAX's collectives and lax.ppermute only.
A program may use at most 320 MiB of HBM per device.

v0:
```python
import jax
import jax.numpy as jnp
from jax import lax
from jax.sharding import PartitionSpec as P

norm_eps = 1e-06
masked_score = -1000000000.0


def norm_rows(rows, gain, shift):
    center = rows - jnp.mean(rows, axis=-1, keepdims=True)
    spread = jnp.mean(center * center, axis=-1, keepdims=True)
    return center * lax.rsqrt(spread + norm_eps) * gain + shift


def gelu_exact(values):
    return jax.nn.gelu(values, approximate=False)


def row_scores(query_row, key_row, labels):
    scores = jnp.einsum("qhd,khd->hqk", query_row, key_row, preferred_element_type=jnp.float32)
    same = labels[:, None] == labels[None, :]
    return jnp.where(same[None], scores, masked_score)


def attend(queries, key_rows, value_rows, segment, heads):
    row_count, seq_len = segment.shape

    def one_row(item):
        query_row, key_row, value_row, labels = item
        scores = row_scores(query_row, key_row, labels)
        top = jnp.max(scores, axis=-1, keepdims=True)
        expo = jnp.exp(scores - top)
        total = jnp.sum(expo, axis=-1, keepdims=True)
        weights = (expo / total).astype(jnp.bfloat16)
        context = jnp.einsum("hqk,khd->qhd", weights, value_row, preferred_element_type=jnp.float32)
        return (context.astype(jnp.bfloat16), top[..., 0] + jnp.log(total[..., 0]))

    def shaped(block):
        return block.reshape(row_count, seq_len, heads, -1)

    context, log_total = lax.map(
        one_row, (shaped(queries), shaped(key_rows), shaped(value_rows), segment)
    )
    return (context.reshape(row_count * seq_len, -1), log_total)


def attend_back(queries, key_rows, value_rows, segment, log_total, grad_context, heads):
    row_count, seq_len = segment.shape

    def one_row(item):
        query_row, key_row, value_row, labels, log_row, grad_row = item
        scores = row_scores(query_row, key_row, labels)
        probs = jnp.exp(scores - log_row[..., None])
        weights = probs.astype(jnp.bfloat16)
        grad_values = jnp.einsum(
            "hqk,qhd->khd", weights, grad_row, preferred_element_type=jnp.float32
        )
        grad_probs = jnp.einsum(
            "qhd,khd->hqk", grad_row, value_row, preferred_element_type=jnp.float32
        )
        delta = jnp.sum(probs * grad_probs, axis=-1, keepdims=True)
        grad_scores = (probs * (grad_probs - delta)).astype(jnp.bfloat16)
        grad_queries = jnp.einsum(
            "hqk,khd->qhd", grad_scores, key_row, preferred_element_type=jnp.float32
        )
        grad_keys = jnp.einsum(
            "hqk,qhd->khd", grad_scores, query_row, preferred_element_type=jnp.float32
        )
        return (
            grad_queries.astype(jnp.bfloat16) * 0.125,
            grad_keys.astype(jnp.bfloat16),
            grad_values.astype(jnp.bfloat16),
        )

    def shaped(block):
        return block.reshape(row_count, seq_len, heads, -1)

    grad_queries, grad_keys, grad_values = lax.map(
        one_row,
        (
            shaped(queries),
            shaped(key_rows),
            shaped(value_rows),
            segment,
            log_total,
            shaped(grad_context),
        ),
    )
    flat = row_count * seq_len
    return jnp.concatenate(
        [
            grad_queries.reshape(flat, -1),
            grad_keys.reshape(flat, -1),
            grad_values.reshape(flat, -1),
        ],
        axis=1,
    )


def per_device(
    tokens_in,
    segment,
    w_qkv,
    qv_bias,
    w_out,
    out_bias,
    ln1_gain,
    ln1_bias,
    w_up,
    up_bias,
    w_down,
    down_bias,
    ln2_gain,
    ln2_bias,
    cotangent,
):
    layers = w_qkv.shape[0]
    width = w_qkv.shape[1]
    local_heads = w_qkv.shape[3]
    head_size = w_qkv.shape[4]
    part = local_heads * head_size
    hidden = tokens_in.astype(jnp.float32)
    saved = []
    for layer_idx in range(layers):
        w_cat = w_qkv[layer_idx].reshape(width, 3 * part)
        rounded = hidden.astype(jnp.bfloat16)
        gathered = lax.all_gather(rounded, "head", axis=0, tiled=True)
        projected = jnp.dot(gathered, w_cat, preferred_element_type=jnp.float32)
        bias_here = qv_bias[layer_idx].reshape(2, part).astype(jnp.float32)
        queries = ((projected[:, :part] + bias_here[0]) * 0.125).astype(jnp.bfloat16)
        key_rows = projected[:, part : 2 * part].astype(jnp.bfloat16)
        value_rows = (projected[:, 2 * part :] + bias_here[1]).astype(jnp.bfloat16)
        context, log_total = attend(queries, key_rows, value_rows, segment, local_heads)
        mixed = lax.all_to_all(context, "head", split_axis=0, concat_axis=1, tiled=True)
        attended = jnp.dot(mixed, w_out[layer_idx], preferred_element_type=jnp.float32) + out_bias[
            layer_idx
        ].astype(jnp.float32)
        resid_one = hidden + attended
        first = norm_rows(
            resid_one,
            ln1_gain[layer_idx].astype(jnp.float32),
            ln1_bias[layer_idx].astype(jnp.float32),
        )
        first_low = first.astype(jnp.bfloat16)
        upward = jnp.dot(first_low, w_up[layer_idx], preferred_element_type=jnp.float32) + up_bias[
            layer_idx
        ].astype(jnp.float32)
        active = gelu_exact(upward).astype(jnp.bfloat16)
        downward = jnp.dot(
            active, w_down[layer_idx], preferred_element_type=jnp.float32
        ) + down_bias[layer_idx].astype(jnp.float32)
        resid_two = first + downward
        saved.append(
            (
                rounded,
                gathered,
                queries,
                key_rows,
                value_rows,
                log_total,
                mixed,
                resid_one,
                first_low,
                upward,
                active,
                resid_two,
            )
        )
        hidden = norm_rows(
            resid_two,
            ln2_gain[layer_idx].astype(jnp.float32),
            ln2_bias[layer_idx].astype(jnp.float32),
        )
    output = hidden.astype(jnp.bfloat16)
    token_terms = [None] * layers
    head_terms = [None] * layers
    grad_hidden = cotangent.astype(jnp.float32)
    for layer_idx in reversed(range(layers)):
        (
            rounded,
            gathered,
            queries,
            key_rows,
            value_rows,
            log_total,
            mixed,
            resid_one,
            first_low,
            upward,
            active,
            resid_two,
        ) = saved[layer_idx]
        w_cat = w_qkv[layer_idx].reshape(width, 3 * part)
        _, norm_pull = jax.vjp(
            norm_rows,
            resid_two,
            ln2_gain[layer_idx].astype(jnp.float32),
            ln2_bias[layer_idx].astype(jnp.float32),
        )
        grad_resid_two, grad_gain_two, grad_shift_two = norm_pull(grad_hidden)
        grad_down_low = grad_resid_two.astype(jnp.bfloat16)
        grad_w_down = jnp.einsum(
            "tf,td->fd", active, grad_down_low, preferred_element_type=jnp.float32
        )
        grad_down_bias = jnp.sum(grad_down_low.astype(jnp.float32), axis=0)
        grad_active = jnp.einsum(
            "td,fd->tf", grad_down_low, w_down[layer_idx], preferred_element_type=jnp.float32
        )
        _, gelu_pull = jax.vjp(gelu_exact, upward)
        grad_up_low = gelu_pull(grad_active)[0].astype(jnp.bfloat16)
        grad_w_up = jnp.einsum(
            "td,tf->df", first_low, grad_up_low, preferred_element_type=jnp.float32
        )
        grad_up_bias = jnp.sum(grad_up_low.astype(jnp.float32), axis=0)
        grad_first = (
            jnp.einsum(
                "tf,df->td", grad_up_low, w_up[layer_idx], preferred_element_type=jnp.float32
            )
            + grad_resid_two
        )
        _, first_pull = jax.vjp(
            norm_rows,
            resid_one,
            ln1_gain[layer_idx].astype(jnp.float32),
            ln1_bias[layer_idx].astype(jnp.float32),
        )
        grad_resid_one, grad_gain_one, grad_shift_one = first_pull(grad_first)
        grad_att_low = grad_resid_one.astype(jnp.bfloat16)
        grad_w_out = jnp.einsum(
            "tc,td->cd", mixed, grad_att_low, preferred_element_type=jnp.float32
        )
        grad_out_bias = jnp.sum(grad_att_low.astype(jnp.float32), axis=0)
        grad_mixed = jnp.einsum(
            "td,cd->tc", grad_att_low, w_out[layer_idx], preferred_element_type=jnp.float32
        ).astype(jnp.bfloat16)
        grad_context = lax.all_to_all(grad_mixed, "head", split_axis=1, concat_axis=0, tiled=True)
        grad_qkv_rows = attend_back(
            queries, key_rows, value_rows, segment, log_total, grad_context, local_heads
        )
        grad_qv = jnp.stack(
            [
                jnp.sum(grad_qkv_rows[:, :part].astype(jnp.float32), axis=0),
                jnp.sum(grad_qkv_rows[:, 2 * part :].astype(jnp.float32), axis=0),
            ]
        ).reshape(2, local_heads, head_size)
        grad_cat = jnp.einsum(
            "td,tc->dc", gathered, grad_qkv_rows, preferred_element_type=jnp.float32
        )
        grad_w_qkv = grad_cat.reshape(width, 3, local_heads, head_size)
        grad_hidden = (
            lax.psum_scatter(
                jnp.einsum(
                    "tc,dc->td", grad_qkv_rows, w_cat, preferred_element_type=jnp.float32
                ).astype(jnp.bfloat16),
                "head",
                scatter_dimension=0,
                tiled=True,
            ).astype(jnp.float32)
            + grad_resid_one
        )
        vectors = jnp.stack(
            [
                grad_out_bias,
                grad_gain_one,
                grad_shift_one,
                grad_down_bias,
                grad_gain_two,
                grad_shift_two,
            ]
        )
        token_terms[layer_idx] = (grad_w_out, grad_w_up, grad_w_down, vectors, grad_up_bias)
        head_terms[layer_idx] = (grad_w_qkv, grad_qv)
    token_stack = tuple(
        (jnp.stack([terms[member] for terms in token_terms]) for member in range(5))
    )
    head_stack = tuple((jnp.stack([terms[member] for terms in head_terms]) for member in range(2)))
    token_stack = (
        lax.psum_scatter(token_stack[0], ("dp", "head"), scatter_dimension=1, tiled=True),
        lax.psum_scatter(token_stack[1], ("dp", "head"), scatter_dimension=1, tiled=True),
        lax.psum_scatter(token_stack[2], ("dp", "head"), scatter_dimension=1, tiled=True),
        lax.psum_scatter(token_stack[3], ("dp", "head"), scatter_dimension=2, tiled=True),
        lax.psum_scatter(token_stack[4], ("dp", "head"), scatter_dimension=1, tiled=True),
    )
    head_stack = (
        lax.psum_scatter(
            head_stack[0].astype(jnp.bfloat16), "dp", scatter_dimension=1, tiled=True
        ).astype(jnp.float32),
        lax.psum_scatter(
            head_stack[1].astype(jnp.bfloat16), "dp", scatter_dimension=3, tiled=True
        ).astype(jnp.float32),
    )
    summed_out_w, summed_up, summed_down, summed_vectors, summed_up_bias = token_stack
    summed_qkv, summed_qv = head_stack
    return (
        output,
        grad_hidden,
        summed_qkv,
        summed_qv,
        summed_out_w,
        summed_vectors[:, 0],
        summed_vectors[:, 1],
        summed_vectors[:, 2],
        summed_up,
        summed_up_bias,
        summed_down,
        summed_vectors[:, 3],
        summed_vectors[:, 4],
        summed_vectors[:, 5],
    )


def solution(mesh):
    return jax.shard_map(
        per_device,
        mesh=mesh,
        in_specs=(
            P(("dp", "head"), None),
            P("dp", None),
            P(None, None, None, "head", None),
            P(None, None, "head", None),
            P(),
            P(),
            P(),
            P(),
            P(),
            P(),
            P(),
            P(),
            P(),
            P(),
            P(("dp", "head"), None),
        ),
        out_specs=(
            P(("dp", "head"), None),
            P(("dp", "head"), None),
            P(None, "dp", None, "head", None),
            P(None, None, "head", "dp"),
            P(None, ("dp", "head"), None),
            P(None, ("dp", "head")),
            P(None, ("dp", "head")),
            P(None, ("dp", "head")),
            P(None, ("dp", "head"), None),
            P(None, ("dp", "head")),
            P(None, ("dp", "head"), None),
            P(None, ("dp", "head")),
            P(None, ("dp", "head")),
            P(None, ("dp", "head")),
        ),
        check_vma=False,
    )
```

profile of v0, /device:TPU:0, one launch (start us, length us, event | category | flops | bytes accessed | tf_op | source)
XLA Modules:
  0.0 1276.6 jit_solution(12847093022919042259)
XLA Ops:
  11.9 63.9 %all-gather.3.cloned.1.call-done = bf16[2048,768]{1,0:T(8,128)(2,1)} async-done(((bf16[512,768]{1,0:T(8,128)(2,1)}), bf16[2048,768]{1,0:T(8,128)(2,1)}) %all-gather.3.cloned.1.call-update) | async-done | bytes 3145744 | tf_op jit(solution)/shard_map/all_gather | solution.py:128
  75.8 3.9 fusion.205
  86.1 26.8 %while.52 = (s32[]{:T(128)}, bf16[2,1024,3,64]{1,3,2,0:T(8,128)(2,1)}, f32[2,3,1024]{2,1,0:T(4,128)S(1)}, bf16[2,1024,3,64]{1,3,2,0:T(8,128)(2,1)}, s32[2,1024]{...) while((s32[]{:T(128)}, ...), condition=%wide.region_3.4_spmd, body=%wide.region_0.3_spmd.sunk | while | flops 834860032 | bytes 47835264 | solution.py:42
  87.0 3.7 select_reduce_fusion.4
  90.7 3.6 fusion.274
  94.3 5.3 fusion.275
  100.3 3.7 select_reduce_fusion.4
  104.0 3.6 fusion.274
  107.6 5.3 fusion.275
  116.2 3.5 all-to-all-start
  122.9 17.1 %all-to-all-done = bf16[4,512,192]{1,2,0:T(8,128)(2,1)S(1)} async-done(((bf16[4,512,192]{1,2,0:T(8,128)(2,1)}), bf16[4,512,192]{1,2,0:T(8,128)(2,1)S(1)}, u32[]{:S(2)}, u32[]{:S(2)}) %all-to-all-start) | async-done | bytes 786464 | tf_op jit(solution)/shard_map/all_to_all | solution.py:135
  143.0 21.2 %multiply_convert_fusion.3 = (bf16[512,3072]{1,0:T(8,128)(2,1)S(1)}, f32[512,3072]{1,0:T(8,128)}, f32[512,3072]{1,0:T(8,128)}) fusion(f32[3072]{0:T(1024)S(1)} %bitcast.451, bf16[2,768,3072]{2,1,0:T(8,128)(2,1)} %param.31, f32[512,768]{1,0:T(8,128)S(1)} %get-tuple-element.480, f32[768]{0:T(1024)S(1)} %get-tuple-element.359, ...), kind=kOutput, calls=%fused_computation.147 | convolution fusion | flops 2521694208 | bytes 22042624 | tf_op jit(solution)/shard_map/dot_general | solution.py:146
  169.6 62.5 %all-gather.5.cloned.1.call-done = bf16[2048,768]{1,0:T(8,128)(2,1)} async-done(((bf16[512,768]{1,0:T(8,128)(2,1)}), bf16[2048,768]{1,0:T(8,128)(2,1)}) %all-gather.5.cloned.1.call-update) | async-done | bytes 3145744 | tf_op jit(solution)/shard_map/all_gather | solution.py:128
  232.1 3.9 fusion.206
  242.4 26.7 %while.53 = (s32[]{:T(128)}, bf16[2,1024,3,64]{1,3,2,0:T(8,128)(2,1)}, f32[2,3,1024]{2,1,0:T(4,128)S(1)}, bf16[2,1024,3,64]{1,3,2,0:T(8,128)(2,1)}, s32[2,1024]{...) while((s32[]{:T(128)}, ...), condition=%wide.region_11.12_spmd, body=%wide.region_8.11_spmd.sunk | while | flops 834860032 | bytes 47835264 | solution.py:42
  243.3 3.7 select_reduce_fusion.5
  247.0 3.6 fusion.277
  250.6 5.3 fusion.278
  256.6 3.7 select_reduce_fusion.5
  260.3 3.6 fusion.277
  263.8 5.3 fusion.278
  271.6 23.0 %all_to_all.70 = bf16[4,512,192]{1,2,0:T(8,128)(2,1)S(1)} all-to-all(bf16[4,512,192]{1,2,0:T(8,128)(2,1)S(1)} %copy.103), channel_id=1, replica_groups=mesh['dp'=8,'head'=4] {'head'}, dimensions={0} | all-to-all | bytes 1572864 | tf_op jit(solution)/shard_map/all_to_all | solution.py:135
  297.7 20.7 %multiply_convert_fusion.2 = (bf16[512,3072]{1,0:T(8,128)(2,1)S(1)}, f32[512,3072]{1,0:T(8,128)}, f32[512,3072]{1,0:T(8,128)}) fusion(f32[3072]{0:T(1024)S(1)} %bitcast.454, bf16[2,768,3072]{2,1,0:T(8,128)(2,1)} %param.31, f32[512,768]{1,0:T(8,128)S(1)} %get-tuple-element.485, f32[768]{0:T(1024)S(1)} %copy-done.114, f32[768]{0:T(1024)S(1)} %copy-done.93, ...), kind=kOutput, calls=%fused_computation.134 | convolution fusion | flops 2521694208 | bytes 22042624 | tf_op jit(solution)/shard_map/dot_general | solution.py:146
  318.4 2.8 fusion.204
  325.2 8.5 convert_reduce_fusion
  333.7 3.6 multiply_reduce_fusion.2
  342.9 3.6 all-to-all-start.2
  346.5 19.6 %all-to-all-done.2 = bf16[512,4,192]{0,2,1:T(8,128)(2,1)S(1)} async-done(((bf16[512,4,192]{0,2,1:T(8,128)(2,1)}), bf16[512,4,192]{0,2,1:T(8,128)(2,1)S(1)}, u32[]{:S(2)}, u32[]{:S(2)}) %all-to-all-start.2) | async-done | bytes 786464 | tf_op jit(solution)/shard_map/all_to_all | solution.py:237
  367.6 3.3 reshape.432
  375.2 48.5 %while.54 = (s32[]{:T(128)}, bf16[2,1024,3,64]{1,3,2,0:T(8,128)(2,1)}, bf16[2,1024,3,64]{1,3,2,0:T(8,128)(2,1)}, bf16[2,1024,3,64]{1,3,2,0:T(8,128)(2,1)}, bf16[...) while((s32[]{:T(128)}, ...), condition=%wide.region_22.23_spmd, body=%wide.region_20.22_spmd.sunk | while | flops 2053436416 | bytes 121484600 | solution.py:79
  377.7 3.4 fusion.290
  381.1 6.9 multiply_reduce_fusion.14
  388.0 7.0 multiply_convert_fusion.6
  401.8 3.4 fusion.290
  405.2 6.9 multiply_reduce_fusion.14
  412.0 7.0 multiply_convert_fusion.6
  430.7 4.1 convolution_convert_fusion.5
  434.8 59.5 %reduce-scatter.14.cloned.1.call-done = bf16[512,768]{1,0:T(8,128)(2,1)} async-done(((bf16[2048,768]{1,0:T(8,128)(2,1)}), bf16[512,768]{1,0:T(8,128)(2,1)}) %reduce-scatter.14.cloned.1.call-update) | async-done | bytes 786448 | tf_op jit(solution)/shard_map/reduce_scatter | solution.py:252
  500.0 8.5 convert_reduce_fusion.1
  508.6 3.6 multiply_reduce_fusion.4
  517.7 3.7 all-to-all-start.3
  521.5 5.6 convolution_convert_fusion.6
  528.8 12.8 %all-to-all-done.3 = bf16[512,4,192]{0,2,1:T(8,128)(2,1)S(1)} async-done(((bf16[512,4,192]{0,2,1:T(8,128)(2,1)}), bf16[512,4,192]{0,2,1:T(8,128)(2,1)S(1)}, u32[]{:S(2)}, u32[]{:S(2)}) %all-to-all-start.3) | async-done | bytes 786464 | tf_op jit(solution)/shard_map/all_to_all | solution.py:237
  543.1 3.3 reshape.436
  550.8 48.4 %while.55 = (s32[]{:T(128)}, bf16[2,1024,3,64]{1,3,2,0:T(8,128)(2,1)}, bf16[2,1024,3,64]{1,3,2,0:T(8,128)(2,1)}, bf16[2,1024,3,64]{1,3,2,0:T(8,128)(2,1)}, bf16[...) while((s32[]{:T(128)}, ...), condition=%wide.region_30.31_spmd, body=%wide.region_28.30_spmd.sunk | while | flops 2053436416 | bytes 121484600 | solution.py:79
  553.3 3.4 fusion.302
  556.7 6.9 multiply_reduce_fusion.15
  563.6 7.1 multiply_convert_fusion.7
  577.4 3.4 fusion.302
  580.8 6.9 multiply_reduce_fusion.15
  587.7 7.1 multiply_convert_fusion.7
  607.5 5.8 copy.131
  613.3 9.1 reshape.462
  622.5 6.1 convolution_convert_fusion.4
  634.6 4.9 convolution_bitcast_fusion.2
  639.6 2.9 convolution_bitcast_fusion.3
  642.5 7.0 pad_maximum_fusion
  650.8 4.7 convolution_bitcast_fusion
  658.3 6.9 pad_maximum_fusion.1
  667.9 42.7 %all-reduce.1 = f32[2,6,768]{2,0,1:T(2,128)S(1)} all-reduce(f32[2,6,768]{2,0,1:T(2,128)S(1)} %pad_maximum_fusion.4), channel_id=7, replica_groups=mesh['dp'=8,'head'=4] {'dp','head'}, use_global_device_ids=true, to_apply=%region_51.52.clone | all-reduce | flops 9216 | bytes 73728
  715.4 13.1 %all-reduce = bf16[2,2,3,64]{3,2,1,0:T(4,128)(2,1)S(1)} all-reduce(bf16[2,2,3,64]{3,2,1,0:T(4,128)(2,1)S(1)} %maximum_maximum_fusion), channel_id=5, replica_groups=mesh['dp'=8,'head'=4] {'dp'}, use_global_device_ids=true, to_apply=%region_37.38.clone | all-reduce | flops 768 | bytes 3072
  735.0 110.6 %reduce-scatter.18.cloned.1.call-done = f32[2,24,768]{2,1,0:T(8,128)} async-done(((f32[2,768,768]{2,1,0:T(8,128)}), f32[2,24,768]{2,1,0:T(8,128)}) %reduce-scatter.18.cloned.1.call-update) | async-done | bytes 147472 | tf_op jit(solution)/shard_map/reduce_scatter | solution.py:279
  845.6 212.3 %reduce-scatter.20.cloned.1.call-done = f32[2,24,3072]{2,1,0:T(8,128)} async-done(((f32[2,768,3072]{2,1,0:T(8,128)}), f32[2,24,3072]{2,1,0:T(8,128)}) %reduce-scatter.20.cloned.1.call-update) | async-done | bytes 589840 | tf_op jit(solution)/shard_map/reduce_scatter | solution.py:280
  1057.8 212.1 %reduce-scatter.22.cloned.1.call-done = f32[2,96,768]{2,1,0:T(8,128)} async-done(((f32[2,3072,768]{2,1,0:T(8,128)}), f32[2,96,768]{2,1,0:T(8,128)}) %reduce-scatter.22.cloned.1.call-update) | async-done | bytes 589840 | tf_op jit(solution)/shard_map/reduce_scatter | solution.py:281
  (525 shorter events, 138.7 us)
Async XLA Ops:
  7.2 68.6 %all-gather.3.cloned.1.call-start = ((), (), s32[]{:S(2)}) async-start(), calls=%async_computation.11 | async-start | bytes 3932160 | tf_op jit(solution)/shard_map/all_gather | solution.py:128
  11.9 63.9 %copy-start.45 = (bf16[1,768,3,3,64]{1,4,3,2,0:T(8,128)(2,1)}, bf16[1,768,3,3,64]{1,4,3,2,0:T(8,128)(2,1)S(1)}, u32[]{:S(2)}) copy-start(bf16[1,768,3,3,64]{1,4,3,2,0:T(8,128)(2,1)S(1)} %get-tuple-element.467) | copy-start | bytes 2654212
  112.9 29.7 %copy-start.56 = (f32[2,3,1024]{2,1,0:T(4,128)}, f32[2,3,1024]{2,1,0:T(4,128)S(1)}, u32[]{:S(2)}) copy-start(f32[2,3,1024]{2,1,0:T(4,128)S(1)} %get-tuple-element.813) | copy-start | bytes 73732
  113.0 8.7 copy-start.99
  113.0 9.3 copy-start.64
  113.0 27.1 %copy-start.51 = (bf16[512,768]{1,0:T(8,128)(2,1)S(1)}, bf16[512,768]{1,0:T(8,128)(2,1)}, u32[]{:S(2)}) copy-start(bf16[512,768]{1,0:T(8,128)(2,1)} %param.23) | copy-start | bytes 2359300
  116.2 23.8 %all-to-all-start = ((bf16[4,512,192]{1,2,0:T(8,128)(2,1)}), bf16[4,512,192]{1,2,0:T(8,128)(2,1)S(1)}, u32[]{:S(2)}, u32[]{:S(2)}) async-start(bf16[4,512,192]{1,2,0:T(8,128)(2,1)} %copy.98), calls=%async_computation | async-start | bytes 1572864 | tf_op jit(solution)/shard_map/all_to_all | solution.py:135
  119.7 112.4 %all-gather.5.cloned.1.call-start = ((), (), s32[]{:S(2)}) async-start(), calls=%async_computation.12 | async-start | bytes 3932160 | tf_op jit(solution)/shard_map/all_gather | solution.py:128
  121.7 42.5 %copy-start.90 = (f32[768]{0:T(1024)}, f32[768]{0:T(1024)S(1)}, u32[]{:S(2)}) copy-start(f32[768]{0:T(1024)S(1)} %get-tuple-element.497) | copy-start | bytes 9220
  121.7 42.5 %copy-start.112 = (f32[768]{0:T(1024)}, f32[768]{0:T(1024)S(1)}, u32[]{:S(2)}) copy-start(f32[768]{0:T(1024)S(1)} %get-tuple-element.359) | copy-start | bytes 9220
  122.3 172.3 %copy-start.60 = (f32[768]{0:T(1024)}, f32[768]{0:T(1024)S(1)}, u32[]{:S(2)}) copy-start(f32[768]{0:T(1024)S(1)} %get-tuple-element.499) | copy-start | bytes 9220
  122.9 41.2 %copy-start.101 = (f32[1,3072]{1,0:T(1,128)}, f32[1,3072]{1,0:T(1,128)S(1)}, u32[]{:S(2)}) copy-start(f32[1,3072]{1,0:T(1,128)S(1)} %get-tuple-element.476) | copy-start | bytes 36868
  140.1 24.1 %copy-start.37 = (bf16[4,512,192]{1,2,0:T(8,128)(2,1)}, bf16[4,512,192]{1,2,0:T(8,128)(2,1)S(1)}, u32[]{:S(2)}) copy-start(bf16[4,512,192]{1,2,0:T(8,128)(2,1)S(1)} %all-to-all-done) | copy-start | bytes 2359300
  140.1 24.2 %slice-start = ((s8[9437184]{0:T(1024)(128)(4,1)}), s8[4194304]{0:T(1024)(128)(4,1)S(1)}, s32[]{:S(2)}) async-start(s8[9437184]{0:T(1024)(128)(4,1)} %bitcast.461), calls=%async_computation.20 | async-start | bytes 8388608
  142.6 21.6 %copy-start.27 = (f32[512,768]{1,0:T(8,128)}, f32[512,768]{1,0:T(8,128)S(1)}, u32[]{:S(2)}) copy-start(f32[512,768]{1,0:T(8,128)S(1)} %get-tuple-element.480) | copy-start | bytes 4718596
  142.6 21.6 %copy-start.72 = (f32[512]{0:T(512)}, f32[512]{0:T(512)S(1)}, u32[]{:S(2)}) copy-start(f32[512]{0:T(512)S(1)} %broadcast_multiply_fusion.3) | copy-start | bytes 6148
  142.9 21.2 %copy-start.77 = (f32[512]{0:T(512)}, f32[512]{0:T(512)S(1)}, u32[]{:S(2)}) copy-start(f32[512]{0:T(512)S(1)} %multiply_reduce_fusion.11) | copy-start | bytes 6148
  143.0 21.3 %copy-start.105 = (f32[512]{0:T(512)}, f32[512]{0:T(512)S(1)}, u32[]{:S(2)}) copy-start(f32[512]{0:T(512)S(1)} %fusion.179) | copy-start | bytes 6148
  143.0 21.3 %slice-start.1 = ((s8[9437184]{0:T(1024)(128)(4,1)}), s8[4194304]{0:T(1024)(128)(4,1)S(1)}, s32[]{:S(2)}) async-start(s8[9437184]{0:T(1024)(128)(4,1)} %bitcast.461), calls=%async_computation.21 | async-start | bytes 8388608
  143.0 21.3 %slice-start.2 = ((s8[9437184]{0:T(1024)(128)(4,1)}), s8[1048576]{0:T(1024)(128)(4,1)S(1)}, s32[]{:S(2)}) async-start(s8[9437184]{0:T(1024)(128)(4,1)} %bitcast.461), calls=%async_computation.22 | async-start | bytes 2097152
  167.1 65.1 %copy-start.47 = (bf16[1,768,3,3,64]{1,4,3,2,0:T(8,128)(2,1)S(1)}, bf16[1,768,3,3,64]{1,4,3,2,0:T(8,128)(2,1)}, u32[]{:S(2)}) copy-start(bf16[1,768,3,3,64]{1,4,3,2,0:T(8,128)(2,1)} %get-tuple-element.466) | copy-start | bytes 2654212
  167.1 127.5 %copy-start.62 = (f32[512]{0:T(512)}, f32[512]{0:T(512)S(1)}, u32[]{:S(2)}) copy-start(f32[512]{0:T(512)S(1)} %broadcast_multiply_fusion.2) | copy-start | bytes 6148
  167.4 68.7 %copy-start.79 = (f32[512]{0:T(512)}, f32[512]{0:T(512)S(1)}, u32[]{:S(2)}) copy-start(f32[512]{0:T(512)S(1)} %multiply_reduce_fusion.10) | copy-start | bytes 6148
  167.4 127.2 %copy-start.66 = (f32[512]{0:T(512)}, f32[512]{0:T(512)S(1)}, u32[]{:S(2)}) copy-start(f32[512]{0:T(512)S(1)} %fusion.180) | copy-start | bytes 6148
  269.2 25.4 %copy-start.7 = (f32[512,768]{1,0:T(8,128)S(1)}, f32[512,768]{1,0:T(8,128)}, u32[]{:S(2)}) copy-start(f32[512,768]{1,0:T(8,128)} %copy-done.6) | copy-start | bytes 4718596
  269.2 25.4 %copy-start.117 = (f32[768]{0:T(1024)S(1)}, f32[768]{0:T(1024)}, u32[]{:S(2)}) copy-start(f32[768]{0:T(1024)} %get-tuple-element.360) | copy-start | bytes 9220
  271.6 26.0 %copy-start.93 = (f32[768]{0:T(1024)S(1)}, f32[768]{0:T(1024)}, u32[]{:S(2)}) copy-start(f32[768]{0:T(1024)} %get-tuple-element.498) | copy-start | bytes 9220
  271.6 26.0 %copy-start.104 = (f32[1,3072]{1,0:T(1,128)S(1)}, f32[1,3072]{1,0:T(1,128)}, u32[]{:S(2)}) copy-start(f32[1,3072]{1,0:T(1,128)} %get-tuple-element.475) | copy-start | bytes 36868
  271.6 26.0 %copy-start.114 = (f32[768]{0:T(1024)S(1)}, f32[768]{0:T(1024)}, u32[]{:S(2)}) copy-start(f32[768]{0:T(1024)} %get-tuple-element.358) | copy-start | bytes 9220
  294.6 23.7 %slice-start.3 = ((s8[9437184]{0:T(1024)(128)(4,1)}), s8[4194304]{0:T(1024)(128)(4,1)S(1)}, s32[]{:S(2)}) async-start(s8[9437184]{0:T(1024)(128)(4,1)} %bitcast.463), calls=%async_computation.23 | async-start | bytes 8388608
  297.3 40.1 %copy-start.30 = (f32[512,768]{1,0:T(8,128)}, f32[512,768]{1,0:T(8,128)S(1)}, u32[]{:S(2)}) copy-start(f32[512,768]{1,0:T(8,128)S(1)} %get-tuple-element.485) | copy-start | bytes 4718596
  297.3 40.1 %copy-start.75 = (f32[512]{0:T(512)}, f32[512]{0:T(512)S(1)}, u32[]{:S(2)}) copy-start(f32[512]{0:T(512)S(1)} %broadcast_multiply_fusion.1) | copy-start | bytes 6148
  297.6 39.8 %copy-start.108 = (f32[512]{0:T(512)}, f32[512]{0:T(512)S(1)}, u32[]{:S(2)}) copy-start(f32[512]{0:T(512)S(1)} %fusion.181) | copy-start | bytes 6148
  297.6 20.7 %copy-start.116 = (f32[768]{0:T(1024)S(1)}, f32[768]{0:T(1024)}, u32[]{:S(2)}) copy-start(f32[768]{0:T(1024)} %get-tuple-element.354) | copy-start | bytes 9220
  297.7 20.7 %slice-start.4 = ((s8[9437184]{0:T(1024)(128)(4,1)}), s8[4194304]{0:T(1024)(128)(4,1)S(1)}, s32[]{:S(2)}) async-start(s8[9437184]{0:T(1024)(128)(4,1)} %bitcast.463), calls=%async_computation.24 | async-start | bytes 8388608
  297.7 20.7 %slice-start.5 = ((s8[9437184]{0:T(1024)(128)(4,1)}), s8[1048576]{0:T(1024)(128)(4,1)S(1)}, s32[]{:S(2)}) async-start(s8[9437184]{0:T(1024)(128)(4,1)} %bitcast.463), calls=%async_computation.25 | async-start | bytes 2097152
  322.8 10.9 slice-start.6
  342.9 32.3 %copy-start.4 = (bf16[2,1024,3,64]{1,3,2,0:T(8,128)(2,1)S(1)}, bf16[2,1024,3,64]{1,3,2,0:T(8,128)(2,1)}, u32[]{:S(2)}) copy-start(bf16[2,1024,3,64]{1,3,2,0:T(8,128)(2,1)} %get-tuple-element.854) | copy-start | bytes 2359300
  342.9 32.3 %copy-start.5 = (bf16[2,1024,3,64]{1,3,2,0:T(8,128)(2,1)S(1)}, bf16[2,1024,3,64]{1,3,2,0:T(8,128)(2,1)}, u32[]{:S(2)}) copy-start(bf16[2,1024,3,64]{1,3,2,0:T(8,128)(2,1)} %get-tuple-element.855) | copy-start | bytes 2359300
  342.9 32.3 %copy-start.14 = (bf16[2,1024,3,64]{1,3,2,0:T(8,128)(2,1)S(1)}, bf16[2,1024,3,64]{1,3,2,0:T(8,128)(2,1)}, u32[]{:S(2)}) copy-start(bf16[2,1024,3,64]{1,3,2,0:T(8,128)(2,1)} %get-tuple-element.859) | copy-start | bytes 2359300
  342.9 23.2 %all-to-all-start.2 = ((bf16[512,4,192]{0,2,1:T(8,128)(2,1)}), bf16[512,4,192]{0,2,1:T(8,128)(2,1)S(1)}, u32[]{:S(2)}, u32[]{:S(2)}) async-start(bf16[512,4,192]{0,2,1:T(8,128)(2,1)} %bitcast.426), calls=%async_computation.2 | async-start | bytes 1572864 | tf_op jit(solution)/shard_map/all_to_all | solution.py:237
  346.5 147.8 %reduce-scatter.14.cloned.1.call-start = ((), (), s32[]{:S(2)}) async-start(), calls=%async_computation.13 | async-start | bytes 3932160 | tf_op jit(solution)/shard_map/reduce_scatter | solution.py:252
  430.7 63.6 %copy-start.8 = (f32[512,768]{1,0:T(8,128)S(1)}, f32[512,768]{1,0:T(8,128)}, u32[]{:S(2)}) copy-start(f32[512,768]{1,0:T(8,128)} %copy-done.6) | copy-start | bytes 4718596
  430.7 63.6 %copy-start.10 = (f32[512,768]{1,0:T(8,128)S(1)}, f32[512,768]{1,0:T(8,128)}, u32[]{:S(2)}) copy-start(f32[512,768]{1,0:T(8,128)} %copy-done.9) | copy-start | bytes 4718596
  430.7 63.6 %copy-start.61 = (f32[768]{0:T(1024)S(1)}, f32[768]{0:T(1024)}, u32[]{:S(2)}) copy-start(f32[768]{0:T(1024)} %copy-done.60) | copy-start | bytes 9220
  430.7 63.6 %copy-start.63 = (f32[512]{0:T(512)S(1)}, f32[512]{0:T(512)}, u32[]{:S(2)}) copy-start(f32[512]{0:T(512)} %copy-done.62) | copy-start | bytes 6148
  430.7 63.6 %copy-start.67 = (f32[512]{0:T(512)S(1)}, f32[512]{0:T(512)}, u32[]{:S(2)}) copy-start(f32[512]{0:T(512)} %copy-done.66) | copy-start | bytes 6148
  430.7 63.6 %copy-start.69 = (f32[512]{0:T(512)S(1)}, f32[512]{0:T(512)}, u32[]{:S(2)}) copy-start(f32[512]{0:T(512)} %copy-done.68) | copy-start | bytes 6148
  434.8 62.2 %copy-start.80 = (f32[512]{0:T(512)S(1)}, f32[512]{0:T(512)}, u32[]{:S(2)}) copy-start(f32[512]{0:T(512)} %copy-done.79) | copy-start | bytes 6148
  499.1 9.4 slice-start.9
  517.7 23.9 %all-to-all-start.3 = ((bf16[512,4,192]{0,2,1:T(8,128)(2,1)}), bf16[512,4,192]{0,2,1:T(8,128)(2,1)S(1)}, u32[]{:S(2)}, u32[]{:S(2)}) async-start(bf16[512,4,192]{0,2,1:T(8,128)(2,1)} %bitcast.54), calls=%async_computation.4 | async-start | bytes 1572864 | tf_op jit(solution)/shard_map/all_to_all | solution.py:237
  521.5 189.8 %reduce-scatter.26.cloned.1.call-start = ((), (), s32[]{:S(2)}) async-start(), calls=%async_computation.19 | async-start | bytes 1622016
  528.7 22.0 %copy-start.2 = (bf16[2,1024,3,64]{1,3,2,0:T(8,128)(2,1)S(1)}, bf16[2,1024,3,64]{1,3,2,0:T(8,128)(2,1)}, u32[]{:S(2)}) copy-start(bf16[2,1024,3,64]{1,3,2,0:T(8,128)(2,1)} %get-tuple-element.852) | copy-start | bytes 2359300
  528.7 22.0 %copy-start.3 = (bf16[2,1024,3,64]{1,3,2,0:T(8,128)(2,1)S(1)}, bf16[2,1024,3,64]{1,3,2,0:T(8,128)(2,1)}, u32[]{:S(2)}) copy-start(bf16[2,1024,3,64]{1,3,2,0:T(8,128)(2,1)} %get-tuple-element.853) | copy-start | bytes 2359300
  528.7 22.0 %copy-start.13 = (bf16[2,1024,3,64]{1,3,2,0:T(8,128)(2,1)S(1)}, bf16[2,1024,3,64]{1,3,2,0:T(8,128)(2,1)}, u32[]{:S(2)}) copy-start(bf16[2,1024,3,64]{1,3,2,0:T(8,128)(2,1)} %get-tuple-element.858) | copy-start | bytes 2359300
  528.7 22.0 %copy-start.57 = (f32[2,3,1024]{2,1,0:T(4,128)S(1)}, f32[2,3,1024]{2,1,0:T(4,128)}, u32[]{:S(2)}) copy-start(f32[2,3,1024]{2,1,0:T(4,128)} %copy-done.56) | copy-start | bytes 73732
  528.8 200.4 %reduce-scatter.24.cloned.1.call-start = ((), (), s32[]{:S(2)}) async-start(), calls=%async_computation.18 | async-start | bytes 1990656
  613.3 9.2 copy-start.46
  622.4 110.1 %reduce-scatter.16.cloned.1.call-start = ((), (), s32[]{:S(2)}) async-start(), calls=%async_computation.14 | async-start | bytes 3932160 | tf_op jit(solution)/shard_map/reduce_scatter | solution.py:252
  628.6 217.0 %reduce-scatter.18.cloned.1.call-start = ((), (), s32[]{:S(2)}) async-start(), calls=%async_computation.15 | async-start | bytes 4866048 | tf_op jit(solution)/shard_map/reduce_scatter | solution.py:279
  633.2 424.6 %reduce-scatter.20.cloned.1.call-start = ((), (), s32[]{:S(2)}) async-start(), calls=%async_computation.16 | async-start | bytes 19464192 | tf_op jit(solution)/shard_map/reduce_scatter | solution.py:280
  649.5 620.5 %reduce-scatter.22.cloned.1.call-start = ((), (), s32[]{:S(2)}) async-start(), calls=%async_computation.17 | async-start | bytes 19464192 | tf_op jit(solution)/shard_map/reduce_scatter | solution.py:281
  665.3 67.2 %copy-start.12 = (f32[512,768]{1,0:T(8,128)S(1)}, f32[512,768]{1,0:T(8,128)}, u32[]{:S(2)}) copy-start(f32[512,768]{1,0:T(8,128)} %copy-done.11) | copy-start | bytes 4718596
  665.3 67.2 %copy-start.71 = (f32[512]{0:T(512)S(1)}, f32[512]{0:T(512)}, u32[]{:S(2)}) copy-start(f32[512]{0:T(512)} %copy-done.70) | copy-start | bytes 6148
  (108 other events, 414.3 us)
Sparse Core Ops, SparseCore 0:
  9.6 66.1 all-gather.2
  169.5 62.5 all-gather.4
  434.9 59.2 reduce-scatter.13
  528.9 98.4 reduce-scatter.25
  630.6 38.3 reduce-scatter.23
  671.2 61.2 reduce-scatter.15
  738.5 106.9 reduce-scatter.17
  853.7 204.1 reduce-scatter.19
  1066.0 203.9 reduce-scatter.21
where the time goes:
time: 1280 us
  waiting for transfers between devices  772 us (60%)
  matrix products  218 us (17%)
  other arithmetic  89.5 us (7%)
  local copies, waits for them, and re-layouts  88.3 us (7%)
  blocking collectives  78.8 us (6%)
  between operations  16.6 us (1%)
    reduce_scatter x1, waiting for transfers between devices, per_device(): lax.psum_scatter(token_stack[1], ('dp', 'head'), scatter_dimension=1, til...  212 us
    reduce_scatter x1, waiting for transfers between devices, per_device(): lax.psum_scatter(token_stack[2], ('dp', 'head'), scatter_dimension=1, til...  212 us
    all_gather x2, waiting for transfers between devices, per_device(): gathered = lax.all_gather(rounded, 'head', axis=0, tiled=True)  126 us
    reduce_scatter x1, waiting for transfers between devices, per_device(): lax.psum_scatter(token_stack[0], ('dp', 'head'), scatter_dimension=1, til...  111 us
    reduce_scatter x2, waiting for transfers between devices, per_device(): lax.psum_scatter(jnp.einsum('tc,dc->td', grad_qkv_rows, w_cat, preferred_...  60 us
    unnamed x2, blocking collectives  55.8 us
    dot_general x2, matrix products, per_device(): jnp.dot(first_low, w_up[layer_idx], preferred_element_type=jnp.float32)  41.8 us
    unnamed x282, local copies, waits for them, and re-layouts  32.5 us
  transfers between devices with their start and end apart: 12, of which 10 were waited for; matrix products, arithmetic and copies ran while one was open for 11% of the time, Pallas kernels for 0%

commit v1 on v0

v1 whole, which is shorter than its diff:
```python
import functools

import jax
import jax.numpy as jnp
from jax import lax
from jax.experimental import pallas as pl
from jax.experimental.pallas import tpu as pltpu
from jax.sharding import PartitionSpec as P

norm_eps = 1e-06
masked_score = -1000000000.0
f32 = jnp.float32
bf16 = jnp.bfloat16

BLK = 128
HALO = 384


def swap(value, axis, bit):
    size = lax.axis_size(axis)
    return lax.ppermute(value, axis, [(i, i ^ bit) for i in range(size)])


def bit_of(axis, place):
    return (lax.axis_index(axis) >> place) & 1


def pick(value, index, axis):
    return lax.dynamic_index_in_dim(value, index, axis, keepdims=False)


def add_low(*terms):
    total = terms[0].astype(f32)
    for term in terms[1:]:
        total = total + term.astype(f32)
    return total


def halve_dp(held, order, low):
    left = sorted(order, reverse=True)
    for place in order:
        axis = left.index(place)
        mine = bit_of("dp", place)
        got = swap(pick(held, 1 - mine, axis), "dp", 1 << place)
        held = add_low(pick(held, mine, axis), got)
        if low:
            held = held.astype(bf16)
        left.remove(place)
    return held


def finish_head(slot):
    size = lax.axis_size("head")
    me = lax.axis_index("head")
    got = [swap(slot(me ^ step), "head", step) for step in range(1, size)]
    return add_low(slot(me), *got)


def head_masks():
    lane = lax.broadcasted_iota(jnp.int32, (BLK, BLK), 1)
    return lane < BLK // 2


def stack_heads(pair, low):
    zero = jnp.zeros_like(pair)
    return jnp.concatenate([jnp.where(low, pair, zero), jnp.where(low, zero, pair)], axis=0)


def nt(left, right):
    return lax.dot_general(left, right, (((1,), (1,)), ((), ())), preferred_element_type=f32)


def nn(left, right):
    return lax.dot_general(left, right, (((1,), (0,)), ((), ())), preferred_element_type=f32)


def attend_kernel(pairs, own_blocks, halo_blocks, bounds, segq, segk, qkv, kvh, ctx, lse, vt, qs, top, total, acc):
    width = pairs * BLK
    low = head_masks()
    half = BLK // 2
    for j in range(own_blocks + halo_blocks):
        for p in range(pairs):
            if j < own_blocks:
                tile = qkv[j * BLK : (j + 1) * BLK, 2 * width + p * BLK : 2 * width + (p + 1) * BLK]
            else:
                at = j - own_blocks
                tile = kvh[at * BLK : (at + 1) * BLK, width + p * BLK : width + (p + 1) * BLK]
            vt[j, p * BLK : (p + 1) * BLK, :] = tile.T

    def q_block(i, carry):
        rows = pl.ds(pl.multiple_of(i * BLK, BLK), BLK)
        for p in range(pairs):
            qs[p] = stack_heads(qkv[rows, p * BLK : (p + 1) * BLK], low)
        top[...] = jnp.full(top.shape, -1e30, f32)
        total[...] = jnp.zeros(total.shape, f32)
        acc[...] = jnp.zeros(acc.shape, f32)
        labels = segq[i]

        def k_block(ref, first, base, j, carry):
            here = pl.ds(pl.multiple_of(j * BLK, BLK), BLK)
            there = pl.ds(pl.multiple_of((base + j) * BLK, BLK), BLK)
            same = segk[there, :] == labels
            for p in range(pairs):
                keys = ref[here, first + p * BLK : first + (p + 1) * BLK]
                scores = jnp.where(same, nt(keys, qs[p]), masked_score)
                old = top[p : p + 1, :]
                new = jnp.maximum(old, jnp.max(scores, axis=0, keepdims=True))
                expo = jnp.exp(scores - new)
                scale = jnp.exp(old - new)
                top[p : p + 1, :] = new
                total[p : p + 1, :] = total[p : p + 1, :] * scale + jnp.sum(expo, axis=0, keepdims=True)
                weights = expo.astype(bf16)
                for h in range(2):
                    values = vt[base + j, p * BLK + h * half : p * BLK + (h + 1) * half, :]
                    part = slice(h * half, (h + 1) * half)
                    cols = slice(h * BLK, (h + 1) * BLK)
                    acc[p, part, :] = acc[p, part, :] * scale[:, cols] + nn(values, weights[:, cols])
            return carry

        lax.fori_loop(bounds[i, 0], bounds[i, 1], functools.partial(k_block, qkv, width, 0), 0)
        lax.fori_loop(bounds[i, 2], bounds[i, 3], functools.partial(k_block, kvh, 0, own_blocks), 0)
        for p in range(pairs):
            inverse = 1.0 / total[p : p + 1, :]
            flat = jnp.concatenate(
                [acc[p, :half, :] * inverse[:, :BLK], acc[p, half:, :] * inverse[:, BLK:]], axis=0
            )
            ctx[rows, p * BLK : (p + 1) * BLK] = flat.T.astype(bf16)
        lse[i] = top[...] + jnp.log(total[...])
        return carry

    lax.fori_loop(0, own_blocks, q_block, 0)


def attend_back_kernel(
    pairs, own_blocks, halo_blocks,
    bounds, segq, segk, qkv, kvh, ctx, lse, dctx,
    dqkv, dkvh, sums,
    kt, qs, cs, delta, dqt, dk, dv,
):
    width = pairs * BLK
    low = head_masks()
    half = BLK // 2
    blocks = own_blocks + halo_blocks
    for j in range(blocks):
        for p in range(pairs):
            if j < own_blocks:
                tile = qkv[j * BLK : (j + 1) * BLK, width + p * BLK : width + (p + 1) * BLK]
            else:
                at = j - own_blocks
                tile = kvh[at * BLK : (at + 1) * BLK, p * BLK : (p + 1) * BLK]
            kt[j, p * BLK : (p + 1) * BLK, :] = tile.T
    dk[...] = jnp.zeros(dk.shape, f32)
    dv[...] = jnp.zeros(dv.shape, f32)
    sums[...] = jnp.zeros(sums.shape, f32)

    def q_block(i, carry):
        rows = pl.ds(pl.multiple_of(i * BLK, BLK), BLK)
        for p in range(pairs):
            cols = slice(p * BLK, (p + 1) * BLK)
            qs[p] = stack_heads(qkv[rows, cols], low)
            pull = dctx[rows, cols]
            cs[p] = stack_heads(pull, low)
            prod = (pull.astype(f32) * ctx[rows, cols].astype(f32)).T
            delta[p : p + 1, :] = jnp.concatenate(
                [jnp.sum(prod[:half], axis=0, keepdims=True), jnp.sum(prod[half:], axis=0, keepdims=True)], axis=1
            )
        dqt[...] = jnp.zeros(dqt.shape, f32)
        labels = segq[i]

        def k_block(ref, first, base, j, carry):
            here = pl.ds(pl.multiple_of(j * BLK, BLK), BLK)
            there = pl.ds(pl.multiple_of((base + j) * BLK, BLK), BLK)
            same = segk[there, :] == labels
            for p in range(pairs):
                cols = slice(p * BLK, (p + 1) * BLK)
                keys = ref[here, first + p * BLK : first + (p + 1) * BLK]
                values = ref[here, first + width + p * BLK : first + width + (p + 1) * BLK]
                scores = jnp.where(same, nt(keys, qs[p]), masked_score)
                probs = jnp.exp(scores - lse[i, p : p + 1, :])
                pulls = nt(values, cs[p])
                dscore = (probs * (pulls - delta[p : p + 1, :])).astype(bf16)
                dv[there, cols] += nn(probs.astype(bf16), cs[p])
                dk[there, cols] += nn(dscore, qs[p])
                for h in range(2):
                    part = slice(h * half, (h + 1) * half)
                    flip = kt[base + j, p * BLK + h * half : p * BLK + (h + 1) * half, :]
                    dqt[p, part, :] += nn(flip, dscore[:, h * BLK : (h + 1) * BLK])
            return carry

        lax.fori_loop(bounds[i, 0], bounds[i, 1], functools.partial(k_block, qkv, width, 0), 0)
        lax.fori_loop(bounds[i, 2], bounds[i, 3], functools.partial(k_block, kvh, 0, own_blocks), 0)
        for p in range(pairs):
            cols = slice(p * BLK, (p + 1) * BLK)
            grad = dqt[p].T.astype(bf16) * jnp.asarray(0.125, bf16)
            dqkv[rows, cols] = grad
            sums[0:1, cols] += jnp.sum(grad.astype(f32), axis=0, keepdims=True)
        return carry

    lax.fori_loop(0, own_blocks, q_block, 0)
    for j in range(blocks):
        rows = slice(j * BLK, (j + 1) * BLK)
        grad_k = dk[rows, :].astype(bf16)
        grad_v = dv[rows, :].astype(bf16)
        if j < own_blocks:
            dqkv[rows, width : 2 * width] = grad_k
            dqkv[rows, 2 * width :] = grad_v
        else:
            back = slice((j - own_blocks) * BLK, (j - own_blocks + 1) * BLK)
            dkvh[back, :width] = grad_k
            dkvh[back, width:] = grad_v
        sums[1:2, :] += jnp.sum(grad_v.astype(f32), axis=0, keepdims=True)


def vmem_specs(count):
    return [pl.BlockSpec(memory_space=pltpu.VMEM)] * count


def attend(bounds, segq, segk, qkv, kvh):
    tokens, width3 = qkv.shape
    width = width3 // 3
    pairs, own_blocks, halo_blocks = width // BLK, tokens // BLK, kvh.shape[0] // BLK
    blocks = own_blocks + halo_blocks
    return pl.pallas_call(
        functools.partial(attend_kernel, pairs, own_blocks, halo_blocks),
        out_shape=(
            jax.ShapeDtypeStruct((tokens, width), bf16),
            jax.ShapeDtypeStruct((own_blocks, 8, 2 * BLK), f32),
        ),
        in_specs=[pl.BlockSpec(memory_space=pltpu.SMEM)] + vmem_specs(4),
        out_specs=tuple(vmem_specs(2)),
        scratch_shapes=[
            pltpu.VMEM((blocks, width, BLK), bf16),
            pltpu.VMEM((pairs, 2 * BLK, BLK), bf16),
            pltpu.VMEM((8, 2 * BLK), f32),
            pltpu.VMEM((8, 2 * BLK), f32),
            pltpu.VMEM((pairs, BLK, BLK), f32),
        ],
        compiler_params=pltpu.CompilerParams(vmem_limit_bytes=32 * 2**20),
        cost_estimate=pl.CostEstimate(flops=2 * 10**9, bytes_accessed=6 * 10**6, transcendentals=10**6),
        name="attend",
    )(bounds, segq, segk, qkv, kvh)


def attend_back(bounds, segq, segk, qkv, kvh, ctx, lse, dctx):
    tokens, width3 = qkv.shape
    width = width3 // 3
    pairs, own_blocks, halo_blocks = width // BLK, tokens // BLK, kvh.shape[0] // BLK
    blocks = own_blocks + halo_blocks
    return pl.pallas_call(
        functools.partial(attend_back_kernel, pairs, own_blocks, halo_blocks),
        out_shape=(
            jax.ShapeDtypeStruct((tokens, width3), bf16),
            jax.ShapeDtypeStruct(kvh.shape, bf16),
            jax.ShapeDtypeStruct((8, width), f32),
        ),
        in_specs=[pl.BlockSpec(memory_space=pltpu.SMEM)] + vmem_specs(7),
        out_specs=tuple(vmem_specs(3)),
        scratch_shapes=[
            pltpu.VMEM((blocks, width, BLK), bf16),
            pltpu.VMEM((pairs, 2 * BLK, BLK), bf16),
            pltpu.VMEM((pairs, 2 * BLK, BLK), bf16),
            pltpu.VMEM((8, 2 * BLK), f32),
            pltpu.VMEM((pairs, BLK, BLK), f32),
            pltpu.VMEM((blocks * BLK, width), f32),
            pltpu.VMEM((blocks * BLK, width), f32),
        ],
        compiler_params=pltpu.CompilerParams(vmem_limit_bytes=40 * 2**20),
        cost_estimate=pl.CostEstimate(flops=6 * 10**9, bytes_accessed=12 * 10**6, transcendentals=10**6),
        name="attend_back",
    )(bounds, segq, segk, qkv, kvh, ctx, lse, dctx)


def erf_parts(values):
    density = jnp.exp(-0.5 * values * values) * 0.3989422804014327
    return 0.5 * (1.0 + lax.erf(values * 0.7071067811865476)), density


def normalized(rows):
    center = rows - jnp.mean(rows, axis=-1, keepdims=True)
    spread = jnp.mean(center * center, axis=-1, keepdims=True)
    scale = lax.rsqrt(spread + norm_eps)
    return center * scale, scale


def norm_back(grad, gain, unit, scale):
    lifted = grad * gain
    first = jnp.mean(lifted, axis=-1, keepdims=True)
    second = jnp.mean(lifted * unit, axis=-1, keepdims=True)
    return (
        scale * (lifted - first - unit * second),
        jnp.sum(grad * unit, axis=0),
        jnp.sum(grad, axis=0),
    )


def nt_low(left, right):
    return nt(left, right).astype(bf16)


def rows_by_core(block, bits):
    tokens, columns = block.shape
    return block.reshape(tokens, 1 << (bits - 1), 2, columns >> bits)


def grad_halves(left, right, bits):
    view = rows_by_core(left, bits)
    mine = bit_of("dp", 0)

    def part(index):
        chosen = pick(view, index, 2).reshape(left.shape[0], -1)
        return lax.dot_general(chosen, right, (((0,), (0,)), ((), ())), preferred_element_type=f32).astype(bf16)

    return part(1 - mine), part(mine)


def per_device(
    tokens_in,
    segment,
    w_qkv,
    qv_bias,
    w_out,
    out_bias,
    ln1_gain,
    ln1_bias,
    w_up,
    up_bias,
    w_down,
    down_bias,
    ln2_gain,
    ln2_bias,
    cotangent,
):
    layers, width = w_qkv.shape[0], w_qkv.shape[1]
    part = w_qkv.shape[3] * w_qkv.shape[4]
    head_size = w_qkv.shape[4]
    tokens = tokens_in.shape[0]
    seq = segment.shape[1]
    dp, head = lax.axis_size("dp"), lax.axis_size("head")
    bits = dp.bit_length() - 1
    shard = lax.axis_index("head")
    halves = seq // tokens
    row, half = shard // halves, shard % halves
    forward_order = list(range(1, bits))
    backward_order = forward_order[::-1]

    labels = pick(segment, row, 0)
    own_labels = lax.dynamic_slice_in_dim(labels, half * tokens, tokens)
    halo_start = jnp.where(half == 0, tokens, tokens - HALO)
    halo_labels = lax.dynamic_slice_in_dim(labels, halo_start, HALO)
    edge = jnp.where(half == 0, tokens - HALO, 0)
    blocks = tokens // BLK
    by_block = own_labels.reshape(blocks, BLK)
    least, most = by_block[:, :1], by_block[:, -1:]

    def count(flags):
        return jnp.sum(flags.astype(jnp.int32), axis=1)

    bounds = jnp.stack(
        [
            count(own_labels[None] < least) // BLK,
            (count(own_labels[None] <= most) + BLK - 1) // BLK,
            count(halo_labels[None] < least) // BLK,
            (count(halo_labels[None] <= most) + BLK - 1) // BLK,
        ],
        axis=1,
    )
    segq = jnp.concatenate([by_block, by_block], axis=1).reshape(blocks, 1, 2 * BLK)
    segk = jnp.concatenate([own_labels, halo_labels]).reshape(-1, 1)

    rows_w = 3 * part

    def gather_weights(layer_idx):
        mine = w_qkv[layer_idx].transpose(1, 2, 3, 0).reshape(rows_w, width)
        piece = pick(mine.reshape(dp, rows_w // dp, width), lax.axis_index("dp"), 0)
        got = jnp.stack([swap(piece, "head", step) for step in range(1, head)])
        grown = got[:, None]
        for place in forward_order + [0]:
            theirs = swap(grown, "dp", 1 << place)
            first = bit_of("dp", place) == 0
            grown = jnp.stack([jnp.where(first, grown, theirs), jnp.where(first, theirs, grown)], axis=1)
        left = forward_order + [0]
        shape = (head - 1,) + (2,) * bits + (rows_w // dp, width)
        grown = grown.reshape(shape)
        now = left[::-1]
        grown = grown.transpose([0] + [1 + now.index(place) for place in range(bits - 1, -1, -1)] + [bits + 1, bits + 2])
        grown = grown.reshape(head - 1, 3, part, width)
        whole = jnp.zeros((3, head, part, width), bf16)
        whole = lax.dynamic_update_slice(whole, mine.reshape(3, 1, part, width), (0, shard, 0, 0))
        for step in range(1, head):
            whole = lax.dynamic_update_slice(whole, grown[step - 1][:, None], (0, shard ^ step, 0, 0))
        return whole.reshape(3 * head * part, width)

    bias_all = lax.all_gather(qv_bias, "head", axis=2, tiled=True).reshape(layers, 2, -1).astype(f32)
    w_cats = [gather_weights(layer_idx) for layer_idx in range(layers)]

    hidden = tokens_in.astype(f32)
    saved = []
    for layer_idx in range(layers):
        w_cat = w_cats[layer_idx]
        low = hidden.astype(bf16)
        halo = swap(lax.dynamic_slice_in_dim(low, edge, HALO), "head", 1)
        zero = jnp.zeros((width,), f32)
        bias_q, bias_v = bias_all[layer_idx, 0], bias_all[layer_idx, 1]
        shift = jnp.concatenate([bias_q, zero, bias_v])
        factor = jnp.concatenate([zero + 0.125, zero + 1.0, zero + 1.0])
        qkv = ((nt(low, w_cat) + shift) * factor).astype(bf16)
        kvh = (nt(halo, w_cat[width:]) + shift[width:]).astype(bf16)
        ctx, lse = attend(bounds, segq, segk, qkv, kvh)
        first_rows = hidden + (nn(ctx, w_out[layer_idx]) + out_bias[layer_idx].astype(f32))
        unit_one, scale_one = normalized(first_rows)
        first = unit_one * ln1_gain[layer_idx].astype(f32) + ln1_bias[layer_idx].astype(f32)
        first_low = first.astype(bf16)
        upward = nn(first_low, w_up[layer_idx]) + up_bias[layer_idx].astype(f32)
        below, density = erf_parts(upward)
        active = (upward * below).astype(bf16)
        slope = below + upward * density
        second_rows = first + (nn(active, w_down[layer_idx]) + down_bias[layer_idx].astype(f32))
        unit_two, scale_two = normalized(second_rows)
        hidden = unit_two * ln2_gain[layer_idx].astype(f32) + ln2_bias[layer_idx].astype(f32)
        saved.append((low, halo, qkv, kvh, ctx, lse, unit_one, scale_one, first_low, active, slope, unit_two, scale_two))
    output = hidden.astype(bf16)

    grad_hidden = cotangent.astype(f32)
    sums_by_layer = []
    results = []
    for layer_idx in reversed(range(layers)):
        low, halo, qkv, kvh, ctx, lse, unit_one, scale_one, first_low, active, slope, unit_two, scale_two = saved[layer_idx]
        w_cat = w_cats[layer_idx]
        grad_two, gain_two, shift_two = norm_back(grad_hidden, ln2_gain[layer_idx].astype(f32), unit_two, scale_two)
        grad_two_low = grad_two.astype(bf16)
        down_bias_sum = jnp.sum(grad_two_low.astype(f32), axis=0)
        down_send, down_keep = grad_halves(active, grad_two_low, bits)
        grad_up_low = (nt(grad_two_low, w_down[layer_idx]) * slope).astype(bf16)
        up_bias_sum = jnp.sum(grad_up_low.astype(f32), axis=0)
        up_send, up_keep = grad_halves(first_low, grad_up_low, bits)
        grad_first = nt(grad_up_low, w_up[layer_idx]) + grad_two
        grad_one, gain_one, shift_one = norm_back(grad_first, ln1_gain[layer_idx].astype(f32), unit_one, scale_one)
        grad_att_low = grad_one.astype(bf16)
        out_bias_sum = jnp.sum(grad_att_low.astype(f32), axis=0)
        grad_ctx = nt_low(grad_att_low, w_out[layer_idx])
        out_send, out_keep = grad_halves(ctx, grad_att_low, bits)
        dqkv, dkvh, qv_sum = attend_back(bounds, segq, segk, qkv, kvh, ctx, lse, grad_ctx)
        part_halo = nn(dkvh, w_cat[width:]).astype(bf16)
        back = swap(part_halo, "head", 1)
        padded = lax.dynamic_update_slice(jnp.zeros((tokens, width), bf16), back, (edge, 0))
        grad_hidden = nn(dqkv, w_cat) + grad_one + padded.astype(f32)

        view, view_halo = rows_by_core(low, bits), rows_by_core(halo, bits)
        mine = bit_of("dp", 0)

        def qkv_part(index, view=view, view_halo=view_halo, dqkv=dqkv, dkvh=dkvh):
            chosen = pick(view, index, 2).reshape(tokens, -1)
            chosen_halo = pick(view_halo, index, 2).reshape(HALO, -1)

            def tn(left, right):
                return lax.dot_general(left, right, (((0,), (0,)), ((), ())), preferred_element_type=f32)

            both = jnp.concatenate([chosen, chosen_halo], axis=0)
            both_kv = jnp.concatenate([dqkv[:, width:], dkvh], axis=0)
            return tn(chosen, dqkv[:, :width]).astype(bf16), tn(both, both_kv).astype(bf16)

        send_q, send_kv = qkv_part(1 - mine)
        keep_q, keep_kv = qkv_part(mine)

        def reduced(send, keep, order):
            got = swap(send, "dp", 1)
            held = add_low(keep, got).astype(bf16)
            held = held.reshape((2,) * (bits - 1) + (held.shape[0] >> (bits - 1), held.shape[1]))
            return halve_dp(held, order, True)

        def by_rows(held):
            view = held.reshape(head, held.shape[0] // head, held.shape[1])
            return finish_head(lambda k: pick(view, k, 0))

        def by_heads(held, count):
            view = held.reshape(held.shape[0], count, head, part)
            return finish_head(lambda k: pick(view, k, 2))

        out_down = by_rows(reduced(down_send, down_keep, backward_order))
        out_up = by_rows(reduced(up_send, up_keep, forward_order))
        out_out = by_rows(reduced(out_send, out_keep, forward_order))
        out_q = by_heads(reduced(send_q, keep_q, forward_order), 1)
        out_kv = by_heads(reduced(send_kv, keep_kv, backward_order), 2)
        out_qkv = jnp.concatenate([out_q, out_kv], axis=1)
        results.append((out_qkv, out_out, out_up, out_down))

        vectors = jnp.stack([out_bias_sum, gain_one, shift_one, down_bias_sum, gain_two, shift_two])
        sums_by_layer.append((vectors, up_bias_sum, qv_sum[:2]))

    results, sums_by_layer = results[::-1], sums_by_layer[::-1]
    out_qkv, out_w_out, out_up, out_down = (jnp.stack([r[k] for r in results]) for k in range(4))
    out_qkv = out_qkv.reshape(layers, out_qkv.shape[1], 3, part // head_size, head_size)

    vectors = jnp.stack([s[0] for s in sums_by_layer])
    ups = jnp.stack([s[1] for s in sums_by_layer])
    qvs = jnp.stack([s[2] for s in sums_by_layer])
    devices = dp * head
    flat = jnp.concatenate(
        [
            vectors.reshape(layers, 6, devices, -1).transpose(2, 0, 1, 3).reshape(devices, -1),
            ups.reshape(layers, devices, -1).transpose(1, 0, 2).reshape(devices, -1),
            qvs.reshape(layers, 2, head, part // head_size, dp, head_size // dp)
            .transpose(4, 2, 0, 1, 3, 5)
            .reshape(devices, -1),
        ],
        axis=1,
    )
    held = flat.reshape((2,) * bits + (head, flat.shape[1]))
    held = halve_dp(held, list(range(bits)), False)
    flat = finish_head(lambda k: pick(held, k, 0))
    cut_one = layers * 6 * (width // devices)
    cut_two = cut_one + layers * (up_bias.shape[1] // devices)
    out_vectors = flat[:cut_one].reshape(layers, 6, -1)
    out_ups = flat[cut_one:cut_two].reshape(layers, -1)
    out_qv = flat[cut_two:].reshape(layers, 2, part // head_size, head_size // dp)
    return (
        output,
        grad_hidden,
        out_qkv,
        out_qv,
        out_w_out,
        out_vectors[:, 0],
        out_vectors[:, 1],
        out_vectors[:, 2],
        out_up,
        out_ups,
        out_down,
        out_vectors[:, 3],
        out_vectors[:, 4],
        out_vectors[:, 5],
    )


def solution(mesh):
    return jax.shard_map(
        per_device,
        mesh=mesh,
        in_specs=(
            P(("dp", "head"), None),
            P("dp", None),
            P(None, None, None, "head", None),
            P(None, None, "head", None),
            P(),
            P(),
            P(),
            P(),
            P(),
            P(),
            P(),
            P(),
            P(),
            P(),
            P(("dp", "head"), None),
        ),
        out_specs=(
            P(("dp", "head"), None),
            P(("dp", "head"), None),
            P(None, "dp", None, "head", None),
            P(None, None, "head", "dp"),
            P(None, ("dp", "head"), None),
            P(None, ("dp", "head")),
            P(None, ("dp", "head")),
            P(None, ("dp", "head")),
            P(None, ("dp", "head"), None),
            P(None, ("dp", "head")),
            P(None, ("dp", "head"), None),
            P(None, ("dp", "head")),
            P(None, ("dp", "head")),
            P(None, ("dp", "head")),
        ),
        check_vma=False,
    )
```

time: 1280 us -> 670 us (0.52)
  waiting for transfers between devices: 772 us -> 150 us
  matrix products: 218 us -> 127 us
  starting transfers between devices: 11.9 us -> 92.6 us
  local copies, waits for them, and re-layouts: 88.3 us -> 162 us
  Pallas kernels: 0 us -> 71.8 us
  blocking collectives: 78.8 us -> 15.9 us
  other arithmetic: 89.5 us -> 36.5 us
  between operations: 16.6 us -> 3.55 us
    reduce_scatter x5 -> x0, waiting for transfers between devices: 595 us -> none  [the longest x1 212 us: per_device(): lax.psum_scatter(token_stack[1], ('dp', 'head'), scatter_dimension=1, til...]
    ppermute x0 -> x82, waiting for transfers between devices: none -> 150 us  [swap(): return lax.ppermute(value, axis, [(i, i ^ bit) for i in range(size)])]
    all_gather x2 -> x0, waiting for transfers between devices: 126 us -> none  [per_device(): gathered = lax.all_gather(rounded, 'head', axis=0, tiled=True)]
    ppermute x0 -> x82, starting transfers between devices: none -> 92.6 us  [swap(): return lax.ppermute(value, axis, [(i, i ^ bit) for i in range(size)])]
    dot_general x52 -> x40, matrix products: 218 us -> 127 us  [the longest x10 41.5 us: nn(): lax.dot_general(left, right, (((1,), (0,)), ((), ())), preferred_element_...]
    pallas_call x0 -> x4, Pallas kernels: none -> 71.8 us  [the longest x2 51.1 us: attend_back(): pl.pallas_call(functools.partial(attend_back_kernel, pairs, own_blocks, h...]
    unnamed x2 -> x0, blocking collectives: 55.8 us -> none
    all_to_all x3 -> x0, waiting for transfers between devices: 49.5 us -> none  [the longest x2 32.4 us: per_device(): lax.all_to_all(grad_mixed, 'head', split_axis=1, concat_axis=0, tiled=True)]
  transfers between devices with their start and end apart: 12 -> 82, of which waited for: 10 -> 33; matrix products, arithmetic and copies ran while one was open for 11% -> 33% of each run, Pallas kernels for 0% -> 4%
where the time goes in v1:
time: 670 us; the launch traced here: 659 us
  local copies, waits for them, and re-layouts  162 us (24%)
  waiting for transfers between devices  150 us (22%)
  matrix products  127 us (19%)
  starting transfers between devices  92.6 us (14%)
  Pallas kernels  71.8 us (11%)
  other arithmetic  36.5 us (5%)
  blocking collectives  15.9 us (2%)
    ppermute x82, waiting for transfers between devices, swap(): return lax.ppermute(value, axis, [(i, i ^ bit) for i in range(size)])  150 us
    ppermute x82, starting transfers between devices, swap(): return lax.ppermute(value, axis, [(i, i ^ bit) for i in range(size)])  92.6 us
    unnamed x304, local copies, waits for them, and re-layouts  54.6 us
    pallas_call x2, Pallas kernels, attend_back(): pl.pallas_call(functools.partial(attend_back_kernel, pairs, own_blocks, h...  51.1 us
    dynamic_slice x27, local copies, waits for them, and re-layouts, pick(): return lax.dynamic_index_in_dim(value, index, axis, keepdims=False)  43.8 us
    dot_general x10, matrix products, nn(): lax.dot_general(left, right, (((1,), (0,)), ((), ())), preferred_element_...  41.5 us
    dot_general x12, matrix products, part(): lax.dot_general(chosen, right, (((0,), (0,)), ((), ())), preferred_elemen...  34.9 us
    dot_general x10, matrix products, nt(): lax.dot_general(left, right, (((1,), (1,)), ((), ())), preferred_element_...  32.8 us
  transfers between devices with their start and end apart: 82, of which 33 were waited for; matrix products, arithmetic and copies ran while one was open for 33% of the time, Pallas kernels for 4%

profile of v1, /device:TPU:0, one launch (start us, length us, event | category | flops | bytes accessed | tf_op | source)
XLA Modules:
  0.0 659.3 jit_solution(8011162338527164833)
XLA Ops:
  3.0 3.0 collective-permute-start
  10.2 3.5 collective-permute-start.8
  14.0 15.9 %all_gather.3 = bf16[2,2,12,64]{3,1,2,0:T(2,128)(2,1)S(1)} all-gather(bf16[2,2,3,64]{3,1,2,0:T(2,128)(2,1)S(1)} %copy-done.122), channel_id=1, replica_groups=mesh['dp'=8,'head'=4] {'head'}, dimensions={2}, use_global_device_ids=true | all-gather | bytes 7680 | tf_op jit(solution)/shard_map/all_gather | solution.py:393
  38.0 4.7 collective-permute-done.9
  48.0 2.9 collective-permute-done.10
  54.2 10.1 %collective-permute-done.4 = bf16[3,2,1,72,768]{4,3,1,0,2:T(8,128)(2,1)S(1)} collective-permute-done((bf16[3,2,1,72,768]{4,3,1,0,2:T(8,128)(2,1)S(1)}, bf16[3,2,1,72,768]{4,3,1,0,2:T(8,128)(2,1)S(1)}, u32[]{:S(2)}, u32[]{:S(2)}) %collective-permute-start.4) | collective-permute-done | bytes 663584 | tf_op jit(solution)/shard_map/ppermute | solution.py:21
  68.8 3.4 collective-permute-done.11
  88.9 2.7 fusion.41.kvh
  91.6 10.5 %attend.2 = (bf16[512,768]{1,0:T(8,128)(2,1)S(1)}, f32[4,8,256]{2,1,0:T(8,128)S(1)}) custom-call(s32[4,4]{1,0:T(4,128)S(1)} %pad_add_fusion.2.bounds, s32[4,1,256]{2,1,0:T(1,128)S(1)} %reshape.699.segq, s32[896,1]{1,0:T(8,128)S(1)} %reshape.800.segk, bf16[512,2304]{1,0:T(8,128)(2,1)S(1)} %fusion.38.qkv, bf16[384,1536]{1,0:T(8,128)(2,1)S(1)} %fusion.41.kvh), custom_call_target="tpu_custom_call" | custom-call | flops 2000000000 | bytes 6000000 | tf_op jit(solution)/shard_map/attend/pallas_call | solution.py:223
  109.5 7.1 %multiply_convert_fusion.1 = (bf16[512,3072]{1,0:T(8,128)(2,1)}, f32[512,3072]{1,0:T(8,128)}) fusion(f32[3072]{0:T(1024)S(1)} %bitcast.591, bf16[512,768]{1,0:T(8,128)(2,1)} %fusion.64, bf16[2,768,3072]{2,1,0:T(8,128)(2,1)} %param.23), kind=kOutput, calls=%fused_computation.18 | convolution fusion | flops 2425356288 | bytes 14954496 | tf_op jit(solution)/shard_map/dot_general | solution.py:74
  116.6 8.5 %reshape.745 = bf16[512,4,2,384]{3,2,1,0:T(2,128)(2,1)} reshape(bf16[512,3072]{1,0:T(8,128)(2,1)} %get-tuple-element.216) | data formatting | bytes 6291456 | tf_op jit(solution)/shard_map/reshape | solution.py:302
  125.2 6.1 fusion.172
  138.5 9.2 %constant_dynamic-slice_fusion.3 = (bf16[512,4,1,384]{3,2,1,0:T(2,128)(2,1)}, bf16[512,4,1,384]{3,2,1,0:T(2,128)(2,1)}) fusion(bf16[512,4,2,384]{3,2,1,0:T(2,128)(2,1)S(1)} %copy-done.21, s32[]{:T(128)S(6)} %select_n.334, s32[]{:T(128)S(6)} %select_n.335), kind=kLoop, calls=%fused_computation.319 | loop fusion | bytes 6291464 | tf_op jit(solution)/shard_map/jit(dynamic_index_in_dim)/dynamic_slice | solution.py:29
  153.8 3.2 slice.282
  157.0 8.1 %copy.223 = bf16[512,4,1,384]{0,3,1,2:T(8,128)(2,1)} copy(bf16[512,4,1,384]{3,2,1,0:T(2,128)(2,1)} %get-tuple-element.130) | data formatting | bytes 3145728
  165.1 8.6 %copy.222 = bf16[512,4,1,384]{0,3,1,2:T(8,128)(2,1)} copy(bf16[512,4,1,384]{3,2,1,0:T(2,128)(2,1)} %get-tuple-element.129) | data formatting | bytes 3145728
  173.8 4.2 fusion.29.qkv
  180.0 10.3 %attend.3 = (bf16[512,768]{1,0:T(8,128)(2,1)S(1)}, f32[4,8,256]{2,1,0:T(8,128)S(1)}) custom-call(s32[4,4]{1,0:T(4,128)S(1)} %pad_add_fusion.2.bounds, s32[4,1,256]{2,1,0:T(1,128)S(1)} %reshape.699.segq, s32[896,1]{1,0:T(8,128)S(1)} %reshape.800.segk, bf16[512,2304]{1,0:T(8,128)(2,1)S(1)} %fusion.29.qkv, bf16[384,1536]{1,0:T(8,128)(2,1)S(1)} %fusion.42.kvh), custom_call_target="tpu_custom_call" | custom-call | flops 2000000000 | bytes 6000000 | tf_op jit(solution)/shard_map/attend/pallas_call | solution.py:223
  191.6 2.7 fusion.173
  197.0 7.0 %multiply_convert_fusion = (bf16[512,3072]{1,0:T(8,128)(2,1)}, f32[512,3072]{1,0:T(8,128)}) fusion(f32[3072]{0:T(1024)S(1)} %bitcast.593, bf16[512,768]{1,0:T(8,128)(2,1)S(1)} %fusion.66, bf16[2,768,3072]{2,1,0:T(8,128)(2,1)} %param.23), kind=kOutput, calls=%fused_computation.16 | convolution fusion | flops 2425356288 | bytes 14954496 | tf_op jit(solution)/shard_map/dot_general | solution.py:74
  203.9 8.5 %reshape.750 = bf16[512,4,2,384]{3,2,1,0:T(2,128)(2,1)} reshape(bf16[512,3072]{1,0:T(8,128)(2,1)} %get-tuple-element.222) | data formatting | bytes 6291456 | tf_op jit(solution)/shard_map/reshape | solution.py:302
  212.5 6.1 fusion.174
  222.8 6.7 %convert_reduce_fusion = (f32[3072]{0:T(1024)S(1)}, bf16[512,3072]{1,0:T(8,128)(2,1)S(1)}) fusion(f32[512,3072]{1,0:T(8,128)S(1)} %copy-done.133, f32[3072]{0:T(1024)S(1)} %bitcast.594, bf16[512,768]{1,0:T(8,128)(2,1)S(1)} %get-tuple-element.125, bf16[2,3072,768]{2,1,0:T(8,128)(2,1)} %param.25), kind=kOutput, calls=%fused_computation.14 | convolution fusion | flops 2436363264 | bytes 14966784 | tf_op jit(solution)/shard_map/dot_general | solution.py:70
  229.6 3.5 multiply_reduce_fusion
  237.2 25.5 %attend_back.2 = (bf16[512,2304]{1,0:T(8,128)(2,1)S(1)}, bf16[384,1536]{1,0:T(8,128)(2,1)S(1)}, f32[8,768]{1,0:T(8,128)S(1)}) custom-call(s32[4,4]{1,0:T(4,128)S(1)} %pad_add_fusion.2.bounds, s32[4,1,256]{2,1,0:T(1,128)S(1)} %reshape.699.segq, s32[896,1]{1,0:T(8,128)S(1)} %copy-done.4, bf16[512,2304]{1,0:T(8,128)(2,1)S(1)} %copy-done.15, ...), custom_call_target="tpu_custom_call" | custom-call | flops 6000000000 | bytes 12000000 | tf_op jit(solution)/shard_map/attend_back/pallas_call | solution.py:249
  266.1 9.1 %constant_dynamic-slice_fusion.1 = (bf16[512,4,1,384]{3,2,1,0:T(2,128)(2,1)}, bf16[512,4,1,384]{3,2,1,0:T(2,128)(2,1)}) fusion(bf16[512,4,2,384]{3,2,1,0:T(2,128)(2,1)S(1)} %copy-done.20, s32[]{:T(128)S(6)} %select_n.334, s32[]{:T(128)S(6)} %select_n.335), kind=kLoop, calls=%fused_computation.317 | loop fusion | bytes 6291464 | tf_op jit(solution)/shard_map/jit(dynamic_index_in_dim)/dynamic_slice | solution.py:29
  275.2 8.1 %copy.225 = bf16[512,4,1,384]{0,3,1,2:T(8,128)(2,1)} copy(bf16[512,4,1,384]{3,2,1,0:T(2,128)(2,1)} %get-tuple-element.132) | data formatting | bytes 3145728
  283.4 4.4 convolution_convert_fusion.4
  287.8 8.3 %copy.224 = bf16[512,4,1,384]{0,3,1,2:T(8,128)(2,1)} copy(bf16[512,4,1,384]{3,2,1,0:T(2,128)(2,1)} %get-tuple-element.131) | data formatting | bytes 3145728
  310.1 4.5 convolution_convert_fusion.8
  315.9 2.9 convolution_convert_fusion
  320.5 3.1 multiply_reduce_fusion.1
  324.3 6.9 %convert_reduce_fusion.1 = (f32[3072]{0:T(1024)S(1)}, bf16[512,3072]{1,0:T(8,128)(2,1)S(1)}) fusion(f32[512,3072]{1,0:T(8,128)S(1)} %bitcast.608, f32[3072]{0:T(1024)S(1)} %bitcast.592, bf16[512,768]{1,0:T(8,128)(2,1)S(1)} %get-tuple-element.119, bf16[2,3072,768]{2,1,0:T(8,128)(2,1)} %param.25), kind=kOutput, calls=%fused_computation.15 | convolution fusion | flops 2436363264 | bytes 14966784 | tf_op jit(solution)/shard_map/dot_general | solution.py:70
  331.3 3.1 multiply_reduce_fusion.2
  345.9 25.5 %attend_back.3 = (bf16[512,2304]{1,0:T(8,128)(2,1)S(1)}, bf16[384,1536]{1,0:T(8,128)(2,1)S(1)}, f32[8,768]{1,0:T(8,128)S(1)}) custom-call(s32[4,4]{1,0:T(4,128)S(1)} %pad_add_fusion.2.bounds, s32[4,1,256]{2,1,0:T(1,128)S(1)} %reshape.699.segq, s32[896,1]{1,0:T(8,128)S(1)} %copy-done.5, bf16[512,2304]{1,0:T(8,128)(2,1)S(1)} %copy-done.13, ...), custom_call_target="tpu_custom_call" | custom-call | flops 6000000000 | bytes 12000000 | tf_op jit(solution)/shard_map/attend_back/pallas_call | solution.py:249
  373.6 4.5 convolution_convert_fusion.6
  381.7 2.8 convolution_convert_fusion.2
  387.8 9.8 %collective-permute-start.41 = (f32[2,4,576]{2,1,0:T(4,128)S(1)}, f32[2,4,576]{2,1,0:T(4,128)S(1)}, u32[]{:S(2)}, u32[]{:S(2)}) collective-permute-start(f32[2,4,576]{2,1,0:T(4,128)S(1)} %fusion.143), channel_id=1, source_target_pairs={{0,8},{4,12},{8,0},{12,4},{16,24},{20,28},{24,16},{28,20},{1,9},{5... | collective-permute-start | bytes 55304 | tf_op jit(solution)/shard_map/ppermute | solution.py:21
  400.9 2.9 collective-permute-done.42
  414.6 8.2 %collective-permute-done.29 = bf16[2,96,768]{2,1,0:T(8,128)(2,1)} collective-permute-done((bf16[2,96,768]{2,1,0:T(8,128)(2,1)}, bf16[2,96,768]{2,1,0:T(8,128)(2,1)}, u32[]{:S(2)}, u32[]{:S(2)}) %collective-permute-start.29) | collective-permute-done | bytes 294944 | tf_op jit(solution)/shard_map/ppermute | solution.py:21
  433.8 3.0 collective-permute-start.32
  441.7 3.0 collective-permute-start.56
  447.7 2.8 collective-permute-done.57
  455.6 2.8 add_convert_fusion.4
  463.4 3.4 convert_add_fusion.4
  469.1 8.2 %collective-permute-done.18 = bf16[96,768]{1,0:T(8,128)(2,1)S(1)} collective-permute-done((bf16[96,768]{1,0:T(8,128)(2,1)S(1)}, bf16[96,768]{1,0:T(8,128)(2,1)S(1)}, u32[]{:S(2)}, u32[]{:S(2)}) %collective-permute-start.18) | collective-permute-done | bytes 147488 | tf_op jit(solution)/shard_map/ppermute | solution.py:21
  478.8 2.7 collective-permute-start.20
  484.4 3.3 collective-permute-done.21
  492.7 2.9 add_convert_fusion.5
  495.6 2.7 collective-permute-done.36
  518.2 3.2 add_convert_fusion.2
  521.5 4.6 add_convert_fusion
  534.6 3.1 collective-permute-start.27
  544.9 3.4 add_convert_fusion.1
  550.1 3.1 add_convert_fusion.3
  554.2 15.3 %collective-permute-done.77 = bf16[2,384,768]{2,1,0:T(8,128)(2,1)S(1)} collective-permute-done((bf16[2,384,768]{2,1,0:T(8,128)(2,1)}, bf16[2,384,768]{2,1,0:T(8,128)(2,1)S(1)}, u32[]{:S(2)}, u32[]{:S(2)}) %collective-permute-start.77) | collective-permute-done | bytes 1179680 | tf_op jit(solution)/shard_map/ppermute | solution.py:21
  573.8 21.0 %collective-permute-done.71 = bf16[2,384,768]{2,1,0:T(8,128)(2,1)S(1)} collective-permute-done((bf16[2,384,768]{2,1,0:T(8,128)(2,1)S(1)}, bf16[2,384,768]{2,1,0:T(8,128)(2,1)S(1)}, u32[]{:S(2)}, u32[]{:S(2)}) %collective-permute-start.71) | collective-permute-done | bytes 1179680 | tf_op jit(solution)/shard_map/ppermute | solution.py:21
  599.1 8.3 %collective-permute-done.66 = bf16[96,3072]{1,0:T(8,128)(2,1)S(1)} collective-permute-done((bf16[96,3072]{1,0:T(8,128)(2,1)S(1)}, bf16[96,3072]{1,0:T(8,128)(2,1)S(1)}, u32[]{:S(2)}, u32[]{:S(2)}) %collective-permute-start.66) | collective-permute-done | bytes 589856 | tf_op jit(solution)/shard_map/ppermute | solution.py:21
  612.3 3.3 collective-permute-done.67
  615.6 6.9 %collective-permute-done.68 = bf16[24,3072]{1,0:T(8,128)(2,1)S(1)} collective-permute-done((bf16[24,3072]{1,0:T(8,128)(2,1)S(1)}, bf16[24,3072]{1,0:T(8,128)(2,1)S(1)}, u32[]{:S(2)}, u32[]{:S(2)}) %collective-permute-start.68) | collective-permute-done | bytes 147488 | tf_op jit(solution)/shard_map/ppermute | solution.py:21
  624.8 7.0 %collective-permute-done.80 = bf16[96,768]{1,0:T(8,128)(2,1)S(1)} collective-permute-done((bf16[96,768]{1,0:T(8,128)(2,1)S(1)}, bf16[96,768]{1,0:T(8,128)(2,1)S(1)}, u32[]{:S(2)}, u32[]{:S(2)}) %collective-permute-start.80) | collective-permute-done | bytes 147488 | tf_op jit(solution)/shard_map/ppermute | solution.py:21
  639.0 3.3 collective-permute-done.73
  643.4 4.9 collective-permute-done.74
  649.3 8.9 %collective-permute-done.62 = bf16[24,3072]{1,0:T(8,128)(2,1)S(1)} collective-permute-done((bf16[24,3072]{1,0:T(8,128)(2,1)S(1)}, bf16[24,3072]{1,0:T(8,128)(2,1)S(1)}, u32[]{:S(2)}, u32[]{:S(2)}) %collective-permute-start.62) | collective-permute-done | bytes 147488 | tf_op jit(solution)/shard_map/ppermute | solution.py:21
  (696 shorter events, 238.7 us)
Async XLA Ops:
  3.0 31.7 %collective-permute-start = (bf16[72,768]{1,0:T(8,128)(2,1)}, bf16[72,768]{1,0:T(8,128)(2,1)}, u32[]{:S(2)}, u32[]{:S(2)}) collective-permute-start(bf16[72,768]{1,0:T(8,128)(2,1)} %dynamic-slice_bitcast_fusion.33), channel_id=1, source_target_pairs={{0,1},{1,0},{2,3},{3,2},{4,5},{5,4},{6,7},{7,6},{8,9},{9,8},{10,11... | collective-permute-start | bytes 331784 | tf_op jit(solution)/shard_map/ppermute | solution.py:21
  6.0 28.7 %collective-permute-start.1 = (bf16[72,768]{1,0:T(8,128)(2,1)}, bf16[72,768]{1,0:T(8,128)(2,1)}, u32[]{:S(2)}, u32[]{:S(2)}) collective-permute-start(bf16[72,768]{1,0:T(8,128)(2,1)} %dynamic-slice_bitcast_fusion.33), channel_id=1, source_target_pairs={{0,2},{1,3},{2,0},{3,1},{4,6},{5,7},{6,4},{7,5},{8,10},{9,11},{10,... | collective-permute-start | bytes 331784 | tf_op jit(solution)/shard_map/ppermute | solution.py:21
  8.6 26.2 %collective-permute-start.2 = (bf16[72,768]{1,0:T(8,128)(2,1)}, bf16[72,768]{1,0:T(8,128)(2,1)}, u32[]{:S(2)}, u32[]{:S(2)}) collective-permute-start(bf16[72,768]{1,0:T(8,128)(2,1)} %dynamic-slice_bitcast_fusion.33), channel_id=1, source_target_pairs={{0,3},{1,2},{2,1},{3,0},{4,7},{5,6},{6,5},{7,4},{8,11},{9,10},{10,... | collective-permute-start | bytes 331784 | tf_op jit(solution)/shard_map/ppermute | solution.py:21
  9.3 28.8 %collective-permute-start.7 = (bf16[72,768]{1,0:T(8,128)(2,1)}, bf16[72,768]{1,0:T(8,128)(2,1)S(1)}, u32[]{:S(2)}, u32[]{:S(2)}) collective-permute-start(bf16[72,768]{1,0:T(8,128)(2,1)} %dynamic-slice_bitcast_fusion.32), channel_id=1, source_target_pairs={{0,1},{1,0},{2,3},{3,2},{4,5},{5,4},{6,7},{7,6},{8,9},{9,8},{10,11... | collective-permute-start | bytes 331784 | tf_op jit(solution)/shard_map/ppermute | solution.py:21
  10.2 27.9 %collective-permute-start.8 = (bf16[72,768]{1,0:T(8,128)(2,1)}, bf16[72,768]{1,0:T(8,128)(2,1)}, u32[]{:S(2)}, u32[]{:S(2)}) collective-permute-start(bf16[72,768]{1,0:T(8,128)(2,1)} %dynamic-slice_bitcast_fusion.32), channel_id=1, source_target_pairs={{0,2},{1,3},{2,0},{3,1},{4,6},{5,7},{6,4},{7,5},{8,10},{9,11},{10,... | collective-permute-start | bytes 331784 | tf_op jit(solution)/shard_map/ppermute | solution.py:21
  34.7 8.0 %collective-permute-start.9 = (bf16[72,768]{1,0:T(8,128)(2,1)}, bf16[72,768]{1,0:T(8,128)(2,1)S(1)}, u32[]{:S(2)}, u32[]{:S(2)}) collective-permute-start(bf16[72,768]{1,0:T(8,128)(2,1)} %dynamic-slice_bitcast_fusion.32), channel_id=1, source_target_pairs={{0,3},{1,2},{2,1},{3,0},{4,7},{5,6},{6,5},{7,4},{8,11},{9,10},{10,... | collective-permute-start | bytes 331784 | tf_op jit(solution)/shard_map/ppermute | solution.py:21
  34.7 42.5 %collective-permute-start.6 = (bf16[384,768]{0,1:T(8,128)(2,1)}, bf16[384,768]{0,1:T(8,128)(2,1)}, u32[]{:S(2)}, u32[]{:S(2)}) collective-permute-start(bf16[384,768]{0,1:T(8,128)(2,1)} %constant_dynamic-slice_fusion.45), channel_id=1, source_target_pairs={{0,1},{1,0},{2,3},{3,2},{4,5},{5,4},{6,7},{7,6},{8,9},{9,8},{10,11... | collective-permute-start | bytes 1769480 | tf_op jit(solution)/shard_map/ppermute | solution.py:21
  35.9 9.4 %collective-permute-start.3 = (bf16[3,1,72,768]{3,2,0,1:T(8,128)(2,1)S(1)}, bf16[3,1,72,768]{3,2,0,1:T(8,128)(2,1)S(1)}, u32[]{:S(2)}, u32[]{:S(2)}) collective-permute-start(bf16[3,1,72,768]{3,2,0,1:T(8,128)(2,1)S(1)} %maximum_bitcast_fusion.2), channel_id=1, source_target_pairs={{0,8},{4,12},{8,0},{12,4},{16,24},{20,28},{24,16},{28,20},{1,9},{5... | collective-permute-start | bytes 995336 | tf_op jit(solution)/shard_map/ppermute | solution.py:21
  46.4 17.9 %collective-permute-start.4 = (bf16[3,2,1,72,768]{4,3,1,0,2:T(8,128)(2,1)S(1)}, bf16[3,2,1,72,768]{4,3,1,0,2:T(8,128)(2,1)S(1)}, u32[]{:S(2)}, u32[]{:S(2)}) collective-permute-start(bf16[3,2,1,72,768]{4,3,1,0,2:T(8,128)(2,1)S(1)} %pad_maximum_fusion.12), channel_id=1, source_target_pairs={{0,16},{4,20},{8,24},{12,28},{16,0},{20,4},{24,8},{28,12},{1,17},{... | collective-permute-start | bytes 1990664 | tf_op jit(solution)/shard_map/ppermute | solution.py:21
  52.7 19.6 %collective-permute-start.11 = (bf16[3,2,1,72,768]{4,3,1,0,2:T(8,128)(2,1)}, bf16[3,2,1,72,768]{4,3,1,0,2:T(8,128)(2,1)}, u32[]{:S(2)}, u32[]{:S(2)}) collective-permute-start(bf16[3,2,1,72,768]{4,3,1,0,2:T(8,128)(2,1)} %pad_maximum_fusion.13), channel_id=1, source_target_pairs={{0,16},{4,20},{8,24},{12,28},{16,0},{20,4},{24,8},{28,12},{1,17},{... | collective-permute-start | bytes 1990664 | tf_op jit(solution)/shard_map/ppermute | solution.py:21
  65.6 13.6 %collective-permute-start.5 = (bf16[3,2,2,1,72,768]{5,4,2,1,0,3:T(8,128)(2,1)}, bf16[3,2,2,1,72,768]{5,4,2,1,0,3:T(8,128)(2,1)}, u32[]{:S(2)}, u32[]{:S(2)}) collective-permute-start(bf16[3,2,2,1,72,768]{5,4,2,1,0,3:T(8,128)(2,1)} %pad_maximum_fusion.10), channel_id=1, source_target_pairs={{0,4},{4,0},{8,12},{12,8},{16,20},{20,16},{24,28},{28,24},{1,5},{5... | collective-permute-start | bytes 3981320 | tf_op jit(solution)/shard_map/ppermute | solution.py:21
  73.6 7.5 %collective-permute-start.12 = (bf16[3,2,2,1,72,768]{5,4,2,1,0,3:T(8,128)(2,1)S(1)}, bf16[3,2,2,1,72,768]{5,4,2,1,0,3:T(8,128)(2,1)S(1)}, u32[]{:S(2)}, u32[]{:S(2)}) collective-permute-start(bf16[3,2,2,1,72,768]{5,4,2,1,0,3:T(8,128)(2,1)S(1)} %pad_maximum_fusion.11), channel_id=1, source_target_pairs={{0,4},{4,0},{8,12},{12,8},{16,20},{20,16},{24,28},{28,24},{1,5},{5... | collective-permute-start | bytes 3981320 | tf_op jit(solution)/shard_map/ppermute | solution.py:21
  138.0 40.0 %collective-permute-start.13 = (bf16[384,768]{1,0:T(8,128)(2,1)}, bf16[384,768]{1,0:T(8,128)(2,1)S(1)}, u32[]{:S(2)}, u32[]{:S(2)}) collective-permute-start(bf16[384,768]{1,0:T(8,128)(2,1)} %constant_dynamic-slice_fusion.44), channel_id=1, source_target_pairs={{0,1},{1,0},{2,3},{3,2},{4,5},{5,4},{6,7},{7,6},{8,9},{9,8},{10,11... | collective-permute-start | bytes 1769480 | tf_op jit(solution)/shard_map/ppermute | solution.py:21
  264.7 54.2 %collective-permute-start.14 = (bf16[384,768]{1,0:T(8,128)(2,1)}, bf16[384,768]{1,0:T(8,128)(2,1)}, u32[]{:S(2)}, u32[]{:S(2)}) collective-permute-start(bf16[384,768]{1,0:T(8,128)(2,1)} %convolution_convert_fusion.15), channel_id=1, source_target_pairs={{0,1},{1,0},{2,3},{3,2},{4,5},{5,4},{6,7},{7,6},{8,9},{9,8},{10,11... | collective-permute-start | bytes 1769480 | tf_op jit(solution)/shard_map/ppermute | solution.py:21
  299.4 80.6 %collective-permute-start.52 = (bf16[384,768]{1,0:T(8,128)(2,1)}, bf16[384,768]{1,0:T(8,128)(2,1)}, u32[]{:S(2)}, u32[]{:S(2)}) collective-permute-start(bf16[384,768]{1,0:T(8,128)(2,1)} %convolution_convert_fusion.16), channel_id=1, source_target_pairs={{0,4},{4,0},{8,12},{12,8},{16,20},{20,16},{24,28},{28,24},{1,5},{5... | collective-permute-start | bytes 1769480 | tf_op jit(solution)/shard_map/ppermute | solution.py:21
  306.1 78.4 %collective-permute-start.28 = (bf16[384,768]{1,0:T(8,128)(2,1)}, bf16[384,768]{1,0:T(8,128)(2,1)}, u32[]{:S(2)}, u32[]{:S(2)}) collective-permute-start(bf16[384,768]{1,0:T(8,128)(2,1)} %convolution_convert_fusion.20), channel_id=1, source_target_pairs={{0,4},{4,0},{8,12},{12,8},{16,20},{20,16},{24,28},{28,24},{1,5},{5... | collective-permute-start | bytes 1769480 | tf_op jit(solution)/shard_map/ppermute | solution.py:21
  314.5 140.5 %collective-permute-start.34 = (bf16[384,1536]{1,0:T(8,128)(2,1)}, bf16[384,1536]{1,0:T(8,128)(2,1)}, u32[]{:S(2)}, u32[]{:S(2)}) collective-permute-start(bf16[384,1536]{1,0:T(8,128)(2,1)} %convolution_convert_fusion.8), channel_id=1, source_target_pairs={{0,4},{4,0},{8,12},{12,8},{16,20},{20,16},{24,28},{28,24},{1,5},{5... | collective-permute-start | bytes 3538952 | tf_op jit(solution)/shard_map/ppermute | solution.py:21
  339.6 111.0 %collective-permute-start.46 = (bf16[384,768]{1,0:T(8,128)(2,1)}, bf16[384,768]{1,0:T(8,128)(2,1)}, u32[]{:S(2)}, u32[]{:S(2)}) collective-permute-start(bf16[384,768]{1,0:T(8,128)(2,1)} %convolution_convert_fusion.18), channel_id=1, source_target_pairs={{0,4},{4,0},{8,12},{12,8},{16,20},{20,16},{24,28},{28,24},{1,5},{5... | collective-permute-start | bytes 1769480 | tf_op jit(solution)/shard_map/ppermute | solution.py:21
  373.0 14.7 %collective-permute-start.40 = (f32[2,2,4,576]{3,2,1,0:T(4,128)S(1)}, f32[2,2,4,576]{3,2,1,0:T(4,128)S(1)}, u32[]{:S(2)}, u32[]{:S(2)}) collective-permute-start(f32[2,2,4,576]{3,2,1,0:T(4,128)S(1)} %dynamic-slice_bitcast_fusion.34), channel_id=1, source_target_pairs={{0,4},{4,0},{8,12},{12,8},{16,20},{20,16},{24,28},{28,24},{1,5},{5... | collective-permute-start | bytes 110600 | tf_op jit(solution)/shard_map/ppermute | solution.py:21
  387.8 12.3 %collective-permute-start.41 = (f32[2,4,576]{2,1,0:T(4,128)S(1)}, f32[2,4,576]{2,1,0:T(4,128)S(1)}, u32[]{:S(2)}, u32[]{:S(2)}) collective-permute-start(f32[2,4,576]{2,1,0:T(4,128)S(1)} %fusion.143), channel_id=1, source_target_pairs={{0,8},{4,12},{8,0},{12,4},{16,24},{20,28},{24,16},{28,20},{1,9},{5... | collective-permute-start | bytes 55304 | tf_op jit(solution)/shard_map/ppermute | solution.py:21
  409.1 15.6 %collective-permute-start.53 = (bf16[2,96,768]{2,1,0:T(8,128)(2,1)}, bf16[2,96,768]{2,1,0:T(8,128)(2,1)S(1)}, u32[]{:S(2)}, u32[]{:S(2)}) collective-permute-start(bf16[2,96,768]{2,1,0:T(8,128)(2,1)} %dynamic-slice_bitcast_fusion.10), channel_id=1, source_target_pairs={{0,8},{4,12},{8,0},{12,4},{16,24},{20,28},{24,16},{28,20},{1,9},{5... | collective-permute-start | bytes 884744 | tf_op jit(solution)/shard_map/ppermute | solution.py:21
  410.4 12.4 %collective-permute-start.29 = (bf16[2,96,768]{2,1,0:T(8,128)(2,1)}, bf16[2,96,768]{2,1,0:T(8,128)(2,1)}, u32[]{:S(2)}, u32[]{:S(2)}) collective-permute-start(bf16[2,96,768]{2,1,0:T(8,128)(2,1)} %dynamic-slice_bitcast_fusion.13), channel_id=1, source_target_pairs={{0,8},{4,12},{8,0},{12,4},{16,24},{20,28},{24,16},{28,20},{1,9},{5... | collective-permute-start | bytes 884744 | tf_op jit(solution)/shard_map/ppermute | solution.py:21
  425.5 12.9 %collective-permute-start.54 = (bf16[96,768]{1,0:T(8,128)(2,1)}, bf16[96,768]{1,0:T(8,128)(2,1)}, u32[]{:S(2)}, u32[]{:S(2)}) collective-permute-start(bf16[96,768]{1,0:T(8,128)(2,1)} %dynamic-slice_bitcast_fusion.28), channel_id=1, source_target_pairs={{0,16},{4,20},{8,24},{12,28},{16,0},{20,4},{24,8},{28,12},{1,17},{... | collective-permute-start | bytes 442376 | tf_op jit(solution)/shard_map/ppermute | solution.py:21
  432.2 9.4 %collective-permute-start.31 = (bf16[96,1,192]{0,2,1:T(8,128)(2,1)}, bf16[96,1,192]{0,2,1:T(8,128)(2,1)S(1)}, u32[]{:S(2)}, u32[]{:S(2)}) collective-permute-start(bf16[96,1,192]{0,2,1:T(8,128)(2,1)} %bitcast.110), channel_id=1, source_target_pairs={{0,1},{1,0},{2,3},{3,2},{4,5},{5,4},{6,7},{7,6},{8,9},{9,8},{10,11... | collective-permute-start | bytes 110600 | tf_op jit(solution)/shard_map/ppermute | solution.py:21
  433.8 7.9 %collective-permute-start.32 = (bf16[96,1,192]{0,2,1:T(8,128)(2,1)}, bf16[96,1,192]{0,2,1:T(8,128)(2,1)}, u32[]{:S(2)}, u32[]{:S(2)}) collective-permute-start(bf16[96,1,192]{0,2,1:T(8,128)(2,1)} %bitcast.111), channel_id=1, source_target_pairs={{0,2},{1,3},{2,0},{3,1},{4,6},{5,7},{6,4},{7,5},{8,10},{9,11},{10,... | collective-permute-start | bytes 110600 | tf_op jit(solution)/shard_map/ppermute | solution.py:21
  447.2 44.3 %collective-permute-start.22 = (bf16[384,1536]{1,0:T(8,128)(2,1)}, bf16[384,1536]{1,0:T(8,128)(2,1)}, u32[]{:S(2)}, u32[]{:S(2)}) collective-permute-start(bf16[384,1536]{1,0:T(8,128)(2,1)} %convolution_convert_fusion.10), channel_id=1, source_target_pairs={{0,4},{4,0},{8,12},{12,8},{16,20},{20,16},{24,28},{28,24},{1,5},{5... | collective-permute-start | bytes 3538952 | tf_op jit(solution)/shard_map/ppermute | solution.py:21
  450.5 12.7 %collective-permute-start.15 = (bf16[384,768]{1,0:T(8,128)(2,1)}, bf16[384,768]{1,0:T(8,128)(2,1)S(1)}, u32[]{:S(2)}, u32[]{:S(2)}) collective-permute-start(bf16[384,768]{1,0:T(8,128)(2,1)} %convolution_convert_fusion.14), channel_id=1, source_target_pairs={{0,1},{1,0},{2,3},{3,2},{4,5},{5,4},{6,7},{7,6},{8,9},{9,8},{10,11... | collective-permute-start | bytes 1769480 | tf_op jit(solution)/shard_map/ppermute | solution.py:21
  452.3 16.2 %collective-permute-start.47 = (bf16[2,96,768]{2,1,0:T(8,128)(2,1)S(1)}, bf16[2,96,768]{2,1,0:T(8,128)(2,1)S(1)}, u32[]{:S(2)}, u32[]{:S(2)}) collective-permute-start(bf16[2,96,768]{2,1,0:T(8,128)(2,1)S(1)} %dynamic-slice_bitcast_fusion.11), channel_id=1, source_target_pairs={{0,8},{4,12},{8,0},{12,4},{16,24},{20,28},{24,16},{28,20},{1,9},{5... | collective-permute-start | bytes 884744 | tf_op jit(solution)/shard_map/ppermute | solution.py:21
  454.4 12.4 %collective-permute-start.17 = (bf16[2,96,768]{2,1,0:T(8,128)(2,1)S(1)}, bf16[2,96,768]{2,1,0:T(8,128)(2,1)S(1)}, u32[]{:S(2)}, u32[]{:S(2)}) collective-permute-start(bf16[2,96,768]{2,1,0:T(8,128)(2,1)S(1)} %dynamic-slice_bitcast_fusion.15), channel_id=1, source_target_pairs={{0,8},{4,12},{8,0},{12,4},{16,24},{20,28},{24,16},{28,20},{1,9},{5... | collective-permute-start | bytes 884744 | tf_op jit(solution)/shard_map/ppermute | solution.py:21
  459.4 29.0 %collective-permute-start.35 = (bf16[2,96,1536]{2,1,0:T(8,128)(2,1)}, bf16[2,96,1536]{2,1,0:T(8,128)(2,1)}, u32[]{:S(2)}, u32[]{:S(2)}) collective-permute-start(bf16[2,96,1536]{2,1,0:T(8,128)(2,1)} %dynamic-slice_bitcast_fusion.8), channel_id=1, source_target_pairs={{0,16},{4,20},{8,24},{12,28},{16,0},{20,4},{24,8},{28,12},{1,17},{... | collective-permute-start | bytes 1769480 | tf_op jit(solution)/shard_map/ppermute | solution.py:21
  466.9 10.4 %collective-permute-start.18 = (bf16[96,768]{1,0:T(8,128)(2,1)S(1)}, bf16[96,768]{1,0:T(8,128)(2,1)S(1)}, u32[]{:S(2)}, u32[]{:S(2)}) collective-permute-start(bf16[96,768]{1,0:T(8,128)(2,1)S(1)} %dynamic-slice_bitcast_fusion.31), channel_id=1, source_target_pairs={{0,16},{4,20},{8,24},{12,28},{16,0},{20,4},{24,8},{28,12},{1,17},{... | collective-permute-start | bytes 442376 | tf_op jit(solution)/shard_map/ppermute | solution.py:21
  468.6 13.0 %collective-permute-start.48 = (bf16[96,768]{1,0:T(8,128)(2,1)S(1)}, bf16[96,768]{1,0:T(8,128)(2,1)S(1)}, u32[]{:S(2)}, u32[]{:S(2)}) collective-permute-start(bf16[96,768]{1,0:T(8,128)(2,1)S(1)} %dynamic-slice_bitcast_fusion.29), channel_id=1, source_target_pairs={{0,16},{4,20},{8,24},{12,28},{16,0},{20,4},{24,8},{28,12},{1,17},{... | collective-permute-start | bytes 442376 | tf_op jit(solution)/shard_map/ppermute | solution.py:21
  483.8 37.6 %collective-permute-start.76 = (bf16[1536,768]{1,0:T(8,128)(2,1)}, bf16[1536,768]{1,0:T(8,128)(2,1)}, u32[]{:S(2)}, u32[]{:S(2)}) collective-permute-start(bf16[1536,768]{1,0:T(8,128)(2,1)} %convolution_convert_fusion.4), channel_id=1, source_target_pairs={{0,4},{4,0},{8,12},{12,8},{16,20},{20,16},{24,28},{28,24},{1,5},{5... | collective-permute-start | bytes 7077896 | tf_op jit(solution)/shard_map/ppermute | solution.py:21
  484.3 33.9 %collective-permute-start.64 = (bf16[384,3072]{1,0:T(8,128)(2,1)}, bf16[384,3072]{1,0:T(8,128)(2,1)}, u32[]{:S(2)}, u32[]{:S(2)}) collective-permute-start(bf16[384,3072]{1,0:T(8,128)(2,1)} %convolution_convert_fusion), channel_id=1, source_target_pairs={{0,4},{4,0},{8,12},{12,8},{16,20},{20,16},{24,28},{28,24},{1,5},{5... | collective-permute-start | bytes 7077896 | tf_op jit(solution)/shard_map/ppermute | solution.py:21
  487.6 14.7 %collective-permute-start.49 = (bf16[24,768]{1,0:T(8,128)(2,1)}, bf16[24,768]{1,0:T(8,128)(2,1)S(1)}, u32[]{:S(2)}, u32[]{:S(2)}) collective-permute-start(bf16[24,768]{1,0:T(8,128)(2,1)} %get-tuple-element.198), channel_id=1, source_target_pairs={{0,1},{1,0},{2,3},{3,2},{4,5},{5,4},{6,7},{7,6},{8,9},{9,8},{10,11... | collective-permute-start | bytes 110600 | tf_op jit(solution)/shard_map/ppermute | solution.py:21
  488.3 15.2 %collective-permute-start.50 = (bf16[24,768]{1,0:T(8,128)(2,1)}, bf16[24,768]{1,0:T(8,128)(2,1)S(1)}, u32[]{:S(2)}, u32[]{:S(2)}) collective-permute-start(bf16[24,768]{1,0:T(8,128)(2,1)} %get-tuple-element.200), channel_id=1, source_target_pairs={{0,2},{1,3},{2,0},{3,1},{4,6},{5,7},{6,4},{7,5},{8,10},{9,11},{10,... | collective-permute-start | bytes 110600 | tf_op jit(solution)/shard_map/ppermute | solution.py:21
  502.4 12.3 %collective-permute-start.23 = (bf16[2,96,1536]{2,1,0:T(8,128)(2,1)S(1)}, bf16[2,96,1536]{2,1,0:T(8,128)(2,1)}, u32[]{:S(2)}, u32[]{:S(2)}) collective-permute-start(bf16[2,96,1536]{2,1,0:T(8,128)(2,1)S(1)} %dynamic-slice_bitcast_fusion.9), channel_id=1, source_target_pairs={{0,16},{4,20},{8,24},{12,28},{16,0},{20,4},{24,8},{28,12},{1,17},{... | collective-permute-start | bytes 1769480 | tf_op jit(solution)/shard_map/ppermute | solution.py:21
  504.3 7.7 %collective-permute-start.38 = (bf16[96,2,192]{0,2,1:T(8,128)(2,1)S(1)}, bf16[96,2,192]{0,2,1:T(8,128)(2,1)S(1)}, u32[]{:S(2)}, u32[]{:S(2)}) collective-permute-start(bf16[96,2,192]{0,2,1:T(8,128)(2,1)S(1)} %bitcast.583), channel_id=1, source_target_pairs={{0,2},{1,3},{2,0},{3,1},{4,6},{5,7},{6,4},{7,5},{8,10},{9,11},{10,... | collective-permute-start | bytes 221192 | tf_op jit(solution)/shard_map/ppermute | solution.py:21
  512.0 32.9 %collective-permute-start.70 = (bf16[1536,768]{1,0:T(8,128)(2,1)}, bf16[1536,768]{1,0:T(8,128)(2,1)}, u32[]{:S(2)}, u32[]{:S(2)}) collective-permute-start(bf16[1536,768]{1,0:T(8,128)(2,1)} %convolution_convert_fusion.6), channel_id=1, source_target_pairs={{0,4},{4,0},{8,12},{12,8},{16,20},{20,16},{24,28},{28,24},{1,5},{5... | collective-permute-start | bytes 7077896 | tf_op jit(solution)/shard_map/ppermute | solution.py:21
  514.6 35.5 %collective-permute-start.58 = (bf16[384,3072]{1,0:T(8,128)(2,1)}, bf16[384,3072]{1,0:T(8,128)(2,1)}, u32[]{:S(2)}, u32[]{:S(2)}) collective-permute-start(bf16[384,3072]{1,0:T(8,128)(2,1)} %convolution_convert_fusion.2), channel_id=1, source_target_pairs={{0,4},{4,0},{8,12},{12,8},{16,20},{20,16},{24,28},{28,24},{1,5},{5... | collective-permute-start | bytes 7077896 | tf_op jit(solution)/shard_map/ppermute | solution.py:21
  516.1 11.0 %collective-permute-start.24 = (bf16[96,1536]{1,0:T(8,128)(2,1)S(1)}, bf16[96,1536]{1,0:T(8,128)(2,1)S(1)}, u32[]{:S(2)}, u32[]{:S(2)}) collective-permute-start(bf16[96,1536]{1,0:T(8,128)(2,1)S(1)} %dynamic-slice_bitcast_fusion.14), channel_id=1, source_target_pairs={{0,8},{4,12},{8,0},{12,4},{16,24},{20,28},{24,16},{28,20},{1,9},{5... | collective-permute-start | bytes 884744 | tf_op jit(solution)/shard_map/ppermute | solution.py:21
  530.8 9.5 %collective-permute-start.25 = (bf16[96,2,192]{0,2,1:T(8,128)(2,1)}, bf16[96,2,192]{0,2,1:T(8,128)(2,1)S(1)}, u32[]{:S(2)}, u32[]{:S(2)}) collective-permute-start(bf16[96,2,192]{0,2,1:T(8,128)(2,1)} %bitcast.97), channel_id=1, source_target_pairs={{0,1},{1,0},{2,3},{3,2},{4,5},{5,4},{6,7},{7,6},{8,9},{9,8},{10,11... | collective-permute-start | bytes 221192 | tf_op jit(solution)/shard_map/ppermute | solution.py:21
  532.5 11.0 %collective-permute-start.26 = (bf16[96,2,192]{0,2,1:T(8,128)(2,1)}, bf16[96,2,192]{0,2,1:T(8,128)(2,1)S(1)}, u32[]{:S(2)}, u32[]{:S(2)}) collective-permute-start(bf16[96,2,192]{0,2,1:T(8,128)(2,1)} %bitcast.98), channel_id=1, source_target_pairs={{0,2},{1,3},{2,0},{3,1},{4,6},{5,7},{6,4},{7,5},{8,10},{9,11},{10,... | collective-permute-start | bytes 221192 | tf_op jit(solution)/shard_map/ppermute | solution.py:21
  534.6 9.4 %collective-permute-start.27 = (bf16[96,2,192]{0,2,1:T(8,128)(2,1)}, bf16[96,2,192]{0,2,1:T(8,128)(2,1)S(1)}, u32[]{:S(2)}, u32[]{:S(2)}) collective-permute-start(bf16[96,2,192]{0,2,1:T(8,128)(2,1)} %bitcast.99), channel_id=1, source_target_pairs={{0,3},{1,2},{2,1},{3,0},{4,7},{5,6},{6,5},{7,4},{8,11},{9,10},{10,... | collective-permute-start | bytes 221192 | tf_op jit(solution)/shard_map/ppermute | solution.py:21
  540.3 29.2 %collective-permute-start.77 = (bf16[2,384,768]{2,1,0:T(8,128)(2,1)}, bf16[2,384,768]{2,1,0:T(8,128)(2,1)S(1)}, u32[]{:S(2)}, u32[]{:S(2)}) collective-permute-start(bf16[2,384,768]{2,1,0:T(8,128)(2,1)} %dynamic-slice_bitcast_fusion), channel_id=1, source_target_pairs={{0,16},{4,20},{8,24},{12,28},{16,0},{20,4},{24,8},{28,12},{1,17},{... | collective-permute-start | bytes 3538952 | tf_op jit(solution)/shard_map/ppermute | solution.py:21
  543.5 29.1 %collective-permute-start.65 = (bf16[2,96,3072]{2,1,0:T(8,128)(2,1)}, bf16[2,96,3072]{2,1,0:T(8,128)(2,1)S(1)}, u32[]{:S(2)}, u32[]{:S(2)}) collective-permute-start(bf16[2,96,3072]{2,1,0:T(8,128)(2,1)} %dynamic-slice_bitcast_fusion.2), channel_id=1, source_target_pairs={{0,8},{4,12},{8,0},{12,4},{16,24},{20,28},{24,16},{28,20},{1,9},{5... | collective-permute-start | bytes 3538952 | tf_op jit(solution)/shard_map/ppermute | solution.py:21
  548.5 46.3 %collective-permute-start.71 = (bf16[2,384,768]{2,1,0:T(8,128)(2,1)S(1)}, bf16[2,384,768]{2,1,0:T(8,128)(2,1)S(1)}, u32[]{:S(2)}, u32[]{:S(2)}) collective-permute-start(bf16[2,384,768]{2,1,0:T(8,128)(2,1)S(1)} %dynamic-slice_bitcast_fusion.1), channel_id=1, source_target_pairs={{0,16},{4,20},{8,24},{12,28},{16,0},{20,4},{24,8},{28,12},{1,17},{... | collective-permute-start | bytes 3538952 | tf_op jit(solution)/shard_map/ppermute | solution.py:21
  553.3 44.6 %collective-permute-start.59 = (bf16[2,96,3072]{2,1,0:T(8,128)(2,1)S(1)}, bf16[2,96,3072]{2,1,0:T(8,128)(2,1)S(1)}, u32[]{:S(2)}, u32[]{:S(2)}) collective-permute-start(bf16[2,96,3072]{2,1,0:T(8,128)(2,1)S(1)} %dynamic-slice_bitcast_fusion.3), channel_id=1, source_target_pairs={{0,8},{4,12},{8,0},{12,4},{16,24},{20,28},{24,16},{28,20},{1,9},{5... | collective-permute-start | bytes 3538952 | tf_op jit(solution)/shard_map/ppermute | solution.py:21
  569.9 40.7 %collective-permute-start.78 = (bf16[384,768]{1,0:T(8,128)(2,1)S(1)}, bf16[384,768]{1,0:T(8,128)(2,1)S(1)}, u32[]{:S(2)}, u32[]{:S(2)}) collective-permute-start(bf16[384,768]{1,0:T(8,128)(2,1)S(1)} %dynamic-slice_bitcast_fusion.4), channel_id=1, source_target_pairs={{0,8},{4,12},{8,0},{12,4},{16,24},{20,28},{24,16},{28,20},{1,9},{5... | collective-permute-start | bytes 1769480 | tf_op jit(solution)/shard_map/ppermute | solution.py:21
  573.1 34.3 %collective-permute-start.66 = (bf16[96,3072]{1,0:T(8,128)(2,1)S(1)}, bf16[96,3072]{1,0:T(8,128)(2,1)S(1)}, u32[]{:S(2)}, u32[]{:S(2)}) collective-permute-start(bf16[96,3072]{1,0:T(8,128)(2,1)S(1)} %dynamic-slice_bitcast_fusion.6), channel_id=1, source_target_pairs={{0,16},{4,20},{8,24},{12,28},{16,0},{20,4},{24,8},{28,12},{1,17},{... | collective-permute-start | bytes 1769480 | tf_op jit(solution)/shard_map/ppermute | solution.py:21
  595.1 36.8 %collective-permute-start.72 = (bf16[384,768]{1,0:T(8,128)(2,1)S(1)}, bf16[384,768]{1,0:T(8,128)(2,1)S(1)}, u32[]{:S(2)}, u32[]{:S(2)}) collective-permute-start(bf16[384,768]{1,0:T(8,128)(2,1)S(1)} %dynamic-slice_bitcast_fusion.5), channel_id=1, source_target_pairs={{0,8},{4,12},{8,0},{12,4},{16,24},{20,28},{24,16},{28,20},{1,9},{5... | collective-permute-start | bytes 1769480 | tf_op jit(solution)/shard_map/ppermute | solution.py:21
  598.3 38.4 %collective-permute-start.60 = (bf16[96,3072]{1,0:T(8,128)(2,1)S(1)}, bf16[96,3072]{1,0:T(8,128)(2,1)S(1)}, u32[]{:S(2)}, u32[]{:S(2)}) collective-permute-start(bf16[96,3072]{1,0:T(8,128)(2,1)S(1)} %dynamic-slice_bitcast_fusion.7), channel_id=1, source_target_pairs={{0,16},{4,20},{8,24},{12,28},{16,0},{20,4},{24,8},{28,12},{1,17},{... | collective-permute-start | bytes 1769480 | tf_op jit(solution)/shard_map/ppermute | solution.py:21
  607.6 8.0 %collective-permute-start.67 = (bf16[24,3072]{1,0:T(8,128)(2,1)S(1)}, bf16[24,3072]{1,0:T(8,128)(2,1)S(1)}, u32[]{:S(2)}, u32[]{:S(2)}) collective-permute-start(bf16[24,3072]{1,0:T(8,128)(2,1)S(1)} %get-tuple-element.175), channel_id=1, source_target_pairs={{0,1},{1,0},{2,3},{3,2},{4,5},{5,4},{6,7},{7,6},{8,9},{9,8},{10,11... | collective-permute-start | bytes 442376 | tf_op jit(solution)/shard_map/ppermute | solution.py:21
  607.7 14.8 %collective-permute-start.68 = (bf16[24,3072]{1,0:T(8,128)(2,1)S(1)}, bf16[24,3072]{1,0:T(8,128)(2,1)S(1)}, u32[]{:S(2)}, u32[]{:S(2)}) collective-permute-start(bf16[24,3072]{1,0:T(8,128)(2,1)S(1)} %get-tuple-element.177), channel_id=1, source_target_pairs={{0,2},{1,3},{2,0},{3,1},{4,6},{5,7},{6,4},{7,5},{8,10},{9,11},{10,... | collective-permute-start | bytes 442376 | tf_op jit(solution)/shard_map/ppermute | solution.py:21
  610.5 12.0 %collective-permute-start.69 = (bf16[24,3072]{1,0:T(8,128)(2,1)S(1)}, bf16[24,3072]{1,0:T(8,128)(2,1)S(1)}, u32[]{:S(2)}, u32[]{:S(2)}) collective-permute-start(bf16[24,3072]{1,0:T(8,128)(2,1)S(1)} %get-tuple-element.176), channel_id=1, source_target_pairs={{0,3},{1,2},{2,1},{3,0},{4,7},{5,6},{6,5},{7,4},{8,11},{9,10},{10,... | collective-permute-start | bytes 442376 | tf_op jit(solution)/shard_map/ppermute | solution.py:21
  615.6 9.2 %collective-permute-start.79 = (bf16[96,768]{1,0:T(8,128)(2,1)S(1)}, bf16[96,768]{1,0:T(8,128)(2,1)S(1)}, u32[]{:S(2)}, u32[]{:S(2)}) collective-permute-start(bf16[96,768]{1,0:T(8,128)(2,1)S(1)} %get-tuple-element.169), channel_id=1, source_target_pairs={{0,1},{1,0},{2,3},{3,2},{4,5},{5,4},{6,7},{7,6},{8,9},{9,8},{10,11... | collective-permute-start | bytes 442376 | tf_op jit(solution)/shard_map/ppermute | solution.py:21
  622.5 9.3 %collective-permute-start.80 = (bf16[96,768]{1,0:T(8,128)(2,1)S(1)}, bf16[96,768]{1,0:T(8,128)(2,1)S(1)}, u32[]{:S(2)}, u32[]{:S(2)}) collective-permute-start(bf16[96,768]{1,0:T(8,128)(2,1)S(1)} %get-tuple-element.171), channel_id=1, source_target_pairs={{0,2},{1,3},{2,0},{3,1},{4,6},{5,7},{6,4},{7,5},{8,10},{9,11},{10,... | collective-permute-start | bytes 442376 | tf_op jit(solution)/shard_map/ppermute | solution.py:21
  622.5 9.3 %collective-permute-start.81 = (bf16[96,768]{1,0:T(8,128)(2,1)S(1)}, bf16[96,768]{1,0:T(8,128)(2,1)S(1)}, u32[]{:S(2)}, u32[]{:S(2)}) collective-permute-start(bf16[96,768]{1,0:T(8,128)(2,1)S(1)} %get-tuple-element.170), channel_id=1, source_target_pairs={{0,3},{1,2},{2,1},{3,0},{4,7},{5,6},{6,5},{7,4},{8,11},{9,10},{10,... | collective-permute-start | bytes 442376 | tf_op jit(solution)/shard_map/ppermute | solution.py:21
  632.1 10.2 %collective-permute-start.73 = (bf16[96,768]{1,0:T(8,128)(2,1)S(1)}, bf16[96,768]{1,0:T(8,128)(2,1)S(1)}, u32[]{:S(2)}, u32[]{:S(2)}) collective-permute-start(bf16[96,768]{1,0:T(8,128)(2,1)S(1)} %get-tuple-element.166), channel_id=1, source_target_pairs={{0,1},{1,0},{2,3},{3,2},{4,5},{5,4},{6,7},{7,6},{8,9},{9,8},{10,11... | collective-permute-start | bytes 442376 | tf_op jit(solution)/shard_map/ppermute | solution.py:21
  634.3 14.0 %collective-permute-start.74 = (bf16[96,768]{1,0:T(8,128)(2,1)S(1)}, bf16[96,768]{1,0:T(8,128)(2,1)S(1)}, u32[]{:S(2)}, u32[]{:S(2)}) collective-permute-start(bf16[96,768]{1,0:T(8,128)(2,1)S(1)} %get-tuple-element.168), channel_id=1, source_target_pairs={{0,2},{1,3},{2,0},{3,1},{4,6},{5,7},{6,4},{7,5},{8,10},{9,11},{10,... | collective-permute-start | bytes 442376 | tf_op jit(solution)/shard_map/ppermute | solution.py:21
  634.4 14.0 %collective-permute-start.75 = (bf16[96,768]{1,0:T(8,128)(2,1)S(1)}, bf16[96,768]{1,0:T(8,128)(2,1)S(1)}, u32[]{:S(2)}, u32[]{:S(2)}) collective-permute-start(bf16[96,768]{1,0:T(8,128)(2,1)S(1)} %get-tuple-element.167), channel_id=1, source_target_pairs={{0,3},{1,2},{2,1},{3,0},{4,7},{5,6},{6,5},{7,4},{8,11},{9,10},{10,... | collective-permute-start | bytes 442376 | tf_op jit(solution)/shard_map/ppermute | solution.py:21
  637.0 12.3 %collective-permute-start.61 = (bf16[24,3072]{1,0:T(8,128)(2,1)S(1)}, bf16[24,3072]{1,0:T(8,128)(2,1)S(1)}, u32[]{:S(2)}, u32[]{:S(2)}) collective-permute-start(bf16[24,3072]{1,0:T(8,128)(2,1)S(1)} %get-tuple-element.172), channel_id=1, source_target_pairs={{0,1},{1,0},{2,3},{3,2},{4,5},{5,4},{6,7},{7,6},{8,9},{9,8},{10,11... | collective-permute-start | bytes 442376 | tf_op jit(solution)/shard_map/ppermute | solution.py:21
  638.1 20.1 %collective-permute-start.62 = (bf16[24,3072]{1,0:T(8,128)(2,1)S(1)}, bf16[24,3072]{1,0:T(8,128)(2,1)S(1)}, u32[]{:S(2)}, u32[]{:S(2)}) collective-permute-start(bf16[24,3072]{1,0:T(8,128)(2,1)S(1)} %get-tuple-element.174), channel_id=1, source_target_pairs={{0,2},{1,3},{2,0},{3,1},{4,6},{5,7},{6,4},{7,5},{8,10},{9,11},{10,... | collective-permute-start | bytes 442376 | tf_op jit(solution)/shard_map/ppermute | solution.py:21
  642.3 15.8 %collective-permute-start.63 = (bf16[24,3072]{1,0:T(8,128)(2,1)S(1)}, bf16[24,3072]{1,0:T(8,128)(2,1)S(1)}, u32[]{:S(2)}, u32[]{:S(2)}) collective-permute-start(bf16[24,3072]{1,0:T(8,128)(2,1)S(1)} %get-tuple-element.173), channel_id=1, source_target_pairs={{0,3},{1,2},{2,1},{3,0},{4,7},{5,6},{6,5},{7,4},{8,11},{9,10},{10,... | collective-permute-start | bytes 442376 | tf_op jit(solution)/shard_map/ppermute | solution.py:21
  (160 other events, 1234.7 us)

commit v2 on v1

v2 whole, which is shorter than its diff:
```python
import functools

import jax
import jax.numpy as jnp
from jax import lax
from jax.experimental import pallas as pl
from jax.experimental.pallas import tpu as pltpu
from jax.sharding import PartitionSpec as P

norm_eps = 1e-06
masked_score = -1000000000.0
f32 = jnp.float32
bf16 = jnp.bfloat16

BLK = 128
TILE = 8
SCALE = 1.0
HALO = 384


def cost(microseconds):
    return pl.CostEstimate(flops=int(microseconds * SCALE * 1.15e9), bytes_accessed=1000, transcendentals=0)


def swap(value, axis, bit):
    size = lax.axis_size(axis)
    return lax.ppermute(value, axis, [(i, i ^ bit) for i in range(size)])


def bit_of(axis, place):
    return (lax.axis_index(axis) >> place) & 1


def pick(value, index, axis):
    return lax.dynamic_index_in_dim(value, index, axis, keepdims=False)


def add_low(*terms):
    total = terms[0].astype(f32)
    for term in terms[1:]:
        total = total + term.astype(f32)
    return total


def finish_head(slot):
    size = lax.axis_size("head")
    me = lax.axis_index("head")
    got = [swap(slot(me ^ step), "head", step) for step in range(1, size)]
    return add_low(slot(me), *got)


def head_masks():
    lane = lax.broadcasted_iota(jnp.int32, (BLK, BLK), 1)
    return lane < BLK // 2


def stack_heads(pair, low):
    zero = jnp.zeros_like(pair)
    return jnp.concatenate([jnp.where(low, pair, zero), jnp.where(low, zero, pair)], axis=0)


def nt(left, right):
    return lax.dot_general(left, right, (((1,), (1,)), ((), ())), preferred_element_type=f32)


def nn(left, right):
    return lax.dot_general(left, right, (((1,), (0,)), ((), ())), preferred_element_type=f32)


def attend_kernel(pairs, own_blocks, halo_blocks, bounds, segq, segk, qkv, kvh, ctx, ctx_t, ctx_low, lse, vt, qs, top, total, acc):
    width = pairs * BLK
    low = head_masks()
    half = BLK // 2
    for j in range(own_blocks + halo_blocks):
        for p in range(pairs):
            if j < own_blocks:
                tile = qkv[j * BLK : (j + 1) * BLK, 2 * width + p * BLK : 2 * width + (p + 1) * BLK]
            else:
                at = j - own_blocks
                tile = kvh[at * BLK : (at + 1) * BLK, width + p * BLK : width + (p + 1) * BLK]
            vt[j, p * BLK : (p + 1) * BLK, :] = tile.T

    def q_block(i, carry):
        rows = pl.ds(pl.multiple_of(i * BLK, BLK), BLK)
        for p in range(pairs):
            qs[p] = stack_heads(qkv[rows, p * BLK : (p + 1) * BLK], low)
        top[...] = jnp.full(top.shape, -1e30, f32)
        total[...] = jnp.zeros(total.shape, f32)
        acc[...] = jnp.zeros(acc.shape, f32)
        labels = segq[i]

        def k_block(ref, first, base, j, carry):
            here = pl.ds(pl.multiple_of(j * BLK, BLK), BLK)
            there = pl.ds(pl.multiple_of((base + j) * BLK, BLK), BLK)
            same = segk[there, :] == labels
            for p in range(pairs):
                keys = ref[here, first + p * BLK : first + (p + 1) * BLK]
                scores = jnp.where(same, nt(keys, qs[p]), masked_score)
                old = top[p : p + 1, :]
                new = jnp.maximum(old, jnp.max(scores, axis=0, keepdims=True))
                expo = jnp.exp(scores - new)
                scale = jnp.exp(old - new)
                top[p : p + 1, :] = new
                total[p : p + 1, :] = total[p : p + 1, :] * scale + jnp.sum(expo, axis=0, keepdims=True)
                weights = expo.astype(bf16)
                for h in range(2):
                    values = vt[base + j, p * BLK + h * half : p * BLK + (h + 1) * half, :]
                    part = slice(h * half, (h + 1) * half)
                    cols = slice(h * BLK, (h + 1) * BLK)
                    acc[p, part, :] = acc[p, part, :] * scale[:, cols] + nn(values, weights[:, cols])
            return carry

        lax.fori_loop(bounds[i, 0], bounds[i, 1], functools.partial(k_block, qkv, width, 0), 0)
        lax.fori_loop(bounds[i, 2], bounds[i, 3], functools.partial(k_block, kvh, 0, own_blocks), 0)
        for p in range(pairs):
            inverse = 1.0 / total[p : p + 1, :]
            flat = jnp.concatenate(
                [acc[p, :half, :] * inverse[:, :BLK], acc[p, half:, :] * inverse[:, BLK:]], axis=0
            )
            rounded = flat.astype(bf16)
            ctx_t[p * BLK : (p + 1) * BLK, rows] = flat
            ctx_low[p * BLK : (p + 1) * BLK, rows] = rounded
            ctx[rows, p * BLK : (p + 1) * BLK] = rounded.T
        lse[i] = top[...] + jnp.log(total[...])
        return carry

    lax.fori_loop(0, own_blocks, q_block, 0)


def attend_back_kernel(
    pairs, own_blocks, halo_blocks,
    bounds, segq, segk, qkv, kvh, ctx_t, lse, dctx, norm_sums, up_sum,
    dqkv, dkvh, sums,
    kt, qs, cs, delta, dqt, dk, dv,
):
    width = pairs * BLK
    low = head_masks()
    half = BLK // 2
    blocks = own_blocks + halo_blocks
    for j in range(blocks):
        for p in range(pairs):
            if j < own_blocks:
                tile = qkv[j * BLK : (j + 1) * BLK, width + p * BLK : width + (p + 1) * BLK]
            else:
                at = j - own_blocks
                tile = kvh[at * BLK : (at + 1) * BLK, p * BLK : (p + 1) * BLK]
            kt[j, p * BLK : (p + 1) * BLK, :] = tile.T
    dk[...] = jnp.zeros(dk.shape, f32)
    dv[...] = jnp.zeros(dv.shape, f32)
    sums[...] = jnp.zeros(sums.shape, f32)
    sums[0:8, :] = norm_sums[...]
    for at in range(up_sum.shape[1] // width):
        sums[8 + at : 9 + at, :] = up_sum[:, at * width : (at + 1) * width]

    def q_block(i, carry):
        rows = pl.ds(pl.multiple_of(i * BLK, BLK), BLK)
        for p in range(pairs):
            cols = slice(p * BLK, (p + 1) * BLK)
            qs[p] = stack_heads(qkv[rows, cols], low)
            pull = dctx[rows, cols]
            cs[p] = stack_heads(pull, low)
            prod = pull.astype(f32).T * ctx_t[cols, rows]
            delta[p : p + 1, :] = jnp.concatenate(
                [jnp.sum(prod[:half], axis=0, keepdims=True), jnp.sum(prod[half:], axis=0, keepdims=True)], axis=1
            )
        dqt[...] = jnp.zeros(dqt.shape, f32)
        labels = segq[i]

        def k_block(ref, first, base, j, carry):
            here = pl.ds(pl.multiple_of(j * BLK, BLK), BLK)
            there = pl.ds(pl.multiple_of((base + j) * BLK, BLK), BLK)
            same = segk[there, :] == labels
            for p in range(pairs):
                cols = slice(p * BLK, (p + 1) * BLK)
                keys = ref[here, first + p * BLK : first + (p + 1) * BLK]
                values = ref[here, first + width + p * BLK : first + width + (p + 1) * BLK]
                scores = jnp.where(same, nt(keys, qs[p]), masked_score)
                probs = jnp.exp(scores - lse[i, p : p + 1, :])
                pulls = nt(values, cs[p])
                dscore = (probs * (pulls - delta[p : p + 1, :])).astype(bf16)
                dv[there, cols] += nn(probs.astype(bf16), cs[p])
                dk[there, cols] += nn(dscore, qs[p])
                for h in range(2):
                    part = slice(h * half, (h + 1) * half)
                    flip = kt[base + j, p * BLK + h * half : p * BLK + (h + 1) * half, :]
                    dqt[p, part, :] += nn(flip, dscore[:, h * BLK : (h + 1) * BLK])
            return carry

        lax.fori_loop(bounds[i, 0], bounds[i, 1], functools.partial(k_block, qkv, width, 0), 0)
        lax.fori_loop(bounds[i, 2], bounds[i, 3], functools.partial(k_block, kvh, 0, own_blocks), 0)
        for p in range(pairs):
            cols = slice(p * BLK, (p + 1) * BLK)
            grad = dqt[p].T.astype(bf16) * jnp.asarray(0.125, bf16)
            dqkv[rows, cols] = grad
            sums[6:7, cols] += jnp.sum(grad.astype(f32), axis=0, keepdims=True)
        return carry

    lax.fori_loop(0, own_blocks, q_block, 0)
    for j in range(blocks):
        rows = slice(j * BLK, (j + 1) * BLK)
        grad_k = dk[rows, :].astype(bf16)
        grad_v = dv[rows, :].astype(bf16)
        if j < own_blocks:
            dqkv[rows, width : 2 * width] = grad_k
            dqkv[rows, 2 * width :] = grad_v
        else:
            back = slice((j - own_blocks) * BLK, (j - own_blocks + 1) * BLK)
            dkvh[back, :width] = grad_k
            dkvh[back, width:] = grad_v
        sums[7:8, :] += jnp.sum(grad_v.astype(f32), axis=0, keepdims=True)


def vmem_specs(count):
    return [pl.BlockSpec(memory_space=pltpu.VMEM)] * count


def any_specs(count):
    return [pl.BlockSpec(memory_space=pl.ANY)] * count


def ordered_call(kernel, args, waits, passes, out_shape, in_specs, out_specs, **options):
    waits, passes = tuple(waits) + tuple(turn.last), tuple(passes)
    given, made = len(args), len(out_shape)
    skipped = len(waits) + len(passes)

    def body(*refs):
        outs = given + skipped
        refs[outs + made][...] = jnp.zeros((8, BLK), f32)
        kernel(*refs[:given], *refs[outs : outs + made], *refs[outs + made + 1 + len(passes) :])

    out = pl.pallas_call(
        body,
        out_shape=tuple(out_shape)
        + (jax.ShapeDtypeStruct((8, BLK), f32),)
        + tuple(jax.ShapeDtypeStruct(p.shape, p.dtype) for p in passes),
        in_specs=list(in_specs) + any_specs(skipped),
        out_specs=tuple(out_specs) + (pl.BlockSpec((8, BLK), lambda *step: (0, 0)),) + tuple(any_specs(len(passes))),
        input_output_aliases={given + len(waits) + k: made + 1 + k for k in range(len(passes))},
        **options,
    )(*args, *waits, *passes)
    turn.last = [out[made]]
    return out[:made], out[made + 1 :]


class Turn:
    last = []


turn = Turn()


def attend(bounds, segq, segk, qkv, kvh, waits, passes):
    tokens, width3 = qkv.shape
    width = width3 // 3
    pairs, own_blocks, halo_blocks = width // BLK, tokens // BLK, kvh.shape[0] // BLK
    blocks = own_blocks + halo_blocks
    return ordered_call(
        functools.partial(attend_kernel, pairs, own_blocks, halo_blocks),
        (bounds, segq, segk, qkv, kvh),
        waits,
        passes,
        out_shape=(
            jax.ShapeDtypeStruct((tokens, width), bf16),
            jax.ShapeDtypeStruct((width, tokens), f32),
            jax.ShapeDtypeStruct((width, tokens), bf16),
            jax.ShapeDtypeStruct((own_blocks, 8, 2 * BLK), f32),
        ),
        in_specs=[pl.BlockSpec(memory_space=pltpu.SMEM)] + vmem_specs(4),
        out_specs=tuple(vmem_specs(4)),
        scratch_shapes=[
            pltpu.VMEM((blocks, width, BLK), bf16),
            pltpu.VMEM((pairs, 2 * BLK, BLK), bf16),
            pltpu.VMEM((8, 2 * BLK), f32),
            pltpu.VMEM((8, 2 * BLK), f32),
            pltpu.VMEM((pairs, BLK, BLK), f32),
        ],
        compiler_params=pltpu.CompilerParams(vmem_limit_bytes=32 * 2**20),
        cost_estimate=cost(9),
        name="attend",
    )


def attend_back(bounds, segq, segk, qkv, kvh, ctx_t, lse, dctx, norm_sums, up_sum, waits, passes):
    tokens, width3 = qkv.shape
    width = width3 // 3
    pairs, own_blocks, halo_blocks = width // BLK, tokens // BLK, kvh.shape[0] // BLK
    blocks = own_blocks + halo_blocks
    return ordered_call(
        functools.partial(attend_back_kernel, pairs, own_blocks, halo_blocks),
        (bounds, segq, segk, qkv, kvh, ctx_t, lse, dctx, norm_sums, up_sum),
        waits,
        passes,
        out_shape=(
            jax.ShapeDtypeStruct((tokens, width3), bf16),
            jax.ShapeDtypeStruct(kvh.shape, bf16),
            jax.ShapeDtypeStruct((16, width), f32),
        ),
        in_specs=[pl.BlockSpec(memory_space=pltpu.SMEM)] + vmem_specs(9),
        out_specs=tuple(vmem_specs(3)),
        scratch_shapes=[
            pltpu.VMEM((blocks, width, BLK), bf16),
            pltpu.VMEM((pairs, 2 * BLK, BLK), bf16),
            pltpu.VMEM((pairs, 2 * BLK, BLK), bf16),
            pltpu.VMEM((8, 2 * BLK), f32),
            pltpu.VMEM((pairs, BLK, BLK), f32),
            pltpu.VMEM((blocks * BLK, width), f32),
            pltpu.VMEM((blocks * BLK, width), f32),
        ],
        compiler_params=pltpu.CompilerParams(vmem_limit_bytes=40 * 2**20),
        cost_estimate=cost(21),
        name="attend_back",
    )


CHUNK = 512


def normalized(rows):
    center = rows - jnp.mean(rows, axis=-1, keepdims=True)
    spread = jnp.mean(center * center, axis=-1, keepdims=True)
    scale = lax.rsqrt(spread + norm_eps)
    return center * scale, scale


def feed_kernel(last, tokens, hidden, ctx, w_out, vec, w_up, up_bias, w_down, *rest):
    if last:
        first_rows, first_t, active_t, slope, second_rows, low, low_rows, first, total = rest
    else:
        first_rows, first_t, active_t, slope, second_rows, low, after, low_t, low_rows, first, total = rest
    step = pl.program_id(0)
    tiles = [slice(at, at + BLK) for at in range(0, tokens, BLK)]

    @pl.when(step == 0)
    def _():
        for rows in tiles:
            resid = hidden[rows, :].astype(f32) + (nn(ctx[rows, :], w_out[...]) + vec[0:1, :])
            first_rows[rows, :] = resid
            unit, _ = normalized(resid)
            value = unit * vec[1:2, :] + vec[2:3, :]
            first[rows, :] = value
            total[rows, :] = jnp.zeros_like(value)
            rounded = value.astype(bf16)
            low_rows[rows, :] = rounded
            first_t[:, rows] = rounded.T

    for rows in tiles:
        upward = nn(low_rows[rows, :], w_up[...]) + up_bias[...]
        density = jnp.exp(-0.5 * upward * upward) * 0.3989422804014327
        below = 0.5 + 0.5 * lax.erf(upward * 0.7071067811865476)
        active = (upward * below).astype(bf16)
        slope[rows, :] = below + upward * density
        active_t[:, rows] = active.T
        total[rows, :] += nn(active, w_down[...])

    @pl.when(step == pl.num_programs(0) - 1)
    def _():
        for rows in tiles:
            resid = first[rows, :] + (total[rows, :] + vec[3:4, :])
            second_rows[rows, :] = resid
            unit, _ = normalized(resid)
            value = unit * vec[4:5, :] + vec[5:6, :]
            rounded = value.astype(bf16)
            low[rows, :] = rounded
            if not last:
                after[rows, :] = value
                low_t[:, rows] = rounded.T


def whole(shape):
    return pl.BlockSpec(shape, lambda step: (0,) * len(shape))


def feed(last, layer_idx, hidden, ctx, w_out, vec, w_up, up_bias, w_down, waits, passes):
    tokens, width = hidden.shape
    wide = w_up.shape[-1]
    rows = whole((tokens, width))
    shapes = [
        jax.ShapeDtypeStruct((tokens, width), f32),
        jax.ShapeDtypeStruct((width, tokens), bf16),
        jax.ShapeDtypeStruct((wide, tokens), bf16),
        jax.ShapeDtypeStruct((tokens, wide), f32),
        jax.ShapeDtypeStruct((tokens, width), f32),
        jax.ShapeDtypeStruct((tokens, width), bf16),
    ]
    specs = [
        rows,
        whole((width, tokens)),
        pl.BlockSpec((CHUNK, tokens), lambda step: (step, 0)),
        pl.BlockSpec((tokens, CHUNK), lambda step: (0, step)),
        rows,
        rows,
    ]
    if not last:
        shapes.append(jax.ShapeDtypeStruct((tokens, width), f32))
        shapes.append(jax.ShapeDtypeStruct((width, tokens), bf16))
        specs.append(rows)
        specs.append(whole((width, tokens)))
    return ordered_call(
        functools.partial(feed_kernel, last, tokens),
        (hidden, ctx, w_out, vec, w_up, up_bias, w_down),
        waits,
        passes,
        grid=(wide // CHUNK,),
        out_shape=tuple(shapes),
        in_specs=[
            rows,
            rows,
            pl.BlockSpec((None, width, width), lambda step: (layer_idx, 0, 0)),
            whole(vec.shape),
            pl.BlockSpec((None, width, CHUNK), lambda step: (layer_idx, 0, step)),
            pl.BlockSpec((1, CHUNK), lambda step: (0, step)),
            pl.BlockSpec((None, CHUNK, width), lambda step: (layer_idx, step, 0)),
        ],
        out_specs=tuple(specs),
        scratch_shapes=[
            pltpu.VMEM((tokens, width), bf16),
            pltpu.VMEM((tokens, width), f32),
            pltpu.VMEM((tokens, width), f32),
        ],
        compiler_params=pltpu.CompilerParams(vmem_limit_bytes=48 * 2**20),
        cost_estimate=cost(17),
        name="feed",
    )


def norm_back(grad, gain, rows):
    unit, scale = normalized(rows)
    lifted = grad * gain
    first = jnp.mean(lifted, axis=-1, keepdims=True)
    second = jnp.mean(lifted * unit, axis=-1, keepdims=True)
    return scale * (lifted - first - unit * second), unit


def over_rows(value):
    return jnp.sum(value, axis=0, keepdims=True)


def feed_back_kernel(
    tokens, grad, second_rows, first_rows, slope, w_down, w_up, w_out, vec,
    dz, du, da, dr, dc, sums, up_sum, dr_two, total,
):
    step = pl.program_id(0)
    tiles = [slice(at, at + BLK) for at in range(0, tokens, BLK)]

    @pl.when(step == 0)
    def _():
        sums[...] = jnp.zeros(sums.shape, f32)
        for rows in tiles:
            pull = grad[rows, :].astype(f32)
            value, unit = norm_back(pull, vec[4:5, :], second_rows[rows, :])
            dr_two[rows, :] = value
            total[rows, :] = jnp.zeros_like(value)
            rounded = value.astype(bf16)
            dz[rows, :] = rounded
            sums[3:4, :] += over_rows(rounded.astype(f32))
            sums[4:5, :] += over_rows(pull * unit)
            sums[5:6, :] += over_rows(pull)

    up_sum[...] = jnp.zeros(up_sum.shape, f32)
    for rows in tiles:
        pull = (nt(dz[rows, :], w_down[...]) * slope[rows, :]).astype(bf16)
        du[rows, :] = pull
        up_sum[...] += over_rows(pull.astype(f32))
        total[rows, :] += nt(pull, w_up[...])

    @pl.when(step == pl.num_programs(0) - 1)
    def _():
        for rows in tiles:
            pull = total[rows, :] + dr_two[rows, :]
            value, unit = norm_back(pull, vec[1:2, :], first_rows[rows, :])
            dr[rows, :] = value
            rounded = value.astype(bf16)
            da[rows, :] = rounded
            sums[0:1, :] += over_rows(rounded.astype(f32))
            sums[1:2, :] += over_rows(pull * unit)
            sums[2:3, :] += over_rows(pull)
            dc[rows, :] = nt(rounded, w_out[...]).astype(bf16)


def feed_back(layer_idx, grad, second_rows, first_rows, slope, w_down, w_up, w_out, vec, waits, passes):
    tokens, width = grad.shape
    wide = w_up.shape[-1]
    rows = whole((tokens, width))
    return ordered_call(
        functools.partial(feed_back_kernel, tokens),
        (grad, second_rows, first_rows, slope, w_down, w_up, w_out, vec),
        waits,
        passes,
        grid=(wide // CHUNK,),
        out_shape=(
            jax.ShapeDtypeStruct((tokens, width), bf16),
            jax.ShapeDtypeStruct((tokens, wide), bf16),
            jax.ShapeDtypeStruct((tokens, width), bf16),
            jax.ShapeDtypeStruct((tokens, width), f32),
            jax.ShapeDtypeStruct((tokens, width), bf16),
            jax.ShapeDtypeStruct((8, width), f32),
            jax.ShapeDtypeStruct((1, wide), f32),
        ),
        in_specs=[
            rows,
            rows,
            rows,
            pl.BlockSpec((tokens, CHUNK), lambda step: (0, step)),
            pl.BlockSpec((None, CHUNK, width), lambda step: (layer_idx, step, 0)),
            pl.BlockSpec((None, width, CHUNK), lambda step: (layer_idx, 0, step)),
            pl.BlockSpec((None, width, width), lambda step: (layer_idx, 0, 0)),
            whole(vec.shape),
        ],
        out_specs=(
            rows,
            pl.BlockSpec((tokens, CHUNK), lambda step: (0, step)),
            rows,
            rows,
            rows,
            whole((8, width)),
            pl.BlockSpec((1, CHUNK), lambda step: (0, step)),
        ),
        scratch_shapes=[pltpu.VMEM((tokens, width), f32), pltpu.VMEM((tokens, width), f32)],
        compiler_params=pltpu.CompilerParams(vmem_limit_bytes=48 * 2**20),
        cost_estimate=cost(21),
        name="feed_back",
    )


def grad_feed_kernel(core, active_t, dz, first_t, du, send, keep, lhs):
    groups, head, _, parts, thin, width = send.shape
    rows = head * thin
    mine = core[0]
    for which, out in ((1 - mine, send), (mine, keep)):
        for group in range(groups):
            value = nn(active_t[2 * group + which], dz[...])
            for shard in range(head):
                for at in range(parts):
                    here = (shard * parts + at) * thin
                    out[group, shard, 0, at] = value[here : here + thin].astype(bf16)
        if rows % 16 == 0:
            for group in range(groups):
                lhs[group * rows : (group + 1) * rows, :] = first_t[2 * group + which]
        for at in range(parts):
            pulls = du[:, at * width : (at + 1) * width]
            if rows % 16 == 0:
                value = nn(lhs[...], pulls)
                values = [value[group * rows : (group + 1) * rows] for group in range(groups)]
            else:
                values = [nn(first_t[2 * group + which], pulls) for group in range(groups)]
            for group in range(groups):
                for shard in range(head):
                    out[group, shard, 1, at] = values[group][shard * thin : (shard + 1) * thin].astype(bf16)


def grad_feed(core, active_t, dz, first_t, du, devices, head, waits, passes):
    tokens, width = dz.shape
    wide = du.shape[1]
    parts, rows = wide // width, width // devices
    out = jax.ShapeDtypeStruct((devices // 2, head, 2, parts, rows // head, width), bf16)
    return ordered_call(
        grad_feed_kernel,
        (core, active_t.reshape(devices, wide // devices, tokens), dz, first_t.reshape(devices, rows, tokens), du),
        waits,
        passes,
        out_shape=(out, out),
        in_specs=[pl.BlockSpec(memory_space=pltpu.SMEM)] + vmem_specs(4),
        out_specs=tuple(vmem_specs(2)),
        scratch_shapes=[pltpu.VMEM((width // 2, tokens), bf16)],
        compiler_params=pltpu.CompilerParams(vmem_limit_bytes=48 * 2**20),
        cost_estimate=cost(10),
        name="grad_feed",
    )


def grad_heads_kernel(core, ctx_t, low_t, halo_t, da, dqkv, dkvh, sums, send, keep, one, two, three):
    groups, thin = ctx_t.shape[0] // 2, ctx_t.shape[1]
    width = send.shape[2] // 4
    high = thin // TILE
    for r in range(sums.shape[0] // TILE):
        value = sums[r * TILE : (r + 1) * TILE, :].astype(bf16)
        for out in (send, keep):
            out[groups * high, :, r * width : (r + 1) * width] = value
    mine = core[0]
    for which, out in ((1 - mine, send), (mine, keep)):
        if thin % 16 == 0:
            for group in range(groups):
                here = slice(group * thin, (group + 1) * thin)
                one[here, :] = ctx_t[2 * group + which]
                two[here, :] = low_t[2 * group + which]
                three[here, :] = halo_t[2 * group + which]
            parts = [(range(groups), one, two, three)]
        else:
            parts = [
                ([group], ctx_t.at[2 * group + which], low_t.at[2 * group + which], halo_t.at[2 * group + which])
                for group in range(groups)
            ]
        for members, left_one, left_two, left_three in parts:
            for at in range(0, 4 * width, width):
                if at < width:
                    value = nn(left_one[...], da[...])
                else:
                    value = nn(left_two[...], dqkv[:, at - width : at])
                    if at >= 2 * width:
                        value = value + nn(left_three[...], dkvh[:, at - 2 * width : at - width])
                for place, group in enumerate(members):
                    here = value[place * thin : (place + 1) * thin].reshape(high, TILE, width)
                    out[group * high : (group + 1) * high, :, at : at + width] = here.astype(bf16)


def grad_heads(core, ctx_t, low_t, halo_t, da, dqkv, dkvh, sums, devices, waits, passes):
    tokens, width = da.shape
    thin = width // devices
    out = jax.ShapeDtypeStruct((devices // 2 * thin // TILE + 1, TILE, 4 * width), bf16)
    extent = halo_t.shape[1]
    return ordered_call(
        grad_heads_kernel,
        (
            core,
            ctx_t.reshape(devices, thin, tokens),
            low_t.reshape(devices, thin, tokens),
            halo_t.reshape(devices, thin, extent),
            da,
            dqkv,
            dkvh,
            sums,
        ),
        waits,
        passes,
        out_shape=(out, out),
        in_specs=[pl.BlockSpec(memory_space=pltpu.SMEM)] + vmem_specs(7),
        out_specs=tuple(vmem_specs(2)),
        scratch_shapes=[
            pltpu.VMEM((width // 2, tokens), bf16),
            pltpu.VMEM((width // 2, tokens), bf16),
            pltpu.VMEM((width // 2, extent), bf16),
        ],
        compiler_params=pltpu.CompilerParams(vmem_limit_bytes=48 * 2**20),
        cost_estimate=cost(8),
        name="grad_heads",
    )


def assemble_kernel(relative, place, own, *refs):
    *refs, out = refs
    shard, group = place[0], place[1]
    kinds = own.shape[0]
    out[:, pl.ds(shard, 1)] = own[...].reshape(kinds, 1, *own.shape[1:])
    lane = 0
    for ref, order in zip(refs, relative):
        lanes = slice(lane, lane + ref.shape[-1])
        lane = lanes.stop % own.shape[-1]
        for at, change in enumerate(order):
            for step in range(ref.shape[1]):
                for kind in range(kinds):
                    out[kind, shard ^ (step + 1), group ^ change, :, lanes] = ref[at, step, kind]


def assemble(relative, place, own, refs):
    head = lax.axis_size("head")
    (out,), _ = ordered_call(
        functools.partial(assemble_kernel, relative),
        (place, own, *refs),
        (),
        (),
        out_shape=(jax.ShapeDtypeStruct((own.shape[0], head) + own.shape[1:], bf16),),
        in_specs=[pl.BlockSpec(memory_space=pltpu.SMEM)] + vmem_specs(1 + len(refs)),
        out_specs=vmem_specs(1),
        compiler_params=pltpu.CompilerParams(vmem_limit_bytes=32 * 2**20),
        cost_estimate=cost(1.5),
        name="assemble",
    )
    return out


def grow(value, order):
    value, relative = value[None], [0]
    for place in order:
        value = jnp.concatenate([value, swap(value, "dp", 1 << place)], axis=0)
        relative = relative + [other ^ (1 << place) for other in relative]
    return value, relative


def flip_kernel(count, *refs):
    for source, target in zip(refs[:count], refs[count:]):
        for at in range(0, source.shape[0], BLK):
            target[:, at : at + BLK] = source[at : at + BLK, :].T


def flip(values, passes):
    return ordered_call(
        functools.partial(flip_kernel, len(values)),
        values,
        (),
        passes,
        out_shape=[jax.ShapeDtypeStruct(v.shape[::-1], v.dtype) for v in values],
        in_specs=vmem_specs(len(values)),
        out_specs=vmem_specs(len(values)),
        compiler_params=pltpu.CompilerParams(vmem_limit_bytes=32 * 2**20),
        cost_estimate=cost(1.5),
        name="flip",
    )


def collect_kernel(*refs):
    *parts, out = refs
    for k, ref in enumerate(parts):
        out[k] = ref[...]


def collect(values):
    (out,), _ = ordered_call(
        collect_kernel,
        values,
        (),
        (),
        out_shape=(jax.ShapeDtypeStruct((len(values),) + values[0].shape, values[0].dtype),),
        in_specs=vmem_specs(len(values)),
        out_specs=vmem_specs(1),
        compiler_params=pltpu.CompilerParams(vmem_limit_bytes=32 * 2**20),
        cost_estimate=cost(1.4),
        name="collect",
    )
    return out


def from_heads_in_turn(piece):
    got = [swap(piece, "head", 1)]
    step = 2
    while step < lax.axis_size("head"):
        far = [swap(value, "head", step) for value in [piece]]
        for value in far:
            got = got + [value, swap(value, "head", 1)]
        step *= 2
    return got


def from_heads(piece):
    return [swap(piece, "head", step) for step in range(1, lax.axis_size("head"))]


def added(keep, got):
    return keep.astype(f32) + got.astype(f32)


def advance_kernel(counts, size, tail, scalars, keep, got, send, out):
    core, mine = scalars[0], scalars[1]
    blocks = (keep.shape[0] - tail) // size
    for target, which in ((send, 1 - mine), (out, mine)):
        for k in range(blocks // 2):
            spots = [2 * (k // after) * after + k % after for after in counts]
            at = jnp.where(core == 0, spots[0] + which * counts[0], spots[1] + which * counts[1])
            here = pl.ds(at * size, size)
            target[k * size : (k + 1) * size] = added(keep[here], got[here]).astype(bf16)
        if tail:
            value = added(keep[blocks * size :], got[blocks * size :]).astype(bf16)
            target[blocks // 2 * size :] = value


def turn_heads_kernel(head, scalars, keep, got, send, out):
    mine = scalars[1]
    tiles, _, columns = keep.shape
    rows, width = (tiles - 1) * TILE, columns // 4
    held = added(keep[: tiles - 1], got[: tiles - 1]).reshape(rows, columns)
    part, thin = width // head, rows // head
    kinds = []
    if rows < BLK:
        filler = jnp.zeros((BLK - rows, width), f32)
    for kind in range(1, 4):
        value = held[:, kind * width : (kind + 1) * width]
        value = jnp.concatenate([value, filler], axis=0) if rows < BLK else value
        kinds.append(value.T)
    high = part // (width // BLK)
    count = part // TILE
    for shard in range(head):
        pieces = [value[shard * part : (shard + 1) * part] for value in kinds]
        own = held[shard * thin : (shard + 1) * thin, :width]
        own = jnp.concatenate([own, jnp.zeros((high - thin, width), f32)], axis=0)
        pieces.append(jnp.concatenate([own[:, at : at + BLK] for at in range(0, width, BLK)], axis=0))
        for chosen, target in ((1 - mine, send), (mine, out)):

            @pl.when(chosen == shard % 2)
            def _(target=target, pieces=pieces, shard=shard):
                for kind, piece in enumerate(pieces):
                    at = (shard // 2 * 4 + kind) * count
                    target[at : at + count] = piece.reshape(count, TILE, BLK).astype(bf16)

    last = added(keep[tiles - 1], got[tiles - 1])
    for target in (send, out):
        for k in range(2 * width // BLK):
            target[head // 2 * 4 * count + k] = last[:, k * BLK : (k + 1) * BLK].astype(bf16)


class Flight:
    def __init__(self, send, keep, turned):
        dp, head = lax.axis_size("dp"), lax.axis_size("head")
        bits = dp.bit_length() - 1
        upper = list(range(1, bits))
        self.orders = [list(upper), list(upper)[::-1]]
        self.left = [upper[::-1], upper[::-1]]
        self.head_bits = list(range(head.bit_length() - 1))
        self.turned = turned
        self.keep, self.got = keep, swap(send, "dp", 1)
        self.tail, self.size = 0, 1
        if turned:
            self.tail, self.size = 1, (keep.shape[0] - 1) // (dp // 2)
        else:
            shape = (keep.shape[0] * keep.shape[1],) + keep.shape[2:]
            self.keep, self.got = self.keep.reshape(shape), self.got.reshape(shape)

    def step(self, waits=(), passes=()):
        blocks = (self.keep.shape[0] - self.tail) // self.size
        core = bit_of("dp", 0)
        rest = self.keep.shape[1:]
        devices = lax.axis_size("dp")
        counts = [1, 1]
        if self.orders[0]:
            places = [order.pop(0) for order in self.orders]
            counts = []
            for left, place in zip(self.left, places):
                axis = left.index(place)
                left.remove(place)
                counts.append((blocks // 2) >> axis)
            mine = jnp.where(core == 0, bit_of("dp", places[0]), bit_of("dp", places[1]))
            axis_name, pairs = "dp", [(i, i ^ (1 << places[i & 1])) for i in range(devices)]
        else:
            place = self.head_bits.pop(0)
            mine = bit_of("head", place)
            head = lax.axis_size("head")
            axis_name, pairs = "head", [(i, i ^ (1 << place)) for i in range(head)]
        if axis_name == "head" and self.turned:
            width = rest[1] // 4
            self.turned = False
            self.size, self.tail = 4 * (width // head) // TILE, 2 * width // BLK
            out_shape = (head // 2 * self.size + self.tail, TILE, BLK)
            kernel = functools.partial(turn_heads_kernel, head)
        else:
            out_shape = (blocks // 2 * self.size + self.tail,) + rest
            kernel = functools.partial(advance_kernel, counts, self.size, self.tail)
        out = jax.ShapeDtypeStruct(out_shape, bf16)
        (send, keep), passed = ordered_call(
            kernel,
            (jnp.stack([core, mine]).astype(jnp.int32), self.keep, self.got),
            waits,
            passes,
            out_shape=[out] * 2,
            in_specs=[pl.BlockSpec(memory_space=pltpu.SMEM)] + vmem_specs(2),
            out_specs=vmem_specs(2),
            compiler_params=pltpu.CompilerParams(vmem_limit_bytes=48 * 2**20),
            cost_estimate=cost(4),
            name="advance",
        )
        self.keep, self.got = keep, lax.ppermute(send, axis_name, pairs)
        return passed

    def finish(self):
        while self.orders[0] or self.head_bits:
            self.step()
        total = added(self.keep, self.got)
        return total if self.tail else total[0]


def per_device(
    tokens_in,
    segment,
    w_qkv,
    qv_bias,
    w_out,
    out_bias,
    ln1_gain,
    ln1_bias,
    w_up,
    up_bias,
    w_down,
    down_bias,
    ln2_gain,
    ln2_bias,
    cotangent,
):
    turn.last = []
    layers, width = w_qkv.shape[0], w_qkv.shape[1]
    part = w_qkv.shape[3] * w_qkv.shape[4]
    head_size = w_qkv.shape[4]
    tokens = tokens_in.shape[0]
    seq = segment.shape[1]
    dp, head = lax.axis_size("dp"), lax.axis_size("head")
    bits = dp.bit_length() - 1
    shard, group = lax.axis_index("head"), lax.axis_index("dp")
    halves = seq // tokens
    row, half = shard // halves, shard % halves
    upper = list(range(1, bits))

    edge = jnp.where(half == 0, tokens - HALO, 0)
    core = bit_of("dp", 0)

    own_w = w_qkv.transpose(0, 2, 3, 4, 1).reshape(layers, 3, part, width)
    own_first = own_w[0].reshape(3, dp, part // dp, width)
    piece = pick(own_first, group, 1).reshape(-1, width)
    rows_w = piece.shape[0]
    bias_own = qv_bias.reshape(1, layers * 2 * part)
    bias_own = jnp.pad(bias_own, ((0, 7), (0, width - bias_own.shape[1])))
    piece = jnp.concatenate([piece, bias_own])
    got = from_heads(piece)
    halo = swap(lax.dynamic_slice_in_dim(tokens_in, edge, HALO), "head", 1)
    biases = jnp.stack([other[rows_w, : layers * 2 * part] for other in [piece] + got])
    biases = biases.reshape(head, layers * 2, 1, part).astype(f32)
    members = jnp.arange(head)
    matches = (members[:, None] ^ shard) == members[None, :]
    bias_all = jnp.sum(jnp.where(matches[:, None, :, None], biases, 0.0), axis=0).reshape(layers, 2, -1)
    got = jnp.stack([other[:rows_w] for other in got]).reshape(head - 1, 3, part // dp, width)
    left, relative_left = grow(got[..., : width // 2], upper)
    right, relative_right = grow(got[..., width // 2 :], upper[::-1])
    both = jnp.stack([left, right])
    both = jnp.concatenate([both, swap(both, "dp", 1)], axis=1)
    relative = [order + [other ^ 1 for other in order] for order in (relative_left, relative_right)]
    place = jnp.stack([shard, group]).astype(jnp.int32)
    own_later = [own_w[k].reshape(3, 2, part // 2, width) for k in range(1, layers)]
    (low_t, halo_t), pieces = flip([tokens_in, halo], [pick(own, core, 1) for own in own_later])
    later_got = [from_heads_in_turn(value) for value in pieces]
    w_cats = [assemble(relative, place, own_first, [both[0], both[1]]).reshape(3 * head * part, width)]

    def later_weights(own, got):
        theirs = swap(got, "dp", 1)
        whole = assemble([[0], [1]], jnp.stack([shard, core]).astype(jnp.int32), own, [got[None], theirs[None]])
        return whole.reshape(3 * head * part, width)

    labels = pick(segment, row, 0)
    own_labels = lax.dynamic_slice_in_dim(labels, half * tokens, tokens)
    halo_start = jnp.where(half == 0, tokens, tokens - HALO)
    halo_labels = lax.dynamic_slice_in_dim(labels, halo_start, HALO)
    blocks = tokens // BLK
    by_block = own_labels.reshape(blocks, BLK)
    least, most = by_block[:, :1], by_block[:, -1:]

    def count(flags):
        return jnp.sum(flags.astype(jnp.int32), axis=1)

    bounds = jnp.stack(
        [
            count(own_labels[None] < least) // BLK,
            (count(own_labels[None] <= most) + BLK - 1) // BLK,
            count(halo_labels[None] < least) // BLK,
            (count(halo_labels[None] <= most) + BLK - 1) // BLK,
        ],
        axis=1,
    )
    segq = jnp.concatenate([by_block, by_block], axis=1).reshape(blocks, 1, 2 * BLK)
    segk = jnp.concatenate([own_labels, halo_labels]).reshape(-1, 1)
    core_at = core.reshape(1).astype(jnp.int32)

    vecs = jnp.stack(
        [out_bias, ln1_gain, ln1_bias, down_bias, ln2_gain, ln2_bias, out_bias, out_bias], axis=1
    ).astype(f32)
    up_bias_wide = up_bias.astype(f32)

    hidden, low = tokens_in, tokens_in
    saved = []
    for layer_idx in range(layers):
        last = layer_idx == layers - 1
        w_cat = w_cats[layer_idx]
        zero = jnp.zeros((width,), f32)
        bias_q, bias_v = bias_all[layer_idx, 0], bias_all[layer_idx, 1]
        shift = jnp.concatenate([bias_q, zero, bias_v])
        factor = jnp.concatenate([zero + 0.125, zero + 1.0, zero + 1.0])
        qkv = ((nt(low, w_cat) + shift) * factor).astype(bf16)
        kvh = (nt(halo, w_cat[width:]) + shift[width:]).astype(bf16)
        (ctx, ctx_t, ctx_low, lse), _ = attend(bounds, segq, segk, qkv, kvh, (), ())
        if not last:
            got = collect(later_got[layer_idx])
        fed, _ = feed(
            last, layer_idx, hidden, ctx, w_out, vecs[layer_idx], w_up, up_bias_wide[layer_idx : layer_idx + 1], w_down, (), ()
        )
        first_rows, first_t, active_t, slope, second_rows, after_low = fed[:6]
        saved.append((low_t, halo_t, qkv, kvh, ctx_t, ctx_low, lse, first_rows, first_t, active_t, slope, second_rows))
        if last:
            output = after_low
        else:
            low, hidden, low_t = after_low, fed[6], fed[7]
            halo = swap(lax.dynamic_slice_in_dim(low, edge, HALO), "head", 1)
            halo_t = halo.T
            w_cats.append(later_weights(own_later[layer_idx], got))

    grad_hidden = cotangent
    flights = []
    for layer_idx in reversed(range(layers)):
        low_t, halo_t, qkv, kvh, ctx_t, ctx_low, lse, first_rows, first_t, active_t, slope, second_rows = saved[layer_idx]
        w_cat = w_cats[layer_idx]
        (dz, du, da, dr, dc, sums, up_sum), _ = feed_back(
            layer_idx, grad_hidden, second_rows, first_rows, slope, w_down, w_up, w_out, vecs[layer_idx], (), ()
        )
        if flights:
            flights[1].step()
        (send, keep), _ = grad_feed(core_at, active_t, dz, first_t, du, dp, head, (), ())
        fed = Flight(send, keep, False)
        if flights:
            flights[0].step()
        (dqkv, dkvh, sums), _ = attend_back(bounds, segq, segk, qkv, kvh, ctx_t, lse, dc, sums, up_sum, (), ())
        part_halo = nn(dkvh, w_cat[width:]).astype(bf16)
        (part_halo,) = fed.step(passes=(part_halo,))
        back = swap(part_halo, "head", 1)
        if flights:
            flights[1].step()
        (send, keep), _ = grad_heads(core_at, ctx_low, low_t, halo_t, da, dqkv, dkvh, sums, dp, (), ())
        heads = Flight(send, keep, True)
        padded = lax.dynamic_update_slice(jnp.zeros((tokens, width), bf16), back, (edge, 0))
        grad_hidden = nn(dqkv, w_cat) + dr + padded.astype(f32)
        if flights:
            flights[0].step()
            flights[1].step()
            heads.step()
            flights[0].step()
            flights[1].step()
            fed.step()
            heads.step()
            fed.step()
            heads.step()
            fed.step()
            heads.step()
        flights = flights + [fed, heads]

    results = []
    for place in range(layers):
        fed, heads = flights[2 * place], flights[2 * place + 1]
        thin = width // (dp * head)
        total = fed.finish()
        out_down = total[0].reshape(-1, width)
        out_up = total[1].transpose(1, 0, 2).reshape(thin, -1)
        total = heads.finish()
        pieces = total[: 4 * part // TILE].reshape(4, part, BLK)
        out_out = pieces[3].reshape(width // BLK, -1, BLK)[:, :thin].transpose(1, 0, 2).reshape(thin, width)
        sums = total[4 * part // TILE :].transpose(1, 0, 2).reshape(TILE, 2, width).transpose(1, 0, 2)
        results.append((pieces[:3, :, : width // dp], out_out, out_up, out_down, sums.reshape(2 * TILE, width)))
    results = results[::-1]
    out_qkv, out_w_out, out_up, out_down, total = (jnp.stack([r[k] for r in results]) for k in range(5))
    out_qkv = out_qkv.reshape(layers, 3, part // head_size, head_size, -1).transpose(0, 4, 1, 2, 3)

    device = group * head + shard
    thin = width // (dp * head)
    mine = lax.dynamic_slice_in_dim(total[:, :6], device * thin, thin, axis=2)
    ups = total[:, 8 : 8 + up_bias.shape[1] // width].reshape(layers, -1)
    thick = ups.shape[1] // (dp * head)
    out_ups = lax.dynamic_slice_in_dim(ups, device * thick, thick, axis=1)
    qvs = total[:, 6:8].reshape(layers, 2, head, part // head_size, dp, head_size // dp)
    out_qv = pick(pick(qvs, shard, 2), group, 3)
    return (
        output,
        grad_hidden,
        out_qkv,
        out_qv,
        out_w_out,
        mine[:, 0],
        mine[:, 1],
        mine[:, 2],
        out_up,
        out_ups,
        out_down,
        mine[:, 3],
        mine[:, 4],
        mine[:, 5],
    )


def solution(mesh):
    return jax.shard_map(
        per_device,
        mesh=mesh,
        in_specs=(
            P(("dp", "head"), None),
            P("dp", None),
            P(None, None, None, "head", None),
            P(None, None, "head", None),
            P(),
            P(),
            P(),
            P(),
            P(),
            P(),
            P(),
            P(),
            P(),
            P(),
            P(("dp", "head"), None),
        ),
        out_specs=(
            P(("dp", "head"), None),
            P(("dp", "head"), None),
            P(None, "dp", None, "head", None),
            P(None, None, "head", "dp"),
            P(None, ("dp", "head"), None),
            P(None, ("dp", "head")),
            P(None, ("dp", "head")),
            P(None, ("dp", "head")),
            P(None, ("dp", "head"), None),
            P(None, ("dp", "head")),
            P(None, ("dp", "head"), None),
            P(None, ("dp", "head")),
            P(None, ("dp", "head")),
            P(None, ("dp", "head")),
        ),
        check_vma=False,
    )
```

time: 670 us -> 493 us (0.74)
  Pallas kernels: 71.8 us -> 228 us
  matrix products: 127 us -> 16.5 us
  local copies, waits for them, and re-layouts: 162 us -> 56.4 us
  starting transfers between devices: 92.6 us -> 37 us
  other arithmetic: 36.5 us -> 11.5 us
  waiting for transfers between devices: 150 us -> 132 us
  blocking collectives: 15.9 us -> 0 us
    pallas_call x4 -> x32, Pallas kernels: 71.8 us -> 228 us  [ordered_call(): pl.pallas_call(body, out_shape=tuple(out_shape) + (jax.ShapeDtypeStruct((...]
    ppermute x82 -> x20, waiting for transfers between devices: 150 us -> 43.3 us  [swap(): return lax.ppermute(value, axis, [(i, i ^ bit) for i in range(size)])]
    ppermute x0 -> x16, waiting for transfers between devices: none -> 89.2 us  [step(): self.keep, self.got = (keep, lax.ppermute(send, axis_name, pairs))]
    ppermute x82 -> x20, starting transfers between devices: 92.6 us -> 17.7 us  [swap(): return lax.ppermute(value, axis, [(i, i ^ bit) for i in range(size)])]
    dot_general x20 -> x0, matrix products: 52.4 us -> none  [the longest x12 34.9 us: part(): lax.dot_general(chosen, right, (((0,), (0,)), ((), ())), preferred_elemen...]
    dynamic_slice x27 -> x2, local copies, waits for them, and re-layouts: 43.8 us -> 0.02 us  [pick(): return lax.dynamic_index_in_dim(value, index, axis, keepdims=False)]
    dot_general x10 -> x4, matrix products: 41.5 us -> 8.69 us  [nn(): lax.dot_general(left, right, (((1,), (0,)), ((), ())), preferred_element_...]
    dot_general x10 -> x4, matrix products: 32.8 us -> 7.81 us  [nt(): lax.dot_general(left, right, (((1,), (1,)), ((), ())), preferred_element_...]
  transfers between devices with their start and end apart: 82 -> 36, of which waited for: 33 -> 17; matrix products, arithmetic and copies ran while one was open for 33% -> 10% of each run, Pallas kernels for 4% -> 31%
where the time goes in v2:
time: 493 us; the launch traced here: 484 us
  Pallas kernels  228 us (46%)
  waiting for transfers between devices  132 us (27%)
  local copies, waits for them, and re-layouts  56.4 us (11%)
  starting transfers between devices  37 us (8%)
  matrix products  16.5 us (3%)
  other arithmetic  11.5 us (2%)
    pallas_call x32, Pallas kernels, ordered_call(): pl.pallas_call(body, out_shape=tuple(out_shape) + (jax.ShapeDtypeStruct((...  228 us
    ppermute x16, waiting for transfers between devices, step(): self.keep, self.got = (keep, lax.ppermute(send, axis_name, pairs))  89.2 us
    ppermute x20, waiting for transfers between devices, swap(): return lax.ppermute(value, axis, [(i, i ^ bit) for i in range(size)])  43.3 us
    unnamed x190, local copies, waits for them, and re-layouts  31.1 us
    ppermute x16, starting transfers between devices, step(): self.keep, self.got = (keep, lax.ppermute(send, axis_name, pairs))  19.4 us
    ppermute x20, starting transfers between devices, swap(): return lax.ppermute(value, axis, [(i, i ^ bit) for i in range(size)])  17.7 us
  transfers between devices with their start and end apart: 36, of which 17 were waited for; matrix products, arithmetic and copies ran while one was open for 10% of the time, Pallas kernels for 31%

profile of v2, /device:TPU:0, one launch (start us, length us, event | category | flops | bytes accessed | tf_op | source)
XLA Modules:
  0.0 484.5 jit_solution(12048905646396344656)
XLA Ops:
  0.7 1.6 fusion.20
  2.5 3.1 collective-permute-start
  5.5 2.6 collective-permute-start.1
  13.5 4.5 collective-permute-done.1
  19.9 1.6 collective-permute-start.3
  21.5 1.5 collective-permute-start.5
  23.0 2.3 collective-permute-done.3
  25.4 1.7 collective-permute-start.4
  27.1 1.5 collective-permute-done.5
  30.3 2.4 collective-permute-done.4
  32.8 3.0 collective-permute-done.6
  44.0 1.5 flip.1
  51.1 2.1 collective-permute-start.9
  53.2 16.9 %collective-permute-done.10.refs_1_ = bf16[3,96,768]{2,1,0:T(8,128)(2,1)} collective-permute-done((bf16[3,96,768]{2,1,0:T(8,128)(2,1)S(1)}, bf16[3,96,768]{2,1,0:T(8,128)(2,1)}, u32[]{:S(2)}, u32[]{:S(2)}) %collective-permute-start.10) | collective-permute-done | bytes 442400 | tf_op jit(solution)/shard_map/ppermute | solution.py:27
  70.1 2.0 pad_maximum_fusion
  73.5 1.6 copy-done
  75.1 2.0 fusion.4.refs_3_
  77.1 2.6 fusion.5.refs_4_
  79.8 11.6 %attend.2 = (bf16[512,768]{1,0:T(8,128)(2,1)S(1)}, f32[768,512]{1,0:T(8,128)S(1)}, bf16[768,512]{1,0:T(8,128)(2,1)S(1)}, f32[4,8,256]{2,1,0:T(8,128)S(1)}, f32[8,128]{1,0:T(8,128)S(1)}) custom-call(s32[4,4]{1,0:T(4,128)S(1)} %pad_add_fusion.2.refs_0_, s32[4,1,256]{2,1,0:T(1,128)S(1)} %reshape.429.refs_1_, s32[896,1]{1,0:T(8,128)S(1)} %reshape.456.refs_2_, ...), custom_call_target="tpu_custom_call" | custom-call | flops 10350000128 | bytes 1000 | tf_op jit(solution)/shard_map/attend/pallas_call | solution.py:231
  91.5 1.4 collect.1
  93.0 17.0 %feed.2 = (f32[512,768]{1,0:T(8,128)S(1)}, bf16[768,512]{1,0:T(8,128)(2,1)S(1)}, bf16[3072,512]{1,0:T(8,128)(2,1)}, f32[512,3072]{1,0:T(8,128)}, f32[512,768]{1,...) custom-call(bf16[512,768]{1,0:T(8,128)(2,1)S(1)} %copy-done.4, ...), custom_call_target="tpu_custom_call" | custom-call | flops 19549999104 | bytes 1000 | tf_op jit(solution)/shard_map/feed/pallas_call | solution.py:231
  111.1 1.8 collective-permute-start.13
  113.9 1.6 copy-done.2
  115.5 2.0 fusion.3.refs_3_
  117.5 9.3 %collective-permute-done.13 = bf16[384,768]{1,0:T(8,128)(2,1)S(1)} collective-permute-done((bf16[384,768]{1,0:T(8,128)(2,1)S(1)}, bf16[384,768]{1,0:T(8,128)(2,1)S(1)}, u32[]{:S(2)}, u32[]{:S(2)}) %collective-permute-start.13) | collective-permute-done | bytes 589856 | tf_op jit(solution)/shard_map/ppermute | solution.py:27
  128.0 11.4 %attend.3 = (bf16[512,768]{1,0:T(8,128)(2,1)S(1)}, f32[768,512]{1,0:T(8,128)S(1)}, bf16[768,512]{1,0:T(8,128)(2,1)S(1)}, f32[4,8,256]{2,1,0:T(8,128)S(1)}, f32[8,128]{1,0:T(8,128)S(1)}) custom-call(s32[4,4]{1,0:T(4,128)S(1)} %pad_add_fusion.2.refs_0_, s32[4,1,256]{2,1,0:T(1,128)S(1)} %reshape.429.refs_1_, s32[896,1]{1,0:T(8,128)S(1)} %reshape.456.refs_2_, ...), custom_call_target="tpu_custom_call" | custom-call | flops 10350000128 | bytes 1000 | tf_op jit(solution)/shard_map/attend/pallas_call | solution.py:231
  141.5 16.7 %feed.3 = (f32[512,768]{1,0:T(8,128)S(1)}, bf16[768,512]{1,0:T(8,128)(2,1)S(1)}, bf16[3072,512]{1,0:T(8,128)(2,1)}, f32[512,3072]{1,0:T(8,128)}, f32[512,768]{1,...) custom-call(f32[512,768]{1,0:T(8,128)} %get-tuple-element.142.refs_0_, ...), custom_call_target="tpu_custom_call" | custom-call | flops 19549999104 | bytes 1000 | tf_op jit(solution)/shard_map/feed/pallas_call | solution.py:231
  160.5 21.8 %feed_back.2 = (bf16[512,768]{1,0:T(8,128)(2,1)S(1)}, bf16[512,3072]{1,0:T(8,128)(2,1)}, bf16[512,768]{1,0:T(8,128)(2,1)S(1)}, f32[512,768]{1,0:T(8,128)S(1)}, b...) custom-call(bf16[512,768]{1,0:T(8,128)(2,1)S(1)} %copy-done.5, ...), custom_call_target="tpu_custom_call" | custom-call | flops 24149999616 | bytes 1000 | tf_op jit(solution)/shard_map/feed_back/pallas_call | solution.py:231
  182.3 10.2 %grad_feed.2 = (bf16[4,4,2,4,24,768]{5,4,3,2,1,0:T(8,128)(2,1)}, bf16[4,4,2,4,24,768]{5,4,3,2,1,0:T(8,128)(2,1)}, f32[8,128]{1,0:T(8,128)S(1)}) custom-call(s32[1]{0:T(128)} %bitcast.32.refs_0_, bf16[8,384,512]{2,1,0:T(8,128)(2,1)S(1)} %bitcast.149, bf16[512,768]{1,0:T(8,128)(2,1)S(1)} %get-tuple-element.163.refs_2_, bf16[8,96,512]{2,1,0:T(8,128)(2,1)S(1)} %bitcast.155, ...), custom_call_target="tpu_custom_call" | custom-call | flops 11500000256 | bytes 1000 | tf_op jit(solution)/shard_map/grad_feed/pallas_call | solution.py:231
  194.1 1.7 copy-done.32
  198.3 28.1 %attend_back.2 = (bf16[512,2304]{1,0:T(8,128)(2,1)S(1)}, bf16[384,1536]{1,0:T(8,128)(2,1)S(1)}, f32[16,768]{1,0:T(8,128)S(1)}, f32[8,128]{1,0:T(8,128)S(1)}) custom-call(s32[4,4]{1,0:T(4,128)S(1)} %pad_add_fusion.2.refs_0_, s32[4,1,256]{2,1,0:T(1,128)S(1)} %reshape.429.refs_1_, s32[896,1]{1,0:T(8,128)S(1)} %reshape.456.refs_2_, ...), custom_call_target="tpu_custom_call" | custom-call | flops 24149999616 | bytes 1000 | tf_op jit(solution)/shard_map/attend_back/pallas_call | solution.py:231
  227.9 6.3 %advance.16 = (bf16[8,2,4,24,768]{4,3,2,1,0:T(8,128)(2,1)}, bf16[8,2,4,24,768]{4,3,2,1,0:T(8,128)(2,1)S(1)}, f32[8,128]{1,0:T(8,128)S(1)}, bf16[384,768]{1,0:T(8,128)(2,1)S(1)}) custom-call(s32[2]{0:T(128)S(1)} %pad_add_fusion.5.refs_0_, bf16[16,2,4,24,768]{4,3,2,1,0:T(8,128)(2,1)} %bitcast.194, ...), custom_call_target="tpu_custom_call", output_to_operand_aliasing={{3}: (4, {})} | custom-call | flops 4600000000 | bytes 1000 | tf_op jit(solution)/shard_map/advance/pallas_call | solution.py:231
  234.2 1.4 copy-done.35
  235.7 7.8 %grad_heads.2 = (bf16[49,8,3072]{2,1,0:T(8,128)(2,1)}, bf16[49,8,3072]{2,1,0:T(8,128)(2,1)}, f32[8,128]{1,0:T(8,128)S(1)}) custom-call(s32[1]{0:T(128)} %bitcast.32.refs_0_, bf16[8,96,512]{2,1,0:T(8,128)(2,1)S(1)} %bitcast.154, bf16[8,96,512]{2,1,0:T(8,128)(2,1)S(1)} %bitcast.153, bf16[8,96,384]{2,1,0:T(8,128)(2,1)S(1)} %bitcast.145, ...), custom_call_target="tpu_custom_call" | custom-call | flops 9200000000 | bytes 1000 | tf_op jit(solution)/shard_map/grad_heads/pallas_call | solution.py:231
  243.8 2.7 collective-permute-start.16
  246.5 3.2 collective-permute-done.15
  249.8 2.0 convert_add_fusion.1.refs_0_
  251.9 21.5 %feed_back.3 = (bf16[512,768]{1,0:T(8,128)(2,1)S(1)}, bf16[512,3072]{1,0:T(8,128)(2,1)}, bf16[512,768]{1,0:T(8,128)(2,1)S(1)}, f32[512,768]{1,0:T(8,128)S(1)}, b...) custom-call(f32[512,768]{1,0:T(8,128)S(1)} %convert_add_fusion.1.refs_0_, ...), custom_call_target="tpu_custom_call" | custom-call | flops 24149999616 | bytes 1000 | tf_op jit(solution)/shard_map/feed_back/pallas_call | solution.py:231
  276.2 3.2 advance.17
  279.4 9.7 %grad_feed.3 = (bf16[4,4,2,4,24,768]{5,4,3,2,1,0:T(8,128)(2,1)}, bf16[4,4,2,4,24,768]{5,4,3,2,1,0:T(8,128)(2,1)}, f32[8,128]{1,0:T(8,128)S(1)}) custom-call(s32[1]{0:T(128)} %bitcast.32.refs_0_, bf16[8,384,512]{2,1,0:T(8,128)(2,1)S(1)} %bitcast.148, bf16[512,768]{1,0:T(8,128)(2,1)S(1)} %get-tuple-element.190.refs_2_, bf16[8,96,512]{2,1,0:T(8,128)(2,1)S(1)} %bitcast.152, ...), custom_call_target="tpu_custom_call" | custom-call | flops 11500000256 | bytes 1000 | tf_op jit(solution)/shard_map/grad_feed/pallas_call | solution.py:231
  289.3 1.7 copy-done.36
  290.9 3.1 advance.18
  294.7 28.2 %attend_back.3 = (bf16[512,2304]{1,0:T(8,128)(2,1)S(1)}, bf16[384,1536]{1,0:T(8,128)(2,1)S(1)}, f32[16,768]{1,0:T(8,128)S(1)}, f32[8,128]{1,0:T(8,128)S(1)}) custom-call(s32[4,4]{1,0:T(4,128)S(1)} %pad_add_fusion.2.refs_0_, s32[4,1,256]{2,1,0:T(1,128)S(1)} %reshape.429.refs_1_, s32[896,1]{1,0:T(8,128)S(1)} %reshape.456.refs_2_, ...), custom_call_target="tpu_custom_call" | custom-call | flops 24149999616 | bytes 1000 | tf_op jit(solution)/shard_map/attend_back/pallas_call | solution.py:231
  324.4 4.9 %advance.19 = (bf16[8,2,4,24,768]{4,3,2,1,0:T(8,128)(2,1)S(1)}, bf16[8,2,4,24,768]{4,3,2,1,0:T(8,128)(2,1)S(1)}, f32[8,128]{1,0:T(8,128)S(1)}, bf16[384,768]{1,0:T(8,128)(2,1)S(1)}) custom-call(s32[2]{0:T(128)S(1)} %pad_add_fusion.5.refs_0_, bf16[16,2,4,24,768]{4,3,2,1,0:T(8,128)(2,1)} %bitcast.193, ...), custom_call_target="tpu_custom_call", output_to_operand_aliasing={{3}: (4, {})} | custom-call | flops 4600000000 | bytes 1000 | tf_op jit(solution)/shard_map/advance/pallas_call | solution.py:231
  333.3 7.6 %grad_heads.3 = (bf16[49,8,3072]{2,1,0:T(8,128)(2,1)}, bf16[49,8,3072]{2,1,0:T(8,128)(2,1)}, f32[8,128]{1,0:T(8,128)S(1)}) custom-call(s32[1]{0:T(128)} %bitcast.32.refs_0_, bf16[8,96,512]{2,1,0:T(8,128)(2,1)S(1)} %bitcast.151, bf16[8,96,512]{2,1,0:T(8,128)(2,1)S(1)} %bitcast.150, bf16[8,96,384]{2,1,0:T(8,128)(2,1)S(1)} %bitcast.156, ...), custom_call_target="tpu_custom_call" | custom-call | flops 9200000000 | bytes 1000 | tf_op jit(solution)/shard_map/grad_heads/pallas_call | solution.py:231
  341.0 2.0 collective-permute-start.22
  343.1 26.2 %collective-permute-done.23.refs_2_ = bf16[4,2,4,24,768]{4,3,2,1,0:T(8,128)(2,1)} collective-permute-done((bf16[4,2,4,24,768]{4,3,2,1,0:T(8,128)(2,1)}, bf16[4,2,4,24,768]{4,3,2,1,0:T(8,128)(2,1)}, u32[]{:S(2)}, u32[]{:S(2)}) %collective-permute-start.23) | collective-permute-done | bytes 1179680 | tf_op jit(solution)/shard_map/ppermute | solution.py:848
  370.6 1.7 advance.21
  372.3 2.6 collective-permute-start.27
  374.9 8.0 %collective-permute-done.22.refs_2_ = bf16[13,8,3072]{2,1,0:T(8,128)(2,1)S(1)} collective-permute-done((bf16[13,8,3072]{2,1,0:T(8,128)(2,1)S(1)}, bf16[13,8,3072]{2,1,0:T(8,128)(2,1)S(1)}, u32[]{:S(2)}, u32[]{:S(2)}) %collective-permute-start.22) | collective-permute-done | bytes 639008 | tf_op jit(solution)/shard_map/ppermute | solution.py:848
  383.8 2.6 collective-permute-start.26
  386.4 2.3 advance.23
  391.3 15.9 %collective-permute-done.26.refs_2_ = bf16[204,8,128]{2,1,0:T(8,128)(2,1)S(1)} collective-permute-done((bf16[204,8,128]{2,1,0:T(8,128)(2,1)S(1)}, bf16[204,8,128]{2,1,0:T(8,128)(2,1)S(1)}, u32[]{:S(2)}, u32[]{:S(2)}) %collective-permute-start.26) | collective-permute-done | bytes 417824 | tf_op jit(solution)/shard_map/ppermute | solution.py:848
  408.9 2.4 advance.26
  413.5 4.5 convert_add_fusion
  418.1 2.9 collective-permute-start.33
  422.7 2.0 collective-permute-start.28
  424.7 3.8 collective-permute-done.29.refs_2_
  429.4 1.8 collective-permute-start.31
  431.2 12.0 %collective-permute-done.33 = bf16[108,8,128]{2,1,0:T(8,128)(2,1)S(1)} collective-permute-done((bf16[108,8,128]{2,1,0:T(8,128)(2,1)S(1)}, bf16[108,8,128]{2,1,0:T(8,128)(2,1)S(1)}, u32[]{:S(2)}, u32[]{:S(2)}) %collective-permute-start.33) | collective-permute-done | bytes 221216 | tf_op jit(solution)/shard_map/ppermute | solution.py:848
  448.3 3.2 collective-permute-done.31.refs_2_
  454.8 9.7 %collective-permute-done.34 = bf16[1,2,4,24,768]{4,3,2,1,0:T(8,128)(2,1)} collective-permute-done((bf16[1,2,4,24,768]{4,3,2,1,0:T(8,128)(2,1)S(1)}, bf16[1,2,4,24,768]{4,3,2,1,0:T(8,128)(2,1)}, u32[]{:S(2)}, u32[]{:S(2)}) %collective-permute-start.34) | collective-permute-done | bytes 294944 | tf_op jit(solution)/shard_map/ppermute | solution.py:848
  466.6 1.9 collective-permute-done.30.refs_2_
  471.7 8.3 %collective-permute-done.32 = bf16[108,8,128]{2,1,0:T(8,128)(2,1)S(1)} collective-permute-done((bf16[108,8,128]{2,1,0:T(8,128)(2,1)S(1)}, bf16[108,8,128]{2,1,0:T(8,128)(2,1)S(1)}, u32[]{:S(2)}, u32[]{:S(2)}) %collective-permute-start.32) | collective-permute-done | bytes 221216 | tf_op jit(solution)/shard_map/ppermute | solution.py:848
  (350 shorter events, 75.4 us)
Async XLA Ops:
  0.7 7.5 %copy-start.4 = (bf16[512,768]{1,0:T(8,128)(2,1)S(1)}, bf16[512,768]{1,0:T(8,128)(2,1)}, u32[]{:S(2)}) copy-start(bf16[512,768]{1,0:T(8,128)(2,1)} %refs_0_.4) | copy-start | bytes 2359300
  0.7 11.8 %copy-start.80 = (bf16[2,3072]{1,0:T(2,128)(2,1)S(1)}, bf16[2,3072]{1,0:T(2,128)(2,1)}, u32[]{:S(2)}) copy-start(bf16[2,3072]{1,0:T(2,128)(2,1)} %param.24) | copy-start | bytes 36868
  2.5 10.1 %collective-permute-start = (bf16[80,768]{1,0:T(8,128)(2,1)S(1)}, bf16[80,768]{1,0:T(8,128)(2,1)}, u32[]{:S(2)}, u32[]{:S(2)}) collective-permute-start(bf16[80,768]{1,0:T(8,128)(2,1)S(1)} %fusion.8), channel_id=1, source_target_pairs={{0,1},{1,0},{2,3},{3,2},{4,5},{5,4},{6,7},{7,6},{8,9},{9,8},{10,11... | collective-permute-start | bytes 368648 | tf_op jit(solution)/shard_map/ppermute | solution.py:27
  5.5 12.4 %collective-permute-start.1 = (bf16[80,768]{1,0:T(8,128)(2,1)S(1)}, bf16[80,768]{1,0:T(8,128)(2,1)}, u32[]{:S(2)}, u32[]{:S(2)}) collective-permute-start(bf16[80,768]{1,0:T(8,128)(2,1)S(1)} %fusion.8), channel_id=1, source_target_pairs={{0,2},{1,3},{2,0},{3,1},{4,6},{5,7},{6,4},{7,5},{8,10},{9,11},{10,... | collective-permute-start | bytes 368648 | tf_op jit(solution)/shard_map/ppermute | solution.py:27
  8.1 10.7 %collective-permute-start.2 = (bf16[80,768]{1,0:T(8,128)(2,1)S(1)}, bf16[80,768]{1,0:T(8,128)(2,1)}, u32[]{:S(2)}, u32[]{:S(2)}) collective-permute-start(bf16[80,768]{1,0:T(8,128)(2,1)S(1)} %fusion.8), channel_id=1, source_target_pairs={{0,3},{1,2},{2,1},{3,0},{4,7},{5,6},{6,5},{7,4},{8,11},{9,10},{10,... | collective-permute-start | bytes 368648 | tf_op jit(solution)/shard_map/ppermute | solution.py:27
  9.0 35.0 %collective-permute-start.8 = (bf16[384,768]{1,0:T(8,128)(2,1)}, bf16[384,768]{1,0:T(8,128)(2,1)}, u32[]{:S(2)}, u32[]{:S(2)}) collective-permute-start(bf16[384,768]{1,0:T(8,128)(2,1)} %constant_dynamic-slice_fusion.3), channel_id=1, source_target_pairs={{0,1},{1,0},{2,3},{3,2},{4,5},{5,4},{6,7},{7,6},{8,9},{9,8},{10,11... | collective-permute-start | bytes 1769480 | tf_op jit(solution)/shard_map/ppermute | solution.py:27
  19.9 5.5 %collective-permute-start.3 = (bf16[1,3,3,24,384]{4,3,2,1,0:T(8,128)(2,1)S(1)}, bf16[1,3,3,24,384]{4,3,2,1,0:T(8,128)(2,1)S(1)}, u32[]{:S(2)}, u32[]{:S(2)}) collective-permute-start(bf16[1,3,3,24,384]{4,3,2,1,0:T(8,128)(2,1)S(1)} %get-tuple-element.274), channel_id=1, source_target_pairs={{0,8},{4,12},{8,0},{12,4},{16,24},{20,28},{24,16},{28,20},{1,9},{5... | collective-permute-start | bytes 497672 | tf_op jit(solution)/shard_map/ppermute | solution.py:27
  21.5 7.2 %collective-permute-start.5 = (bf16[1,3,3,24,384]{4,3,2,1,0:T(8,128)(2,1)S(1)}, bf16[1,3,3,24,384]{4,3,2,1,0:T(8,128)(2,1)S(1)}, u32[]{:S(2)}, u32[]{:S(2)}) collective-permute-start(bf16[1,3,3,24,384]{4,3,2,1,0:T(8,128)(2,1)S(1)} %get-tuple-element.275), channel_id=1, source_target_pairs={{0,16},{4,20},{8,24},{12,28},{16,0},{20,4},{24,8},{28,12},{1,17},{... | collective-permute-start | bytes 497672 | tf_op jit(solution)/shard_map/ppermute | solution.py:27
  25.4 7.3 %collective-permute-start.4 = (bf16[2,3,3,24,384]{4,3,2,1,0:T(8,128)(2,1)S(1)}, bf16[2,3,3,24,384]{4,3,2,1,0:T(8,128)(2,1)S(1)}, u32[]{:S(2)}, u32[]{:S(2)}) collective-permute-start(bf16[2,3,3,24,384]{4,3,2,1,0:T(8,128)(2,1)S(1)} %pad_maximum_fusion.5), channel_id=1, source_target_pairs={{0,16},{4,20},{8,24},{12,28},{16,0},{20,4},{24,8},{28,12},{1,17},{... | collective-permute-start | bytes 995336 | tf_op jit(solution)/shard_map/ppermute | solution.py:27
  28.7 7.2 %collective-permute-start.6 = (bf16[2,3,3,24,384]{4,3,2,1,0:T(8,128)(2,1)S(1)}, bf16[2,3,3,24,384]{4,3,2,1,0:T(8,128)(2,1)S(1)}, u32[]{:S(2)}, u32[]{:S(2)}) collective-permute-start(bf16[2,3,3,24,384]{4,3,2,1,0:T(8,128)(2,1)S(1)} %pad_maximum_fusion.6), channel_id=1, source_target_pairs={{0,8},{4,12},{8,0},{12,4},{16,24},{20,28},{24,16},{28,20},{1,9},{5... | collective-permute-start | bytes 995336 | tf_op jit(solution)/shard_map/ppermute | solution.py:27
  37.3 32.9 %collective-permute-start.7 = (bf16[2,4,3,3,24,384]{5,4,3,2,1,0:T(8,128)(2,1)}, bf16[2,4,3,3,24,384]{5,4,3,2,1,0:T(8,128)(2,1)}, u32[]{:S(2)}, u32[]{:S(2)}) collective-permute-start(bf16[2,4,3,3,24,384]{5,4,3,2,1,0:T(8,128)(2,1)} %pad_maximum_fusion.1), channel_id=1, source_target_pairs={{0,4},{4,0},{8,12},{12,8},{16,20},{20,16},{24,28},{28,24},{1,5},{5... | collective-permute-start | bytes 3981320 | tf_op jit(solution)/shard_map/ppermute | solution.py:27
  47.2 22.9 %collective-permute-start.10 = (bf16[3,96,768]{2,1,0:T(8,128)(2,1)S(1)}, bf16[3,96,768]{2,1,0:T(8,128)(2,1)}, u32[]{:S(2)}, u32[]{:S(2)}) collective-permute-start(bf16[3,96,768]{2,1,0:T(8,128)(2,1)S(1)} %get-tuple-element.139), channel_id=1, source_target_pairs={{0,2},{1,3},{2,0},{3,1},{4,6},{5,7},{6,4},{7,5},{8,10},{9,11},{10,... | collective-permute-start | bytes 1327112 | tf_op jit(solution)/shard_map/ppermute | solution.py:27
  51.1 40.3 %collective-permute-start.9 = (bf16[3,96,768]{2,1,0:T(8,128)(2,1)S(1)}, bf16[3,96,768]{2,1,0:T(8,128)(2,1)S(1)}, u32[]{:S(2)}, u32[]{:S(2)}) collective-permute-start(bf16[3,96,768]{2,1,0:T(8,128)(2,1)S(1)} %get-tuple-element.139), channel_id=1, source_target_pairs={{0,1},{1,0},{2,3},{3,2},{4,5},{5,4},{6,7},{7,6},{8,9},{9,8},{10,11... | collective-permute-start | bytes 1327112 | tf_op jit(solution)/shard_map/ppermute | solution.py:27
  70.1 21.3 %collective-permute-start.11 = (bf16[3,96,768]{2,1,0:T(8,128)(2,1)}, bf16[3,96,768]{2,1,0:T(8,128)(2,1)S(1)}, u32[]{:S(2)}, u32[]{:S(2)}) collective-permute-start(bf16[3,96,768]{2,1,0:T(8,128)(2,1)} %collective-permute-done.10.refs_1_), channel_id=1, source_target_pairs={{0,1},{1,0},{2,3},{3,2},{4,5},{5,4},{6,7},{7,6},{8,9},{9,8},{10,11... | collective-permute-start | bytes 1327112 | tf_op jit(solution)/shard_map/ppermute | solution.py:27
  79.8 11.7 %copy-start.22 = (bf16[384,1536]{1,0:T(8,128)(2,1)}, bf16[384,1536]{1,0:T(8,128)(2,1)S(1)}, u32[]{:S(2)}) copy-start(bf16[384,1536]{1,0:T(8,128)(2,1)S(1)} %fusion.5.refs_4_) | copy-start | bytes 3538948
  92.9 20.0 %collective-permute-start.12 = (bf16[3,3,96,768]{3,2,1,0:T(8,128)(2,1)S(1)}, bf16[3,3,96,768]{3,2,1,0:T(8,128)(2,1)S(1)}, u32[]{:S(2)}, u32[]{:S(2)}) collective-permute-start(bf16[3,3,96,768]{3,2,1,0:T(8,128)(2,1)S(1)} %get-tuple-element.144), channel_id=1, source_target_pairs={{0,4},{4,0},{8,12},{12,8},{16,20},{20,16},{24,28},{28,24},{1,5},{5... | collective-permute-start | bytes 3981320 | tf_op jit(solution)/shard_map/ppermute | solution.py:27
  111.1 15.7 %collective-permute-start.13 = (bf16[384,768]{1,0:T(8,128)(2,1)S(1)}, bf16[384,768]{1,0:T(8,128)(2,1)S(1)}, u32[]{:S(2)}, u32[]{:S(2)}) collective-permute-start(bf16[384,768]{1,0:T(8,128)(2,1)S(1)} %constant_dynamic-slice_fusion.2), channel_id=1, source_target_pairs={{0,1},{1,0},{2,3},{3,2},{4,5},{5,4},{6,7},{7,6},{8,9},{9,8},{10,11... | collective-permute-start | bytes 1769480 | tf_op jit(solution)/shard_map/ppermute | solution.py:27
  113.9 13.0 %copy-start.74 = (bf16[2,4,2,96,768]{4,3,2,1,0:T(8,128)(2,1)}, bf16[2,4,2,96,768]{4,3,2,1,0:T(8,128)(2,1)S(1)}, u32[]{:S(2)}) copy-start(bf16[2,4,2,96,768]{4,3,2,1,0:T(8,128)(2,1)S(1)} %slice.188) | copy-start | bytes 7077892
  117.5 10.5 %copy-start.31 = (bf16[512,2304]{1,0:T(8,128)(2,1)}, bf16[512,2304]{1,0:T(8,128)(2,1)S(1)}, u32[]{:S(2)}) copy-start(bf16[512,2304]{1,0:T(8,128)(2,1)S(1)} %fusion.3.refs_3_) | copy-start | bytes 7077892
  141.5 19.1 %copy-start.5 = (bf16[512,768]{1,0:T(8,128)(2,1)S(1)}, bf16[512,768]{1,0:T(8,128)(2,1)}, u32[]{:S(2)}) copy-start(bf16[512,768]{1,0:T(8,128)(2,1)} %refs_0_.5) | copy-start | bytes 2359300
  160.5 21.8 %copy-start.9 = (bf16[3072,512]{1,0:T(8,128)(2,1)S(1)}, bf16[3072,512]{1,0:T(8,128)(2,1)}, u32[]{:S(2)}) copy-start(bf16[3072,512]{1,0:T(8,128)(2,1)} %get-tuple-element.162) | copy-start | bytes 9437188
  182.3 10.3 %copy-start.29 = (f32[512,768]{1,0:T(8,128)}, f32[512,768]{1,0:T(8,128)S(1)}, u32[]{:S(2)}) copy-start(f32[512,768]{1,0:T(8,128)S(1)} %get-tuple-element.169) | copy-start | bytes 4718596
  182.3 10.3 %copy-start.61 = (bf16[512,768]{1,0:T(8,128)(2,1)}, bf16[512,768]{1,0:T(8,128)(2,1)S(1)}, u32[]{:S(2)}) copy-start(bf16[512,768]{1,0:T(8,128)(2,1)S(1)} %get-tuple-element.180.refs_4_) | copy-start | bytes 2359300
  182.3 10.3 %copy-start.68 = (bf16[512,768]{1,0:T(8,128)(2,1)}, bf16[512,768]{1,0:T(8,128)(2,1)S(1)}, u32[]{:S(2)}) copy-start(bf16[512,768]{1,0:T(8,128)(2,1)S(1)} %get-tuple-element.159.refs_7_) | copy-start | bytes 2359300
  192.6 35.3 %collective-permute-start.14 = (bf16[4,4,2,4,24,768]{5,4,3,2,1,0:T(8,128)(2,1)}, bf16[4,4,2,4,24,768]{5,4,3,2,1,0:T(8,128)(2,1)}, u32[]{:S(2)}, u32[]{:S(2)}) collective-permute-start(bf16[4,4,2,4,24,768]{5,4,3,2,1,0:T(8,128)(2,1)} %get-tuple-element.171), channel_id=1, source_target_pairs={{0,4},{4,0},{8,12},{12,8},{16,20},{20,16},{24,28},{28,24},{1,5},{5... | collective-permute-start | bytes 14155784 | tf_op jit(solution)/shard_map/ppermute | solution.py:27
  198.3 28.1 %copy-start.75 = (bf16[2,4,2,96,768]{4,3,2,1,0:T(8,128)(2,1)S(1)}, bf16[2,4,2,96,768]{4,3,2,1,0:T(8,128)(2,1)}, u32[]{:S(2)}) copy-start(bf16[2,4,2,96,768]{4,3,2,1,0:T(8,128)(2,1)} %copy-done.74) | copy-start | bytes 7077892
  227.9 7.8 %copy-start.17 = (bf16[768,512]{1,0:T(8,128)(2,1)S(1)}, bf16[768,512]{1,0:T(8,128)(2,1)}, u32[]{:S(2)}) copy-start(bf16[768,512]{1,0:T(8,128)(2,1)} %copy-done.16) | copy-start | bytes 2359300
  227.9 7.8 %copy-start.19 = (bf16[768,512]{1,0:T(8,128)(2,1)S(1)}, bf16[768,512]{1,0:T(8,128)(2,1)}, u32[]{:S(2)}) copy-start(bf16[768,512]{1,0:T(8,128)(2,1)} %copy-done.18) | copy-start | bytes 2359300
  227.9 7.8 %copy-start.62 = (bf16[512,768]{1,0:T(8,128)(2,1)S(1)}, bf16[512,768]{1,0:T(8,128)(2,1)}, u32[]{:S(2)}) copy-start(bf16[512,768]{1,0:T(8,128)(2,1)} %copy-done.61) | copy-start | bytes 2359300
  235.7 14.0 %collective-permute-start.15 = (bf16[384,768]{1,0:T(8,128)(2,1)S(1)}, bf16[384,768]{1,0:T(8,128)(2,1)S(1)}, u32[]{:S(2)}, u32[]{:S(2)}) collective-permute-start(bf16[384,768]{1,0:T(8,128)(2,1)S(1)} %get-tuple-element.174), channel_id=1, source_target_pairs={{0,1},{1,0},{2,3},{3,2},{4,5},{5,4},{6,7},{7,6},{8,9},{9,8},{10,11... | collective-permute-start | bytes 1769480 | tf_op jit(solution)/shard_map/ppermute | solution.py:27
  235.7 14.1 %copy-start.3 = (bf16[3,4,2,96,768]{4,3,2,1,0:T(8,128)(2,1)S(1)}, bf16[3,4,2,96,768]{4,3,2,1,0:T(8,128)(2,1)}, u32[]{:S(2)}) copy-start(bf16[3,4,2,96,768]{4,3,2,1,0:T(8,128)(2,1)} %copy-done.2) | copy-start | bytes 10616836
  235.7 14.1 %copy-start.27 = (bf16[512,2304]{1,0:T(8,128)(2,1)S(1)}, bf16[512,2304]{1,0:T(8,128)(2,1)}, u32[]{:S(2)}) copy-start(bf16[512,2304]{1,0:T(8,128)(2,1)} %copy-done.26) | copy-start | bytes 7077892
  235.7 14.1 %copy-start.30 = (f32[512,768]{1,0:T(8,128)S(1)}, f32[512,768]{1,0:T(8,128)}, u32[]{:S(2)}) copy-start(f32[512,768]{1,0:T(8,128)} %copy-done.29) | copy-start | bytes 4718596
  243.5 32.7 %collective-permute-start.17 = (bf16[49,8,3072]{2,1,0:T(8,128)(2,1)}, bf16[49,8,3072]{2,1,0:T(8,128)(2,1)}, u32[]{:S(2)}, u32[]{:S(2)}) collective-permute-start(bf16[49,8,3072]{2,1,0:T(8,128)(2,1)} %get-tuple-element.194), channel_id=1, source_target_pairs={{0,4},{4,0},{8,12},{12,8},{16,20},{20,16},{24,28},{28,24},{1,5},{5... | collective-permute-start | bytes 7225352 | tf_op jit(solution)/shard_map/ppermute | solution.py:27
  243.8 45.5 %collective-permute-start.16 = (bf16[8,2,4,24,768]{4,3,2,1,0:T(8,128)(2,1)}, bf16[8,2,4,24,768]{4,3,2,1,0:T(8,128)(2,1)}, u32[]{:S(2)}, u32[]{:S(2)}) collective-permute-start(bf16[8,2,4,24,768]{4,3,2,1,0:T(8,128)(2,1)} %get-tuple-element.188), channel_id=1, source_target_pairs={{0,8},{4,20},{8,0},{12,28},{16,24},{20,4},{24,16},{28,12},{1,9},{5... | collective-permute-start | bytes 7077896 | tf_op jit(solution)/shard_map/ppermute | solution.py:848
  251.8 24.4 %copy-start.40 = (bf16[49,8,3072]{2,1,0:T(8,128)(2,1)S(1)}, bf16[49,8,3072]{2,1,0:T(8,128)(2,1)}, u32[]{:S(2)}) copy-start(bf16[49,8,3072]{2,1,0:T(8,128)(2,1)} %get-tuple-element.193.refs_1_) | copy-start | bytes 7225348
  279.4 9.8 %copy-start.41 = (bf16[25,8,3072]{2,1,0:T(8,128)(2,1)}, bf16[25,8,3072]{2,1,0:T(8,128)(2,1)S(1)}, u32[]{:S(2)}) copy-start(bf16[25,8,3072]{2,1,0:T(8,128)(2,1)S(1)} %get-tuple-element.211.refs_1_) | copy-start | bytes 3686404
  289.2 35.2 %collective-permute-start.18 = (bf16[4,4,2,4,24,768]{5,4,3,2,1,0:T(8,128)(2,1)}, bf16[4,4,2,4,24,768]{5,4,3,2,1,0:T(8,128)(2,1)}, u32[]{:S(2)}, u32[]{:S(2)}) collective-permute-start(bf16[4,4,2,4,24,768]{5,4,3,2,1,0:T(8,128)(2,1)} %get-tuple-element.202), channel_id=1, source_target_pairs={{0,4},{4,0},{8,12},{12,8},{16,20},{20,16},{24,28},{28,24},{1,5},{5... | collective-permute-start | bytes 14155784 | tf_op jit(solution)/shard_map/ppermute | solution.py:27
  289.2 42.3 %collective-permute-start.20 = (bf16[25,8,3072]{2,1,0:T(8,128)(2,1)}, bf16[25,8,3072]{2,1,0:T(8,128)(2,1)S(1)}, u32[]{:S(2)}, u32[]{:S(2)}) collective-permute-start(bf16[25,8,3072]{2,1,0:T(8,128)(2,1)} %get-tuple-element.212), channel_id=1, source_target_pairs={{0,8},{4,20},{8,0},{12,28},{16,24},{20,4},{24,16},{28,12},{1,9},{5... | collective-permute-start | bytes 3686408 | tf_op jit(solution)/shard_map/ppermute | solution.py:848
  294.0 28.9 %copy-start.43 = (bf16[4,2,4,24,768]{4,3,2,1,0:T(8,128)(2,1)}, bf16[4,2,4,24,768]{4,3,2,1,0:T(8,128)(2,1)S(1)}, u32[]{:S(2)}) copy-start(bf16[4,2,4,24,768]{4,3,2,1,0:T(8,128)(2,1)S(1)} %get-tuple-element.219.refs_1_) | copy-start | bytes 3538948
  294.7 28.2 %copy-start.73 = (bf16[2,4,8,24,768]{4,3,2,1,0:T(8,128)(2,1)S(1)}, bf16[2,4,8,24,768]{4,3,2,1,0:T(8,128)(2,1)}, u32[]{:S(2)}) copy-start(bf16[2,4,8,24,768]{4,3,2,1,0:T(8,128)(2,1)} %copy-done.72) | copy-start | bytes 7077892
  332.4 8.5 %copy-start.47 = (bf16[13,8,3072]{2,1,0:T(8,128)(2,1)}, bf16[13,8,3072]{2,1,0:T(8,128)(2,1)S(1)}, u32[]{:S(2)}) copy-start(bf16[13,8,3072]{2,1,0:T(8,128)(2,1)S(1)} %get-tuple-element.217.refs_1_) | copy-start | bytes 1916932
  340.9 45.5 %collective-permute-start.21 = (bf16[49,8,3072]{2,1,0:T(8,128)(2,1)}, bf16[49,8,3072]{2,1,0:T(8,128)(2,1)}, u32[]{:S(2)}, u32[]{:S(2)}) collective-permute-start(bf16[49,8,3072]{2,1,0:T(8,128)(2,1)} %get-tuple-element.216), channel_id=1, source_target_pairs={{0,4},{4,0},{8,12},{12,8},{16,20},{20,16},{24,28},{28,24},{1,5},{5... | collective-permute-start | bytes 7225352 | tf_op jit(solution)/shard_map/ppermute | solution.py:27
  340.9 28.4 %collective-permute-start.23 = (bf16[4,2,4,24,768]{4,3,2,1,0:T(8,128)(2,1)}, bf16[4,2,4,24,768]{4,3,2,1,0:T(8,128)(2,1)}, u32[]{:S(2)}, u32[]{:S(2)}) collective-permute-start(bf16[4,2,4,24,768]{4,3,2,1,0:T(8,128)(2,1)} %get-tuple-element.220), channel_id=1, source_target_pairs={{0,16},{4,12},{8,24},{12,4},{16,0},{20,28},{24,8},{28,20},{1,17},{... | collective-permute-start | bytes 3538952 | tf_op jit(solution)/shard_map/ppermute | solution.py:848
  341.0 42.0 %collective-permute-start.22 = (bf16[13,8,3072]{2,1,0:T(8,128)(2,1)S(1)}, bf16[13,8,3072]{2,1,0:T(8,128)(2,1)S(1)}, u32[]{:S(2)}, u32[]{:S(2)}) collective-permute-start(bf16[13,8,3072]{2,1,0:T(8,128)(2,1)S(1)} %get-tuple-element.218), channel_id=1, source_target_pairs={{0,16},{4,12},{8,24},{12,4},{16,0},{20,28},{24,8},{28,20},{1,17},{... | collective-permute-start | bytes 1916936 | tf_op jit(solution)/shard_map/ppermute | solution.py:848
  343.0 64.9 %collective-permute-start.25 = (bf16[8,2,4,24,768]{4,3,2,1,0:T(8,128)(2,1)S(1)}, bf16[8,2,4,24,768]{4,3,2,1,0:T(8,128)(2,1)}, u32[]{:S(2)}, u32[]{:S(2)}) collective-permute-start(bf16[8,2,4,24,768]{4,3,2,1,0:T(8,128)(2,1)S(1)} %get-tuple-element.227), channel_id=1, source_target_pairs={{0,8},{4,20},{8,0},{12,28},{16,24},{20,4},{24,16},{28,12},{1,9},{5... | collective-permute-start | bytes 7077896 | tf_op jit(solution)/shard_map/ppermute | solution.py:848
  370.6 12.3 %copy-start.48 = (bf16[13,8,3072]{2,1,0:T(8,128)(2,1)S(1)}, bf16[13,8,3072]{2,1,0:T(8,128)(2,1)}, u32[]{:S(2)}) copy-start(bf16[13,8,3072]{2,1,0:T(8,128)(2,1)} %copy-done.47) | copy-start | bytes 1916932
  372.3 17.7 %collective-permute-start.27 = (bf16[2,2,4,24,768]{4,3,2,1,0:T(8,128)(2,1)S(1)}, bf16[2,2,4,24,768]{4,3,2,1,0:T(8,128)(2,1)S(1)}, u32[]{:S(2)}, u32[]{:S(2)}) collective-permute-start(bf16[2,2,4,24,768]{4,3,2,1,0:T(8,128)(2,1)S(1)} %get-tuple-element.231), channel_id=1, source_target_pairs={{0,1},{1,0},{2,3},{3,2},{4,5},{5,4},{6,7},{7,6},{8,9},{9,8},{10,11... | collective-permute-start | bytes 1769480 | tf_op jit(solution)/shard_map/ppermute | solution.py:848
  374.8 37.5 %collective-permute-start.19 = (bf16[384,768]{1,0:T(8,128)(2,1)S(1)}, bf16[384,768]{1,0:T(8,128)(2,1)}, u32[]{:S(2)}, u32[]{:S(2)}) collective-permute-start(bf16[384,768]{1,0:T(8,128)(2,1)S(1)} %copy-done.7), channel_id=1, source_target_pairs={{0,1},{1,0},{2,3},{3,2},{4,5},{5,4},{6,7},{7,6},{8,9},{9,8},{10,11... | collective-permute-start | bytes 1769480 | tf_op jit(solution)/shard_map/ppermute | solution.py:27
  383.8 23.4 %collective-permute-start.26 = (bf16[204,8,128]{2,1,0:T(8,128)(2,1)S(1)}, bf16[204,8,128]{2,1,0:T(8,128)(2,1)S(1)}, u32[]{:S(2)}, u32[]{:S(2)}) collective-permute-start(bf16[204,8,128]{2,1,0:T(8,128)(2,1)S(1)} %get-tuple-element.229), channel_id=1, source_target_pairs={{0,1},{1,0},{2,3},{3,2},{4,5},{5,4},{6,7},{7,6},{8,9},{9,8},{10,11... | collective-permute-start | bytes 1253384 | tf_op jit(solution)/shard_map/ppermute | solution.py:848
  388.7 32.3 %collective-permute-start.24 = (bf16[25,8,3072]{2,1,0:T(8,128)(2,1)S(1)}, bf16[25,8,3072]{2,1,0:T(8,128)(2,1)S(1)}, u32[]{:S(2)}, u32[]{:S(2)}) collective-permute-start(bf16[25,8,3072]{2,1,0:T(8,128)(2,1)S(1)} %get-tuple-element.225), channel_id=1, source_target_pairs={{0,8},{4,20},{8,0},{12,28},{16,24},{20,4},{24,16},{28,12},{1,9},{5... | collective-permute-start | bytes 3686408 | tf_op jit(solution)/shard_map/ppermute | solution.py:848
  412.3 16.2 %collective-permute-start.29 = (bf16[4,2,4,24,768]{4,3,2,1,0:T(8,128)(2,1)S(1)}, bf16[4,2,4,24,768]{4,3,2,1,0:T(8,128)(2,1)S(1)}, u32[]{:S(2)}, u32[]{:S(2)}) collective-permute-start(bf16[4,2,4,24,768]{4,3,2,1,0:T(8,128)(2,1)S(1)} %get-tuple-element.239), channel_id=1, source_target_pairs={{0,16},{4,12},{8,24},{12,4},{16,0},{20,28},{24,8},{28,20},{1,17},{... | collective-permute-start | bytes 3538952 | tf_op jit(solution)/shard_map/ppermute | solution.py:848
  418.1 34.2 %collective-permute-start.35 = (bf16[1,2,4,24,768]{4,3,2,1,0:T(8,128)(2,1)}, bf16[1,2,4,24,768]{4,3,2,1,0:T(8,128)(2,1)}, u32[]{:S(2)}, u32[]{:S(2)}) collective-permute-start(bf16[1,2,4,24,768]{4,3,2,1,0:T(8,128)(2,1)} %get-tuple-element.255), channel_id=1, source_target_pairs={{0,2},{1,3},{2,0},{3,1},{4,6},{5,7},{6,4},{7,5},{8,10},{9,11},{10,... | collective-permute-start | bytes 884744 | tf_op jit(solution)/shard_map/ppermute | solution.py:848
  418.1 25.1 %collective-permute-start.33 = (bf16[108,8,128]{2,1,0:T(8,128)(2,1)S(1)}, bf16[108,8,128]{2,1,0:T(8,128)(2,1)S(1)}, u32[]{:S(2)}, u32[]{:S(2)}) collective-permute-start(bf16[108,8,128]{2,1,0:T(8,128)(2,1)S(1)} %get-tuple-element.251), channel_id=1, source_target_pairs={{0,2},{1,3},{2,0},{3,1},{4,6},{5,7},{6,4},{7,5},{8,10},{9,11},{10,... | collective-permute-start | bytes 663560 | tf_op jit(solution)/shard_map/ppermute | solution.py:848
  421.0 7.5 %copy-start.46 = (bf16[4,2,4,24,768]{4,3,2,1,0:T(8,128)(2,1)S(1)}, bf16[4,2,4,24,768]{4,3,2,1,0:T(8,128)(2,1)}, u32[]{:S(2)}) copy-start(bf16[4,2,4,24,768]{4,3,2,1,0:T(8,128)(2,1)} %copy-done.45) | copy-start | bytes 3538948
  422.7 23.6 %collective-permute-start.28 = (bf16[13,8,3072]{2,1,0:T(8,128)(2,1)S(1)}, bf16[13,8,3072]{2,1,0:T(8,128)(2,1)S(1)}, u32[]{:S(2)}, u32[]{:S(2)}) collective-permute-start(bf16[13,8,3072]{2,1,0:T(8,128)(2,1)S(1)} %get-tuple-element.237), channel_id=1, source_target_pairs={{0,16},{4,12},{8,24},{12,4},{16,0},{20,28},{24,8},{28,20},{1,17},{... | collective-permute-start | bytes 1916936 | tf_op jit(solution)/shard_map/ppermute | solution.py:848
  429.4 13.8 %copy-start.51 = (bf16[2,2,4,24,768]{4,3,2,1,0:T(8,128)(2,1)}, bf16[2,2,4,24,768]{4,3,2,1,0:T(8,128)(2,1)S(1)}, u32[]{:S(2)}) copy-start(bf16[2,2,4,24,768]{4,3,2,1,0:T(8,128)(2,1)S(1)} %get-tuple-element.244.refs_1_) | copy-start | bytes 1769476
  429.4 22.2 %collective-permute-start.31 = (bf16[2,2,4,24,768]{4,3,2,1,0:T(8,128)(2,1)S(1)}, bf16[2,2,4,24,768]{4,3,2,1,0:T(8,128)(2,1)S(1)}, u32[]{:S(2)}, u32[]{:S(2)}) collective-permute-start(bf16[2,2,4,24,768]{4,3,2,1,0:T(8,128)(2,1)S(1)} %get-tuple-element.245), channel_id=1, source_target_pairs={{0,1},{1,0},{2,3},{3,2},{4,5},{5,4},{6,7},{7,6},{8,9},{9,8},{10,11... | collective-permute-start | bytes 1769480 | tf_op jit(solution)/shard_map/ppermute | solution.py:848
  452.2 12.3 %collective-permute-start.34 = (bf16[1,2,4,24,768]{4,3,2,1,0:T(8,128)(2,1)S(1)}, bf16[1,2,4,24,768]{4,3,2,1,0:T(8,128)(2,1)}, u32[]{:S(2)}, u32[]{:S(2)}) collective-permute-start(bf16[1,2,4,24,768]{4,3,2,1,0:T(8,128)(2,1)S(1)} %get-tuple-element.253), channel_id=1, source_target_pairs={{0,2},{1,3},{2,0},{3,1},{4,6},{5,7},{6,4},{7,5},{8,10},{9,11},{10,... | collective-permute-start | bytes 884744 | tf_op jit(solution)/shard_map/ppermute | solution.py:848
  453.4 15.1 %copy-start.54 = (bf16[204,8,128]{2,1,0:T(8,128)(2,1)S(1)}, bf16[204,8,128]{2,1,0:T(8,128)(2,1)}, u32[]{:S(2)}) copy-start(bf16[204,8,128]{2,1,0:T(8,128)(2,1)} %copy-done.53) | copy-start | bytes 1253380
  453.7 14.8 %collective-permute-start.30 = (bf16[204,8,128]{2,1,0:T(8,128)(2,1)S(1)}, bf16[204,8,128]{2,1,0:T(8,128)(2,1)S(1)}, u32[]{:S(2)}, u32[]{:S(2)}) collective-permute-start(bf16[204,8,128]{2,1,0:T(8,128)(2,1)S(1)} %get-tuple-element.243), channel_id=1, source_target_pairs={{0,1},{1,0},{2,3},{3,2},{4,5},{5,4},{6,7},{7,6},{8,9},{9,8},{10,11... | collective-permute-start | bytes 1253384 | tf_op jit(solution)/shard_map/ppermute | solution.py:848
  469.7 10.5 %copy-start.77 = (f32[1,16,768]{2,0,1:T(1,128)S(1)}, f32[1,16,768]{2,0,1:T(1,128)}, u32[]{:S(2)}) copy-start(f32[1,16,768]{2,0,1:T(1,128)} %stack_reshape.19) | copy-start | bytes 147460
  469.7 10.4 %collective-permute-start.32 = (bf16[108,8,128]{2,1,0:T(8,128)(2,1)S(1)}, bf16[108,8,128]{2,1,0:T(8,128)(2,1)S(1)}, u32[]{:S(2)}, u32[]{:S(2)}) collective-permute-start(bf16[108,8,128]{2,1,0:T(8,128)(2,1)S(1)} %get-tuple-element.249), channel_id=1, source_target_pairs={{0,2},{1,3},{2,0},{3,1},{4,6},{5,7},{6,4},{7,5},{8,10},{9,11},{10,... | collective-permute-start | bytes 663560 | tf_op jit(solution)/shard_map/ppermute | solution.py:848
  470.8 11.6 %copy-start.79 = (f32[1,24,768]{2,1,0:T(8,128)S(1)}, f32[1,24,768]{2,1,0:T(8,128)}, u32[]{:S(2)}) copy-start(f32[1,24,768]{2,1,0:T(8,128)} %stack_reshape.21) | copy-start | bytes 221188
  (65 other events, 167.2 us)

commit v3 on v2

--- a/solution.py
+++ b/solution.py
@@ -14,7 +14,7 @@
 
 BLK = 128
 TILE = 8
-SCALE = 1.0
+SCALE = 0.5
 HALO = 384
 
 
@@ -312,7 +312,8 @@
     )
 
 
-CHUNK = 512
+CHUNK = 1536
+ROWS = 256
 
 
 def normalized(rows):
@@ -329,6 +330,7 @@
         first_rows, first_t, active_t, slope, second_rows, low, after, low_t, low_rows, first, total = rest
     step = pl.program_id(0)
     tiles = [slice(at, at + BLK) for at in range(0, tokens, BLK)]
+    passes = [slice(at, at + ROWS) for at in range(0, tokens, ROWS)]
 
     @pl.when(step == 0)
     def _():
@@ -343,7 +345,7 @@
             low_rows[rows, :] = rounded
             first_t[:, rows] = rounded.T
 
-    for rows in tiles:
+    for rows in passes:
         upward = nn(low_rows[rows, :], w_up[...]) + up_bias[...]
         density = jnp.exp(-0.5 * upward * upward) * 0.3989422804014327
         below = 0.5 + 0.5 * lax.erf(upward * 0.7071067811865476)
@@ -418,7 +420,7 @@
             pltpu.VMEM((tokens, width), f32),
         ],
         compiler_params=pltpu.CompilerParams(vmem_limit_bytes=48 * 2**20),
-        cost_estimate=cost(17),
+        cost_estimate=cost(15),
         name="feed",
     )
 
@@ -441,6 +443,7 @@
 ):
     step = pl.program_id(0)
     tiles = [slice(at, at + BLK) for at in range(0, tokens, BLK)]
+    passes = [slice(at, at + ROWS) for at in range(0, tokens, ROWS)]
 
     @pl.when(step == 0)
     def _():
@@ -457,7 +460,7 @@
             sums[5:6, :] += over_rows(pull)
 
     up_sum[...] = jnp.zeros(up_sum.shape, f32)
-    for rows in tiles:
+    for rows in passes:
         pull = (nt(dz[rows, :], w_down[...]) * slope[rows, :]).astype(bf16)
         du[rows, :] = pull
         up_sum[...] += over_rows(pull.astype(f32))
@@ -517,14 +520,13 @@
         ),
         scratch_shapes=[pltpu.VMEM((tokens, width), f32), pltpu.VMEM((tokens, width), f32)],
         compiler_params=pltpu.CompilerParams(vmem_limit_bytes=48 * 2**20),
-        cost_estimate=cost(21),
+        cost_estimate=cost(17),
         name="feed_back",
     )
 
 
-def grad_feed_kernel(core, active_t, dz, first_t, du, send, keep, lhs):
-    groups, head, _, parts, thin, width = send.shape
-    rows = head * thin
+def grad_down_kernel(core, active_t, dz, send, keep):
+    groups, head, parts, thin, width = send.shape
     mine = core[0]
     for which, out in ((1 - mine, send), (mine, keep)):
         for group in range(groups):
@@ -532,7 +534,14 @@
             for shard in range(head):
                 for at in range(parts):
                     here = (shard * parts + at) * thin
-                    out[group, shard, 0, at] = value[here : here + thin].astype(bf16)
+                    out[group, shard, at] = value[here : here + thin].astype(bf16)
+
+
+def grad_up_kernel(core, first_t, du, send, keep, lhs):
+    groups, head, parts, thin, width = send.shape
+    rows = head * thin
+    mine = core[0]
+    for which, out in ((1 - mine, send), (mine, keep)):
         if rows % 16 == 0:
             for group in range(groups):
                 lhs[group * rows : (group + 1) * rows, :] = first_t[2 * group + which]
@@ -545,27 +554,28 @@
                 values = [nn(first_t[2 * group + which], pulls) for group in range(groups)]
             for group in range(groups):
                 for shard in range(head):
-                    out[group, shard, 1, at] = values[group][shard * thin : (shard + 1) * thin].astype(bf16)
-
-
-def grad_feed(core, active_t, dz, first_t, du, devices, head, waits, passes):
-    tokens, width = dz.shape
-    wide = du.shape[1]
-    parts, rows = wide // width, width // devices
-    out = jax.ShapeDtypeStruct((devices // 2, head, 2, parts, rows // head, width), bf16)
-    return ordered_call(
-        grad_feed_kernel,
-        (core, active_t.reshape(devices, wide // devices, tokens), dz, first_t.reshape(devices, rows, tokens), du),
-        waits,
-        passes,
+                    out[group, shard, at] = values[group][shard * thin : (shard + 1) * thin].astype(bf16)
+
+
+def grad_feed(core, left_t, right, parts, devices, head, scratch):
+    rows, tokens = left_t.shape
+    thin = rows // devices // head // (1 if scratch else parts)
+    width = right.shape[1] // (parts if scratch else 1)
+    out = jax.ShapeDtypeStruct((devices // 2, head, parts, thin, width), bf16)
+    halves, _ = ordered_call(
+        grad_up_kernel if scratch else grad_down_kernel,
+        (core, left_t.reshape(devices, rows // devices, tokens), right),
+        (),
+        (),
         out_shape=(out, out),
-        in_specs=[pl.BlockSpec(memory_space=pltpu.SMEM)] + vmem_specs(4),
+        in_specs=[pl.BlockSpec(memory_space=pltpu.SMEM)] + vmem_specs(2),
         out_specs=tuple(vmem_specs(2)),
-        scratch_shapes=[pltpu.VMEM((width // 2, tokens), bf16)],
+        scratch_shapes=[pltpu.VMEM((rows // 2, tokens), bf16)] if scratch else [],
         compiler_params=pltpu.CompilerParams(vmem_limit_bytes=48 * 2**20),
-        cost_estimate=cost(10),
-        name="grad_feed",
+        cost_estimate=cost(5),
+        name="grad_up" if scratch else "grad_down",
     )
+    return halves
 
 
 def grad_heads_kernel(core, ctx_t, low_t, halo_t, da, dqkv, dkvh, sums, send, keep, one, two, three):
@@ -651,13 +661,13 @@
                     out[kind, shard ^ (step + 1), group ^ change, :, lanes] = ref[at, step, kind]
 
 
-def assemble(relative, place, own, refs):
+def assemble(relative, place, own, refs, passes):
     head = lax.axis_size("head")
-    (out,), _ = ordered_call(
+    (out,), passed = ordered_call(
         functools.partial(assemble_kernel, relative),
         (place, own, *refs),
         (),
-        (),
+        passes,
         out_shape=(jax.ShapeDtypeStruct((own.shape[0], head) + own.shape[1:], bf16),),
         in_specs=[pl.BlockSpec(memory_space=pltpu.SMEM)] + vmem_specs(1 + len(refs)),
         out_specs=vmem_specs(1),
@@ -665,7 +675,7 @@
         cost_estimate=cost(1.5),
         name="assemble",
     )
-    return out
+    return out, passed
 
 
 def grow(value, order):
@@ -738,17 +748,23 @@
     return keep.astype(f32) + got.astype(f32)
 
 
-def advance_kernel(counts, size, tail, scalars, keep, got, send, out):
+def advance_kernel(counts, size, tail, sources, scalars, *refs):
     core, mine = scalars[0], scalars[1]
-    blocks = (keep.shape[0] - tail) // size
+    keeps, gots, (send, out) = refs[:sources], refs[sources : 2 * sources], refs[2 * sources :]
+    blocks = (keeps[0].shape[0] - tail) // size
     for target, which in ((send, 1 - mine), (out, mine)):
         for k in range(blocks // 2):
             spots = [2 * (k // after) * after + k % after for after in counts]
             at = jnp.where(core == 0, spots[0] + which * counts[0], spots[1] + which * counts[1])
             here = pl.ds(at * size, size)
-            target[k * size : (k + 1) * size] = added(keep[here], got[here]).astype(bf16)
+            for source, (keep, got) in enumerate(zip(keeps, gots)):
+                value = added(keep[here], got[here]).astype(bf16)
+                if sources > 1:
+                    target[k * size : (k + 1) * size, source] = value
+                else:
+                    target[k * size : (k + 1) * size] = value
         if tail:
-            value = added(keep[blocks * size :], got[blocks * size :]).astype(bf16)
+            value = added(keeps[0][blocks * size :], gots[0][blocks * size :]).astype(bf16)
             target[blocks // 2 * size :] = value
 
 
@@ -787,7 +803,7 @@
 
 
 class Flight:
-    def __init__(self, send, keep, turned):
+    def __init__(self, keeps, gots, turned):
         dp, head = lax.axis_size("dp"), lax.axis_size("head")
         bits = dp.bit_length() - 1
         upper = list(range(1, bits))
@@ -795,18 +811,21 @@
         self.left = [upper[::-1], upper[::-1]]
         self.head_bits = list(range(head.bit_length() - 1))
         self.turned = turned
-        self.keep, self.got = keep, swap(send, "dp", 1)
         self.tail, self.size = 0, 1
         if turned:
-            self.tail, self.size = 1, (keep.shape[0] - 1) // (dp // 2)
+            self.tail, self.size = 1, (keeps[0].shape[0] - 1) // (dp // 2)
         else:
-            shape = (keep.shape[0] * keep.shape[1],) + keep.shape[2:]
-            self.keep, self.got = self.keep.reshape(shape), self.got.reshape(shape)
+            shape = (keeps[0].shape[0] * keeps[0].shape[1],) + keeps[0].shape[2:]
+            keeps, gots = [k.reshape(shape) for k in keeps], [g.reshape(shape) for g in gots]
+        self.keeps, self.gots = list(keeps), list(gots)
 
     def step(self, waits=(), passes=()):
-        blocks = (self.keep.shape[0] - self.tail) // self.size
+        blocks = (self.keeps[0].shape[0] - self.tail) // self.size
+        sources = len(self.keeps)
         core = bit_of("dp", 0)
-        rest = self.keep.shape[1:]
+        rest = self.keeps[0].shape[1:]
+        if sources > 1:
+            rest = (sources,) + rest
         devices = lax.axis_size("dp")
         counts = [1, 1]
         if self.orders[0]:
@@ -831,27 +850,27 @@
             kernel = functools.partial(turn_heads_kernel, head)
         else:
             out_shape = (blocks // 2 * self.size + self.tail,) + rest
-            kernel = functools.partial(advance_kernel, counts, self.size, self.tail)
+            kernel = functools.partial(advance_kernel, counts, self.size, self.tail, sources)
         out = jax.ShapeDtypeStruct(out_shape, bf16)
         (send, keep), passed = ordered_call(
             kernel,
-            (jnp.stack([core, mine]).astype(jnp.int32), self.keep, self.got),
+            (jnp.stack([core, mine]).astype(jnp.int32), *self.keeps, *self.gots),
             waits,
             passes,
             out_shape=[out] * 2,
-            in_specs=[pl.BlockSpec(memory_space=pltpu.SMEM)] + vmem_specs(2),
+            in_specs=[pl.BlockSpec(memory_space=pltpu.SMEM)] + vmem_specs(2 * sources),
             out_specs=vmem_specs(2),
             compiler_params=pltpu.CompilerParams(vmem_limit_bytes=48 * 2**20),
-            cost_estimate=cost(4),
+            cost_estimate=cost(1 + 2e-6 * out.size),
             name="advance",
         )
-        self.keep, self.got = keep, lax.ppermute(send, axis_name, pairs)
+        self.keeps, self.gots = [keep], [lax.ppermute(send, axis_name, pairs)]
         return passed
 
     def finish(self):
         while self.orders[0] or self.head_bits:
             self.step()
-        total = added(self.keep, self.got)
+        total = added(self.keeps[0], self.gots[0])
         return total if self.tail else total[0]
 
 
@@ -910,13 +929,14 @@
     relative = [order + [other ^ 1 for other in order] for order in (relative_left, relative_right)]
     place = jnp.stack([shard, group]).astype(jnp.int32)
     own_later = [own_w[k].reshape(3, 2, part // 2, width) for k in range(1, layers)]
-    (low_t, halo_t), pieces = flip([tokens_in, halo], [pick(own, core, 1) for own in own_later])
+    (low_t, halo_t), _ = flip([tokens_in, halo], [])
+    w_first, pieces = assemble(relative, place, own_first, [both[0], both[1]], [pick(own, core, 1) for own in own_later])
     later_got = [from_heads_in_turn(value) for value in pieces]
-    w_cats = [assemble(relative, place, own_first, [both[0], both[1]]).reshape(3 * head * part, width)]
+    w_cats = [w_first.reshape(3 * head * part, width)]
 
     def later_weights(own, got):
         theirs = swap(got, "dp", 1)
-        whole = assemble([[0], [1]], jnp.stack([shard, core]).astype(jnp.int32), own, [got[None], theirs[None]])
+        whole = assemble([[0], [1]], jnp.stack([shard, core]).astype(jnp.int32), own, [got[None], theirs[None]], [])[0]
         return whole.reshape(3 * head * part, width)
 
     labels = pick(segment, row, 0)
@@ -960,8 +980,6 @@
         qkv = ((nt(low, w_cat) + shift) * factor).astype(bf16)
         kvh = (nt(halo, w_cat[width:]) + shift[width:]).astype(bf16)
         (ctx, ctx_t, ctx_low, lse), _ = attend(bounds, segq, segk, qkv, kvh, (), ())
-        if not last:
-            got = collect(later_got[layer_idx])
         fed, _ = feed(
             last, layer_idx, hidden, ctx, w_out, vecs[layer_idx], w_up, up_bias_wide[layer_idx : layer_idx + 1], w_down, (), ()
         )
@@ -973,7 +991,7 @@
             low, hidden, low_t = after_low, fed[6], fed[7]
             halo = swap(lax.dynamic_slice_in_dim(low, edge, HALO), "head", 1)
             halo_t = halo.T
-            w_cats.append(later_weights(own_later[layer_idx], got))
+            w_cats.append(later_weights(own_later[layer_idx], collect(later_got[layer_idx])))
 
     grad_hidden = cotangent
     flights = []
@@ -985,31 +1003,34 @@
         )
         if flights:
             flights[1].step()
-        (send, keep), _ = grad_feed(core_at, active_t, dz, first_t, du, dp, head, (), ())
-        fed = Flight(send, keep, False)
+            flights[0].step()
+        parts = du.shape[1] // width
+        down_send, down_keep = grad_feed(core_at, active_t, dz, parts, dp, head, False)
+        down_got = swap(down_send, "dp", 1)
+        up_send, up_keep = grad_feed(core_at, first_t, du, parts, dp, head, True)
+        up_got = swap(up_send, "dp", 1)
+        fed = Flight([down_keep, up_keep], [down_got, up_got], False)
         if flights:
             flights[0].step()
+        fed.step()
         (dqkv, dkvh, sums), _ = attend_back(bounds, segq, segk, qkv, kvh, ctx_t, lse, dc, sums, up_sum, (), ())
         part_halo = nn(dkvh, w_cat[width:]).astype(bf16)
-        (part_halo,) = fed.step(passes=(part_halo,))
         back = swap(part_halo, "head", 1)
         if flights:
             flights[1].step()
-        (send, keep), _ = grad_heads(core_at, ctx_low, low_t, halo_t, da, dqkv, dkvh, sums, dp, (), ())
-        heads = Flight(send, keep, True)
+        (send, keep), _ = grad_heads(core_at, ctx_low, low_t, halo_t, da, dqkv, dkvh, sums, dp, (part_halo,), ())
+        heads = Flight([keep], [swap(send, "dp", 1)], True)
         padded = lax.dynamic_update_slice(jnp.zeros((tokens, width), bf16), back, (edge, 0))
         grad_hidden = nn(dqkv, w_cat) + dr + padded.astype(f32)
+        fed.step()
         if flights:
-            flights[0].step()
             flights[1].step()
             heads.step()
-            flights[0].step()
             flights[1].step()
             fed.step()
             heads.step()
             fed.step()
             heads.step()
-            fed.step()
             heads.step()
         flights = flights + [fed, heads]
 

time: 493 us -> 440 us (0.89)
  waiting for transfers between devices: 132 us -> 92.9 us
  Pallas kernels: 228 us -> 191 us
  starting transfers between devices: 37 us -> 63.9 us
    pallas_call x32 -> x34, Pallas kernels: 228 us -> 191 us  [ordered_call(): pl.pallas_call(body, out_shape=tuple(out_shape) + (jax.ShapeDtypeStruct((...]
    ppermute x16, waiting for transfers between devices: 89.2 us -> 52.5 us  [step(): self.keeps, self.gots = ([keep], [lax.ppermute(send, axis_name, pairs)])]
    ppermute x16, starting transfers between devices: 19.4 us -> 34.2 us  [step(): self.keeps, self.gots = ([keep], [lax.ppermute(send, axis_name, pairs)])]
    ppermute x20 -> x22, starting transfers between devices: 17.7 us -> 29.6 us  [swap(): return lax.ppermute(value, axis, [(i, i ^ bit) for i in range(size)])]
    unnamed x190 -> x192, local copies, waits for them, and re-layouts: 31.1 us -> 34.1 us
    ppermute x20 -> x22, waiting for transfers between devices: 43.3 us -> 40.5 us  [swap(): return lax.ppermute(value, axis, [(i, i ^ bit) for i in range(size)])]
  transfers between devices with their start and end apart: 36 -> 38, of which waited for: 17 -> 18; matrix products, arithmetic and copies ran while one was open for 10% -> 10% of each run, Pallas kernels for 31% -> 28%
where the time goes in v3:
time: 440 us; the launch traced here: 435 us
  Pallas kernels  191 us (43%)
  waiting for transfers between devices  92.9 us (21%)
  starting transfers between devices  63.9 us (15%)
  local copies, waits for them, and re-layouts  54.5 us (12%)
  other arithmetic  15.4 us (4%)
  matrix products  14.7 us (3%)
    pallas_call x34, Pallas kernels, ordered_call(): pl.pallas_call(body, out_shape=tuple(out_shape) + (jax.ShapeDtypeStruct((...  191 us
    ppermute x16, waiting for transfers between devices, step(): self.keeps, self.gots = ([keep], [lax.ppermute(send, axis_name, pairs)])  52.5 us
    ppermute x22, waiting for transfers between devices, swap(): return lax.ppermute(value, axis, [(i, i ^ bit) for i in range(size)])  40.5 us
    ppermute x16, starting transfers between devices, step(): self.keeps, self.gots = ([keep], [lax.ppermute(send, axis_name, pairs)])  34.2 us
    unnamed x192, local copies, waits for them, and re-layouts  34.1 us
    ppermute x22, starting transfers between devices, swap(): return lax.ppermute(value, axis, [(i, i ^ bit) for i in range(size)])  29.6 us
  transfers between devices with their start and end apart: 38, of which 18 were waited for; matrix products, arithmetic and copies ran while one was open for 10% of the time, Pallas kernels for 28%

profile of v3, /device:TPU:0, one launch (start us, length us, event | category | flops | bytes accessed | tf_op | source)
XLA Modules:
  0.0 435.2 jit_solution(3570971065104383230)
XLA Ops:
  0.7 1.6 fusion.20
  2.5 3.1 collective-permute-start
  5.6 2.6 collective-permute-start.1
  12.9 5.1 %collective-permute-done.1 = bf16[80,768]{1,0:T(8,128)(2,1)} collective-permute-done((bf16[80,768]{1,0:T(8,128)(2,1)S(1)}, bf16[80,768]{1,0:T(8,128)(2,1)}, u32[]{:S(2)}, u32[]{:S(2)}) %collective-permute-start.1) | collective-permute-done | bytes 122912 | tf_op jit(solution)/shard_map/ppermute | solution.py:27
  24.0 2.3 collective-permute-done.3
  27.3 1.6 collective-permute-start.4
  31.6 2.9 collective-permute-done.4
  35.6 2.2 collective-permute-done.6
  46.2 1.6 pad_maximum_fusion
  49.0 1.6 collective-permute-start.10
  53.3 2.0 fusion.4.refs_3_
  56.7 8.7 %attend.2 = (bf16[512,768]{1,0:T(8,128)(2,1)S(1)}, f32[768,512]{1,0:T(8,128)S(1)}, bf16[768,512]{1,0:T(8,128)(2,1)S(1)}, f32[4,8,256]{2,1,0:T(8,128)S(1)}, f32[8,128]{1,0:T(8,128)S(1)}) custom-call(s32[4,4]{1,0:T(4,128)S(1)} %pad_add_fusion.2.refs_0_, s32[4,1,256]{2,1,0:T(1,128)S(1)} %reshape.441.refs_1_, s32[896,1]{1,0:T(8,128)S(1)} %reshape.472.refs_2_, ...), custom_call_target="tpu_custom_call" | custom-call | flops 5175000064 | bytes 1000 | tf_op jit(solution)/shard_map/attend/pallas_call | solution.py:231
  67.6 4.3 collective-permute-done.10.refs_1_
  71.9 14.4 %feed.2 = (f32[512,768]{1,0:T(8,128)S(1)}, bf16[768,512]{1,0:T(8,128)(2,1)S(1)}, bf16[3072,512]{1,0:T(8,128)(2,1)}, f32[512,3072]{1,0:T(8,128)}, f32[512,768]{1,...) custom-call(bf16[512,768]{1,0:T(8,128)(2,1)S(1)} %copy-done.14, ...), custom_call_target="tpu_custom_call" | custom-call | flops 8625000448 | bytes 1000 | tf_op jit(solution)/shard_map/feed/pallas_call | solution.py:231
  86.7 2.1 collective-permute-start.13
  90.6 1.7 copy-done.8
  92.2 2.0 fusion.3.refs_3_
  94.3 8.4 %collective-permute-done.13 = bf16[384,768]{1,0:T(8,128)(2,1)S(1)} collective-permute-done((bf16[384,768]{1,0:T(8,128)(2,1)S(1)}, bf16[384,768]{1,0:T(8,128)(2,1)S(1)}, u32[]{:S(2)}, u32[]{:S(2)}) %collective-permute-start.13) | collective-permute-done | bytes 589856 | tf_op jit(solution)/shard_map/ppermute | solution.py:27
  103.9 8.6 %attend.3 = (bf16[512,768]{1,0:T(8,128)(2,1)S(1)}, f32[768,512]{1,0:T(8,128)S(1)}, bf16[768,512]{1,0:T(8,128)(2,1)S(1)}, f32[4,8,256]{2,1,0:T(8,128)S(1)}, f32[8,128]{1,0:T(8,128)S(1)}) custom-call(s32[4,4]{1,0:T(4,128)S(1)} %pad_add_fusion.2.refs_0_, s32[4,1,256]{2,1,0:T(1,128)S(1)} %reshape.441.refs_1_, s32[896,1]{1,0:T(8,128)S(1)} %reshape.472.refs_2_, ...), custom_call_target="tpu_custom_call" | custom-call | flops 5175000064 | bytes 1000 | tf_op jit(solution)/shard_map/attend/pallas_call | solution.py:231
  114.5 14.2 %feed.3 = (f32[512,768]{1,0:T(8,128)S(1)}, bf16[768,512]{1,0:T(8,128)(2,1)S(1)}, bf16[3072,512]{1,0:T(8,128)(2,1)}, f32[512,3072]{1,0:T(8,128)}, f32[512,768]{1,...) custom-call(f32[512,768]{1,0:T(8,128)} %get-tuple-element.144.refs_0_, ...), custom_call_target="tpu_custom_call" | custom-call | flops 8625000448 | bytes 1000 | tf_op jit(solution)/shard_map/feed/pallas_call | solution.py:231
  131.1 15.8 %feed_back.2 = (bf16[512,768]{1,0:T(8,128)(2,1)S(1)}, bf16[512,3072]{1,0:T(8,128)(2,1)}, bf16[512,768]{1,0:T(8,128)(2,1)S(1)}, f32[512,768]{1,0:T(8,128)S(1)}, b...) custom-call(bf16[512,768]{1,0:T(8,128)(2,1)S(1)} %copy-done.22, ...), custom_call_target="tpu_custom_call" | custom-call | flops 9774999552 | bytes 1000 | tf_op jit(solution)/shard_map/feed_back/pallas_call | solution.py:231
  148.9 4.8 %grad_down.2 = (bf16[4,4,4,24,768]{4,3,2,1,0:T(8,128)(2,1)S(1)}, bf16[4,4,4,24,768]{4,3,2,1,0:T(8,128)(2,1)S(1)}, f32[8,128]{1,0:T(8,128)S(1)}) custom-call(s32[1]{0:T(128)} %bitcast.32.refs_0_, bf16[8,384,512]{2,1,0:T(8,128)(2,1)} %bitcast.200, bf16[512,768]{1,0:T(8,128)(2,1)S(1)} %get-tuple-element.167.refs_2_, f32[8,128]{1,0:T(8,128)S(1)} %get-tuple-element.168.refs_3_), custom_call_target="tpu_custom_call" | custom-call | flops 2875000064 | bytes 1000 | tf_op jit(solution)/shard_map/grad_down/pallas_call | solution.py:231
  155.2 4.7 %grad_up.2 = (bf16[4,4,4,24,768]{4,3,2,1,0:T(8,128)(2,1)}, bf16[4,4,4,24,768]{4,3,2,1,0:T(8,128)(2,1)S(1)}, f32[8,128]{1,0:T(8,128)S(1)}) custom-call(s32[1]{0:T(128)} %bitcast.32.refs_0_, bf16[8,96,512]{2,1,0:T(8,128)(2,1)S(1)} %bitcast.161, bf16[512,3072]{1,0:T(8,128)(2,1)} %get-tuple-element.171.refs_2_, f32[8,128]{1,0:T(8,128)S(1)} %get-tuple-element.172.refs_3_), custom_call_target="tpu_custom_call" | custom-call | flops 2875000064 | bytes 1000 | tf_op jit(solution)/shard_map/grad_up/pallas_call | solution.py:231
  161.3 1.6 collective-permute-start.15
  164.4 6.4 %collective-permute-done.15 = bf16[4,4,4,24,768]{4,3,2,1,0:T(8,128)(2,1)} collective-permute-done((bf16[4,4,4,24,768]{4,3,2,1,0:T(8,128)(2,1)}, bf16[4,4,4,24,768]{4,3,2,1,0:T(8,128)(2,1)}, u32[]{:S(2)}, u32[]{:S(2)}) %collective-permute-start.15) | collective-permute-done | bytes 2359328 | tf_op jit(solution)/shard_map/ppermute | solution.py:27
  170.8 6.3 %advance.16 = (bf16[8,2,4,24,768]{4,3,2,1,0:T(8,128)(2,1)}, bf16[8,2,4,24,768]{4,3,2,1,0:T(8,128)(2,1)S(1)}, f32[8,128]{1,0:T(8,128)S(1)}) custom-call(s32[2]{0:T(128)S(1)} %pad_add_fusion.5.refs_0_, bf16[16,4,24,768]{3,2,1,0:T(8,128)(2,1)} %bitcast.147, bf16[16,4,24,768]{3,2,1,0:T(8,128)(2,1)} %bitcast.148, bf16[16,4,24,768]{3,2,1,0:T(8,128)(2,1)} %bitcast.43.refs_3_, ...), custom_call_target="tpu_custom_call" | custom-call | flops 1931595264 | bytes 1000 | tf_op jit(solution)/shard_map/advance/pallas_call | solution.py:231
  178.3 20.9 %attend_back.2 = (bf16[512,2304]{1,0:T(8,128)(2,1)S(1)}, bf16[384,1536]{1,0:T(8,128)(2,1)S(1)}, f32[16,768]{1,0:T(8,128)S(1)}, f32[8,128]{1,0:T(8,128)S(1)}) custom-call(s32[4,4]{1,0:T(4,128)S(1)} %pad_add_fusion.2.refs_0_, s32[4,1,256]{2,1,0:T(1,128)S(1)} %reshape.441.refs_1_, s32[896,1]{1,0:T(8,128)S(1)} %reshape.472.refs_2_, ...), custom_call_target="tpu_custom_call" | custom-call | flops 12074999808 | bytes 1000 | tf_op jit(solution)/shard_map/attend_back/pallas_call | solution.py:231
  200.6 1.9 convolution_convert_fusion.1.refs_8_
  202.5 7.6 %grad_heads.2 = (bf16[49,8,3072]{2,1,0:T(8,128)(2,1)}, bf16[49,8,3072]{2,1,0:T(8,128)(2,1)}, f32[8,128]{1,0:T(8,128)S(1)}) custom-call(s32[1]{0:T(128)} %bitcast.32.refs_0_, bf16[8,96,512]{2,1,0:T(8,128)(2,1)S(1)} %bitcast.160, bf16[8,96,512]{2,1,0:T(8,128)(2,1)S(1)} %bitcast.159, bf16[8,96,384]{2,1,0:T(8,128)(2,1)S(1)} %bitcast.155, ...), custom_call_target="tpu_custom_call" | custom-call | flops 4600000000 | bytes 1000 | tf_op jit(solution)/shard_map/grad_heads/pallas_call | solution.py:231
  210.1 4.1 collective-permute-start.19
  217.1 2.4 advance.17
  219.5 5.6 %collective-permute-start.18 = (bf16[4,2,4,24,768]{4,3,2,1,0:T(8,128)(2,1)S(1)}, bf16[4,2,4,24,768]{4,3,2,1,0:T(8,128)(2,1)S(1)}, u32[]{:S(2)}, u32[]{:S(2)}) collective-permute-start(bf16[4,2,4,24,768]{4,3,2,1,0:T(8,128)(2,1)S(1)} %get-tuple-element.199), channel_id=1, source_target_pairs={{0,16},{4,12},{8,24},{12,4},{16,0},{20,28},{24,8},{28,20},{1,17},{... | collective-permute-start | bytes 3538952 | tf_op jit(solution)/shard_map/ppermute | solution.py:867
  225.1 3.5 convert_add_fusion.1.refs_0_
  228.6 15.8 %feed_back.3 = (bf16[512,768]{1,0:T(8,128)(2,1)S(1)}, bf16[512,3072]{1,0:T(8,128)(2,1)}, bf16[512,768]{1,0:T(8,128)(2,1)S(1)}, f32[512,768]{1,0:T(8,128)S(1)}, b...) custom-call(f32[512,768]{1,0:T(8,128)S(1)} %convert_add_fusion.1.refs_0_, ...), custom_call_target="tpu_custom_call" | custom-call | flops 9774999552 | bytes 1000 | tf_op jit(solution)/shard_map/feed_back/pallas_call | solution.py:231
  246.4 2.5 advance.18
  252.4 4.6 %grad_down.3 = (bf16[4,4,4,24,768]{4,3,2,1,0:T(8,128)(2,1)S(1)}, bf16[4,4,4,24,768]{4,3,2,1,0:T(8,128)(2,1)S(1)}, f32[8,128]{1,0:T(8,128)S(1)}) custom-call(s32[1]{0:T(128)} %bitcast.32.refs_0_, bf16[8,384,512]{2,1,0:T(8,128)(2,1)} %bitcast.199, bf16[512,768]{1,0:T(8,128)(2,1)S(1)} %get-tuple-element.197.refs_2_, f32[8,128]{1,0:T(8,128)S(1)} %get-tuple-element.204.refs_3_), custom_call_target="tpu_custom_call" | custom-call | flops 2875000064 | bytes 1000 | tf_op jit(solution)/shard_map/grad_down/pallas_call | solution.py:231
  258.3 4.7 %grad_up.3 = (bf16[4,4,4,24,768]{4,3,2,1,0:T(8,128)(2,1)}, bf16[4,4,4,24,768]{4,3,2,1,0:T(8,128)(2,1)S(1)}, f32[8,128]{1,0:T(8,128)S(1)}) custom-call(s32[1]{0:T(128)} %bitcast.32.refs_0_, bf16[8,96,512]{2,1,0:T(8,128)(2,1)S(1)} %bitcast.158, bf16[512,3072]{1,0:T(8,128)(2,1)} %get-tuple-element.207.refs_2_, f32[8,128]{1,0:T(8,128)S(1)} %get-tuple-element.208.refs_3_), custom_call_target="tpu_custom_call" | custom-call | flops 2875000064 | bytes 1000 | tf_op jit(solution)/shard_map/grad_up/pallas_call | solution.py:231
  264.5 1.8 collective-permute-start.21
  266.3 2.1 collective-permute-start.22
  269.6 13.2 %collective-permute-done.22.refs_2_ = bf16[2,2,4,24,768]{4,3,2,1,0:T(8,128)(2,1)} collective-permute-done((bf16[2,2,4,24,768]{4,3,2,1,0:T(8,128)(2,1)}, bf16[2,2,4,24,768]{4,3,2,1,0:T(8,128)(2,1)}, u32[]{:S(2)}, u32[]{:S(2)}) %collective-permute-start.22) | collective-permute-done | bytes 589856 | tf_op jit(solution)/shard_map/ppermute | solution.py:867
  283.8 1.9 advance.20
  285.7 5.0 %advance.21 = (bf16[8,2,4,24,768]{4,3,2,1,0:T(8,128)(2,1)S(1)}, bf16[8,2,4,24,768]{4,3,2,1,0:T(8,128)(2,1)S(1)}, f32[8,128]{1,0:T(8,128)S(1)}) custom-call(s32[2]{0:T(128)S(1)} %pad_add_fusion.5.refs_0_, bf16[16,4,24,768]{3,2,1,0:T(8,128)(2,1)} %bitcast.145, bf16[16,4,24,768]{3,2,1,0:T(8,128)(2,1)} %bitcast.146, bf16[16,4,24,768]{3,2,1,0:T(8,128)(2,1)} %bitcast.55.refs_3_, ...), custom_call_target="tpu_custom_call" | custom-call | flops 1931595264 | bytes 1000 | tf_op jit(solution)/shard_map/advance/pallas_call | solution.py:231
  291.5 21.0 %attend_back.3 = (bf16[512,2304]{1,0:T(8,128)(2,1)S(1)}, bf16[384,1536]{1,0:T(8,128)(2,1)S(1)}, f32[16,768]{1,0:T(8,128)S(1)}, f32[8,128]{1,0:T(8,128)S(1)}) custom-call(s32[4,4]{1,0:T(4,128)S(1)} %pad_add_fusion.2.refs_0_, s32[4,1,256]{2,1,0:T(1,128)S(1)} %reshape.441.refs_1_, s32[896,1]{1,0:T(8,128)S(1)} %reshape.472.refs_2_, ...), custom_call_target="tpu_custom_call" | custom-call | flops 12074999808 | bytes 1000 | tf_op jit(solution)/shard_map/attend_back/pallas_call | solution.py:231
  317.1 7.7 %grad_heads.3 = (bf16[49,8,3072]{2,1,0:T(8,128)(2,1)}, bf16[49,8,3072]{2,1,0:T(8,128)(2,1)}, f32[8,128]{1,0:T(8,128)S(1)}) custom-call(s32[1]{0:T(128)} %bitcast.32.refs_0_, bf16[8,96,512]{2,1,0:T(8,128)(2,1)S(1)} %bitcast.157, bf16[8,96,512]{2,1,0:T(8,128)(2,1)S(1)} %bitcast.156, bf16[8,96,384]{2,1,0:T(8,128)(2,1)S(1)} %bitcast.162, ...), custom_call_target="tpu_custom_call" | custom-call | flops 4600000000 | bytes 1000 | tf_op jit(solution)/shard_map/grad_heads/pallas_call | solution.py:231
  324.8 4.2 collective-permute-start.25
  329.0 3.1 advance.23
  333.1 2.0 collective-permute-start.29
  335.1 7.2 %collective-permute-start.37 = (bf16[1,2,4,24,768]{4,3,2,1,0:T(8,128)(2,1)}, bf16[1,2,4,24,768]{4,3,2,1,0:T(8,128)(2,1)}, u32[]{:S(2)}, u32[]{:S(2)}) collective-permute-start(bf16[1,2,4,24,768]{4,3,2,1,0:T(8,128)(2,1)} %get-tuple-element.263), channel_id=1, source_target_pairs={{0,2},{1,3},{2,0},{3,1},{4,6},{5,7},{6,4},{7,5},{8,10},{9,11},{10,... | collective-permute-start | bytes 884744 | tf_op jit(solution)/shard_map/ppermute | solution.py:867
  343.3 2.2 advance.24
  345.5 1.9 collective-permute-start.30
  347.5 3.0 advance.25
  351.9 4.4 %collective-permute-done.37 = bf16[1,2,4,24,768]{4,3,2,1,0:T(8,128)(2,1)} collective-permute-done((bf16[1,2,4,24,768]{4,3,2,1,0:T(8,128)(2,1)}, bf16[1,2,4,24,768]{4,3,2,1,0:T(8,128)(2,1)}, u32[]{:S(2)}, u32[]{:S(2)}) %collective-permute-start.37) | collective-permute-done | bytes 294944 | tf_op jit(solution)/shard_map/ppermute | solution.py:867
  359.9 3.5 collective-permute-done.30.refs_2_
  365.6 2.1 advance.27
  367.9 2.0 fusion.24
  369.9 6.0 %collective-permute-done.23 = bf16[384,768]{1,0:T(8,128)(2,1)S(1)} collective-permute-done((bf16[384,768]{1,0:T(8,128)(2,1)S(1)}, bf16[384,768]{1,0:T(8,128)(2,1)S(1)}, u32[]{:S(2)}, u32[]{:S(2)}) %collective-permute-start.23) | collective-permute-done | bytes 589856 | tf_op jit(solution)/shard_map/ppermute | solution.py:27
  376.0 3.7 collective-permute-start.35
  382.0 10.3 %collective-permute-done.32.refs_2_ = bf16[2,2,4,24,768]{4,3,2,1,0:T(8,128)(2,1)S(1)} collective-permute-done((bf16[2,2,4,24,768]{4,3,2,1,0:T(8,128)(2,1)S(1)}, bf16[2,2,4,24,768]{4,3,2,1,0:T(8,128)(2,1)S(1)}, u32[]{:S(2)}, u32[]{:S(2)}) %collective-permute-start.32) | collective-permute-done | bytes 589856 | tf_op jit(solution)/shard_map/ppermute | solution.py:867
  393.1 4.3 collective-permute-start.36
  399.0 1.7 slice.238
  401.6 2.5 collective-permute-start.33
  404.1 6.8 %collective-permute-done.36 = bf16[1,2,4,24,768]{4,3,2,1,0:T(8,128)(2,1)} collective-permute-done((bf16[1,2,4,24,768]{4,3,2,1,0:T(8,128)(2,1)S(1)}, bf16[1,2,4,24,768]{4,3,2,1,0:T(8,128)(2,1)}, u32[]{:S(2)}, u32[]{:S(2)}) %collective-permute-start.36) | collective-permute-done | bytes 294944 | tf_op jit(solution)/shard_map/ppermute | solution.py:867
  412.3 5.5 %collective-permute-done.33.refs_2_ = bf16[204,8,128]{2,1,0:T(8,128)(2,1)S(1)} collective-permute-done((bf16[204,8,128]{2,1,0:T(8,128)(2,1)S(1)}, bf16[204,8,128]{2,1,0:T(8,128)(2,1)S(1)}, u32[]{:S(2)}, u32[]{:S(2)}) %collective-permute-start.33) | collective-permute-done | bytes 417824 | tf_op jit(solution)/shard_map/ppermute | solution.py:867
  422.1 8.8 %collective-permute-done.34 = bf16[108,8,128]{2,1,0:T(8,128)(2,1)S(1)} collective-permute-done((bf16[108,8,128]{2,1,0:T(8,128)(2,1)S(1)}, bf16[108,8,128]{2,1,0:T(8,128)(2,1)S(1)}, u32[]{:S(2)}, u32[]{:S(2)}) %collective-permute-start.34) | collective-permute-done | bytes 221216 | tf_op jit(solution)/shard_map/ppermute | solution.py:867
  (359 shorter events, 90.6 us)
Async XLA Ops:
  0.7 11.8 %copy-start.87 = (bf16[2,768]{1,0:T(2,128)(2,1)S(1)}, bf16[2,768]{1,0:T(2,128)(2,1)}, u32[]{:S(2)}) copy-start(bf16[2,768]{1,0:T(2,128)(2,1)} %param.20) | copy-start | bytes 9220
  0.7 11.8 %copy-start.88 = (bf16[2,768]{1,0:T(2,128)(2,1)S(1)}, bf16[2,768]{1,0:T(2,128)(2,1)}, u32[]{:S(2)}) copy-start(bf16[2,768]{1,0:T(2,128)(2,1)} %param.21) | copy-start | bytes 9220
  0.7 11.8 %copy-start.89 = (bf16[2,768]{1,0:T(2,128)(2,1)S(1)}, bf16[2,768]{1,0:T(2,128)(2,1)}, u32[]{:S(2)}) copy-start(bf16[2,768]{1,0:T(2,128)(2,1)} %param.22) | copy-start | bytes 9220
  0.7 11.9 %copy-start.90 = (bf16[2,768]{1,0:T(2,128)(2,1)S(1)}, bf16[2,768]{1,0:T(2,128)(2,1)}, u32[]{:S(2)}) copy-start(bf16[2,768]{1,0:T(2,128)(2,1)} %param.26) | copy-start | bytes 9220
  0.7 11.9 %copy-start.91 = (bf16[2,768]{1,0:T(2,128)(2,1)S(1)}, bf16[2,768]{1,0:T(2,128)(2,1)}, u32[]{:S(2)}) copy-start(bf16[2,768]{1,0:T(2,128)(2,1)} %param.27) | copy-start | bytes 9220
  0.7 11.9 %copy-start.92 = (bf16[2,768]{1,0:T(2,128)(2,1)S(1)}, bf16[2,768]{1,0:T(2,128)(2,1)}, u32[]{:S(2)}) copy-start(bf16[2,768]{1,0:T(2,128)(2,1)} %param.28) | copy-start | bytes 9220
  2.5 10.4 %collective-permute-start = (bf16[80,768]{1,0:T(8,128)(2,1)S(1)}, bf16[80,768]{1,0:T(8,128)(2,1)S(1)}, u32[]{:S(2)}, u32[]{:S(2)}) collective-permute-start(bf16[80,768]{1,0:T(8,128)(2,1)S(1)} %fusion.8), channel_id=1, source_target_pairs={{0,1},{1,0},{2,3},{3,2},{4,5},{5,4},{6,7},{7,6},{8,9},{9,8},{10,11... | collective-permute-start | bytes 368648 | tf_op jit(solution)/shard_map/ppermute | solution.py:27
  5.6 12.4 %collective-permute-start.1 = (bf16[80,768]{1,0:T(8,128)(2,1)S(1)}, bf16[80,768]{1,0:T(8,128)(2,1)}, u32[]{:S(2)}, u32[]{:S(2)}) collective-permute-start(bf16[80,768]{1,0:T(8,128)(2,1)S(1)} %fusion.8), channel_id=1, source_target_pairs={{0,2},{1,3},{2,0},{3,1},{4,6},{5,7},{6,4},{7,5},{8,10},{9,11},{10,... | collective-permute-start | bytes 368648 | tf_op jit(solution)/shard_map/ppermute | solution.py:27
  8.2 10.7 %collective-permute-start.2 = (bf16[80,768]{1,0:T(8,128)(2,1)S(1)}, bf16[80,768]{1,0:T(8,128)(2,1)}, u32[]{:S(2)}, u32[]{:S(2)}) collective-permute-start(bf16[80,768]{1,0:T(8,128)(2,1)S(1)} %fusion.8), channel_id=1, source_target_pairs={{0,3},{1,2},{2,1},{3,0},{4,7},{5,6},{6,5},{7,4},{8,11},{9,10},{10,... | collective-permute-start | bytes 368648 | tf_op jit(solution)/shard_map/ppermute | solution.py:27
  9.0 33.9 %collective-permute-start.8 = (bf16[384,768]{1,0:T(8,128)(2,1)}, bf16[384,768]{1,0:T(8,128)(2,1)S(1)}, u32[]{:S(2)}, u32[]{:S(2)}) collective-permute-start(bf16[384,768]{1,0:T(8,128)(2,1)} %constant_dynamic-slice_fusion.3), channel_id=1, source_target_pairs={{0,1},{1,0},{2,3},{3,2},{4,5},{5,4},{6,7},{7,6},{8,9},{9,8},{10,11... | collective-permute-start | bytes 1769480 | tf_op jit(solution)/shard_map/ppermute | solution.py:27
  20.6 5.7 %collective-permute-start.3 = (bf16[1,3,3,24,384]{4,3,2,1,0:T(8,128)(2,1)}, bf16[1,3,3,24,384]{4,3,2,1,0:T(8,128)(2,1)}, u32[]{:S(2)}, u32[]{:S(2)}) collective-permute-start(bf16[1,3,3,24,384]{4,3,2,1,0:T(8,128)(2,1)} %get-tuple-element.282), channel_id=1, source_target_pairs={{0,8},{4,12},{8,0},{12,4},{16,24},{20,28},{24,16},{28,20},{1,9},{5... | collective-permute-start | bytes 497672 | tf_op jit(solution)/shard_map/ppermute | solution.py:27
  22.1 7.4 %collective-permute-start.5 = (bf16[1,3,3,24,384]{4,3,2,1,0:T(8,128)(2,1)}, bf16[1,3,3,24,384]{4,3,2,1,0:T(8,128)(2,1)}, u32[]{:S(2)}, u32[]{:S(2)}) collective-permute-start(bf16[1,3,3,24,384]{4,3,2,1,0:T(8,128)(2,1)} %get-tuple-element.283), channel_id=1, source_target_pairs={{0,16},{4,20},{8,24},{12,28},{16,0},{20,4},{24,8},{28,12},{1,17},{... | collective-permute-start | bytes 497672 | tf_op jit(solution)/shard_map/ppermute | solution.py:27
  27.3 7.2 %collective-permute-start.4 = (bf16[2,3,3,24,384]{4,3,2,1,0:T(8,128)(2,1)S(1)}, bf16[2,3,3,24,384]{4,3,2,1,0:T(8,128)(2,1)S(1)}, u32[]{:S(2)}, u32[]{:S(2)}) collective-permute-start(bf16[2,3,3,24,384]{4,3,2,1,0:T(8,128)(2,1)S(1)} %pad_maximum_fusion.5), channel_id=1, source_target_pairs={{0,16},{4,20},{8,24},{12,28},{16,0},{20,4},{24,8},{28,12},{1,17},{... | collective-permute-start | bytes 995336 | tf_op jit(solution)/shard_map/ppermute | solution.py:27
  30.6 7.2 %collective-permute-start.6 = (bf16[2,3,3,24,384]{4,3,2,1,0:T(8,128)(2,1)S(1)}, bf16[2,3,3,24,384]{4,3,2,1,0:T(8,128)(2,1)S(1)}, u32[]{:S(2)}, u32[]{:S(2)}) collective-permute-start(bf16[2,3,3,24,384]{4,3,2,1,0:T(8,128)(2,1)S(1)} %pad_maximum_fusion.6), channel_id=1, source_target_pairs={{0,8},{4,12},{8,0},{12,4},{16,24},{20,28},{24,16},{28,20},{1,9},{5... | collective-permute-start | bytes 995336 | tf_op jit(solution)/shard_map/ppermute | solution.py:27
  31.6 8.6 %copy-start.85 = (bf16[2,3072]{1,0:T(2,128)(2,1)S(1)}, bf16[2,3072]{1,0:T(2,128)(2,1)}, u32[]{:S(2)}) copy-start(bf16[2,3072]{1,0:T(2,128)(2,1)} %param.24) | copy-start | bytes 36868
  40.2 6.1 %collective-permute-start.7 = (bf16[2,4,3,3,24,384]{5,4,3,2,1,0:T(8,128)(2,1)}, bf16[2,4,3,3,24,384]{5,4,3,2,1,0:T(8,128)(2,1)}, u32[]{:S(2)}, u32[]{:S(2)}) collective-permute-start(bf16[2,4,3,3,24,384]{5,4,3,2,1,0:T(8,128)(2,1)} %pad_maximum_fusion.1), channel_id=1, source_target_pairs={{0,4},{4,0},{8,12},{12,8},{16,20},{20,16},{24,28},{28,24},{1,5},{5... | collective-permute-start | bytes 3981320 | tf_op jit(solution)/shard_map/ppermute | solution.py:27
  49.0 22.9 %collective-permute-start.10 = (bf16[3,96,768]{2,1,0:T(8,128)(2,1)S(1)}, bf16[3,96,768]{2,1,0:T(8,128)(2,1)S(1)}, u32[]{:S(2)}, u32[]{:S(2)}) collective-permute-start(bf16[3,96,768]{2,1,0:T(8,128)(2,1)S(1)} %get-tuple-element.146), channel_id=1, source_target_pairs={{0,2},{1,3},{2,0},{3,1},{4,6},{5,7},{6,4},{7,5},{8,10},{9,11},{10,... | collective-permute-start | bytes 1327112 | tf_op jit(solution)/shard_map/ppermute | solution.py:27
  50.6 35.7 %collective-permute-start.9 = (bf16[3,96,768]{2,1,0:T(8,128)(2,1)S(1)}, bf16[3,96,768]{2,1,0:T(8,128)(2,1)S(1)}, u32[]{:S(2)}, u32[]{:S(2)}) collective-permute-start(bf16[3,96,768]{2,1,0:T(8,128)(2,1)S(1)} %get-tuple-element.146), channel_id=1, source_target_pairs={{0,1},{1,0},{2,3},{3,2},{4,5},{5,4},{6,7},{7,6},{8,9},{9,8},{10,11... | collective-permute-start | bytes 1327112 | tf_op jit(solution)/shard_map/ppermute | solution.py:27
  56.5 9.0 %copy-start.41 = (bf16[384,1536]{1,0:T(8,128)(2,1)}, bf16[384,1536]{1,0:T(8,128)(2,1)S(1)}, u32[]{:S(2)}) copy-start(bf16[384,1536]{1,0:T(8,128)(2,1)S(1)} %fusion.5.refs_4_) | copy-start | bytes 3538948
  71.9 14.5 %collective-permute-start.11 = (bf16[3,96,768]{2,1,0:T(8,128)(2,1)S(1)}, bf16[3,96,768]{2,1,0:T(8,128)(2,1)S(1)}, u32[]{:S(2)}, u32[]{:S(2)}) collective-permute-start(bf16[3,96,768]{2,1,0:T(8,128)(2,1)S(1)} %collective-permute-done.10.refs_1_), channel_id=1, source_target_pairs={{0,1},{1,0},{2,3},{3,2},{4,5},{5,4},{6,7},{7,6},{8,9},{9,8},{10,11... | collective-permute-start | bytes 1327112 | tf_op jit(solution)/shard_map/ppermute | solution.py:27
  86.4 3.1 collective-permute-start.12
  86.7 16.1 %collective-permute-start.13 = (bf16[384,768]{1,0:T(8,128)(2,1)S(1)}, bf16[384,768]{1,0:T(8,128)(2,1)S(1)}, u32[]{:S(2)}, u32[]{:S(2)}) collective-permute-start(bf16[384,768]{1,0:T(8,128)(2,1)S(1)} %constant_dynamic-slice_fusion.2), channel_id=1, source_target_pairs={{0,1},{1,0},{2,3},{3,2},{4,5},{5,4},{6,7},{7,6},{8,9},{9,8},{10,11... | collective-permute-start | bytes 1769480 | tf_op jit(solution)/shard_map/ppermute | solution.py:27
  90.6 12.2 %copy-start.77 = (bf16[2,4,2,96,768]{4,3,2,1,0:T(8,128)(2,1)}, bf16[2,4,2,96,768]{4,3,2,1,0:T(8,128)(2,1)S(1)}, u32[]{:S(2)}) copy-start(bf16[2,4,2,96,768]{4,3,2,1,0:T(8,128)(2,1)S(1)} %slice.188) | copy-start | bytes 7077892
  94.3 9.6 %copy-start.53 = (bf16[512,2304]{1,0:T(8,128)(2,1)}, bf16[512,2304]{1,0:T(8,128)(2,1)S(1)}, u32[]{:S(2)}) copy-start(bf16[512,2304]{1,0:T(8,128)(2,1)S(1)} %fusion.3.refs_3_) | copy-start | bytes 7077892
  102.7 9.7 %copy-start.82 = (bf16[384,768]{1,0:T(8,128)(2,1)}, bf16[384,768]{1,0:T(8,128)(2,1)S(1)}, u32[]{:S(2)}) copy-start(bf16[384,768]{1,0:T(8,128)(2,1)S(1)} %collective-permute-done.13) | copy-start | bytes 1769476
  103.8 8.6 %copy-start.43 = (bf16[384,1536]{1,0:T(8,128)(2,1)}, bf16[384,1536]{1,0:T(8,128)(2,1)S(1)}, u32[]{:S(2)}) copy-start(bf16[384,1536]{1,0:T(8,128)(2,1)S(1)} %fusion.6.refs_4_) | copy-start | bytes 3538948
  114.5 16.6 %copy-start.22 = (bf16[512,768]{1,0:T(8,128)(2,1)S(1)}, bf16[512,768]{1,0:T(8,128)(2,1)}, u32[]{:S(2)}) copy-start(bf16[512,768]{1,0:T(8,128)(2,1)} %refs_0_.5) | copy-start | bytes 2359300
  161.3 9.4 %collective-permute-start.15 = (bf16[4,4,4,24,768]{4,3,2,1,0:T(8,128)(2,1)}, bf16[4,4,4,24,768]{4,3,2,1,0:T(8,128)(2,1)}, u32[]{:S(2)}, u32[]{:S(2)}) collective-permute-start(bf16[4,4,4,24,768]{4,3,2,1,0:T(8,128)(2,1)} %get-tuple-element.175), channel_id=1, source_target_pairs={{0,4},{4,0},{8,12},{12,8},{16,20},{20,16},{24,28},{28,24},{1,5},{5... | collective-permute-start | bytes 7077896 | tf_op jit(solution)/shard_map/ppermute | solution.py:27
  162.9 7.8 %collective-permute-start.14 = (bf16[4,4,4,24,768]{4,3,2,1,0:T(8,128)(2,1)S(1)}, bf16[4,4,4,24,768]{4,3,2,1,0:T(8,128)(2,1)}, u32[]{:S(2)}, u32[]{:S(2)}) collective-permute-start(bf16[4,4,4,24,768]{4,3,2,1,0:T(8,128)(2,1)S(1)} %get-tuple-element.174), channel_id=1, source_target_pairs={{0,4},{4,0},{8,12},{12,8},{16,20},{20,16},{24,28},{28,24},{1,5},{5... | collective-permute-start | bytes 7077896 | tf_op jit(solution)/shard_map/ppermute | solution.py:27
  177.1 40.0 %collective-permute-start.17 = (bf16[8,2,4,24,768]{4,3,2,1,0:T(8,128)(2,1)}, bf16[8,2,4,24,768]{4,3,2,1,0:T(8,128)(2,1)}, u32[]{:S(2)}, u32[]{:S(2)}) collective-permute-start(bf16[8,2,4,24,768]{4,3,2,1,0:T(8,128)(2,1)} %get-tuple-element.185), channel_id=1, source_target_pairs={{0,8},{4,20},{8,0},{12,28},{16,24},{20,4},{24,16},{28,12},{1,9},{5... | collective-permute-start | bytes 7077896 | tf_op jit(solution)/shard_map/ppermute | solution.py:867
  178.3 22.3 %copy-start.78 = (bf16[2,4,2,96,768]{4,3,2,1,0:T(8,128)(2,1)S(1)}, bf16[2,4,2,96,768]{4,3,2,1,0:T(8,128)(2,1)}, u32[]{:S(2)}) copy-start(bf16[2,4,2,96,768]{4,3,2,1,0:T(8,128)(2,1)} %copy-done.77) | copy-start | bytes 7077892
  202.5 13.3 %collective-permute-start.16 = (bf16[384,768]{1,0:T(8,128)(2,1)}, bf16[384,768]{1,0:T(8,128)(2,1)}, u32[]{:S(2)}, u32[]{:S(2)}) collective-permute-start(bf16[384,768]{1,0:T(8,128)(2,1)} %convolution_convert_fusion.1.refs_8_), channel_id=1, source_target_pairs={{0,1},{1,0},{2,3},{3,2},{4,5},{5,4},{6,7},{7,6},{8,9},{9,8},{10,11... | collective-permute-start | bytes 1769480 | tf_op jit(solution)/shard_map/ppermute | solution.py:27
  210.1 36.3 %collective-permute-start.19 = (bf16[49,8,3072]{2,1,0:T(8,128)(2,1)}, bf16[49,8,3072]{2,1,0:T(8,128)(2,1)}, u32[]{:S(2)}, u32[]{:S(2)}) collective-permute-start(bf16[49,8,3072]{2,1,0:T(8,128)(2,1)} %get-tuple-element.201), channel_id=1, source_target_pairs={{0,4},{4,0},{8,12},{12,8},{16,20},{20,16},{24,28},{28,24},{1,5},{5... | collective-permute-start | bytes 7225352 | tf_op jit(solution)/shard_map/ppermute | solution.py:27
  215.8 9.2 %copy-start.48 = (bf16[512,2304]{1,0:T(8,128)(2,1)S(1)}, bf16[512,2304]{1,0:T(8,128)(2,1)}, u32[]{:S(2)}) copy-start(bf16[512,2304]{1,0:T(8,128)(2,1)} %copy-done.47) | copy-start | bytes 7077892
  217.1 8.0 %copy-start.9 = (bf16[3,4,2,96,768]{4,3,2,1,0:T(8,128)(2,1)S(1)}, bf16[3,4,2,96,768]{4,3,2,1,0:T(8,128)(2,1)}, u32[]{:S(2)}) copy-start(bf16[3,4,2,96,768]{4,3,2,1,0:T(8,128)(2,1)} %copy-done.8) | copy-start | bytes 10616836
  219.5 30.5 %collective-permute-start.18 = (bf16[4,2,4,24,768]{4,3,2,1,0:T(8,128)(2,1)S(1)}, bf16[4,2,4,24,768]{4,3,2,1,0:T(8,128)(2,1)S(1)}, u32[]{:S(2)}, u32[]{:S(2)}) collective-permute-start(bf16[4,2,4,24,768]{4,3,2,1,0:T(8,128)(2,1)S(1)} %get-tuple-element.199), channel_id=1, source_target_pairs={{0,16},{4,12},{8,24},{12,4},{16,0},{20,28},{24,8},{28,20},{1,17},{... | collective-permute-start | bytes 3538952 | tf_op jit(solution)/shard_map/ppermute | solution.py:867
  228.6 17.9 %copy-start.1 = (bf16[49,8,3072]{2,1,0:T(8,128)(2,1)S(1)}, bf16[49,8,3072]{2,1,0:T(8,128)(2,1)}, u32[]{:S(2)}) copy-start(bf16[49,8,3072]{2,1,0:T(8,128)(2,1)} %get-tuple-element.200.refs_1_) | copy-start | bytes 7225348
  264.5 21.1 %collective-permute-start.21 = (bf16[4,4,4,24,768]{4,3,2,1,0:T(8,128)(2,1)}, bf16[4,4,4,24,768]{4,3,2,1,0:T(8,128)(2,1)}, u32[]{:S(2)}, u32[]{:S(2)}) collective-permute-start(bf16[4,4,4,24,768]{4,3,2,1,0:T(8,128)(2,1)} %get-tuple-element.211), channel_id=1, source_target_pairs={{0,4},{4,0},{8,12},{12,8},{16,20},{20,16},{24,28},{28,24},{1,5},{5... | collective-permute-start | bytes 7077896 | tf_op jit(solution)/shard_map/ppermute | solution.py:27
  266.3 19.4 %collective-permute-start.20 = (bf16[4,4,4,24,768]{4,3,2,1,0:T(8,128)(2,1)S(1)}, bf16[4,4,4,24,768]{4,3,2,1,0:T(8,128)(2,1)}, u32[]{:S(2)}, u32[]{:S(2)}) collective-permute-start(bf16[4,4,4,24,768]{4,3,2,1,0:T(8,128)(2,1)S(1)} %get-tuple-element.210), channel_id=1, source_target_pairs={{0,4},{4,0},{8,12},{12,8},{16,20},{20,16},{24,28},{28,24},{1,5},{5... | collective-permute-start | bytes 7077896 | tf_op jit(solution)/shard_map/ppermute | solution.py:27
  266.3 16.4 %collective-permute-start.22 = (bf16[2,2,4,24,768]{4,3,2,1,0:T(8,128)(2,1)}, bf16[2,2,4,24,768]{4,3,2,1,0:T(8,128)(2,1)}, u32[]{:S(2)}, u32[]{:S(2)}) collective-permute-start(bf16[2,2,4,24,768]{4,3,2,1,0:T(8,128)(2,1)} %get-tuple-element.213), channel_id=1, source_target_pairs={{0,1},{1,0},{2,3},{3,2},{4,5},{5,4},{6,7},{7,6},{8,9},{9,8},{10,11... | collective-permute-start | bytes 1769480 | tf_op jit(solution)/shard_map/ppermute | solution.py:867
  268.5 46.5 %collective-permute-start.24 = (bf16[25,8,3072]{2,1,0:T(8,128)(2,1)}, bf16[25,8,3072]{2,1,0:T(8,128)(2,1)S(1)}, u32[]{:S(2)}, u32[]{:S(2)}) collective-permute-start(bf16[25,8,3072]{2,1,0:T(8,128)(2,1)} %copy-done.17), channel_id=1, source_target_pairs={{0,8},{4,20},{8,0},{12,28},{16,24},{20,4},{24,16},{28,12},{1,9},{5... | collective-permute-start | bytes 3686408 | tf_op jit(solution)/shard_map/ppermute | solution.py:867
  290.7 38.3 %collective-permute-start.27 = (bf16[8,2,4,24,768]{4,3,2,1,0:T(8,128)(2,1)S(1)}, bf16[8,2,4,24,768]{4,3,2,1,0:T(8,128)(2,1)}, u32[]{:S(2)}, u32[]{:S(2)}) collective-permute-start(bf16[8,2,4,24,768]{4,3,2,1,0:T(8,128)(2,1)S(1)} %get-tuple-element.234), channel_id=1, source_target_pairs={{0,8},{4,20},{8,0},{12,28},{16,24},{20,4},{24,16},{28,12},{1,9},{5... | collective-permute-start | bytes 7077896 | tf_op jit(solution)/shard_map/ppermute | solution.py:867
  291.5 22.4 %copy-start.76 = (bf16[2,4,8,24,768]{4,3,2,1,0:T(8,128)(2,1)S(1)}, bf16[2,4,8,24,768]{4,3,2,1,0:T(8,128)(2,1)}, u32[]{:S(2)}) copy-start(bf16[2,4,8,24,768]{4,3,2,1,0:T(8,128)(2,1)} %copy-done.75) | copy-start | bytes 7077892
  314.9 9.8 %copy-start.23 = (bf16[384,768]{1,0:T(8,128)(2,1)}, bf16[384,768]{1,0:T(8,128)(2,1)S(1)}, u32[]{:S(2)}) copy-start(bf16[384,768]{1,0:T(8,128)(2,1)S(1)} %convolution_convert_fusion.refs_8_) | copy-start | bytes 1769476
  324.8 22.7 %collective-permute-start.25 = (bf16[49,8,3072]{2,1,0:T(8,128)(2,1)}, bf16[49,8,3072]{2,1,0:T(8,128)(2,1)}, u32[]{:S(2)}, u32[]{:S(2)}) collective-permute-start(bf16[49,8,3072]{2,1,0:T(8,128)(2,1)} %get-tuple-element.230), channel_id=1, source_target_pairs={{0,4},{4,0},{8,12},{12,8},{16,20},{20,16},{24,28},{28,24},{1,5},{5... | collective-permute-start | bytes 7225352 | tf_op jit(solution)/shard_map/ppermute | solution.py:27
  329.0 13.3 %collective-permute-start.26 = (bf16[13,8,3072]{2,1,0:T(8,128)(2,1)S(1)}, bf16[13,8,3072]{2,1,0:T(8,128)(2,1)}, u32[]{:S(2)}, u32[]{:S(2)}) collective-permute-start(bf16[13,8,3072]{2,1,0:T(8,128)(2,1)S(1)} %get-tuple-element.232), channel_id=1, source_target_pairs={{0,16},{4,12},{8,24},{12,4},{16,0},{20,28},{24,8},{28,20},{1,17},{... | collective-permute-start | bytes 1916936 | tf_op jit(solution)/shard_map/ppermute | solution.py:867
  333.1 14.4 %copy-start = (bf16[49,8,3072]{2,1,0:T(8,128)(2,1)S(1)}, bf16[49,8,3072]{2,1,0:T(8,128)(2,1)}, u32[]{:S(2)}) copy-start(bf16[49,8,3072]{2,1,0:T(8,128)(2,1)} %get-tuple-element.229.refs_1_) | copy-start | bytes 7225348
  333.1 32.5 %collective-permute-start.29 = (bf16[4,2,4,24,768]{4,3,2,1,0:T(8,128)(2,1)}, bf16[4,2,4,24,768]{4,3,2,1,0:T(8,128)(2,1)}, u32[]{:S(2)}, u32[]{:S(2)}) collective-permute-start(bf16[4,2,4,24,768]{4,3,2,1,0:T(8,128)(2,1)} %get-tuple-element.241), channel_id=1, source_target_pairs={{0,16},{4,12},{8,24},{12,4},{16,0},{20,28},{24,8},{28,20},{1,17},{... | collective-permute-start | bytes 3538952 | tf_op jit(solution)/shard_map/ppermute | solution.py:867
  335.1 21.3 %collective-permute-start.37 = (bf16[1,2,4,24,768]{4,3,2,1,0:T(8,128)(2,1)}, bf16[1,2,4,24,768]{4,3,2,1,0:T(8,128)(2,1)}, u32[]{:S(2)}, u32[]{:S(2)}) collective-permute-start(bf16[1,2,4,24,768]{4,3,2,1,0:T(8,128)(2,1)} %get-tuple-element.263), channel_id=1, source_target_pairs={{0,2},{1,3},{2,0},{3,1},{4,6},{5,7},{6,4},{7,5},{8,10},{9,11},{10,... | collective-permute-start | bytes 884744 | tf_op jit(solution)/shard_map/ppermute | solution.py:867
  345.5 17.8 %collective-permute-start.30 = (bf16[204,8,128]{2,1,0:T(8,128)(2,1)}, bf16[204,8,128]{2,1,0:T(8,128)(2,1)}, u32[]{:S(2)}, u32[]{:S(2)}) collective-permute-start(bf16[204,8,128]{2,1,0:T(8,128)(2,1)} %get-tuple-element.243), channel_id=1, source_target_pairs={{0,1},{1,0},{2,3},{3,2},{4,5},{5,4},{6,7},{7,6},{8,9},{9,8},{10,11... | collective-permute-start | bytes 1253384 | tf_op jit(solution)/shard_map/ppermute | solution.py:867
  351.6 28.1 %collective-permute-start.28 = (bf16[25,8,3072]{2,1,0:T(8,128)(2,1)}, bf16[25,8,3072]{2,1,0:T(8,128)(2,1)S(1)}, u32[]{:S(2)}, u32[]{:S(2)}) collective-permute-start(bf16[25,8,3072]{2,1,0:T(8,128)(2,1)} %get-tuple-element.239), channel_id=1, source_target_pairs={{0,8},{4,20},{8,0},{12,28},{16,24},{20,4},{24,16},{28,12},{1,9},{5... | collective-permute-start | bytes 3686408 | tf_op jit(solution)/shard_map/ppermute | solution.py:867
  357.4 8.2 %copy-start.21 = (bf16[4,2,4,24,768]{4,3,2,1,0:T(8,128)(2,1)S(1)}, bf16[4,2,4,24,768]{4,3,2,1,0:T(8,128)(2,1)}, u32[]{:S(2)}) copy-start(bf16[4,2,4,24,768]{4,3,2,1,0:T(8,128)(2,1)} %copy-done.20) | copy-start | bytes 3538948
  359.2 16.7 %collective-permute-start.23 = (bf16[384,768]{1,0:T(8,128)(2,1)S(1)}, bf16[384,768]{1,0:T(8,128)(2,1)S(1)}, u32[]{:S(2)}, u32[]{:S(2)}) collective-permute-start(bf16[384,768]{1,0:T(8,128)(2,1)S(1)} %copy-done.24), channel_id=1, source_target_pairs={{0,1},{1,0},{2,3},{3,2},{4,5},{5,4},{6,7},{7,6},{8,9},{9,8},{10,11... | collective-permute-start | bytes 1769480 | tf_op jit(solution)/shard_map/ppermute | solution.py:27
  367.7 11.9 %copy-start.19 = (bf16[25,8,3072]{2,1,0:T(8,128)(2,1)S(1)}, bf16[25,8,3072]{2,1,0:T(8,128)(2,1)}, u32[]{:S(2)}) copy-start(bf16[25,8,3072]{2,1,0:T(8,128)(2,1)} %copy-done.18) | copy-start | bytes 3686404
  367.8 24.6 %collective-permute-start.32 = (bf16[2,2,4,24,768]{4,3,2,1,0:T(8,128)(2,1)S(1)}, bf16[2,2,4,24,768]{4,3,2,1,0:T(8,128)(2,1)S(1)}, u32[]{:S(2)}, u32[]{:S(2)}) collective-permute-start(bf16[2,2,4,24,768]{4,3,2,1,0:T(8,128)(2,1)S(1)} %get-tuple-element.250), channel_id=1, source_target_pairs={{0,1},{1,0},{2,3},{3,2},{4,5},{5,4},{6,7},{7,6},{8,9},{9,8},{10,11... | collective-permute-start | bytes 1769480 | tf_op jit(solution)/shard_map/ppermute | solution.py:867
  376.0 21.4 %collective-permute-start.35 = (bf16[108,8,128]{2,1,0:T(8,128)(2,1)S(1)}, bf16[108,8,128]{2,1,0:T(8,128)(2,1)S(1)}, u32[]{:S(2)}, u32[]{:S(2)}) collective-permute-start(bf16[108,8,128]{2,1,0:T(8,128)(2,1)S(1)} %get-tuple-element.259), channel_id=1, source_target_pairs={{0,2},{1,3},{2,0},{3,1},{4,6},{5,7},{6,4},{7,5},{8,10},{9,11},{10,... | collective-permute-start | bytes 663560 | tf_op jit(solution)/shard_map/ppermute | solution.py:867
  380.5 20.1 %collective-permute-start.31 = (bf16[13,8,3072]{2,1,0:T(8,128)(2,1)S(1)}, bf16[13,8,3072]{2,1,0:T(8,128)(2,1)S(1)}, u32[]{:S(2)}, u32[]{:S(2)}) collective-permute-start(bf16[13,8,3072]{2,1,0:T(8,128)(2,1)S(1)} %get-tuple-element.248), channel_id=1, source_target_pairs={{0,16},{4,12},{8,24},{12,4},{16,0},{20,28},{24,8},{28,20},{1,17},{... | collective-permute-start | bytes 1916936 | tf_op jit(solution)/shard_map/ppermute | solution.py:867
  393.1 17.8 %collective-permute-start.36 = (bf16[1,2,4,24,768]{4,3,2,1,0:T(8,128)(2,1)S(1)}, bf16[1,2,4,24,768]{4,3,2,1,0:T(8,128)(2,1)}, u32[]{:S(2)}, u32[]{:S(2)}) collective-permute-start(bf16[1,2,4,24,768]{4,3,2,1,0:T(8,128)(2,1)S(1)} %get-tuple-element.261), channel_id=1, source_target_pairs={{0,2},{1,3},{2,0},{3,1},{4,6},{5,7},{6,4},{7,5},{8,10},{9,11},{10,... | collective-permute-start | bytes 884744 | tf_op jit(solution)/shard_map/ppermute | solution.py:867
  401.6 16.2 %collective-permute-start.33 = (bf16[204,8,128]{2,1,0:T(8,128)(2,1)S(1)}, bf16[204,8,128]{2,1,0:T(8,128)(2,1)S(1)}, u32[]{:S(2)}, u32[]{:S(2)}) collective-permute-start(bf16[204,8,128]{2,1,0:T(8,128)(2,1)S(1)} %get-tuple-element.254), channel_id=1, source_target_pairs={{0,1},{1,0},{2,3},{3,2},{4,5},{5,4},{6,7},{7,6},{8,9},{9,8},{10,11... | collective-permute-start | bytes 1253384 | tf_op jit(solution)/shard_map/ppermute | solution.py:867
  411.9 8.5 %copy-start.79 = (f32[1,24,3072]{2,1,0:T(8,128)S(1)}, f32[1,24,3072]{2,1,0:T(8,128)}, u32[]{:S(2)}) copy-start(f32[1,24,3072]{2,1,0:T(8,128)} %stack_reshape.23) | copy-start | bytes 884740
  412.0 9.3 %copy-start.81 = (f32[1,1,4,24,768]{4,3,2,1,0:T(8,128)S(1)}, f32[1,1,4,24,768]{4,3,2,1,0:T(8,128)}, u32[]{:S(2)}) copy-start(f32[1,1,4,24,768]{4,3,2,1,0:T(8,128)} %get-tuple-element.280) | copy-start | bytes 884740
  418.9 12.0 %collective-permute-start.34 = (bf16[108,8,128]{2,1,0:T(8,128)(2,1)S(1)}, bf16[108,8,128]{2,1,0:T(8,128)(2,1)S(1)}, u32[]{:S(2)}, u32[]{:S(2)}) collective-permute-start(bf16[108,8,128]{2,1,0:T(8,128)(2,1)S(1)} %get-tuple-element.257), channel_id=1, source_target_pairs={{0,2},{1,3},{2,0},{3,1},{4,6},{5,7},{6,4},{7,5},{8,10},{9,11},{10,... | collective-permute-start | bytes 663560 | tf_op jit(solution)/shard_map/ppermute | solution.py:867
  421.2 12.0 %copy-start.83 = (f32[1,24,768]{2,1,0:T(8,128)S(1)}, f32[1,24,768]{2,1,0:T(8,128)}, u32[]{:S(2)}) copy-start(f32[1,24,768]{2,1,0:T(8,128)} %stack_reshape.21) | copy-start | bytes 221188
  421.2 12.7 %copy-start.80 = (f32[3,192,96]{2,1,0:T(8,128)S(1)}, f32[3,192,96]{2,1,0:T(8,128)}, u32[]{:S(2)}) copy-start(f32[3,192,96]{2,1,0:T(8,128)} %slice.238) | copy-start | bytes 663556
  (68 other events, 188.2 us)

commit v4 on v3

--- a/solution.py
+++ b/solution.py
@@ -65,6 +65,26 @@
 
 def nn(left, right):
     return lax.dot_general(left, right, (((1,), (0,)), ((), ())), preferred_element_type=f32)
+
+
+def each_block(step, low, high):
+    def one(j, carry):
+        step(j, 1)
+        return carry
+
+    lax.fori_loop(low, high, one, 0)
+
+
+def all_blocks(step, low, high, most):
+    for count in range(1, most + 1):
+
+        @pl.when(high - low == count)
+        def _(count=count):
+            step(low, count)
+
+
+def beside(ref, j, count, rows):
+    return jnp.concatenate([ref[j + k, rows, :] for k in range(count)], axis=1)
 
 
 def attend_kernel(pairs, own_blocks, halo_blocks, bounds, segq, segk, qkv, kvh, ctx, ctx_t, ctx_low, lse, vt, qs, top, total, acc):
@@ -89,9 +109,9 @@
         acc[...] = jnp.zeros(acc.shape, f32)
         labels = segq[i]
 
-        def k_block(ref, first, base, j, carry):
-            here = pl.ds(pl.multiple_of(j * BLK, BLK), BLK)
-            there = pl.ds(pl.multiple_of((base + j) * BLK, BLK), BLK)
+        def k_block(ref, first, base, j, count):
+            here = pl.ds(pl.multiple_of(j * BLK, BLK), count * BLK)
+            there = pl.ds(pl.multiple_of((base + j) * BLK, BLK), count * BLK)
             same = segk[there, :] == labels
             for p in range(pairs):
                 keys = ref[here, first + p * BLK : first + (p + 1) * BLK]
@@ -104,14 +124,13 @@
                 total[p : p + 1, :] = total[p : p + 1, :] * scale + jnp.sum(expo, axis=0, keepdims=True)
                 weights = expo.astype(bf16)
                 for h in range(2):
-                    values = vt[base + j, p * BLK + h * half : p * BLK + (h + 1) * half, :]
+                    values = beside(vt, base + j, count, slice(p * BLK + h * half, p * BLK + (h + 1) * half))
                     part = slice(h * half, (h + 1) * half)
                     cols = slice(h * BLK, (h + 1) * BLK)
                     acc[p, part, :] = acc[p, part, :] * scale[:, cols] + nn(values, weights[:, cols])
-            return carry
-
-        lax.fori_loop(bounds[i, 0], bounds[i, 1], functools.partial(k_block, qkv, width, 0), 0)
-        lax.fori_loop(bounds[i, 2], bounds[i, 3], functools.partial(k_block, kvh, 0, own_blocks), 0)
+
+        each_block(functools.partial(k_block, qkv, width, 0), bounds[i, 0], bounds[i, 1])
+        each_block(functools.partial(k_block, kvh, 0, own_blocks), bounds[i, 2], bounds[i, 3])
         for p in range(pairs):
             inverse = 1.0 / total[p : p + 1, :]
             flat = jnp.concatenate(
@@ -159,16 +178,16 @@
             qs[p] = stack_heads(qkv[rows, cols], low)
             pull = dctx[rows, cols]
             cs[p] = stack_heads(pull, low)
-            prod = pull.astype(f32).T * ctx_t[cols, rows]
+            prod = pull.T.astype(f32) * ctx_t[cols, rows]
             delta[p : p + 1, :] = jnp.concatenate(
                 [jnp.sum(prod[:half], axis=0, keepdims=True), jnp.sum(prod[half:], axis=0, keepdims=True)], axis=1
             )
         dqt[...] = jnp.zeros(dqt.shape, f32)
         labels = segq[i]
 
-        def k_block(ref, first, base, j, carry):
-            here = pl.ds(pl.multiple_of(j * BLK, BLK), BLK)
-            there = pl.ds(pl.multiple_of((base + j) * BLK, BLK), BLK)
+        def k_block(ref, first, base, j, count):
+            here = pl.ds(pl.multiple_of(j * BLK, BLK), count * BLK)
+            there = pl.ds(pl.multiple_of((base + j) * BLK, BLK), count * BLK)
             same = segk[there, :] == labels
             for p in range(pairs):
                 cols = slice(p * BLK, (p + 1) * BLK)
@@ -182,15 +201,14 @@
                 dk[there, cols] += nn(dscore, qs[p])
                 for h in range(2):
                     part = slice(h * half, (h + 1) * half)
-                    flip = kt[base + j, p * BLK + h * half : p * BLK + (h + 1) * half, :]
+                    flip = beside(kt, base + j, count, slice(p * BLK + h * half, p * BLK + (h + 1) * half))
                     dqt[p, part, :] += nn(flip, dscore[:, h * BLK : (h + 1) * BLK])
-            return carry
-
-        lax.fori_loop(bounds[i, 0], bounds[i, 1], functools.partial(k_block, qkv, width, 0), 0)
-        lax.fori_loop(bounds[i, 2], bounds[i, 3], functools.partial(k_block, kvh, 0, own_blocks), 0)
+
+        all_blocks(functools.partial(k_block, qkv, width, 0), bounds[i, 0], bounds[i, 1], own_blocks)
+        all_blocks(functools.partial(k_block, kvh, 0, own_blocks), bounds[i, 2], bounds[i, 3], halo_blocks)
         for p in range(pairs):
             cols = slice(p * BLK, (p + 1) * BLK)
-            grad = dqt[p].T.astype(bf16) * jnp.asarray(0.125, bf16)
+            grad = dqt[p].astype(bf16).T * jnp.asarray(0.125, bf16)
             dqkv[rows, cols] = grad
             sums[6:7, cols] += jnp.sum(grad.astype(f32), axis=0, keepdims=True)
         return carry
@@ -274,7 +292,7 @@
             pltpu.VMEM((8, 2 * BLK), f32),
             pltpu.VMEM((pairs, BLK, BLK), f32),
         ],
-        compiler_params=pltpu.CompilerParams(vmem_limit_bytes=32 * 2**20),
+        compiler_params=pltpu.CompilerParams(vmem_limit_bytes=16 * 2**20),
         cost_estimate=cost(9),
         name="attend",
     )
@@ -306,7 +324,7 @@
             pltpu.VMEM((blocks * BLK, width), f32),
             pltpu.VMEM((blocks * BLK, width), f32),
         ],
-        compiler_params=pltpu.CompilerParams(vmem_limit_bytes=40 * 2**20),
+        compiler_params=pltpu.CompilerParams(vmem_limit_bytes=24 * 2**20),
         cost_estimate=cost(21),
         name="attend_back",
     )
@@ -571,7 +589,7 @@
         in_specs=[pl.BlockSpec(memory_space=pltpu.SMEM)] + vmem_specs(2),
         out_specs=tuple(vmem_specs(2)),
         scratch_shapes=[pltpu.VMEM((rows // 2, tokens), bf16)] if scratch else [],
-        compiler_params=pltpu.CompilerParams(vmem_limit_bytes=48 * 2**20),
+        compiler_params=pltpu.CompilerParams(vmem_limit_bytes=18 * 2**20),
         cost_estimate=cost(5),
         name="grad_up" if scratch else "grad_down",
     )
@@ -640,7 +658,7 @@
             pltpu.VMEM((width // 2, tokens), bf16),
             pltpu.VMEM((width // 2, extent), bf16),
         ],
-        compiler_params=pltpu.CompilerParams(vmem_limit_bytes=48 * 2**20),
+        compiler_params=pltpu.CompilerParams(vmem_limit_bytes=20 * 2**20),
         cost_estimate=cost(8),
         name="grad_heads",
     )
@@ -671,7 +689,7 @@
         out_shape=(jax.ShapeDtypeStruct((own.shape[0], head) + own.shape[1:], bf16),),
         in_specs=[pl.BlockSpec(memory_space=pltpu.SMEM)] + vmem_specs(1 + len(refs)),
         out_specs=vmem_specs(1),
-        compiler_params=pltpu.CompilerParams(vmem_limit_bytes=32 * 2**20),
+        compiler_params=pltpu.CompilerParams(vmem_limit_bytes=16 * 2**20),
         cost_estimate=cost(1.5),
         name="assemble",
     )
@@ -686,22 +704,38 @@
     return value, relative
 
 
-def flip_kernel(count, *refs):
-    for source, target in zip(refs[:count], refs[count:]):
+def flip_kernel(count, shard, biases, *refs):
+    for source, target in zip(refs[:count], refs[count : 2 * count]):
         for at in range(0, source.shape[0], BLK):
             target[:, at : at + BLK] = source[at : at + BLK, :].T
-
-
-def flip(values, passes):
+    shifts = refs[2 * count]
+    members, _, width = biases.shape
+    layers, part = shifts.shape[0], width // members
+    shifts[...] = jnp.zeros(shifts.shape, f32)
+    rows = [biases[step].astype(f32) for step in range(members)]
+    for member in range(members):
+        value = jnp.zeros((1, width), f32)
+        for step, row in enumerate(rows):
+            value = jnp.where((shard[0] ^ step) == member, row, value)
+        for layer_idx in range(layers):
+            for at, kind in ((0, 0), (1, 2)):
+                here = (2 * layer_idx + at) * part
+                there = kind * width + member * part
+                shifts[layer_idx, :, there : there + part] = value[:, here : here + part]
+
+
+def flip(values, shard, biases, layers):
+    width = biases.shape[2]
+    shapes = [jax.ShapeDtypeStruct(v.shape[::-1], v.dtype) for v in values]
     return ordered_call(
         functools.partial(flip_kernel, len(values)),
-        values,
+        (shard, biases, *values),
         (),
-        passes,
-        out_shape=[jax.ShapeDtypeStruct(v.shape[::-1], v.dtype) for v in values],
-        in_specs=vmem_specs(len(values)),
-        out_specs=vmem_specs(len(values)),
-        compiler_params=pltpu.CompilerParams(vmem_limit_bytes=32 * 2**20),
+        (),
+        out_shape=shapes + [jax.ShapeDtypeStruct((layers, 1, 3 * width), f32)],
+        in_specs=[pl.BlockSpec(memory_space=pltpu.SMEM)] + vmem_specs(1 + len(values)),
+        out_specs=vmem_specs(1 + len(values)),
+        compiler_params=pltpu.CompilerParams(vmem_limit_bytes=8 * 2**20),
         cost_estimate=cost(1.5),
         name="flip",
     )
@@ -722,7 +756,7 @@
         out_shape=(jax.ShapeDtypeStruct((len(values),) + values[0].shape, values[0].dtype),),
         in_specs=vmem_specs(len(values)),
         out_specs=vmem_specs(1),
-        compiler_params=pltpu.CompilerParams(vmem_limit_bytes=32 * 2**20),
+        compiler_params=pltpu.CompilerParams(vmem_limit_bytes=8 * 2**20),
         cost_estimate=cost(1.4),
         name="collect",
     )
@@ -860,7 +894,7 @@
             out_shape=[out] * 2,
             in_specs=[pl.BlockSpec(memory_space=pltpu.SMEM)] + vmem_specs(2 * sources),
             out_specs=vmem_specs(2),
-            compiler_params=pltpu.CompilerParams(vmem_limit_bytes=48 * 2**20),
+            compiler_params=pltpu.CompilerParams(vmem_limit_bytes=20 * 2**20),
             cost_estimate=cost(1 + 2e-6 * out.size),
             name="advance",
         )
@@ -916,11 +950,7 @@
     piece = jnp.concatenate([piece, bias_own])
     got = from_heads(piece)
     halo = swap(lax.dynamic_slice_in_dim(tokens_in, edge, HALO), "head", 1)
-    biases = jnp.stack([other[rows_w, : layers * 2 * part] for other in [piece] + got])
-    biases = biases.reshape(head, layers * 2, 1, part).astype(f32)
-    members = jnp.arange(head)
-    matches = (members[:, None] ^ shard) == members[None, :]
-    bias_all = jnp.sum(jnp.where(matches[:, None, :, None], biases, 0.0), axis=0).reshape(layers, 2, -1)
+    biases = jnp.stack([other[rows_w : rows_w + 1] for other in [piece] + got])
     got = jnp.stack([other[:rows_w] for other in got]).reshape(head - 1, 3, part // dp, width)
     left, relative_left = grow(got[..., : width // 2], upper)
     right, relative_right = grow(got[..., width // 2 :], upper[::-1])
@@ -929,7 +959,7 @@
     relative = [order + [other ^ 1 for other in order] for order in (relative_left, relative_right)]
     place = jnp.stack([shard, group]).astype(jnp.int32)
     own_later = [own_w[k].reshape(3, 2, part // 2, width) for k in range(1, layers)]
-    (low_t, halo_t), _ = flip([tokens_in, halo], [])
+    (low_t, halo_t, shifts), _ = flip([tokens_in, halo], shard.reshape(1).astype(jnp.int32), biases, layers)
     w_first, pieces = assemble(relative, place, own_first, [both[0], both[1]], [pick(own, core, 1) for own in own_later])
     later_got = [from_heads_in_turn(value) for value in pieces]
     w_cats = [w_first.reshape(3 * head * part, width)]
@@ -973,12 +1003,10 @@
     for layer_idx in range(layers):
         last = layer_idx == layers - 1
         w_cat = w_cats[layer_idx]
-        zero = jnp.zeros((width,), f32)
-        bias_q, bias_v = bias_all[layer_idx, 0], bias_all[layer_idx, 1]
-        shift = jnp.concatenate([bias_q, zero, bias_v])
-        factor = jnp.concatenate([zero + 0.125, zero + 1.0, zero + 1.0])
+        shift = shifts[layer_idx]
+        factor = jnp.where(jnp.arange(3 * width) < width, 0.125, 1.0).astype(f32)
         qkv = ((nt(low, w_cat) + shift) * factor).astype(bf16)
-        kvh = (nt(halo, w_cat[width:]) + shift[width:]).astype(bf16)
+        kvh = (nt(halo, w_cat[width:]) + shift[:, width:]).astype(bf16)
         (ctx, ctx_t, ctx_low, lse), _ = attend(bounds, segq, segk, qkv, kvh, (), ())
         fed, _ = feed(
             last, layer_idx, hidden, ctx, w_out, vecs[layer_idx], w_up, up_bias_wide[layer_idx : layer_idx + 1], w_down, (), ()

time: 440 us -> 401 us (0.911)
  starting transfers between devices: 63.9 us -> 33.7 us
  Pallas kernels: 191 us -> 171 us
  waiting for transfers between devices: 92.9 us -> 107 us
    pallas_call x34, Pallas kernels: 191 us -> 171 us  [ordered_call(): pl.pallas_call(body, out_shape=tuple(out_shape) + (jax.ShapeDtypeStruct((...]
    ppermute x16, starting transfers between devices: 34.2 us -> 15.5 us  [step(): self.keeps, self.gots = ([keep], [lax.ppermute(send, axis_name, pairs)])]
    ppermute x22, starting transfers between devices: 29.6 us -> 18.3 us  [swap(): return lax.ppermute(value, axis, [(i, i ^ bit) for i in range(size)])]
    ppermute x16, waiting for transfers between devices: 52.5 us -> 62.9 us  [step(): self.keeps, self.gots = ([keep], [lax.ppermute(send, axis_name, pairs)])]
    unnamed x192 -> x208, local copies, waits for them, and re-layouts: 34.1 us -> 32.9 us
  transfers between devices with their start and end apart: 38 -> 38, of which waited for: 18 -> 21; matrix products, arithmetic and copies ran while one was open for 10% -> 11% of each run, Pallas kernels for 28% -> 28%
where the time goes in v4:
time: 401 us; the launch traced here: 396 us
  Pallas kernels  171 us (43%)
  waiting for transfers between devices  107 us (27%)
  local copies, waits for them, and re-layouts  52.4 us (13%)
  starting transfers between devices  33.7 us (8%)
  matrix products  16.5 us (4%)
  other arithmetic  13.7 us (3%)
    pallas_call x34, Pallas kernels, ordered_call(): pl.pallas_call(body, out_shape=tuple(out_shape) + (jax.ShapeDtypeStruct((...  171 us
    ppermute x16, waiting for transfers between devices, step(): self.keeps, self.gots = ([keep], [lax.ppermute(send, axis_name, pairs)])  62.9 us
    ppermute x22, waiting for transfers between devices, swap(): return lax.ppermute(value, axis, [(i, i ^ bit) for i in range(size)])  44 us
    unnamed x208, local copies, waits for them, and re-layouts  32.9 us
    ppermute x22, starting transfers between devices, swap(): return lax.ppermute(value, axis, [(i, i ^ bit) for i in range(size)])  18.3 us
    ppermute x16, starting transfers between devices, step(): self.keeps, self.gots = ([keep], [lax.ppermute(send, axis_name, pairs)])  15.5 us
    dot_general x4, matrix products, nn(): lax.dot_general(left, right, (((1,), (0,)), ((), ())), preferred_element_...  8.66 us
  transfers between devices with their start and end apart: 38, of which 21 were waited for; matrix products, arithmetic and copies ran while one was open for 11% of the time, Pallas kernels for 28%

profile of v4, /device:TPU:0, one launch (start us, length us, event | category | flops | bytes accessed | tf_op | source)
XLA Modules:
  0.0 396.2 jit_solution(391907674688350064)
XLA Ops:
  0.7 1.6 fusion.17
  2.5 3.1 collective-permute-start
  5.5 2.6 collective-permute-start.1
  13.7 4.1 %collective-permute-done.1 = bf16[80,768]{1,0:T(8,128)(2,1)S(1)} collective-permute-done((bf16[80,768]{1,0:T(8,128)(2,1)S(1)}, bf16[80,768]{1,0:T(8,128)(2,1)S(1)}, u32[]{:S(2)}, u32[]{:S(2)}) %collective-permute-start.1) | collective-permute-done | bytes 122912 | tf_op jit(solution)/shard_map/ppermute | solution.py:27
  22.3 2.3 collective-permute-done.3
  24.7 1.6 collective-permute-start.4
  26.3 1.6 collective-permute-done.5
  28.9 3.4 collective-permute-done.4
  33.4 1.7 collective-permute-done.6
  45.5 1.6 pad_maximum_fusion
  48.3 1.8 collective-permute-start.10
  52.1 2.0 fusion.4.refs_3_
  54.1 2.6 fusion.2.refs_4_
  56.8 10.4 %attend.2 = (bf16[512,768]{1,0:T(8,128)(2,1)S(1)}, f32[768,512]{1,0:T(8,128)S(1)}, bf16[768,512]{1,0:T(8,128)(2,1)S(1)}, f32[4,8,256]{2,1,0:T(8,128)S(1)}, f32[8,128]{1,0:T(8,128)S(1)}) custom-call(s32[4,4]{1,0:T(4,128)S(1)} %pad_add_fusion.2.refs_0_, s32[4,1,256]{2,1,0:T(1,128)S(1)} %reshape.377.refs_1_, s32[896,1]{1,0:T(8,128)S(1)} %reshape.407.refs_2_, ...), custom_call_target="tpu_custom_call" | custom-call | flops 5175000064 | bytes 1000 | tf_op jit(solution)/shard_map/attend/pallas_call | solution.py:249
  69.2 2.2 collective-permute-done.10.refs_1_
  71.4 14.4 %feed.2 = (f32[512,768]{1,0:T(8,128)S(1)}, bf16[768,512]{1,0:T(8,128)(2,1)S(1)}, bf16[3072,512]{1,0:T(8,128)(2,1)}, f32[512,3072]{1,0:T(8,128)}, f32[512,768]{1,...) custom-call(bf16[512,768]{1,0:T(8,128)(2,1)S(1)} %copy-done.12, ...), custom_call_target="tpu_custom_call" | custom-call | flops 8625000448 | bytes 1000 | tf_op jit(solution)/shard_map/feed/pallas_call | solution.py:249
  86.3 2.1 collective-permute-start.13
  90.2 1.6 copy-done.8
  91.8 2.0 fusion.1.refs_3_
  93.8 8.5 %collective-permute-done.13 = bf16[384,768]{1,0:T(8,128)(2,1)S(1)} collective-permute-done((bf16[384,768]{1,0:T(8,128)(2,1)S(1)}, bf16[384,768]{1,0:T(8,128)(2,1)S(1)}, u32[]{:S(2)}, u32[]{:S(2)}) %collective-permute-start.13) | collective-permute-done | bytes 589856 | tf_op jit(solution)/shard_map/ppermute | solution.py:27
  103.5 10.2 %attend.3 = (bf16[512,768]{1,0:T(8,128)(2,1)S(1)}, f32[768,512]{1,0:T(8,128)S(1)}, bf16[768,512]{1,0:T(8,128)(2,1)S(1)}, f32[4,8,256]{2,1,0:T(8,128)S(1)}, f32[8,128]{1,0:T(8,128)S(1)}) custom-call(s32[4,4]{1,0:T(4,128)S(1)} %pad_add_fusion.2.refs_0_, s32[4,1,256]{2,1,0:T(1,128)S(1)} %reshape.377.refs_1_, s32[896,1]{1,0:T(8,128)S(1)} %reshape.407.refs_2_, ...), custom_call_target="tpu_custom_call" | custom-call | flops 5175000064 | bytes 1000 | tf_op jit(solution)/shard_map/attend/pallas_call | solution.py:249
  116.4 14.2 %feed.3 = (f32[512,768]{1,0:T(8,128)S(1)}, bf16[768,512]{1,0:T(8,128)(2,1)S(1)}, bf16[3072,512]{1,0:T(8,128)(2,1)}, f32[512,3072]{1,0:T(8,128)}, f32[512,768]{1,...) custom-call(f32[512,768]{1,0:T(8,128)} %get-tuple-element.146.refs_0_, ...), custom_call_target="tpu_custom_call" | custom-call | flops 8625000448 | bytes 1000 | tf_op jit(solution)/shard_map/feed/pallas_call | solution.py:249
  133.0 16.0 %feed_back.2 = (bf16[512,768]{1,0:T(8,128)(2,1)S(1)}, bf16[512,3072]{1,0:T(8,128)(2,1)}, bf16[512,768]{1,0:T(8,128)(2,1)S(1)}, f32[512,768]{1,0:T(8,128)S(1)}, b...) custom-call(bf16[512,768]{1,0:T(8,128)(2,1)S(1)} %copy-done.20, ...), custom_call_target="tpu_custom_call" | custom-call | flops 9774999552 | bytes 1000 | tf_op jit(solution)/shard_map/feed_back/pallas_call | solution.py:249
  149.1 2.9 grad_down.2
  153.0 2.9 grad_up.2
  159.3 2.9 collective-permute-done.15
  162.2 3.4 collective-permute-done.14
  165.6 1.7 copy-done.5
  167.3 5.0 %advance.16 = (bf16[8,2,4,24,768]{4,3,2,1,0:T(8,128)(2,1)}, bf16[8,2,4,24,768]{4,3,2,1,0:T(8,128)(2,1)S(1)}, f32[8,128]{1,0:T(8,128)S(1)}) custom-call(s32[2]{0:T(128)S(1)} %pad_add_fusion.5.refs_0_, bf16[16,4,24,768]{3,2,1,0:T(8,128)(2,1)S(1)} %bitcast.157, bf16[16,4,24,768]{3,2,1,0:T(8,128)(2,1)S(1)} %bitcast.158, ...), custom_call_target="tpu_custom_call" | custom-call | flops 1931595264 | bytes 1000 | tf_op jit(solution)/shard_map/advance/pallas_call | solution.py:249
  175.1 16.1 %attend_back.2 = (bf16[512,2304]{1,0:T(8,128)(2,1)S(1)}, bf16[384,1536]{1,0:T(8,128)(2,1)S(1)}, f32[16,768]{1,0:T(8,128)S(1)}, f32[8,128]{1,0:T(8,128)S(1)}) custom-call(s32[4,4]{1,0:T(4,128)S(1)} %pad_add_fusion.2.refs_0_, s32[4,1,256]{2,1,0:T(1,128)S(1)} %reshape.377.refs_1_, s32[896,1]{1,0:T(8,128)S(1)} %reshape.407.refs_2_, ...), custom_call_target="tpu_custom_call" | custom-call | flops 12074999808 | bytes 1000 | tf_op jit(solution)/shard_map/attend_back/pallas_call | solution.py:249
  191.3 1.9 convolution_convert_fusion.1.refs_8_
  193.9 5.2 %grad_heads.2 = (bf16[49,8,3072]{2,1,0:T(8,128)(2,1)}, bf16[49,8,3072]{2,1,0:T(8,128)(2,1)S(1)}, f32[8,128]{1,0:T(8,128)S(1)}) custom-call(s32[1]{0:T(128)} %bitcast.36.refs_0_, bf16[8,96,512]{2,1,0:T(8,128)(2,1)S(1)} %bitcast.172, bf16[8,96,512]{2,1,0:T(8,128)(2,1)S(1)} %bitcast.171, bf16[8,96,384]{2,1,0:T(8,128)(2,1)S(1)} %bitcast.165, ...), custom_call_target="tpu_custom_call" | custom-call | flops 4600000000 | bytes 1000 | tf_op jit(solution)/shard_map/grad_heads/pallas_call | solution.py:249
  199.3 6.9 %collective-permute-done.16 = bf16[384,768]{1,0:T(8,128)(2,1)} collective-permute-done((bf16[384,768]{1,0:T(8,128)(2,1)}, bf16[384,768]{1,0:T(8,128)(2,1)}, u32[]{:S(2)}, u32[]{:S(2)}) %collective-permute-start.16) | collective-permute-done | bytes 589856 | tf_op jit(solution)/shard_map/ppermute | solution.py:27
  207.5 1.7 copy-done.1
  209.1 2.4 advance.17
  211.8 3.7 convert_add_fusion.1.refs_0_
  215.5 15.8 %feed_back.3 = (bf16[512,768]{1,0:T(8,128)(2,1)S(1)}, bf16[512,3072]{1,0:T(8,128)(2,1)}, bf16[512,768]{1,0:T(8,128)(2,1)S(1)}, f32[512,768]{1,0:T(8,128)S(1)}, b...) custom-call(f32[512,768]{1,0:T(8,128)S(1)} %convert_add_fusion.1.refs_0_, ...), custom_call_target="tpu_custom_call" | custom-call | flops 9774999552 | bytes 1000 | tf_op jit(solution)/shard_map/feed_back/pallas_call | solution.py:249
  231.4 3.4 advance.18
  235.9 2.0 copy-done.23
  237.9 2.8 grad_down.3
  240.7 2.9 grad_up.3
  245.5 2.3 collective-permute-start.22
  247.9 3.4 collective-permute-start.24
  251.3 10.7 %collective-permute-done.22.refs_2_ = bf16[2,2,4,24,768]{4,3,2,1,0:T(8,128)(2,1)} collective-permute-done((bf16[2,2,4,24,768]{4,3,2,1,0:T(8,128)(2,1)S(1)}, bf16[2,2,4,24,768]{4,3,2,1,0:T(8,128)(2,1)}, u32[]{:S(2)}, u32[]{:S(2)}) %collective-permute-start.22) | collective-permute-done | bytes 589856 | tf_op jit(solution)/shard_map/ppermute | solution.py:901
  263.0 1.9 advance.20
  264.9 3.6 advance.21
  268.6 2.9 collective-permute-start.27
  271.5 16.1 %attend_back.3 = (bf16[512,2304]{1,0:T(8,128)(2,1)S(1)}, bf16[384,1536]{1,0:T(8,128)(2,1)S(1)}, f32[16,768]{1,0:T(8,128)S(1)}, f32[8,128]{1,0:T(8,128)S(1)}) custom-call(s32[4,4]{1,0:T(4,128)S(1)} %pad_add_fusion.2.refs_0_, s32[4,1,256]{2,1,0:T(1,128)S(1)} %reshape.377.refs_1_, s32[896,1]{1,0:T(8,128)S(1)} %reshape.407.refs_2_, ...), custom_call_target="tpu_custom_call" | custom-call | flops 12074999808 | bytes 1000 | tf_op jit(solution)/shard_map/attend_back/pallas_call | solution.py:249
  291.6 5.2 %grad_heads.3 = (bf16[49,8,3072]{2,1,0:T(8,128)(2,1)}, bf16[49,8,3072]{2,1,0:T(8,128)(2,1)S(1)}, f32[8,128]{1,0:T(8,128)S(1)}) custom-call(s32[1]{0:T(128)} %bitcast.36.refs_0_, bf16[8,96,512]{2,1,0:T(8,128)(2,1)S(1)} %bitcast.169, bf16[8,96,512]{2,1,0:T(8,128)(2,1)S(1)} %bitcast.168, bf16[8,96,384]{2,1,0:T(8,128)(2,1)S(1)} %bitcast.174, ...), custom_call_target="tpu_custom_call" | custom-call | flops 4600000000 | bytes 1000 | tf_op jit(solution)/shard_map/grad_heads/pallas_call | solution.py:249
  298.3 1.8 advance.23
  302.5 2.9 collective-permute-start.37
  305.4 2.0 collective-permute-done.26.refs_2_
  308.4 2.2 advance.24
  310.6 3.2 advance.25
  315.4 2.8 collective-permute-done.37
  321.0 6.2 %collective-permute-done.30.refs_2_ = bf16[204,8,128]{2,1,0:T(8,128)(2,1)} collective-permute-done((bf16[204,8,128]{2,1,0:T(8,128)(2,1)}, bf16[204,8,128]{2,1,0:T(8,128)(2,1)}, u32[]{:S(2)}, u32[]{:S(2)}) %collective-permute-start.30) | collective-permute-done | bytes 417824 | tf_op jit(solution)/shard_map/ppermute | solution.py:901
  329.5 2.1 advance.27
  331.7 2.0 fusion.21
  333.7 6.0 %collective-permute-done.23 = bf16[384,768]{1,0:T(8,128)(2,1)S(1)} collective-permute-done((bf16[384,768]{1,0:T(8,128)(2,1)S(1)}, bf16[384,768]{1,0:T(8,128)(2,1)S(1)}, u32[]{:S(2)}, u32[]{:S(2)}) %collective-permute-start.23) | collective-permute-done | bytes 589856 | tf_op jit(solution)/shard_map/ppermute | solution.py:27
  342.6 14.4 %collective-permute-done.32.refs_2_ = bf16[2,2,4,24,768]{4,3,2,1,0:T(8,128)(2,1)S(1)} collective-permute-done((bf16[2,2,4,24,768]{4,3,2,1,0:T(8,128)(2,1)S(1)}, bf16[2,2,4,24,768]{4,3,2,1,0:T(8,128)(2,1)S(1)}, u32[]{:S(2)}, u32[]{:S(2)}) %collective-permute-start.32) | collective-permute-done | bytes 589856 | tf_op jit(solution)/shard_map/ppermute | solution.py:901
  359.4 1.7 slice.232
  362.4 10.7 %collective-permute-done.36 = bf16[1,2,4,24,768]{4,3,2,1,0:T(8,128)(2,1)} collective-permute-done((bf16[1,2,4,24,768]{4,3,2,1,0:T(8,128)(2,1)S(1)}, bf16[1,2,4,24,768]{4,3,2,1,0:T(8,128)(2,1)}, u32[]{:S(2)}, u32[]{:S(2)}) %collective-permute-start.36) | collective-permute-done | bytes 294944 | tf_op jit(solution)/shard_map/ppermute | solution.py:901
  374.4 5.4 %collective-permute-done.33.refs_2_ = bf16[204,8,128]{2,1,0:T(8,128)(2,1)S(1)} collective-permute-done((bf16[204,8,128]{2,1,0:T(8,128)(2,1)S(1)}, bf16[204,8,128]{2,1,0:T(8,128)(2,1)S(1)}, u32[]{:S(2)}, u32[]{:S(2)}) %collective-permute-start.33) | collective-permute-done | bytes 417824 | tf_op jit(solution)/shard_map/ppermute | solution.py:901
  382.6 9.4 %collective-permute-done.34 = bf16[108,8,128]{2,1,0:T(8,128)(2,1)S(1)} collective-permute-done((bf16[108,8,128]{2,1,0:T(8,128)(2,1)S(1)}, bf16[108,8,128]{2,1,0:T(8,128)(2,1)S(1)}, u32[]{:S(2)}, u32[]{:S(2)}) %collective-permute-start.34) | collective-permute-done | bytes 221216 | tf_op jit(solution)/shard_map/ppermute | solution.py:901
  (367 shorter events, 79.5 us)
Async XLA Ops:
  0.7 7.5 %copy-start.12 = (bf16[512,768]{1,0:T(8,128)(2,1)S(1)}, bf16[512,768]{1,0:T(8,128)(2,1)}, u32[]{:S(2)}) copy-start(bf16[512,768]{1,0:T(8,128)(2,1)} %refs_0_.2) | copy-start | bytes 2359300
  0.7 11.8 %copy-start.93 = (bf16[2,3072]{1,0:T(2,128)(2,1)S(1)}, bf16[2,3072]{1,0:T(2,128)(2,1)}, u32[]{:S(2)}) copy-start(bf16[2,3072]{1,0:T(2,128)(2,1)} %param.24) | copy-start | bytes 36868
  2.5 10.7 %collective-permute-start = (bf16[80,768]{1,0:T(8,128)(2,1)S(1)}, bf16[80,768]{1,0:T(8,128)(2,1)S(1)}, u32[]{:S(2)}, u32[]{:S(2)}) collective-permute-start(bf16[80,768]{1,0:T(8,128)(2,1)S(1)} %fusion.6), channel_id=1, source_target_pairs={{0,1},{1,0},{2,3},{3,2},{4,5},{5,4},{6,7},{7,6},{8,9},{9,8},{10,11... | collective-permute-start | bytes 368648 | tf_op jit(solution)/shard_map/ppermute | solution.py:27
  5.5 12.3 %collective-permute-start.1 = (bf16[80,768]{1,0:T(8,128)(2,1)S(1)}, bf16[80,768]{1,0:T(8,128)(2,1)S(1)}, u32[]{:S(2)}, u32[]{:S(2)}) collective-permute-start(bf16[80,768]{1,0:T(8,128)(2,1)S(1)} %fusion.6), channel_id=1, source_target_pairs={{0,2},{1,3},{2,0},{3,1},{4,6},{5,7},{6,4},{7,5},{8,10},{9,11},{10,... | collective-permute-start | bytes 368648 | tf_op jit(solution)/shard_map/ppermute | solution.py:27
  8.1 10.4 %collective-permute-start.2 = (bf16[80,768]{1,0:T(8,128)(2,1)S(1)}, bf16[80,768]{1,0:T(8,128)(2,1)S(1)}, u32[]{:S(2)}, u32[]{:S(2)}) collective-permute-start(bf16[80,768]{1,0:T(8,128)(2,1)S(1)} %fusion.6), channel_id=1, source_target_pairs={{0,3},{1,2},{2,1},{3,0},{4,7},{5,6},{6,5},{7,4},{8,11},{9,10},{10,... | collective-permute-start | bytes 368648 | tf_op jit(solution)/shard_map/ppermute | solution.py:27
  9.0 33.2 %collective-permute-start.8 = (bf16[384,768]{1,0:T(8,128)(2,1)}, bf16[384,768]{1,0:T(8,128)(2,1)}, u32[]{:S(2)}, u32[]{:S(2)}) collective-permute-start(bf16[384,768]{1,0:T(8,128)(2,1)} %constant_dynamic-slice_fusion.3), channel_id=1, source_target_pairs={{0,1},{1,0},{2,3},{3,2},{4,5},{5,4},{6,7},{7,6},{8,9},{9,8},{10,11... | collective-permute-start | bytes 1769480 | tf_op jit(solution)/shard_map/ppermute | solution.py:27
  19.2 5.4 %collective-permute-start.3 = (bf16[1,3,3,24,384]{4,3,2,1,0:T(8,128)(2,1)S(1)}, bf16[1,3,3,24,384]{4,3,2,1,0:T(8,128)(2,1)S(1)}, u32[]{:S(2)}, u32[]{:S(2)}) collective-permute-start(bf16[1,3,3,24,384]{4,3,2,1,0:T(8,128)(2,1)S(1)} %get-tuple-element.282), channel_id=1, source_target_pairs={{0,8},{4,12},{8,0},{12,4},{16,24},{20,28},{24,16},{28,20},{1,9},{5... | collective-permute-start | bytes 497672 | tf_op jit(solution)/shard_map/ppermute | solution.py:27
  20.8 7.1 %collective-permute-start.5 = (bf16[1,3,3,24,384]{4,3,2,1,0:T(8,128)(2,1)S(1)}, bf16[1,3,3,24,384]{4,3,2,1,0:T(8,128)(2,1)S(1)}, u32[]{:S(2)}, u32[]{:S(2)}) collective-permute-start(bf16[1,3,3,24,384]{4,3,2,1,0:T(8,128)(2,1)S(1)} %get-tuple-element.283), channel_id=1, source_target_pairs={{0,16},{4,20},{8,24},{12,28},{16,0},{20,4},{24,8},{28,12},{1,17},{... | collective-permute-start | bytes 497672 | tf_op jit(solution)/shard_map/ppermute | solution.py:27
  24.7 7.6 %collective-permute-start.4 = (bf16[2,3,3,24,384]{4,3,2,1,0:T(8,128)(2,1)S(1)}, bf16[2,3,3,24,384]{4,3,2,1,0:T(8,128)(2,1)S(1)}, u32[]{:S(2)}, u32[]{:S(2)}) collective-permute-start(bf16[2,3,3,24,384]{4,3,2,1,0:T(8,128)(2,1)S(1)} %pad_maximum_fusion.5), channel_id=1, source_target_pairs={{0,16},{4,20},{8,24},{12,28},{16,0},{20,4},{24,8},{28,12},{1,17},{... | collective-permute-start | bytes 995336 | tf_op jit(solution)/shard_map/ppermute | solution.py:27
  28.0 7.2 %collective-permute-start.6 = (bf16[2,3,3,24,384]{4,3,2,1,0:T(8,128)(2,1)S(1)}, bf16[2,3,3,24,384]{4,3,2,1,0:T(8,128)(2,1)S(1)}, u32[]{:S(2)}, u32[]{:S(2)}) collective-permute-start(bf16[2,3,3,24,384]{4,3,2,1,0:T(8,128)(2,1)S(1)} %pad_maximum_fusion.6), channel_id=1, source_target_pairs={{0,8},{4,12},{8,0},{12,4},{16,24},{20,28},{24,16},{28,20},{1,9},{5... | collective-permute-start | bytes 995336 | tf_op jit(solution)/shard_map/ppermute | solution.py:27
  37.4 8.1 %collective-permute-start.7 = (bf16[2,4,3,3,24,384]{5,4,3,2,1,0:T(8,128)(2,1)}, bf16[2,4,3,3,24,384]{5,4,3,2,1,0:T(8,128)(2,1)}, u32[]{:S(2)}, u32[]{:S(2)}) collective-permute-start(bf16[2,4,3,3,24,384]{5,4,3,2,1,0:T(8,128)(2,1)} %pad_maximum_fusion.1), channel_id=1, source_target_pairs={{0,4},{4,0},{8,12},{12,8},{16,20},{20,16},{24,28},{28,24},{1,5},{5... | collective-permute-start | bytes 3981320 | tf_op jit(solution)/shard_map/ppermute | solution.py:27
  48.3 23.1 %collective-permute-start.10 = (bf16[3,96,768]{2,1,0:T(8,128)(2,1)S(1)}, bf16[3,96,768]{2,1,0:T(8,128)(2,1)S(1)}, u32[]{:S(2)}, u32[]{:S(2)}) collective-permute-start(bf16[3,96,768]{2,1,0:T(8,128)(2,1)S(1)} %get-tuple-element.148), channel_id=1, source_target_pairs={{0,2},{1,3},{2,0},{3,1},{4,6},{5,7},{6,4},{7,5},{8,10},{9,11},{10,... | collective-permute-start | bytes 1327112 | tf_op jit(solution)/shard_map/ppermute | solution.py:27
  50.1 35.8 %collective-permute-start.9 = (bf16[3,96,768]{2,1,0:T(8,128)(2,1)S(1)}, bf16[3,96,768]{2,1,0:T(8,128)(2,1)S(1)}, u32[]{:S(2)}, u32[]{:S(2)}) collective-permute-start(bf16[3,96,768]{2,1,0:T(8,128)(2,1)S(1)} %get-tuple-element.148), channel_id=1, source_target_pairs={{0,1},{1,0},{2,3},{3,2},{4,5},{5,4},{6,7},{7,6},{8,9},{9,8},{10,11... | collective-permute-start | bytes 1327112 | tf_op jit(solution)/shard_map/ppermute | solution.py:27
  56.8 10.4 %copy-start.42 = (bf16[384,1536]{1,0:T(8,128)(2,1)}, bf16[384,1536]{1,0:T(8,128)(2,1)S(1)}, u32[]{:S(2)}) copy-start(bf16[384,1536]{1,0:T(8,128)(2,1)S(1)} %fusion.2.refs_4_) | copy-start | bytes 3538948
  71.4 14.5 %collective-permute-start.11 = (bf16[3,96,768]{2,1,0:T(8,128)(2,1)S(1)}, bf16[3,96,768]{2,1,0:T(8,128)(2,1)S(1)}, u32[]{:S(2)}, u32[]{:S(2)}) collective-permute-start(bf16[3,96,768]{2,1,0:T(8,128)(2,1)S(1)} %collective-permute-done.10.refs_1_), channel_id=1, source_target_pairs={{0,1},{1,0},{2,3},{3,2},{4,5},{5,4},{6,7},{7,6},{8,9},{9,8},{10,11... | collective-permute-start | bytes 1327112 | tf_op jit(solution)/shard_map/ppermute | solution.py:27
  86.0 3.1 collective-permute-start.12
  86.3 16.1 %collective-permute-start.13 = (bf16[384,768]{1,0:T(8,128)(2,1)S(1)}, bf16[384,768]{1,0:T(8,128)(2,1)S(1)}, u32[]{:S(2)}, u32[]{:S(2)}) collective-permute-start(bf16[384,768]{1,0:T(8,128)(2,1)S(1)} %constant_dynamic-slice_fusion.2), channel_id=1, source_target_pairs={{0,1},{1,0},{2,3},{3,2},{4,5},{5,4},{6,7},{7,6},{8,9},{9,8},{10,11... | collective-permute-start | bytes 1769480 | tf_op jit(solution)/shard_map/ppermute | solution.py:27
  90.1 12.2 %copy-start.81 = (bf16[2,4,2,96,768]{4,3,2,1,0:T(8,128)(2,1)}, bf16[2,4,2,96,768]{4,3,2,1,0:T(8,128)(2,1)S(1)}, u32[]{:S(2)}) copy-start(bf16[2,4,2,96,768]{4,3,2,1,0:T(8,128)(2,1)S(1)} %slice.183) | copy-start | bytes 7077892
  93.8 9.7 %copy-start.55 = (bf16[512,2304]{1,0:T(8,128)(2,1)}, bf16[512,2304]{1,0:T(8,128)(2,1)S(1)}, u32[]{:S(2)}) copy-start(bf16[512,2304]{1,0:T(8,128)(2,1)S(1)} %fusion.1.refs_3_) | copy-start | bytes 7077892
  103.5 10.3 %copy-start.44 = (bf16[384,1536]{1,0:T(8,128)(2,1)}, bf16[384,1536]{1,0:T(8,128)(2,1)S(1)}, u32[]{:S(2)}) copy-start(bf16[384,1536]{1,0:T(8,128)(2,1)S(1)} %fusion.3.refs_4_) | copy-start | bytes 3538948
  116.4 16.6 %copy-start.20 = (bf16[512,768]{1,0:T(8,128)(2,1)S(1)}, bf16[512,768]{1,0:T(8,128)(2,1)}, u32[]{:S(2)}) copy-start(bf16[512,768]{1,0:T(8,128)(2,1)} %refs_0_.3) | copy-start | bytes 2359300
  133.0 16.1 %copy-start.24 = (bf16[3072,512]{1,0:T(8,128)(2,1)S(1)}, bf16[3072,512]{1,0:T(8,128)(2,1)}, u32[]{:S(2)}) copy-start(bf16[3072,512]{1,0:T(8,128)(2,1)} %get-tuple-element.168) | copy-start | bytes 9437188
  157.3 4.9 %collective-permute-start.15 = (bf16[4,4,4,24,768]{4,3,2,1,0:T(8,128)(2,1)}, bf16[4,4,4,24,768]{4,3,2,1,0:T(8,128)(2,1)}, u32[]{:S(2)}, u32[]{:S(2)}) collective-permute-start(bf16[4,4,4,24,768]{4,3,2,1,0:T(8,128)(2,1)} %get-tuple-element.177), channel_id=1, source_target_pairs={{0,4},{4,0},{8,12},{12,8},{16,20},{20,16},{24,28},{28,24},{1,5},{5... | collective-permute-start | bytes 7077896 | tf_op jit(solution)/shard_map/ppermute | solution.py:27
  157.3 8.2 %collective-permute-start.14 = (bf16[4,4,4,24,768]{4,3,2,1,0:T(8,128)(2,1)}, bf16[4,4,4,24,768]{4,3,2,1,0:T(8,128)(2,1)}, u32[]{:S(2)}, u32[]{:S(2)}) collective-permute-start(bf16[4,4,4,24,768]{4,3,2,1,0:T(8,128)(2,1)} %get-tuple-element.176), channel_id=1, source_target_pairs={{0,4},{4,0},{8,12},{12,8},{16,20},{20,16},{24,28},{28,24},{1,5},{5... | collective-permute-start | bytes 7077896 | tf_op jit(solution)/shard_map/ppermute | solution.py:27
  167.2 7.8 %copy-start.45 = (bf16[384,1536]{1,0:T(8,128)(2,1)S(1)}, bf16[384,1536]{1,0:T(8,128)(2,1)}, u32[]{:S(2)}) copy-start(bf16[384,1536]{1,0:T(8,128)(2,1)} %copy-done.44) | copy-start | bytes 3538948
  167.3 7.8 %copy-start.56 = (bf16[512,2304]{1,0:T(8,128)(2,1)S(1)}, bf16[512,2304]{1,0:T(8,128)(2,1)}, u32[]{:S(2)}) copy-start(bf16[512,2304]{1,0:T(8,128)(2,1)} %copy-done.55) | copy-start | bytes 7077892
  167.3 7.8 %copy-start.64 = (bf16[512,768]{1,0:T(8,128)(2,1)S(1)}, bf16[512,768]{1,0:T(8,128)(2,1)}, u32[]{:S(2)}) copy-start(bf16[512,768]{1,0:T(8,128)(2,1)} %copy-done.63) | copy-start | bytes 2359300
  167.3 7.8 %copy-start.72 = (f32[768,512]{1,0:T(8,128)S(1)}, f32[768,512]{1,0:T(8,128)}, u32[]{:S(2)}) copy-start(f32[768,512]{1,0:T(8,128)} %copy-done.71) | copy-start | bytes 4718596
  167.3 7.8 %copy-start.74 = (f32[4,8,256]{2,1,0:T(8,128)S(1)}, f32[4,8,256]{2,1,0:T(8,128)}, u32[]{:S(2)}) copy-start(f32[4,8,256]{2,1,0:T(8,128)} %copy-done.73) | copy-start | bytes 98308
  173.7 33.7 %collective-permute-start.17 = (bf16[8,2,4,24,768]{4,3,2,1,0:T(8,128)(2,1)}, bf16[8,2,4,24,768]{4,3,2,1,0:T(8,128)(2,1)}, u32[]{:S(2)}, u32[]{:S(2)}) collective-permute-start(bf16[8,2,4,24,768]{4,3,2,1,0:T(8,128)(2,1)} %get-tuple-element.187), channel_id=1, source_target_pairs={{0,8},{4,20},{8,0},{12,28},{16,24},{20,4},{24,16},{28,12},{1,9},{5... | collective-permute-start | bytes 7077896 | tf_op jit(solution)/shard_map/ppermute | solution.py:901
  175.1 16.1 %copy-start.82 = (bf16[2,4,2,96,768]{4,3,2,1,0:T(8,128)(2,1)S(1)}, bf16[2,4,2,96,768]{4,3,2,1,0:T(8,128)(2,1)}, u32[]{:S(2)}) copy-start(bf16[2,4,2,96,768]{4,3,2,1,0:T(8,128)(2,1)} %copy-done.81) | copy-start | bytes 7077892
  191.2 7.9 %copy-start.49 = (bf16[512,2304]{1,0:T(8,128)(2,1)}, bf16[512,2304]{1,0:T(8,128)(2,1)S(1)}, u32[]{:S(2)}) copy-start(bf16[512,2304]{1,0:T(8,128)(2,1)S(1)} %get-tuple-element.180.refs_5_) | copy-start | bytes 7077892
  193.2 13.0 %collective-permute-start.16 = (bf16[384,768]{1,0:T(8,128)(2,1)}, bf16[384,768]{1,0:T(8,128)(2,1)}, u32[]{:S(2)}, u32[]{:S(2)}) collective-permute-start(bf16[384,768]{1,0:T(8,128)(2,1)} %convolution_convert_fusion.1.refs_8_), channel_id=1, source_target_pairs={{0,1},{1,0},{2,3},{3,2},{4,5},{5,4},{6,7},{7,6},{8,9},{9,8},{10,11... | collective-permute-start | bytes 1769480 | tf_op jit(solution)/shard_map/ppermute | solution.py:27
  199.2 32.3 %collective-permute-start.19 = (bf16[49,8,3072]{2,1,0:T(8,128)(2,1)}, bf16[49,8,3072]{2,1,0:T(8,128)(2,1)}, u32[]{:S(2)}, u32[]{:S(2)}) collective-permute-start(bf16[49,8,3072]{2,1,0:T(8,128)(2,1)} %get-tuple-element.203), channel_id=1, source_target_pairs={{0,4},{4,0},{8,12},{12,8},{16,20},{20,16},{24,28},{28,24},{1,5},{5... | collective-permute-start | bytes 7225352 | tf_op jit(solution)/shard_map/ppermute | solution.py:27
  211.5 23.4 %collective-permute-start.18 = (bf16[4,2,4,24,768]{4,3,2,1,0:T(8,128)(2,1)S(1)}, bf16[4,2,4,24,768]{4,3,2,1,0:T(8,128)(2,1)S(1)}, u32[]{:S(2)}, u32[]{:S(2)}) collective-permute-start(bf16[4,2,4,24,768]{4,3,2,1,0:T(8,128)(2,1)S(1)} %get-tuple-element.201), channel_id=1, source_target_pairs={{0,16},{4,12},{8,24},{12,4},{16,0},{20,28},{24,8},{28,20},{1,17},{... | collective-permute-start | bytes 3538952 | tf_op jit(solution)/shard_map/ppermute | solution.py:901
  245.0 19.9 %collective-permute-start.21 = (bf16[4,4,4,24,768]{4,3,2,1,0:T(8,128)(2,1)}, bf16[4,4,4,24,768]{4,3,2,1,0:T(8,128)(2,1)}, u32[]{:S(2)}, u32[]{:S(2)}) collective-permute-start(bf16[4,4,4,24,768]{4,3,2,1,0:T(8,128)(2,1)} %get-tuple-element.213), channel_id=1, source_target_pairs={{0,4},{4,0},{8,12},{12,8},{16,20},{20,16},{24,28},{28,24},{1,5},{5... | collective-permute-start | bytes 7077896 | tf_op jit(solution)/shard_map/ppermute | solution.py:27
  245.4 19.5 %collective-permute-start.20 = (bf16[4,4,4,24,768]{4,3,2,1,0:T(8,128)(2,1)}, bf16[4,4,4,24,768]{4,3,2,1,0:T(8,128)(2,1)}, u32[]{:S(2)}, u32[]{:S(2)}) collective-permute-start(bf16[4,4,4,24,768]{4,3,2,1,0:T(8,128)(2,1)} %get-tuple-element.212), channel_id=1, source_target_pairs={{0,4},{4,0},{8,12},{12,8},{16,20},{20,16},{24,28},{28,24},{1,5},{5... | collective-permute-start | bytes 7077896 | tf_op jit(solution)/shard_map/ppermute | solution.py:27
  245.5 16.4 %collective-permute-start.22 = (bf16[2,2,4,24,768]{4,3,2,1,0:T(8,128)(2,1)S(1)}, bf16[2,2,4,24,768]{4,3,2,1,0:T(8,128)(2,1)}, u32[]{:S(2)}, u32[]{:S(2)}) collective-permute-start(bf16[2,2,4,24,768]{4,3,2,1,0:T(8,128)(2,1)S(1)} %get-tuple-element.215), channel_id=1, source_target_pairs={{0,1},{1,0},{2,3},{3,2},{4,5},{5,4},{6,7},{7,6},{8,9},{9,8},{10,11... | collective-permute-start | bytes 1769480 | tf_op jit(solution)/shard_map/ppermute | solution.py:901
  247.9 17.0 %copy-start.3 = (bf16[4,4,4,24,768]{4,3,2,1,0:T(8,128)(2,1)S(1)}, bf16[4,4,4,24,768]{4,3,2,1,0:T(8,128)(2,1)}, u32[]{:S(2)}) copy-start(bf16[4,4,4,24,768]{4,3,2,1,0:T(8,128)(2,1)} %copy-done.2) | copy-start | bytes 7077892
  247.9 40.8 %collective-permute-start.24 = (bf16[25,8,3072]{2,1,0:T(8,128)(2,1)}, bf16[25,8,3072]{2,1,0:T(8,128)(2,1)S(1)}, u32[]{:S(2)}, u32[]{:S(2)}) collective-permute-start(bf16[25,8,3072]{2,1,0:T(8,128)(2,1)} %copy-done.15), channel_id=1, source_target_pairs={{0,8},{4,20},{8,0},{12,28},{16,24},{20,4},{24,16},{28,12},{1,9},{5... | collective-permute-start | bytes 3686408 | tf_op jit(solution)/shard_map/ppermute | solution.py:901
  264.9 6.6 %copy-start.43 = (bf16[384,1536]{1,0:T(8,128)(2,1)S(1)}, bf16[384,1536]{1,0:T(8,128)(2,1)}, u32[]{:S(2)}) copy-start(bf16[384,1536]{1,0:T(8,128)(2,1)} %copy-done.42) | copy-start | bytes 3538948
  264.9 6.6 %copy-start.60 = (bf16[512,768]{1,0:T(8,128)(2,1)S(1)}, bf16[512,768]{1,0:T(8,128)(2,1)}, u32[]{:S(2)}) copy-start(bf16[512,768]{1,0:T(8,128)(2,1)} %copy-done.59) | copy-start | bytes 2359300
  268.6 29.7 %collective-permute-start.27 = (bf16[8,2,4,24,768]{4,3,2,1,0:T(8,128)(2,1)S(1)}, bf16[8,2,4,24,768]{4,3,2,1,0:T(8,128)(2,1)S(1)}, u32[]{:S(2)}, u32[]{:S(2)}) collective-permute-start(bf16[8,2,4,24,768]{4,3,2,1,0:T(8,128)(2,1)S(1)} %get-tuple-element.236), channel_id=1, source_target_pairs={{0,8},{4,20},{8,0},{12,28},{16,24},{20,4},{24,16},{28,12},{1,9},{5... | collective-permute-start | bytes 7077896 | tf_op jit(solution)/shard_map/ppermute | solution.py:901
  271.5 16.1 %copy-start.80 = (bf16[2,4,8,24,768]{4,3,2,1,0:T(8,128)(2,1)S(1)}, bf16[2,4,8,24,768]{4,3,2,1,0:T(8,128)(2,1)}, u32[]{:S(2)}) copy-start(bf16[2,4,8,24,768]{4,3,2,1,0:T(8,128)(2,1)} %copy-done.79) | copy-start | bytes 7077892
  288.7 8.1 %copy-start.21 = (bf16[384,768]{1,0:T(8,128)(2,1)}, bf16[384,768]{1,0:T(8,128)(2,1)S(1)}, u32[]{:S(2)}) copy-start(bf16[384,768]{1,0:T(8,128)(2,1)S(1)} %convolution_convert_fusion.refs_8_) | copy-start | bytes 1769476
  296.8 13.8 %collective-permute-start.25 = (bf16[49,8,3072]{2,1,0:T(8,128)(2,1)}, bf16[49,8,3072]{2,1,0:T(8,128)(2,1)}, u32[]{:S(2)}, u32[]{:S(2)}) collective-permute-start(bf16[49,8,3072]{2,1,0:T(8,128)(2,1)} %get-tuple-element.232), channel_id=1, source_target_pairs={{0,4},{4,0},{8,12},{12,8},{16,20},{20,16},{24,28},{28,24},{1,5},{5... | collective-permute-start | bytes 7225352 | tf_op jit(solution)/shard_map/ppermute | solution.py:27
  296.8 10.5 %collective-permute-start.26 = (bf16[13,8,3072]{2,1,0:T(8,128)(2,1)S(1)}, bf16[13,8,3072]{2,1,0:T(8,128)(2,1)}, u32[]{:S(2)}, u32[]{:S(2)}) collective-permute-start(bf16[13,8,3072]{2,1,0:T(8,128)(2,1)S(1)} %get-tuple-element.234), channel_id=1, source_target_pairs={{0,16},{4,12},{8,24},{12,4},{16,0},{20,28},{24,8},{28,20},{1,17},{... | collective-permute-start | bytes 1916936 | tf_op jit(solution)/shard_map/ppermute | solution.py:901
  301.2 28.3 %collective-permute-start.29 = (bf16[4,2,4,24,768]{4,3,2,1,0:T(8,128)(2,1)}, bf16[4,2,4,24,768]{4,3,2,1,0:T(8,128)(2,1)}, u32[]{:S(2)}, u32[]{:S(2)}) collective-permute-start(bf16[4,2,4,24,768]{4,3,2,1,0:T(8,128)(2,1)} %get-tuple-element.243), channel_id=1, source_target_pairs={{0,16},{4,12},{8,24},{12,4},{16,0},{20,28},{24,8},{28,20},{1,17},{... | collective-permute-start | bytes 3538952 | tf_op jit(solution)/shard_map/ppermute | solution.py:901
  302.5 15.8 %collective-permute-start.37 = (bf16[1,2,4,24,768]{4,3,2,1,0:T(8,128)(2,1)}, bf16[1,2,4,24,768]{4,3,2,1,0:T(8,128)(2,1)}, u32[]{:S(2)}, u32[]{:S(2)}) collective-permute-start(bf16[1,2,4,24,768]{4,3,2,1,0:T(8,128)(2,1)} %get-tuple-element.265), channel_id=1, source_target_pairs={{0,2},{1,3},{2,0},{3,1},{4,6},{5,7},{6,4},{7,5},{8,10},{9,11},{10,... | collective-permute-start | bytes 884744 | tf_op jit(solution)/shard_map/ppermute | solution.py:901
  310.6 16.5 %collective-permute-start.30 = (bf16[204,8,128]{2,1,0:T(8,128)(2,1)}, bf16[204,8,128]{2,1,0:T(8,128)(2,1)}, u32[]{:S(2)}, u32[]{:S(2)}) collective-permute-start(bf16[204,8,128]{2,1,0:T(8,128)(2,1)} %get-tuple-element.245), channel_id=1, source_target_pairs={{0,1},{1,0},{2,3},{3,2},{4,5},{5,4},{6,7},{7,6},{8,9},{9,8},{10,11... | collective-permute-start | bytes 1253384 | tf_op jit(solution)/shard_map/ppermute | solution.py:901
  314.9 25.0 %collective-permute-start.28 = (bf16[25,8,3072]{2,1,0:T(8,128)(2,1)}, bf16[25,8,3072]{2,1,0:T(8,128)(2,1)S(1)}, u32[]{:S(2)}, u32[]{:S(2)}) collective-permute-start(bf16[25,8,3072]{2,1,0:T(8,128)(2,1)} %get-tuple-element.241), channel_id=1, source_target_pairs={{0,8},{4,20},{8,0},{12,28},{16,24},{20,4},{24,16},{28,12},{1,9},{5... | collective-permute-start | bytes 3686408 | tf_op jit(solution)/shard_map/ppermute | solution.py:901
  319.2 10.2 %copy-start.19 = (bf16[4,2,4,24,768]{4,3,2,1,0:T(8,128)(2,1)S(1)}, bf16[4,2,4,24,768]{4,3,2,1,0:T(8,128)(2,1)}, u32[]{:S(2)}) copy-start(bf16[4,2,4,24,768]{4,3,2,1,0:T(8,128)(2,1)} %copy-done.18) | copy-start | bytes 3538948
  321.0 18.7 %collective-permute-start.23 = (bf16[384,768]{1,0:T(8,128)(2,1)S(1)}, bf16[384,768]{1,0:T(8,128)(2,1)S(1)}, u32[]{:S(2)}, u32[]{:S(2)}) collective-permute-start(bf16[384,768]{1,0:T(8,128)(2,1)S(1)} %copy-done.22), channel_id=1, source_target_pairs={{0,1},{1,0},{2,3},{3,2},{4,5},{5,4},{6,7},{7,6},{8,9},{9,8},{10,11... | collective-permute-start | bytes 1769480 | tf_op jit(solution)/shard_map/ppermute | solution.py:27
  331.6 8.3 %copy-start.17 = (bf16[25,8,3072]{2,1,0:T(8,128)(2,1)S(1)}, bf16[25,8,3072]{2,1,0:T(8,128)(2,1)}, u32[]{:S(2)}) copy-start(bf16[25,8,3072]{2,1,0:T(8,128)(2,1)} %copy-done.16) | copy-start | bytes 3686404
  331.6 25.4 %collective-permute-start.32 = (bf16[2,2,4,24,768]{4,3,2,1,0:T(8,128)(2,1)S(1)}, bf16[2,2,4,24,768]{4,3,2,1,0:T(8,128)(2,1)S(1)}, u32[]{:S(2)}, u32[]{:S(2)}) collective-permute-start(bf16[2,2,4,24,768]{4,3,2,1,0:T(8,128)(2,1)S(1)} %get-tuple-element.252), channel_id=1, source_target_pairs={{0,1},{1,0},{2,3},{3,2},{4,5},{5,4},{6,7},{7,6},{8,9},{9,8},{10,11... | collective-permute-start | bytes 1769480 | tf_op jit(solution)/shard_map/ppermute | solution.py:901
  339.8 17.9 %collective-permute-start.35 = (bf16[108,8,128]{2,1,0:T(8,128)(2,1)S(1)}, bf16[108,8,128]{2,1,0:T(8,128)(2,1)S(1)}, u32[]{:S(2)}, u32[]{:S(2)}) collective-permute-start(bf16[108,8,128]{2,1,0:T(8,128)(2,1)S(1)} %get-tuple-element.261), channel_id=1, source_target_pairs={{0,2},{1,3},{2,0},{3,1},{4,6},{5,7},{6,4},{7,5},{8,10},{9,11},{10,... | collective-permute-start | bytes 663560 | tf_op jit(solution)/shard_map/ppermute | solution.py:901
  340.8 20.3 %collective-permute-start.31 = (bf16[13,8,3072]{2,1,0:T(8,128)(2,1)S(1)}, bf16[13,8,3072]{2,1,0:T(8,128)(2,1)S(1)}, u32[]{:S(2)}, u32[]{:S(2)}) collective-permute-start(bf16[13,8,3072]{2,1,0:T(8,128)(2,1)S(1)} %get-tuple-element.250), channel_id=1, source_target_pairs={{0,16},{4,12},{8,24},{12,4},{16,0},{20,28},{24,8},{28,20},{1,17},{... | collective-permute-start | bytes 1916936 | tf_op jit(solution)/shard_map/ppermute | solution.py:901
  357.7 15.4 %collective-permute-start.36 = (bf16[1,2,4,24,768]{4,3,2,1,0:T(8,128)(2,1)S(1)}, bf16[1,2,4,24,768]{4,3,2,1,0:T(8,128)(2,1)}, u32[]{:S(2)}, u32[]{:S(2)}) collective-permute-start(bf16[1,2,4,24,768]{4,3,2,1,0:T(8,128)(2,1)S(1)} %get-tuple-element.263), channel_id=1, source_target_pairs={{0,2},{1,3},{2,0},{3,1},{4,6},{5,7},{6,4},{7,5},{8,10},{9,11},{10,... | collective-permute-start | bytes 884744 | tf_op jit(solution)/shard_map/ppermute | solution.py:901
  362.0 17.8 %collective-permute-start.33 = (bf16[204,8,128]{2,1,0:T(8,128)(2,1)S(1)}, bf16[204,8,128]{2,1,0:T(8,128)(2,1)S(1)}, u32[]{:S(2)}, u32[]{:S(2)}) collective-permute-start(bf16[204,8,128]{2,1,0:T(8,128)(2,1)S(1)} %get-tuple-element.256), channel_id=1, source_target_pairs={{0,1},{1,0},{2,3},{3,2},{4,5},{5,4},{6,7},{7,6},{8,9},{9,8},{10,11... | collective-permute-start | bytes 1253384 | tf_op jit(solution)/shard_map/ppermute | solution.py:901
  374.1 6.9 %copy-start.83 = (f32[1,24,3072]{2,1,0:T(8,128)S(1)}, f32[1,24,3072]{2,1,0:T(8,128)}, u32[]{:S(2)}) copy-start(f32[1,24,3072]{2,1,0:T(8,128)} %stack_reshape.23) | copy-start | bytes 884740
  374.1 7.7 %copy-start.85 = (f32[1,1,4,24,768]{4,3,2,1,0:T(8,128)S(1)}, f32[1,1,4,24,768]{4,3,2,1,0:T(8,128)}, u32[]{:S(2)}) copy-start(f32[1,1,4,24,768]{4,3,2,1,0:T(8,128)} %get-tuple-element.280) | copy-start | bytes 884740
  380.9 11.1 %collective-permute-start.34 = (bf16[108,8,128]{2,1,0:T(8,128)(2,1)S(1)}, bf16[108,8,128]{2,1,0:T(8,128)(2,1)S(1)}, u32[]{:S(2)}, u32[]{:S(2)}) collective-permute-start(bf16[108,8,128]{2,1,0:T(8,128)(2,1)S(1)} %get-tuple-element.259), channel_id=1, source_target_pairs={{0,2},{1,3},{2,0},{3,1},{4,6},{5,7},{6,4},{7,5},{8,10},{9,11},{10,... | collective-permute-start | bytes 663560 | tf_op jit(solution)/shard_map/ppermute | solution.py:901
  381.8 12.6 %copy-start.89 = (f32[1,24,768]{2,1,0:T(8,128)S(1)}, f32[1,24,768]{2,1,0:T(8,128)}, u32[]{:S(2)}) copy-start(f32[1,24,768]{2,1,0:T(8,128)} %stack_reshape.21) | copy-start | bytes 221188
  381.8 13.3 %copy-start.84 = (f32[3,192,96]{2,1,0:T(8,128)S(1)}, f32[3,192,96]{2,1,0:T(8,128)}, u32[]{:S(2)}) copy-start(f32[3,192,96]{2,1,0:T(8,128)} %slice.232) | copy-start | bytes 663556
  (76 other events, 206.8 us)

commit v5 on v4

--- a/solution.py
+++ b/solution.py
@@ -456,7 +456,7 @@
 
 
 def feed_back_kernel(
-    tokens, grad, second_rows, first_rows, slope, w_down, w_up, w_out, vec,
+    tokens, grad, back, edge, second_rows, first_rows, slope, w_down, w_up, w_out, vec,
     dz, du, da, dr, dc, sums, up_sum, dr_two, total,
 ):
     step = pl.program_id(0)
@@ -468,6 +468,11 @@
         sums[...] = jnp.zeros(sums.shape, f32)
         for rows in tiles:
             pull = grad[rows, :].astype(f32)
+            if back.shape[0] > BLK:
+                at = rows.start - edge[0]
+                inside = (at >= 0) & (at < back.shape[0])
+                here = pl.ds(pl.multiple_of(jnp.where(inside, at, 0), BLK), BLK)
+                pull = pull + jnp.where(inside, back[here, :].astype(f32), 0.0)
             value, unit = norm_back(pull, vec[4:5, :], second_rows[rows, :])
             dr_two[rows, :] = value
             total[rows, :] = jnp.zeros_like(value)
@@ -498,13 +503,13 @@
             dc[rows, :] = nt(rounded, w_out[...]).astype(bf16)
 
 
-def feed_back(layer_idx, grad, second_rows, first_rows, slope, w_down, w_up, w_out, vec, waits, passes):
+def feed_back(layer_idx, grad, back, edge, second_rows, first_rows, slope, w_down, w_up, w_out, vec, waits, passes):
     tokens, width = grad.shape
     wide = w_up.shape[-1]
     rows = whole((tokens, width))
     return ordered_call(
         functools.partial(feed_back_kernel, tokens),
-        (grad, second_rows, first_rows, slope, w_down, w_up, w_out, vec),
+        (grad, back, edge, second_rows, first_rows, slope, w_down, w_up, w_out, vec),
         waits,
         passes,
         grid=(wide // CHUNK,),
@@ -519,6 +524,8 @@
         ),
         in_specs=[
             rows,
+            whole(back.shape),
+            pl.BlockSpec(memory_space=pltpu.SMEM),
             rows,
             rows,
             pl.BlockSpec((tokens, CHUNK), lambda step: (0, step)),
@@ -1021,13 +1028,13 @@
             halo_t = halo.T
             w_cats.append(later_weights(own_later[layer_idx], collect(later_got[layer_idx])))
 
-    grad_hidden = cotangent
+    grad_hidden, back = cotangent, jnp.zeros((BLK, width), bf16)
     flights = []
     for layer_idx in reversed(range(layers)):
         low_t, halo_t, qkv, kvh, ctx_t, ctx_low, lse, first_rows, first_t, active_t, slope, second_rows = saved[layer_idx]
         w_cat = w_cats[layer_idx]
         (dz, du, da, dr, dc, sums, up_sum), _ = feed_back(
-            layer_idx, grad_hidden, second_rows, first_rows, slope, w_down, w_up, w_out, vecs[layer_idx], (), ()
+            layer_idx, grad_hidden, back, edge.reshape(1).astype(jnp.int32), second_rows, first_rows, slope, w_down, w_up, w_out, vecs[layer_idx], (), ()
         )
         if flights:
             flights[1].step()
@@ -1038,29 +1045,32 @@
         up_send, up_keep = grad_feed(core_at, first_t, du, parts, dp, head, True)
         up_got = swap(up_send, "dp", 1)
         fed = Flight([down_keep, up_keep], [down_got, up_got], False)
-        if flights:
-            flights[0].step()
         fed.step()
         (dqkv, dkvh, sums), _ = attend_back(bounds, segq, segk, qkv, kvh, ctx_t, lse, dc, sums, up_sum, (), ())
         part_halo = nn(dkvh, w_cat[width:]).astype(bf16)
         back = swap(part_halo, "head", 1)
         if flights:
             flights[1].step()
+            flights[0].step()
         (send, keep), _ = grad_heads(core_at, ctx_low, low_t, halo_t, da, dqkv, dkvh, sums, dp, (part_halo,), ())
         heads = Flight([keep], [swap(send, "dp", 1)], True)
-        padded = lax.dynamic_update_slice(jnp.zeros((tokens, width), bf16), back, (edge, 0))
-        grad_hidden = nn(dqkv, w_cat) + dr + padded.astype(f32)
+        grad_hidden = nn(dqkv, w_cat) + dr
         fed.step()
         if flights:
             flights[1].step()
             heads.step()
-            flights[1].step()
             fed.step()
             heads.step()
             fed.step()
             heads.step()
-            heads.step()
+            flights[1].step()
+            first, second = flights
+            passed = heads.step(passes=(first.keeps[0], second.keeps[0]))
+            first.keeps, second.keeps = [passed[0]], [passed[1]]
         flights = flights + [fed, heads]
+
+    padded = lax.dynamic_update_slice(jnp.zeros((tokens, width), bf16), back, (edge, 0))
+    grad_hidden = grad_hidden + padded.astype(f32)
 
     results = []
     for place in range(layers):

time: 401 us -> 388 us (0.968)
  starting transfers between devices: 33.7 us -> 45.3 us
  Pallas kernels: 171 us -> 162 us
  waiting for transfers between devices: 107 us -> 98.3 us
  local copies, waits for them, and re-layouts: 52.4 us -> 43.9 us
    ppermute x22, waiting for transfers between devices: 44 us -> 34.4 us  [swap(): return lax.ppermute(value, axis, [(i, i ^ bit) for i in range(size)])]
    pallas_call x34, Pallas kernels: 171 us -> 162 us  [ordered_call(): pl.pallas_call(body, out_shape=tuple(out_shape) + (jax.ShapeDtypeStruct((...]
    ppermute x22, starting transfers between devices: 18.3 us -> 26 us  [swap(): return lax.ppermute(value, axis, [(i, i ^ bit) for i in range(size)])]
    unnamed x208 -> x188, local copies, waits for them, and re-layouts: 32.9 us -> 30.2 us
  transfers between devices with their start and end apart: 38 -> 38, of which waited for: 21 -> 21; matrix products, arithmetic and copies ran while one was open for 11% -> 9% of each run, Pallas kernels for 28% -> 27%
where the time goes in v5:
time: 388 us; the launch traced here: 382 us
  Pallas kernels  162 us (42%)
  waiting for transfers between devices  98.3 us (25%)
  starting transfers between devices  45.3 us (12%)
  local copies, waits for them, and re-layouts  43.9 us (11%)
  matrix products  18.1 us (5%)
  other arithmetic  12.2 us (3%)
    pallas_call x34, Pallas kernels, ordered_call(): pl.pallas_call(body, out_shape=tuple(out_shape) + (jax.ShapeDtypeStruct((...  162 us
    ppermute x16, waiting for transfers between devices, step(): self.keeps, self.gots = ([keep], [lax.ppermute(send, axis_name, pairs)])  63.9 us
    ppermute x22, waiting for transfers between devices, swap(): return lax.ppermute(value, axis, [(i, i ^ bit) for i in range(size)])  34.4 us
    unnamed x188, local copies, waits for them, and re-layouts  30.2 us
    ppermute x22, starting transfers between devices, swap(): return lax.ppermute(value, axis, [(i, i ^ bit) for i in range(size)])  26 us
    ppermute x16, starting transfers between devices, step(): self.keeps, self.gots = ([keep], [lax.ppermute(send, axis_name, pairs)])  19.3 us
    dot_general x4, matrix products, nn(): lax.dot_general(left, right, (((1,), (0,)), ((), ())), preferred_element_...  10.3 us
    dot_general x4, matrix products, nt(): lax.dot_general(left, right, (((1,), (1,)), ((), ())), preferred_element_...  7.82 us
  transfers between devices with their start and end apart: 38, of which 21 were waited for; matrix products, arithmetic and copies ran while one was open for 9% of the time, Pallas kernels for 27%

profile of v5, /device:TPU:0, one launch (start us, length us, event | category | flops | bytes accessed | tf_op | source)
XLA Modules:
  0.0 382.3 jit_solution(8836247196565788805)
XLA Ops:
  0.7 1.6 fusion.17
  2.5 3.1 collective-permute-start
  5.5 2.6 collective-permute-start.1
  13.8 4.1 %collective-permute-done.1 = bf16[80,768]{1,0:T(8,128)(2,1)S(1)} collective-permute-done((bf16[80,768]{1,0:T(8,128)(2,1)S(1)}, bf16[80,768]{1,0:T(8,128)(2,1)S(1)}, u32[]{:S(2)}, u32[]{:S(2)}) %collective-permute-start.1) | collective-permute-done | bytes 122912 | tf_op jit(solution)/shard_map/ppermute | solution.py:27
  22.3 2.3 collective-permute-done.3
  26.3 1.6 collective-permute-done.5
  28.9 3.4 collective-permute-done.4
  33.4 1.7 collective-permute-done.6
  45.5 1.6 pad_maximum_fusion
  48.3 1.8 collective-permute-start.10
  52.1 2.0 fusion.4.refs_3_
  54.1 2.6 fusion.2.refs_4_
  56.8 9.8 %attend.2 = (bf16[512,768]{1,0:T(8,128)(2,1)S(1)}, f32[768,512]{1,0:T(8,128)S(1)}, bf16[768,512]{1,0:T(8,128)(2,1)S(1)}, f32[4,8,256]{2,1,0:T(8,128)S(1)}, f32[8,128]{1,0:T(8,128)S(1)}) custom-call(s32[4,4]{1,0:T(4,128)S(1)} %pad_add_fusion.2.refs_0_, s32[4,1,256]{2,1,0:T(1,128)S(1)} %reshape.381.refs_1_, s32[896,1]{1,0:T(8,128)S(1)} %reshape.412.refs_2_, ...), custom_call_target="tpu_custom_call" | custom-call | flops 5175000064 | bytes 1000 | tf_op jit(solution)/shard_map/attend/pallas_call | solution.py:249
  69.4 2.0 collective-permute-done.10.refs_1_
  71.4 14.4 %feed.2 = (f32[512,768]{1,0:T(8,128)S(1)}, bf16[768,512]{1,0:T(8,128)(2,1)S(1)}, bf16[3072,512]{1,0:T(8,128)(2,1)}, f32[512,3072]{1,0:T(8,128)}, f32[512,768]{1,...) custom-call(bf16[512,768]{1,0:T(8,128)(2,1)S(1)} %copy-done.10, ...), custom_call_target="tpu_custom_call" | custom-call | flops 8625000448 | bytes 1000 | tf_op jit(solution)/shard_map/feed/pallas_call | solution.py:249
  90.4 1.7 copy-done.8
  92.1 2.0 fusion.1.refs_3_
  94.1 8.2 %collective-permute-done.13 = bf16[384,768]{1,0:T(8,128)(2,1)S(1)} collective-permute-done((bf16[384,768]{1,0:T(8,128)(2,1)S(1)}, bf16[384,768]{1,0:T(8,128)(2,1)S(1)}, u32[]{:S(2)}, u32[]{:S(2)}) %collective-permute-start.13) | collective-permute-done | bytes 589856 | tf_op jit(solution)/shard_map/ppermute | solution.py:27
  103.5 9.7 %attend.3 = (bf16[512,768]{1,0:T(8,128)(2,1)S(1)}, f32[768,512]{1,0:T(8,128)S(1)}, bf16[768,512]{1,0:T(8,128)(2,1)S(1)}, f32[4,8,256]{2,1,0:T(8,128)S(1)}, f32[8,128]{1,0:T(8,128)S(1)}) custom-call(s32[4,4]{1,0:T(4,128)S(1)} %pad_add_fusion.2.refs_0_, s32[4,1,256]{2,1,0:T(1,128)S(1)} %reshape.381.refs_1_, s32[896,1]{1,0:T(8,128)S(1)} %reshape.412.refs_2_, ...), custom_call_target="tpu_custom_call" | custom-call | flops 5175000064 | bytes 1000 | tf_op jit(solution)/shard_map/attend/pallas_call | solution.py:249
  115.3 14.2 %feed.3 = (f32[512,768]{1,0:T(8,128)S(1)}, bf16[768,512]{1,0:T(8,128)(2,1)S(1)}, bf16[3072,512]{1,0:T(8,128)(2,1)}, f32[512,3072]{1,0:T(8,128)}, f32[512,768]{1,...) custom-call(f32[512,768]{1,0:T(8,128)} %get-tuple-element.148.refs_0_, ...), custom_call_target="tpu_custom_call" | custom-call | flops 8625000448 | bytes 1000 | tf_op jit(solution)/shard_map/feed/pallas_call | solution.py:249
  131.9 16.0 %feed_back.2 = (bf16[512,768]{1,0:T(8,128)(2,1)S(1)}, bf16[512,3072]{1,0:T(8,128)(2,1)}, bf16[512,768]{1,0:T(8,128)(2,1)S(1)}, f32[512,768]{1,0:T(8,128)S(1)}, b...) custom-call(bf16[512,768]{1,0:T(8,128)(2,1)S(1)} %copy-done.14, ...), custom_call_target="tpu_custom_call" | custom-call | flops 9774999552 | bytes 1000 | tf_op jit(solution)/shard_map/feed_back/pallas_call | solution.py:249
  148.0 2.8 grad_down.2
  151.8 2.9 grad_up.2
  158.0 2.9 collective-permute-done.15
  160.9 3.4 collective-permute-done.14
  164.3 1.7 copy-done.5
  166.0 5.0 %advance.16 = (bf16[8,2,4,24,768]{4,3,2,1,0:T(8,128)(2,1)}, bf16[8,2,4,24,768]{4,3,2,1,0:T(8,128)(2,1)S(1)}, f32[8,128]{1,0:T(8,128)S(1)}) custom-call(s32[2]{0:T(128)S(1)} %pad_add_fusion.5.refs_0_, bf16[16,4,24,768]{3,2,1,0:T(8,128)(2,1)S(1)} %bitcast.157, bf16[16,4,24,768]{3,2,1,0:T(8,128)(2,1)S(1)} %bitcast.159, ...), custom_call_target="tpu_custom_call" | custom-call | flops 1931595264 | bytes 1000 | tf_op jit(solution)/shard_map/advance/pallas_call | solution.py:249
  172.7 14.6 %attend_back.2 = (bf16[512,2304]{1,0:T(8,128)(2,1)S(1)}, bf16[384,1536]{1,0:T(8,128)(2,1)S(1)}, f32[16,768]{1,0:T(8,128)S(1)}, f32[8,128]{1,0:T(8,128)S(1)}) custom-call(s32[4,4]{1,0:T(4,128)S(1)} %pad_add_fusion.2.refs_0_, s32[4,1,256]{2,1,0:T(1,128)S(1)} %reshape.381.refs_1_, s32[896,1]{1,0:T(8,128)S(1)} %reshape.412.refs_2_, ...), custom_call_target="tpu_custom_call" | custom-call | flops 12074999808 | bytes 1000 | tf_op jit(solution)/shard_map/attend_back/pallas_call | solution.py:249
  190.0 5.2 %grad_heads.2 = (bf16[49,8,3072]{2,1,0:T(8,128)(2,1)}, bf16[49,8,3072]{2,1,0:T(8,128)(2,1)S(1)}, f32[8,128]{1,0:T(8,128)S(1)}) custom-call(s32[1]{0:T(128)} %bitcast.36.refs_0_, bf16[8,96,512]{2,1,0:T(8,128)(2,1)S(1)} %bitcast.173, bf16[8,96,512]{2,1,0:T(8,128)(2,1)S(1)} %bitcast.172, bf16[8,96,384]{2,1,0:T(8,128)(2,1)S(1)} %bitcast.166, ...), custom_call_target="tpu_custom_call" | custom-call | flops 4600000000 | bytes 1000 | tf_op jit(solution)/shard_map/grad_heads/pallas_call | solution.py:249
  195.2 2.0 collective-permute-start.19
  197.3 2.1 collective-permute-start.16
  199.4 2.2 collective-permute-done.17.refs_2_
  201.6 1.7 copy-done.1
  203.3 2.4 advance.17
  205.6 2.7 collective-permute-start.18
  208.4 4.1 %convolution_add_fusion.3.refs_0_ = f32[512,768]{1,0:T(8,128)S(1)} fusion(f32[512,768]{1,0:T(8,128)} %copy-done.48, bf16[512,2304]{1,0:T(8,128)(2,1)} %copy-done.47, bf16[2304,768]{1,0:T(8,128)(2,1)S(1)} %bitcast.163), kind=kOutput, calls=%fused_computation.11 | convolution fusion | flops 1812332544 | bytes 9043968 | tf_op jit(solution)/shard_map/dot_general | solution.py:67
  213.1 16.2 %feed_back.3 = (bf16[512,768]{1,0:T(8,128)(2,1)S(1)}, bf16[512,3072]{1,0:T(8,128)(2,1)}, bf16[512,768]{1,0:T(8,128)(2,1)S(1)}, f32[512,768]{1,0:T(8,128)S(1)}, b...) custom-call(f32[512,768]{1,0:T(8,128)S(1)} %convolution_add_fusion.3.refs_0_, ...), custom_call_target="tpu_custom_call" | custom-call | flops 9774999552 | bytes 1000 | tf_op jit(solution)/shard_map/feed_back/pallas_call | solution.py:249
  229.3 3.4 advance.18
  236.0 2.8 grad_down.3
  238.8 2.9 grad_up.3
  243.7 3.0 collective-permute-start.24
  246.7 1.7 collective-permute-start.23
  248.4 3.0 collective-permute-done.20
  251.4 1.7 copy-done.3
  253.1 3.6 advance.20
  256.7 3.0 collective-permute-start.27
  259.7 14.6 %attend_back.3 = (bf16[512,2304]{1,0:T(8,128)(2,1)S(1)}, bf16[384,1536]{1,0:T(8,128)(2,1)S(1)}, f32[16,768]{1,0:T(8,128)S(1)}, f32[8,128]{1,0:T(8,128)S(1)}) custom-call(s32[4,4]{1,0:T(4,128)S(1)} %pad_add_fusion.2.refs_0_, s32[4,1,256]{2,1,0:T(1,128)S(1)} %reshape.381.refs_1_, s32[896,1]{1,0:T(8,128)S(1)} %reshape.412.refs_2_, ...), custom_call_target="tpu_custom_call" | custom-call | flops 12074999808 | bytes 1000 | tf_op jit(solution)/shard_map/attend_back/pallas_call | solution.py:249
  275.2 1.6 copy-done.74
  276.9 1.9 convolution_convert_fusion.refs_8_
  280.3 3.8 %grad_heads.3 = (bf16[49,8,3072]{2,1,0:T(8,128)(2,1)S(1)}, bf16[49,8,3072]{2,1,0:T(8,128)(2,1)S(1)}, f32[8,128]{1,0:T(8,128)S(1)}) custom-call(s32[1]{0:T(128)} %bitcast.36.refs_0_, bf16[8,96,512]{2,1,0:T(8,128)(2,1)S(1)} %bitcast.170, bf16[8,96,512]{2,1,0:T(8,128)(2,1)S(1)} %bitcast.169, bf16[8,96,384]{2,1,0:T(8,128)(2,1)S(1)} %bitcast.175, ...), custom_call_target="tpu_custom_call" | custom-call | flops 4600000000 | bytes 1000 | tf_op jit(solution)/shard_map/grad_heads/pallas_call | solution.py:249
  285.4 2.2 collective-permute-done.27.refs_2_
  289.9 4.8 %collective-permute-done.26.refs_2_ = bf16[13,8,3072]{2,1,0:T(8,128)(2,1)S(1)} collective-permute-done((bf16[13,8,3072]{2,1,0:T(8,128)(2,1)S(1)}, bf16[13,8,3072]{2,1,0:T(8,128)(2,1)S(1)}, u32[]{:S(2)}, u32[]{:S(2)}) %collective-permute-start.26) | collective-permute-done | bytes 639008 | tf_op jit(solution)/shard_map/ppermute | solution.py:908
  294.7 1.6 advance.24
  296.4 2.1 advance.25
  298.6 3.6 collective-permute-start.22
  302.1 11.6 %collective-permute-done.29.refs_2_ = bf16[4,2,4,24,768]{4,3,2,1,0:T(8,128)(2,1)S(1)} collective-permute-done((bf16[4,2,4,24,768]{4,3,2,1,0:T(8,128)(2,1)S(1)}, bf16[4,2,4,24,768]{4,3,2,1,0:T(8,128)(2,1)S(1)}, u32[]{:S(2)}, u32[]{:S(2)}) %collective-permute-start.29) | collective-permute-done | bytes 1179680 | tf_op jit(solution)/shard_map/ppermute | solution.py:908
  316.1 1.6 collective-permute-start.31
  318.4 1.6 collective-permute-done.28.refs_2_
  322.0 16.4 %collective-permute-done.31.refs_2_ = bf16[2,2,4,24,768]{4,3,2,1,0:T(8,128)(2,1)} collective-permute-done((bf16[2,2,4,24,768]{4,3,2,1,0:T(8,128)(2,1)}, bf16[2,2,4,24,768]{4,3,2,1,0:T(8,128)(2,1)}, u32[]{:S(2)}, u32[]{:S(2)}) %collective-permute-start.31) | collective-permute-done | bytes 589856 | tf_op jit(solution)/shard_map/ppermute | solution.py:908
  339.8 3.2 convert_add_fusion
  343.8 2.2 collective-permute-start.32
  346.0 7.4 %collective-permute-done.33.refs_2_ = bf16[204,8,128]{2,1,0:T(8,128)(2,1)S(1)} collective-permute-done((bf16[204,8,128]{2,1,0:T(8,128)(2,1)}, bf16[204,8,128]{2,1,0:T(8,128)(2,1)S(1)}, u32[]{:S(2)}, u32[]{:S(2)}) %collective-permute-start.33) | collective-permute-done | bytes 417824 | tf_op jit(solution)/shard_map/ppermute | solution.py:908
  354.6 10.4 %collective-permute-done.32.refs_2_ = bf16[204,8,128]{2,1,0:T(8,128)(2,1)S(1)} collective-permute-done((bf16[204,8,128]{2,1,0:T(8,128)(2,1)S(1)}, bf16[204,8,128]{2,1,0:T(8,128)(2,1)S(1)}, u32[]{:S(2)}, u32[]{:S(2)}) %collective-permute-start.32) | collective-permute-done | bytes 417824 | tf_op jit(solution)/shard_map/ppermute | solution.py:908
  371.0 7.1 %collective-permute-done.34 = bf16[108,8,128]{2,1,0:T(8,128)(2,1)S(1)} collective-permute-done((bf16[108,8,128]{2,1,0:T(8,128)(2,1)S(1)}, bf16[108,8,128]{2,1,0:T(8,128)(2,1)S(1)}, u32[]{:S(2)}, u32[]{:S(2)}) %collective-permute-start.34) | collective-permute-done | bytes 221216 | tf_op jit(solution)/shard_map/ppermute | solution.py:908
  (345 shorter events, 78.5 us)
Async XLA Ops:
  0.7 7.5 %copy-start.10 = (bf16[512,768]{1,0:T(8,128)(2,1)S(1)}, bf16[512,768]{1,0:T(8,128)(2,1)}, u32[]{:S(2)}) copy-start(bf16[512,768]{1,0:T(8,128)(2,1)} %refs_0_.2) | copy-start | bytes 2359300
  0.7 11.8 %copy-start.83 = (bf16[2,3072]{1,0:T(2,128)(2,1)S(1)}, bf16[2,3072]{1,0:T(2,128)(2,1)}, u32[]{:S(2)}) copy-start(bf16[2,3072]{1,0:T(2,128)(2,1)} %param.24) | copy-start | bytes 36868
  2.5 10.7 %collective-permute-start = (bf16[80,768]{1,0:T(8,128)(2,1)S(1)}, bf16[80,768]{1,0:T(8,128)(2,1)S(1)}, u32[]{:S(2)}, u32[]{:S(2)}) collective-permute-start(bf16[80,768]{1,0:T(8,128)(2,1)S(1)} %fusion.6), channel_id=1, source_target_pairs={{0,1},{1,0},{2,3},{3,2},{4,5},{5,4},{6,7},{7,6},{8,9},{9,8},{10,11... | collective-permute-start | bytes 368648 | tf_op jit(solution)/shard_map/ppermute | solution.py:27
  5.5 12.3 %collective-permute-start.1 = (bf16[80,768]{1,0:T(8,128)(2,1)S(1)}, bf16[80,768]{1,0:T(8,128)(2,1)S(1)}, u32[]{:S(2)}, u32[]{:S(2)}) collective-permute-start(bf16[80,768]{1,0:T(8,128)(2,1)S(1)} %fusion.6), channel_id=1, source_target_pairs={{0,2},{1,3},{2,0},{3,1},{4,6},{5,7},{6,4},{7,5},{8,10},{9,11},{10,... | collective-permute-start | bytes 368648 | tf_op jit(solution)/shard_map/ppermute | solution.py:27
  8.1 10.4 %collective-permute-start.2 = (bf16[80,768]{1,0:T(8,128)(2,1)S(1)}, bf16[80,768]{1,0:T(8,128)(2,1)S(1)}, u32[]{:S(2)}, u32[]{:S(2)}) collective-permute-start(bf16[80,768]{1,0:T(8,128)(2,1)S(1)} %fusion.6), channel_id=1, source_target_pairs={{0,3},{1,2},{2,1},{3,0},{4,7},{5,6},{6,5},{7,4},{8,11},{9,10},{10,... | collective-permute-start | bytes 368648 | tf_op jit(solution)/shard_map/ppermute | solution.py:27
  9.0 33.2 %collective-permute-start.8 = (bf16[384,768]{1,0:T(8,128)(2,1)}, bf16[384,768]{1,0:T(8,128)(2,1)}, u32[]{:S(2)}, u32[]{:S(2)}) collective-permute-start(bf16[384,768]{1,0:T(8,128)(2,1)} %constant_dynamic-slice_fusion.3), channel_id=1, source_target_pairs={{0,1},{1,0},{2,3},{3,2},{4,5},{5,4},{6,7},{7,6},{8,9},{9,8},{10,11... | collective-permute-start | bytes 1769480 | tf_op jit(solution)/shard_map/ppermute | solution.py:27
  19.2 5.4 %collective-permute-start.3 = (bf16[1,3,3,24,384]{4,3,2,1,0:T(8,128)(2,1)S(1)}, bf16[1,3,3,24,384]{4,3,2,1,0:T(8,128)(2,1)S(1)}, u32[]{:S(2)}, u32[]{:S(2)}) collective-permute-start(bf16[1,3,3,24,384]{4,3,2,1,0:T(8,128)(2,1)S(1)} %get-tuple-element.286), channel_id=1, source_target_pairs={{0,8},{4,12},{8,0},{12,4},{16,24},{20,28},{24,16},{28,20},{1,9},{5... | collective-permute-start | bytes 497672 | tf_op jit(solution)/shard_map/ppermute | solution.py:27
  20.8 7.1 %collective-permute-start.5 = (bf16[1,3,3,24,384]{4,3,2,1,0:T(8,128)(2,1)S(1)}, bf16[1,3,3,24,384]{4,3,2,1,0:T(8,128)(2,1)S(1)}, u32[]{:S(2)}, u32[]{:S(2)}) collective-permute-start(bf16[1,3,3,24,384]{4,3,2,1,0:T(8,128)(2,1)S(1)} %get-tuple-element.287), channel_id=1, source_target_pairs={{0,16},{4,20},{8,24},{12,28},{16,0},{20,4},{24,8},{28,12},{1,17},{... | collective-permute-start | bytes 497672 | tf_op jit(solution)/shard_map/ppermute | solution.py:27
  24.7 7.6 %collective-permute-start.4 = (bf16[2,3,3,24,384]{4,3,2,1,0:T(8,128)(2,1)S(1)}, bf16[2,3,3,24,384]{4,3,2,1,0:T(8,128)(2,1)S(1)}, u32[]{:S(2)}, u32[]{:S(2)}) collective-permute-start(bf16[2,3,3,24,384]{4,3,2,1,0:T(8,128)(2,1)S(1)} %pad_maximum_fusion.5), channel_id=1, source_target_pairs={{0,16},{4,20},{8,24},{12,28},{16,0},{20,4},{24,8},{28,12},{1,17},{... | collective-permute-start | bytes 995336 | tf_op jit(solution)/shard_map/ppermute | solution.py:27
  28.0 7.2 %collective-permute-start.6 = (bf16[2,3,3,24,384]{4,3,2,1,0:T(8,128)(2,1)S(1)}, bf16[2,3,3,24,384]{4,3,2,1,0:T(8,128)(2,1)S(1)}, u32[]{:S(2)}, u32[]{:S(2)}) collective-permute-start(bf16[2,3,3,24,384]{4,3,2,1,0:T(8,128)(2,1)S(1)} %pad_maximum_fusion.6), channel_id=1, source_target_pairs={{0,8},{4,12},{8,0},{12,4},{16,24},{20,28},{24,16},{28,20},{1,9},{5... | collective-permute-start | bytes 995336 | tf_op jit(solution)/shard_map/ppermute | solution.py:27
  37.4 8.1 %collective-permute-start.7 = (bf16[2,4,3,3,24,384]{5,4,3,2,1,0:T(8,128)(2,1)}, bf16[2,4,3,3,24,384]{5,4,3,2,1,0:T(8,128)(2,1)}, u32[]{:S(2)}, u32[]{:S(2)}) collective-permute-start(bf16[2,4,3,3,24,384]{5,4,3,2,1,0:T(8,128)(2,1)} %pad_maximum_fusion.1), channel_id=1, source_target_pairs={{0,4},{4,0},{8,12},{12,8},{16,20},{20,16},{24,28},{28,24},{1,5},{5... | collective-permute-start | bytes 3981320 | tf_op jit(solution)/shard_map/ppermute | solution.py:27
  48.3 23.1 %collective-permute-start.10 = (bf16[3,96,768]{2,1,0:T(8,128)(2,1)S(1)}, bf16[3,96,768]{2,1,0:T(8,128)(2,1)S(1)}, u32[]{:S(2)}, u32[]{:S(2)}) collective-permute-start(bf16[3,96,768]{2,1,0:T(8,128)(2,1)S(1)} %get-tuple-element.150), channel_id=1, source_target_pairs={{0,2},{1,3},{2,0},{3,1},{4,6},{5,7},{6,4},{7,5},{8,10},{9,11},{10,... | collective-permute-start | bytes 1327112 | tf_op jit(solution)/shard_map/ppermute | solution.py:27
  50.1 35.9 %collective-permute-start.9 = (bf16[3,96,768]{2,1,0:T(8,128)(2,1)S(1)}, bf16[3,96,768]{2,1,0:T(8,128)(2,1)S(1)}, u32[]{:S(2)}, u32[]{:S(2)}) collective-permute-start(bf16[3,96,768]{2,1,0:T(8,128)(2,1)S(1)} %get-tuple-element.150), channel_id=1, source_target_pairs={{0,1},{1,0},{2,3},{3,2},{4,5},{5,4},{6,7},{7,6},{8,9},{9,8},{10,11... | collective-permute-start | bytes 1327112 | tf_op jit(solution)/shard_map/ppermute | solution.py:27
  56.8 9.9 %copy-start.35 = (bf16[384,1536]{1,0:T(8,128)(2,1)}, bf16[384,1536]{1,0:T(8,128)(2,1)S(1)}, u32[]{:S(2)}) copy-start(bf16[384,1536]{1,0:T(8,128)(2,1)S(1)} %fusion.2.refs_4_) | copy-start | bytes 3538948
  71.4 14.5 %collective-permute-start.11 = (bf16[3,96,768]{2,1,0:T(8,128)(2,1)S(1)}, bf16[3,96,768]{2,1,0:T(8,128)(2,1)S(1)}, u32[]{:S(2)}, u32[]{:S(2)}) collective-permute-start(bf16[3,96,768]{2,1,0:T(8,128)(2,1)S(1)} %collective-permute-done.10.refs_1_), channel_id=1, source_target_pairs={{0,1},{1,0},{2,3},{3,2},{4,5},{5,4},{6,7},{7,6},{8,9},{9,8},{10,11... | collective-permute-start | bytes 1327112 | tf_op jit(solution)/shard_map/ppermute | solution.py:27
  86.0 3.3 collective-permute-start.12
  86.9 15.5 %collective-permute-start.13 = (bf16[384,768]{1,0:T(8,128)(2,1)S(1)}, bf16[384,768]{1,0:T(8,128)(2,1)S(1)}, u32[]{:S(2)}, u32[]{:S(2)}) collective-permute-start(bf16[384,768]{1,0:T(8,128)(2,1)S(1)} %constant_dynamic-slice_fusion.2), channel_id=1, source_target_pairs={{0,1},{1,0},{2,3},{3,2},{4,5},{5,4},{6,7},{7,6},{8,9},{9,8},{10,11... | collective-permute-start | bytes 1769480 | tf_op jit(solution)/shard_map/ppermute | solution.py:27
  90.4 12.0 %copy-start.75 = (bf16[2,4,2,96,768]{4,3,2,1,0:T(8,128)(2,1)}, bf16[2,4,2,96,768]{4,3,2,1,0:T(8,128)(2,1)S(1)}, u32[]{:S(2)}) copy-start(bf16[2,4,2,96,768]{4,3,2,1,0:T(8,128)(2,1)S(1)} %slice.183) | copy-start | bytes 7077892
  94.1 9.4 %copy-start.55 = (bf16[512,2304]{1,0:T(8,128)(2,1)}, bf16[512,2304]{1,0:T(8,128)(2,1)S(1)}, u32[]{:S(2)}) copy-start(bf16[512,2304]{1,0:T(8,128)(2,1)S(1)} %fusion.1.refs_3_) | copy-start | bytes 7077892
  103.5 9.7 %copy-start.37 = (bf16[384,1536]{1,0:T(8,128)(2,1)}, bf16[384,1536]{1,0:T(8,128)(2,1)S(1)}, u32[]{:S(2)}) copy-start(bf16[384,1536]{1,0:T(8,128)(2,1)S(1)} %fusion.3.refs_4_) | copy-start | bytes 3538948
  115.3 16.6 %copy-start.14 = (bf16[512,768]{1,0:T(8,128)(2,1)S(1)}, bf16[512,768]{1,0:T(8,128)(2,1)}, u32[]{:S(2)}) copy-start(bf16[512,768]{1,0:T(8,128)(2,1)} %refs_0_.3) | copy-start | bytes 2359300
  131.9 16.0 %copy-start.17 = (bf16[3072,512]{1,0:T(8,128)(2,1)S(1)}, bf16[3072,512]{1,0:T(8,128)(2,1)}, u32[]{:S(2)}) copy-start(bf16[3072,512]{1,0:T(8,128)(2,1)} %get-tuple-element.170) | copy-start | bytes 9437188
  156.1 4.9 %collective-permute-start.15 = (bf16[4,4,4,24,768]{4,3,2,1,0:T(8,128)(2,1)}, bf16[4,4,4,24,768]{4,3,2,1,0:T(8,128)(2,1)}, u32[]{:S(2)}, u32[]{:S(2)}) collective-permute-start(bf16[4,4,4,24,768]{4,3,2,1,0:T(8,128)(2,1)} %get-tuple-element.179), channel_id=1, source_target_pairs={{0,4},{4,0},{8,12},{12,8},{16,20},{20,16},{24,28},{28,24},{1,5},{5... | collective-permute-start | bytes 7077896 | tf_op jit(solution)/shard_map/ppermute | solution.py:27
  156.1 8.2 %collective-permute-start.14 = (bf16[4,4,4,24,768]{4,3,2,1,0:T(8,128)(2,1)}, bf16[4,4,4,24,768]{4,3,2,1,0:T(8,128)(2,1)}, u32[]{:S(2)}, u32[]{:S(2)}) collective-permute-start(bf16[4,4,4,24,768]{4,3,2,1,0:T(8,128)(2,1)} %get-tuple-element.178), channel_id=1, source_target_pairs={{0,4},{4,0},{8,12},{12,8},{16,20},{20,16},{24,28},{28,24},{1,5},{5... | collective-permute-start | bytes 7077896 | tf_op jit(solution)/shard_map/ppermute | solution.py:27
  166.0 6.7 %copy-start.38 = (bf16[384,1536]{1,0:T(8,128)(2,1)S(1)}, bf16[384,1536]{1,0:T(8,128)(2,1)}, u32[]{:S(2)}) copy-start(bf16[384,1536]{1,0:T(8,128)(2,1)} %copy-done.37) | copy-start | bytes 3538948
  166.0 6.7 %copy-start.56 = (bf16[512,2304]{1,0:T(8,128)(2,1)S(1)}, bf16[512,2304]{1,0:T(8,128)(2,1)}, u32[]{:S(2)}) copy-start(bf16[512,2304]{1,0:T(8,128)(2,1)} %copy-done.55) | copy-start | bytes 7077892
  166.0 6.7 %copy-start.60 = (bf16[512,768]{1,0:T(8,128)(2,1)S(1)}, bf16[512,768]{1,0:T(8,128)(2,1)}, u32[]{:S(2)}) copy-start(bf16[512,768]{1,0:T(8,128)(2,1)} %copy-done.59) | copy-start | bytes 2359300
  166.0 6.7 %copy-start.66 = (f32[768,512]{1,0:T(8,128)S(1)}, f32[768,512]{1,0:T(8,128)}, u32[]{:S(2)}) copy-start(f32[768,512]{1,0:T(8,128)} %copy-done.65) | copy-start | bytes 4718596
  172.4 29.2 %collective-permute-start.17 = (bf16[8,2,4,24,768]{4,3,2,1,0:T(8,128)(2,1)}, bf16[8,2,4,24,768]{4,3,2,1,0:T(8,128)(2,1)}, u32[]{:S(2)}, u32[]{:S(2)}) collective-permute-start(bf16[8,2,4,24,768]{4,3,2,1,0:T(8,128)(2,1)} %get-tuple-element.189), channel_id=1, source_target_pairs={{0,8},{4,20},{8,0},{12,28},{16,24},{20,4},{24,16},{28,12},{1,9},{5... | collective-permute-start | bytes 7077896 | tf_op jit(solution)/shard_map/ppermute | solution.py:908
  172.7 14.7 %copy-start.76 = (bf16[2,4,2,96,768]{4,3,2,1,0:T(8,128)(2,1)S(1)}, bf16[2,4,2,96,768]{4,3,2,1,0:T(8,128)(2,1)}, u32[]{:S(2)}) copy-start(bf16[2,4,2,96,768]{4,3,2,1,0:T(8,128)(2,1)} %copy-done.75) | copy-start | bytes 7077892
  187.3 7.9 %copy-start.47 = (bf16[512,2304]{1,0:T(8,128)(2,1)}, bf16[512,2304]{1,0:T(8,128)(2,1)S(1)}, u32[]{:S(2)}) copy-start(bf16[512,2304]{1,0:T(8,128)(2,1)S(1)} %get-tuple-element.182.refs_5_) | copy-start | bytes 7077892
  188.4 6.7 %copy-start.15 = (bf16[384,768]{1,0:T(8,128)(2,1)}, bf16[384,768]{1,0:T(8,128)(2,1)S(1)}, u32[]{:S(2)}) copy-start(bf16[384,768]{1,0:T(8,128)(2,1)S(1)} %convolution_convert_fusion.1.refs_8_) | copy-start | bytes 1769476
  195.2 34.2 %collective-permute-start.19 = (bf16[49,8,3072]{2,1,0:T(8,128)(2,1)}, bf16[49,8,3072]{2,1,0:T(8,128)(2,1)}, u32[]{:S(2)}, u32[]{:S(2)}) collective-permute-start(bf16[49,8,3072]{2,1,0:T(8,128)(2,1)} %get-tuple-element.205), channel_id=1, source_target_pairs={{0,4},{4,0},{8,12},{12,8},{16,20},{20,16},{24,28},{28,24},{1,5},{5... | collective-permute-start | bytes 7225352 | tf_op jit(solution)/shard_map/ppermute | solution.py:27
  197.3 15.8 %collective-permute-start.16 = (bf16[384,768]{1,0:T(8,128)(2,1)}, bf16[384,768]{1,0:T(8,128)(2,1)S(1)}, u32[]{:S(2)}, u32[]{:S(2)}) collective-permute-start(bf16[384,768]{1,0:T(8,128)(2,1)} %copy-done.15), channel_id=1, source_target_pairs={{0,1},{1,0},{2,3},{3,2},{4,5},{5,4},{6,7},{7,6},{8,9},{9,8},{10,11... | collective-permute-start | bytes 1769480 | tf_op jit(solution)/shard_map/ppermute | solution.py:27
  205.6 27.1 %collective-permute-start.18 = (bf16[4,2,4,24,768]{4,3,2,1,0:T(8,128)(2,1)S(1)}, bf16[4,2,4,24,768]{4,3,2,1,0:T(8,128)(2,1)S(1)}, u32[]{:S(2)}, u32[]{:S(2)}) collective-permute-start(bf16[4,2,4,24,768]{4,3,2,1,0:T(8,128)(2,1)S(1)} %get-tuple-element.203), channel_id=1, source_target_pairs={{0,16},{4,12},{8,24},{12,4},{16,0},{20,28},{24,8},{28,20},{1,17},{... | collective-permute-start | bytes 3538952 | tf_op jit(solution)/shard_map/ppermute | solution.py:908
  243.1 5.3 %collective-permute-start.21 = (bf16[4,4,4,24,768]{4,3,2,1,0:T(8,128)(2,1)}, bf16[4,4,4,24,768]{4,3,2,1,0:T(8,128)(2,1)}, u32[]{:S(2)}, u32[]{:S(2)}) collective-permute-start(bf16[4,4,4,24,768]{4,3,2,1,0:T(8,128)(2,1)} %get-tuple-element.215), channel_id=1, source_target_pairs={{0,4},{4,0},{8,12},{12,8},{16,20},{20,16},{24,28},{28,24},{1,5},{5... | collective-permute-start | bytes 7077896 | tf_op jit(solution)/shard_map/ppermute | solution.py:27
  243.1 8.2 %collective-permute-start.20 = (bf16[4,4,4,24,768]{4,3,2,1,0:T(8,128)(2,1)}, bf16[4,4,4,24,768]{4,3,2,1,0:T(8,128)(2,1)}, u32[]{:S(2)}, u32[]{:S(2)}) collective-permute-start(bf16[4,4,4,24,768]{4,3,2,1,0:T(8,128)(2,1)} %get-tuple-element.214), channel_id=1, source_target_pairs={{0,4},{4,0},{8,12},{12,8},{16,20},{20,16},{24,28},{28,24},{1,5},{5... | collective-permute-start | bytes 7077896 | tf_op jit(solution)/shard_map/ppermute | solution.py:27
  243.7 30.6 %collective-permute-start.24 = (bf16[25,8,3072]{2,1,0:T(8,128)(2,1)}, bf16[25,8,3072]{2,1,0:T(8,128)(2,1)S(1)}, u32[]{:S(2)}, u32[]{:S(2)}) collective-permute-start(bf16[25,8,3072]{2,1,0:T(8,128)(2,1)} %copy-done.13), channel_id=1, source_target_pairs={{0,8},{4,20},{8,0},{12,28},{16,24},{20,4},{24,16},{28,12},{1,9},{5... | collective-permute-start | bytes 3686408 | tf_op jit(solution)/shard_map/ppermute | solution.py:908
  246.7 32.1 %collective-permute-start.23 = (bf16[2,2,4,24,768]{4,3,2,1,0:T(8,128)(2,1)}, bf16[2,2,4,24,768]{4,3,2,1,0:T(8,128)(2,1)S(1)}, u32[]{:S(2)}, u32[]{:S(2)}) collective-permute-start(bf16[2,2,4,24,768]{4,3,2,1,0:T(8,128)(2,1)} %get-tuple-element.227), channel_id=1, source_target_pairs={{0,1},{1,0},{2,3},{3,2},{4,5},{5,4},{6,7},{7,6},{8,9},{9,8},{10,11... | collective-permute-start | bytes 1769480 | tf_op jit(solution)/shard_map/ppermute | solution.py:908
  253.0 6.7 %copy-start.36 = (bf16[384,1536]{1,0:T(8,128)(2,1)S(1)}, bf16[384,1536]{1,0:T(8,128)(2,1)}, u32[]{:S(2)}) copy-start(bf16[384,1536]{1,0:T(8,128)(2,1)} %copy-done.35) | copy-start | bytes 3538948
  253.0 6.7 %copy-start.54 = (bf16[512,768]{1,0:T(8,128)(2,1)S(1)}, bf16[512,768]{1,0:T(8,128)(2,1)}, u32[]{:S(2)}) copy-start(bf16[512,768]{1,0:T(8,128)(2,1)} %copy-done.53) | copy-start | bytes 2359300
  253.1 6.7 %copy-start.62 = (bf16[512,2304]{1,0:T(8,128)(2,1)S(1)}, bf16[512,2304]{1,0:T(8,128)(2,1)}, u32[]{:S(2)}) copy-start(bf16[512,2304]{1,0:T(8,128)(2,1)} %copy-done.61) | copy-start | bytes 7077892
  253.1 6.7 %copy-start.64 = (f32[768,512]{1,0:T(8,128)S(1)}, f32[768,512]{1,0:T(8,128)}, u32[]{:S(2)}) copy-start(f32[768,512]{1,0:T(8,128)} %copy-done.63) | copy-start | bytes 4718596
  253.1 6.7 %copy-start.68 = (f32[4,8,256]{2,1,0:T(8,128)S(1)}, f32[4,8,256]{2,1,0:T(8,128)}, u32[]{:S(2)}) copy-start(f32[4,8,256]{2,1,0:T(8,128)} %copy-done.67) | copy-start | bytes 98308
  256.7 31.0 %collective-permute-start.27 = (bf16[8,2,4,24,768]{4,3,2,1,0:T(8,128)(2,1)S(1)}, bf16[8,2,4,24,768]{4,3,2,1,0:T(8,128)(2,1)S(1)}, u32[]{:S(2)}, u32[]{:S(2)}) collective-permute-start(bf16[8,2,4,24,768]{4,3,2,1,0:T(8,128)(2,1)S(1)} %get-tuple-element.238), channel_id=1, source_target_pairs={{0,8},{4,20},{8,0},{12,28},{16,24},{20,4},{24,16},{28,12},{1,9},{5... | collective-permute-start | bytes 7077896 | tf_op jit(solution)/shard_map/ppermute | solution.py:908
  259.7 14.6 %copy-start.12 = (bf16[25,8,3072]{2,1,0:T(8,128)(2,1)S(1)}, bf16[25,8,3072]{2,1,0:T(8,128)(2,1)}, u32[]{:S(2)}) copy-start(bf16[25,8,3072]{2,1,0:T(8,128)(2,1)} %copy-done.11) | copy-start | bytes 3686404
  284.2 12.2 %collective-permute-start.25 = (bf16[49,8,3072]{2,1,0:T(8,128)(2,1)S(1)}, bf16[49,8,3072]{2,1,0:T(8,128)(2,1)S(1)}, u32[]{:S(2)}, u32[]{:S(2)}) collective-permute-start(bf16[49,8,3072]{2,1,0:T(8,128)(2,1)S(1)} %get-tuple-element.234), channel_id=1, source_target_pairs={{0,4},{4,0},{8,12},{12,8},{16,20},{20,16},{24,28},{28,24},{1,5},{5... | collective-permute-start | bytes 7225352 | tf_op jit(solution)/shard_map/ppermute | solution.py:27
  284.2 10.5 %collective-permute-start.26 = (bf16[13,8,3072]{2,1,0:T(8,128)(2,1)S(1)}, bf16[13,8,3072]{2,1,0:T(8,128)(2,1)S(1)}, u32[]{:S(2)}, u32[]{:S(2)}) collective-permute-start(bf16[13,8,3072]{2,1,0:T(8,128)(2,1)S(1)} %get-tuple-element.236), channel_id=1, source_target_pairs={{0,16},{4,12},{8,24},{12,4},{16,0},{20,28},{24,8},{28,20},{1,17},{... | collective-permute-start | bytes 1916936 | tf_op jit(solution)/shard_map/ppermute | solution.py:908
  288.7 25.0 %collective-permute-start.29 = (bf16[4,2,4,24,768]{4,3,2,1,0:T(8,128)(2,1)S(1)}, bf16[4,2,4,24,768]{4,3,2,1,0:T(8,128)(2,1)S(1)}, u32[]{:S(2)}, u32[]{:S(2)}) collective-permute-start(bf16[4,2,4,24,768]{4,3,2,1,0:T(8,128)(2,1)S(1)} %get-tuple-element.245), channel_id=1, source_target_pairs={{0,16},{4,12},{8,24},{12,4},{16,0},{20,28},{24,8},{28,20},{1,17},{... | collective-permute-start | bytes 3538952 | tf_op jit(solution)/shard_map/ppermute | solution.py:908
  298.5 21.5 %collective-permute-start.28 = (bf16[25,8,3072]{2,1,0:T(8,128)(2,1)}, bf16[25,8,3072]{2,1,0:T(8,128)(2,1)S(1)}, u32[]{:S(2)}, u32[]{:S(2)}) collective-permute-start(bf16[25,8,3072]{2,1,0:T(8,128)(2,1)} %get-tuple-element.243), channel_id=1, source_target_pairs={{0,8},{4,20},{8,0},{12,28},{16,24},{20,4},{24,16},{28,12},{1,9},{5... | collective-permute-start | bytes 3686408 | tf_op jit(solution)/shard_map/ppermute | solution.py:908
  298.6 19.1 %collective-permute-start.22 = (bf16[384,768]{1,0:T(8,128)(2,1)}, bf16[384,768]{1,0:T(8,128)(2,1)S(1)}, u32[]{:S(2)}, u32[]{:S(2)}) collective-permute-start(bf16[384,768]{1,0:T(8,128)(2,1)} %convolution_convert_fusion.refs_8_), channel_id=1, source_target_pairs={{0,1},{1,0},{2,3},{3,2},{4,5},{5,4},{6,7},{7,6},{8,9},{9,8},{10,11... | collective-permute-start | bytes 1769480 | tf_op jit(solution)/shard_map/ppermute | solution.py:27
  316.1 22.4 %collective-permute-start.31 = (bf16[2,2,4,24,768]{4,3,2,1,0:T(8,128)(2,1)}, bf16[2,2,4,24,768]{4,3,2,1,0:T(8,128)(2,1)}, u32[]{:S(2)}, u32[]{:S(2)}) collective-permute-start(bf16[2,2,4,24,768]{4,3,2,1,0:T(8,128)(2,1)} %get-tuple-element.251), channel_id=1, source_target_pairs={{0,1},{1,0},{2,3},{3,2},{4,5},{5,4},{6,7},{7,6},{8,9},{9,8},{10,11... | collective-permute-start | bytes 1769480 | tf_op jit(solution)/shard_map/ppermute | solution.py:908
  317.7 48.5 %collective-permute-start.37 = (bf16[1,2,4,24,768]{4,3,2,1,0:T(8,128)(2,1)}, bf16[1,2,4,24,768]{4,3,2,1,0:T(8,128)(2,1)}, u32[]{:S(2)}, u32[]{:S(2)}) collective-permute-start(bf16[1,2,4,24,768]{4,3,2,1,0:T(8,128)(2,1)} %get-tuple-element.269), channel_id=1, source_target_pairs={{0,2},{1,3},{2,0},{3,1},{4,6},{5,7},{6,4},{7,5},{8,10},{9,11},{10,... | collective-permute-start | bytes 884744 | tf_op jit(solution)/shard_map/ppermute | solution.py:908
  317.7 22.0 %copy-start.46 = (bf16[512,2304]{1,0:T(8,128)(2,1)S(1)}, bf16[512,2304]{1,0:T(8,128)(2,1)}, u32[]{:S(2)}) copy-start(bf16[512,2304]{1,0:T(8,128)(2,1)} %copy-done.45) | copy-start | bytes 7077892
  317.8 20.7 %copy-start.33 = (bf16[2,2,4,24,768]{4,3,2,1,0:T(8,128)(2,1)S(1)}, bf16[2,2,4,24,768]{4,3,2,1,0:T(8,128)(2,1)}, u32[]{:S(2)}) copy-start(bf16[2,2,4,24,768]{4,3,2,1,0:T(8,128)(2,1)} %copy-done.32) | copy-start | bytes 1769476
  317.8 35.6 %collective-permute-start.33 = (bf16[204,8,128]{2,1,0:T(8,128)(2,1)}, bf16[204,8,128]{2,1,0:T(8,128)(2,1)S(1)}, u32[]{:S(2)}, u32[]{:S(2)}) collective-permute-start(bf16[204,8,128]{2,1,0:T(8,128)(2,1)} %get-tuple-element.257), channel_id=1, source_target_pairs={{0,1},{1,0},{2,3},{3,2},{4,5},{5,4},{6,7},{7,6},{8,9},{9,8},{10,11... | collective-permute-start | bytes 1253384 | tf_op jit(solution)/shard_map/ppermute | solution.py:908
  320.0 19.8 %copy-start.7 = (bf16[3,4,8,24,768]{4,3,2,1,0:T(8,128)(2,1)S(1)}, bf16[3,4,8,24,768]{4,3,2,1,0:T(8,128)(2,1)}, u32[]{:S(2)}) copy-start(bf16[3,4,8,24,768]{4,3,2,1,0:T(8,128)(2,1)} %copy-done.6) | copy-start | bytes 10616836
  320.0 19.8 %copy-start.41 = (f32[512,768]{1,0:T(8,128)S(1)}, f32[512,768]{1,0:T(8,128)}, u32[]{:S(2)}) copy-start(f32[512,768]{1,0:T(8,128)} %copy-done.40) | copy-start | bytes 4718596
  320.8 22.1 %collective-permute-start.30 = (bf16[13,8,3072]{2,1,0:T(8,128)(2,1)S(1)}, bf16[13,8,3072]{2,1,0:T(8,128)(2,1)S(1)}, u32[]{:S(2)}, u32[]{:S(2)}) collective-permute-start(bf16[13,8,3072]{2,1,0:T(8,128)(2,1)S(1)} %get-tuple-element.249), channel_id=1, source_target_pairs={{0,16},{4,12},{8,24},{12,4},{16,0},{20,28},{24,8},{28,20},{1,17},{... | collective-permute-start | bytes 1916936 | tf_op jit(solution)/shard_map/ppermute | solution.py:908
  339.7 14.5 %collective-permute-start.36 = (bf16[1,2,4,24,768]{4,3,2,1,0:T(8,128)(2,1)S(1)}, bf16[1,2,4,24,768]{4,3,2,1,0:T(8,128)(2,1)S(1)}, u32[]{:S(2)}, u32[]{:S(2)}) collective-permute-start(bf16[1,2,4,24,768]{4,3,2,1,0:T(8,128)(2,1)S(1)} %get-tuple-element.267), channel_id=1, source_target_pairs={{0,2},{1,3},{2,0},{3,1},{4,6},{5,7},{6,4},{7,5},{8,10},{9,11},{10,... | collective-permute-start | bytes 884744 | tf_op jit(solution)/shard_map/ppermute | solution.py:908
  342.9 10.5 %copy-start.44 = (bf16[204,8,128]{2,1,0:T(8,128)(2,1)S(1)}, bf16[204,8,128]{2,1,0:T(8,128)(2,1)}, u32[]{:S(2)}) copy-start(bf16[204,8,128]{2,1,0:T(8,128)(2,1)} %copy-done.43) | copy-start | bytes 1253380
  343.8 21.2 %collective-permute-start.32 = (bf16[204,8,128]{2,1,0:T(8,128)(2,1)S(1)}, bf16[204,8,128]{2,1,0:T(8,128)(2,1)S(1)}, u32[]{:S(2)}, u32[]{:S(2)}) collective-permute-start(bf16[204,8,128]{2,1,0:T(8,128)(2,1)S(1)} %get-tuple-element.255), channel_id=1, source_target_pairs={{0,1},{1,0},{2,3},{3,2},{4,5},{5,4},{6,7},{7,6},{8,9},{9,8},{10,11... | collective-permute-start | bytes 1253384 | tf_op jit(solution)/shard_map/ppermute | solution.py:908
  354.1 14.8 %collective-permute-start.35 = (bf16[108,8,128]{2,1,0:T(8,128)(2,1)S(1)}, bf16[108,8,128]{2,1,0:T(8,128)(2,1)}, u32[]{:S(2)}, u32[]{:S(2)}) collective-permute-start(bf16[108,8,128]{2,1,0:T(8,128)(2,1)S(1)} %get-tuple-element.265), channel_id=1, source_target_pairs={{0,2},{1,3},{2,0},{3,1},{4,6},{5,7},{6,4},{7,5},{8,10},{9,11},{10,... | collective-permute-start | bytes 663560 | tf_op jit(solution)/shard_map/ppermute | solution.py:908
  367.2 10.9 %collective-permute-start.34 = (bf16[108,8,128]{2,1,0:T(8,128)(2,1)S(1)}, bf16[108,8,128]{2,1,0:T(8,128)(2,1)S(1)}, u32[]{:S(2)}, u32[]{:S(2)}) collective-permute-start(bf16[108,8,128]{2,1,0:T(8,128)(2,1)S(1)} %get-tuple-element.263), channel_id=1, source_target_pairs={{0,2},{1,3},{2,0},{3,1},{4,6},{5,7},{6,4},{7,5},{8,10},{9,11},{10,... | collective-permute-start | bytes 663560 | tf_op jit(solution)/shard_map/ppermute | solution.py:908
  (66 other events, 169.7 us)

commit v6 on v5

--- a/solution.py
+++ b/solution.py
@@ -330,7 +330,7 @@
     )
 
 
-CHUNK = 1536
+CHUNK = 1024
 ROWS = 256
 
 
@@ -437,7 +437,7 @@
             pltpu.VMEM((tokens, width), f32),
             pltpu.VMEM((tokens, width), f32),
         ],
-        compiler_params=pltpu.CompilerParams(vmem_limit_bytes=48 * 2**20),
+        compiler_params=pltpu.CompilerParams(vmem_limit_bytes=30 * 2**20),
         cost_estimate=cost(15),
         name="feed",
     )
@@ -544,7 +544,7 @@
             pl.BlockSpec((1, CHUNK), lambda step: (0, step)),
         ),
         scratch_shapes=[pltpu.VMEM((tokens, width), f32), pltpu.VMEM((tokens, width), f32)],
-        compiler_params=pltpu.CompilerParams(vmem_limit_bytes=48 * 2**20),
+        compiler_params=pltpu.CompilerParams(vmem_limit_bytes=30 * 2**20),
         cost_estimate=cost(17),
         name="feed_back",
     )

time: 388 us -> 378 us (0.974)
  starting transfers between devices: 45.3 us -> 30.4 us
  waiting for transfers between devices: 98.3 us -> 109 us
  Pallas kernels: 162 us -> 154 us
    ppermute x16, starting transfers between devices: 19.3 us -> 11.4 us  [step(): self.keeps, self.gots = ([keep], [lax.ppermute(send, axis_name, pairs)])]
    pallas_call x34, Pallas kernels: 162 us -> 154 us  [ordered_call(): pl.pallas_call(body, out_shape=tuple(out_shape) + (jax.ShapeDtypeStruct((...]
    ppermute x22, starting transfers between devices: 26 us -> 19 us  [swap(): return lax.ppermute(value, axis, [(i, i ^ bit) for i in range(size)])]
    ppermute x16, waiting for transfers between devices: 63.9 us -> 70.2 us  [step(): self.keeps, self.gots = ([keep], [lax.ppermute(send, axis_name, pairs)])]
    ppermute x22, waiting for transfers between devices: 34.4 us -> 38.5 us  [swap(): return lax.ppermute(value, axis, [(i, i ^ bit) for i in range(size)])]
    unnamed x188 -> x200, local copies, waits for them, and re-layouts: 30.2 us -> 31.5 us
  transfers between devices with their start and end apart: 38 -> 38, of which waited for: 21 -> 22; matrix products, arithmetic and copies ran while one was open for 9% -> 10% of each run, Pallas kernels for 27% -> 27%
where the time goes in v6:
time: 378 us; the launch traced here: 372 us
  Pallas kernels  154 us (41%)
  waiting for transfers between devices  109 us (29%)
  local copies, waits for them, and re-layouts  45.3 us (12%)
  starting transfers between devices  30.4 us (8%)
  matrix products  18.2 us (5%)
  other arithmetic  12.2 us (3%)
    pallas_call x34, Pallas kernels, ordered_call(): pl.pallas_call(body, out_shape=tuple(out_shape) + (jax.ShapeDtypeStruct((...  154 us
    ppermute x16, waiting for transfers between devices, step(): self.keeps, self.gots = ([keep], [lax.ppermute(send, axis_name, pairs)])  70.2 us
    ppermute x22, waiting for transfers between devices, swap(): return lax.ppermute(value, axis, [(i, i ^ bit) for i in range(size)])  38.5 us
    unnamed x200, local copies, waits for them, and re-layouts  31.5 us
    ppermute x22, starting transfers between devices, swap(): return lax.ppermute(value, axis, [(i, i ^ bit) for i in range(size)])  19 us
    ppermute x16, starting transfers between devices, step(): self.keeps, self.gots = ([keep], [lax.ppermute(send, axis_name, pairs)])  11.4 us
    dot_general x4, matrix products, nn(): lax.dot_general(left, right, (((1,), (0,)), ((), ())), preferred_element_...  10.4 us
    dot_general x4, matrix products, nt(): lax.dot_general(left, right, (((1,), (1,)), ((), ())), preferred_element_...  7.82 us
  transfers between devices with their start and end apart: 38, of which 22 were waited for; matrix products, arithmetic and copies ran while one was open for 10% of the time, Pallas kernels for 27%

profile of v6, /device:TPU:0, one launch (start us, length us, event | category | flops | bytes accessed | tf_op | source)
XLA Modules:
  0.0 371.7 jit_solution(13287300297272792520)
XLA Ops:
  0.7 1.6 fusion.17
  2.5 3.1 collective-permute-start
  5.5 2.6 collective-permute-start.1
  13.8 4.1 %collective-permute-done.1 = bf16[80,768]{1,0:T(8,128)(2,1)S(1)} collective-permute-done((bf16[80,768]{1,0:T(8,128)(2,1)S(1)}, bf16[80,768]{1,0:T(8,128)(2,1)S(1)}, u32[]{:S(2)}, u32[]{:S(2)}) %collective-permute-start.1) | collective-permute-done | bytes 122912 | tf_op jit(solution)/shard_map/ppermute | solution.py:27
  19.2 1.6 collective-permute-start.3
  20.8 1.5 collective-permute-start.5
  22.3 2.3 collective-permute-done.3
  24.7 1.6 collective-permute-start.4
  26.3 1.6 collective-permute-done.5
  28.9 3.4 collective-permute-done.4
  33.4 1.7 collective-permute-done.6
  45.5 1.6 pad_maximum_fusion
  48.3 1.8 collective-permute-start.10
  52.1 2.0 fusion.4.refs_3_
  54.1 2.6 fusion.2.refs_4_
  56.8 10.7 %attend.2 = (bf16[512,768]{1,0:T(8,128)(2,1)S(1)}, f32[768,512]{1,0:T(8,128)S(1)}, bf16[768,512]{1,0:T(8,128)(2,1)S(1)}, f32[4,8,256]{2,1,0:T(8,128)S(1)}, f32[8,128]{1,0:T(8,128)S(1)}) custom-call(s32[4,4]{1,0:T(4,128)S(1)} %pad_add_fusion.2.refs_0_, s32[4,1,256]{2,1,0:T(1,128)S(1)} %reshape.381.refs_1_, s32[896,1]{1,0:T(8,128)S(1)} %reshape.412.refs_2_, ...), custom_call_target="tpu_custom_call" | custom-call | flops 5175000064 | bytes 1000 | tf_op jit(solution)/shard_map/attend/pallas_call | solution.py:249
  71.5 11.3 %feed.2 = (f32[512,768]{1,0:T(8,128)S(1)}, bf16[768,512]{1,0:T(8,128)(2,1)S(1)}, bf16[3072,512]{1,0:T(8,128)(2,1)S(1)}, f32[512,3072]{1,0:T(8,128)S(1)}, f32[512...) custom-call(bf16[512,768]{1,0:T(8,128)(2,1)S(1)} %copy-done.10, ...), custom_call_target="tpu_custom_call" | custom-call | flops 8625000448 | bytes 1000 | tf_op jit(solution)/shard_map/feed/pallas_call | solution.py:249
  82.8 2.6 copy-done.32
  88.1 2.1 collective-permute-start.13
  92.0 1.6 copy-done.8
  93.7 2.0 fusion.1.refs_3_
  95.7 8.5 %collective-permute-done.13 = bf16[384,768]{1,0:T(8,128)(2,1)S(1)} collective-permute-done((bf16[384,768]{1,0:T(8,128)(2,1)S(1)}, bf16[384,768]{1,0:T(8,128)(2,1)S(1)}, u32[]{:S(2)}, u32[]{:S(2)}) %collective-permute-start.13) | collective-permute-done | bytes 589856 | tf_op jit(solution)/shard_map/ppermute | solution.py:27
  105.4 10.3 %attend.3 = (bf16[512,768]{1,0:T(8,128)(2,1)S(1)}, f32[768,512]{1,0:T(8,128)S(1)}, bf16[768,512]{1,0:T(8,128)(2,1)S(1)}, f32[4,8,256]{2,1,0:T(8,128)S(1)}, f32[8,128]{1,0:T(8,128)S(1)}) custom-call(s32[4,4]{1,0:T(4,128)S(1)} %pad_add_fusion.2.refs_0_, s32[4,1,256]{2,1,0:T(1,128)S(1)} %reshape.381.refs_1_, s32[896,1]{1,0:T(8,128)S(1)} %reshape.412.refs_2_, ...), custom_call_target="tpu_custom_call" | custom-call | flops 5175000064 | bytes 1000 | tf_op jit(solution)/shard_map/attend/pallas_call | solution.py:249
  117.7 12.2 %feed.3 = (f32[512,768]{1,0:T(8,128)S(1)}, bf16[768,512]{1,0:T(8,128)(2,1)S(1)}, bf16[3072,512]{1,0:T(8,128)(2,1)S(1)}, f32[512,3072]{1,0:T(8,128)S(1)}, f32[512...) custom-call(f32[512,768]{1,0:T(8,128)S(1)} %copy-done.66, ...), custom_call_target="tpu_custom_call" | custom-call | flops 8625000448 | bytes 1000 | tf_op jit(solution)/shard_map/feed/pallas_call | solution.py:249
  130.0 12.2 %feed_back.2 = (bf16[512,768]{1,0:T(8,128)(2,1)S(1)}, bf16[512,3072]{1,0:T(8,128)(2,1)S(1)}, bf16[512,768]{1,0:T(8,128)(2,1)S(1)}, f32[512,768]{1,0:T(8,128)S(1)...) custom-call(bf16[512,768]{1,0:T(8,128)(2,1)S(1)} %copy-done.16, ...), custom_call_target="tpu_custom_call" | custom-call | flops 9774999552 | bytes 1000 | tf_op jit(solution)/shard_map/feed_back/pallas_call | solution.py:249
  142.2 2.8 grad_down.2
  145.1 2.8 grad_up.2
  151.2 2.9 collective-permute-done.15
  154.2 3.4 collective-permute-done.14
  157.5 1.7 copy-done.5
  159.2 5.0 %advance.16 = (bf16[8,2,4,24,768]{4,3,2,1,0:T(8,128)(2,1)}, bf16[8,2,4,24,768]{4,3,2,1,0:T(8,128)(2,1)S(1)}, f32[8,128]{1,0:T(8,128)S(1)}) custom-call(s32[2]{0:T(128)S(1)} %pad_add_fusion.5.refs_0_, bf16[16,4,24,768]{3,2,1,0:T(8,128)(2,1)S(1)} %bitcast.157, bf16[16,4,24,768]{3,2,1,0:T(8,128)(2,1)S(1)} %bitcast.159, ...), custom_call_target="tpu_custom_call" | custom-call | flops 1931595264 | bytes 1000 | tf_op jit(solution)/shard_map/advance/pallas_call | solution.py:249
  166.5 16.3 %attend_back.2 = (bf16[512,2304]{1,0:T(8,128)(2,1)S(1)}, bf16[384,1536]{1,0:T(8,128)(2,1)S(1)}, f32[16,768]{1,0:T(8,128)S(1)}, f32[8,128]{1,0:T(8,128)S(1)}) custom-call(s32[4,4]{1,0:T(4,128)S(1)} %pad_add_fusion.2.refs_0_, s32[4,1,256]{2,1,0:T(1,128)S(1)} %reshape.381.refs_1_, s32[896,1]{1,0:T(8,128)S(1)} %reshape.412.refs_2_, ...), custom_call_target="tpu_custom_call" | custom-call | flops 12074999808 | bytes 1000 | tf_op jit(solution)/shard_map/attend_back/pallas_call | solution.py:249
  185.5 5.2 %grad_heads.2 = (bf16[49,8,3072]{2,1,0:T(8,128)(2,1)}, bf16[49,8,3072]{2,1,0:T(8,128)(2,1)S(1)}, f32[8,128]{1,0:T(8,128)S(1)}) custom-call(s32[1]{0:T(128)} %bitcast.36.refs_0_, bf16[8,96,512]{2,1,0:T(8,128)(2,1)S(1)} %bitcast.173, bf16[8,96,512]{2,1,0:T(8,128)(2,1)S(1)} %bitcast.172, bf16[8,96,384]{2,1,0:T(8,128)(2,1)S(1)} %bitcast.166, ...), custom_call_target="tpu_custom_call" | custom-call | flops 4600000000 | bytes 1000 | tf_op jit(solution)/shard_map/grad_heads/pallas_call | solution.py:249
  191.2 3.7 collective-permute-done.17.refs_2_
  194.9 1.7 copy-done.1
  196.5 2.4 advance.17
  200.0 4.3 %convolution_add_fusion.3.refs_0_ = f32[512,768]{1,0:T(8,128)S(1)} fusion(f32[512,768]{1,0:T(8,128)} %copy-done.52, bf16[512,2304]{1,0:T(8,128)(2,1)} %copy-done.51, bf16[2304,768]{1,0:T(8,128)(2,1)S(1)} %bitcast.163), kind=kOutput, calls=%fused_computation.11 | convolution fusion | flops 1812332544 | bytes 9043968 | tf_op jit(solution)/shard_map/dot_general | solution.py:67
  204.3 2.4 collective-permute-done.16.refs_1_
  206.8 12.5 %feed_back.3 = (bf16[512,768]{1,0:T(8,128)(2,1)S(1)}, bf16[512,3072]{1,0:T(8,128)(2,1)S(1)}, bf16[512,768]{1,0:T(8,128)(2,1)S(1)}, f32[512,768]{1,0:T(8,128)S(1)...) custom-call(f32[512,768]{1,0:T(8,128)S(1)} %convolution_add_fusion.3.refs_, ...), custom_call_target="tpu_custom_call" | custom-call | flops 9774999552 | bytes 1000 | tf_op jit(solution)/shard_map/feed_back/pallas_call | solution.py:249
  219.3 3.4 advance.18
  222.8 1.5 advance.19
  225.9 2.8 grad_down.3
  228.7 2.8 grad_up.3
  235.2 2.7 collective-permute-done.21
  237.9 3.4 collective-permute-done.20
  241.3 1.7 copy-done.3
  243.0 3.6 advance.20
  247.9 16.3 %attend_back.3 = (bf16[512,2304]{1,0:T(8,128)(2,1)S(1)}, bf16[384,1536]{1,0:T(8,128)(2,1)S(1)}, f32[16,768]{1,0:T(8,128)S(1)}, f32[8,128]{1,0:T(8,128)S(1)}) custom-call(s32[4,4]{1,0:T(4,128)S(1)} %pad_add_fusion.2.refs_0_, s32[4,1,256]{2,1,0:T(1,128)S(1)} %reshape.381.refs_1_, s32[896,1]{1,0:T(8,128)S(1)} %reshape.412.refs_2_, ...), custom_call_target="tpu_custom_call" | custom-call | flops 12074999808 | bytes 1000 | tf_op jit(solution)/shard_map/attend_back/pallas_call | solution.py:249
  265.1 1.6 copy-done.78
  266.8 1.9 convolution_convert_fusion.refs_8_
  270.2 3.8 %grad_heads.3 = (bf16[49,8,3072]{2,1,0:T(8,128)(2,1)S(1)}, bf16[49,8,3072]{2,1,0:T(8,128)(2,1)S(1)}, f32[8,128]{1,0:T(8,128)S(1)}) custom-call(s32[1]{0:T(128)} %bitcast.36.refs_0_, bf16[8,96,512]{2,1,0:T(8,128)(2,1)S(1)} %bitcast.170, bf16[8,96,512]{2,1,0:T(8,128)(2,1)S(1)} %bitcast.169, bf16[8,96,384]{2,1,0:T(8,128)(2,1)S(1)} %bitcast.175, ...), custom_call_target="tpu_custom_call" | custom-call | flops 4600000000 | bytes 1000 | tf_op jit(solution)/shard_map/grad_heads/pallas_call | solution.py:249
  274.2 1.6 collective-permute-done.27.refs_2_
  278.1 6.5 %collective-permute-done.26.refs_2_ = bf16[13,8,3072]{2,1,0:T(8,128)(2,1)S(1)} collective-permute-done((bf16[13,8,3072]{2,1,0:T(8,128)(2,1)S(1)}, bf16[13,8,3072]{2,1,0:T(8,128)(2,1)S(1)}, u32[]{:S(2)}, u32[]{:S(2)}) %collective-permute-start.26) | collective-permute-done | bytes 639008 | tf_op jit(solution)/shard_map/ppermute | solution.py:908
  284.6 1.6 advance.24
  286.2 2.1 advance.25
  289.4 14.2 %collective-permute-done.29.refs_2_ = bf16[4,2,4,24,768]{4,3,2,1,0:T(8,128)(2,1)S(1)} collective-permute-done((bf16[4,2,4,24,768]{4,3,2,1,0:T(8,128)(2,1)S(1)}, bf16[4,2,4,24,768]{4,3,2,1,0:T(8,128)(2,1)S(1)}, u32[]{:S(2)}, u32[]{:S(2)}) %collective-permute-start.29) | collective-permute-done | bytes 1179680 | tf_op jit(solution)/shard_map/ppermute | solution.py:908
  305.9 1.9 collective-permute-start.37
  308.2 1.7 collective-permute-done.28.refs_2_
  310.8 15.7 %collective-permute-done.31.refs_2_ = bf16[2,2,4,24,768]{4,3,2,1,0:T(8,128)(2,1)} collective-permute-done((bf16[2,2,4,24,768]{4,3,2,1,0:T(8,128)(2,1)}, bf16[2,2,4,24,768]{4,3,2,1,0:T(8,128)(2,1)}, u32[]{:S(2)}, u32[]{:S(2)}) %collective-permute-start.31) | collective-permute-done | bytes 589856 | tf_op jit(solution)/shard_map/ppermute | solution.py:908
  327.9 3.2 convert_add_fusion
  331.9 2.2 collective-permute-start.32
  334.2 7.5 %collective-permute-done.33.refs_2_ = bf16[204,8,128]{2,1,0:T(8,128)(2,1)S(1)} collective-permute-done((bf16[204,8,128]{2,1,0:T(8,128)(2,1)}, bf16[204,8,128]{2,1,0:T(8,128)(2,1)S(1)}, u32[]{:S(2)}, u32[]{:S(2)}) %collective-permute-start.33) | collective-permute-done | bytes 417824 | tf_op jit(solution)/shard_map/ppermute | solution.py:908
  342.8 11.5 %collective-permute-done.32.refs_2_ = bf16[204,8,128]{2,1,0:T(8,128)(2,1)S(1)} collective-permute-done((bf16[204,8,128]{2,1,0:T(8,128)(2,1)S(1)}, bf16[204,8,128]{2,1,0:T(8,128)(2,1)S(1)}, u32[]{:S(2)}, u32[]{:S(2)}) %collective-permute-start.32) | collective-permute-done | bytes 417824 | tf_op jit(solution)/shard_map/ppermute | solution.py:908
  359.8 7.8 %collective-permute-done.34 = bf16[108,8,128]{2,1,0:T(8,128)(2,1)S(1)} collective-permute-done((bf16[108,8,128]{2,1,0:T(8,128)(2,1)S(1)}, bf16[108,8,128]{2,1,0:T(8,128)(2,1)S(1)}, u32[]{:S(2)}, u32[]{:S(2)}) %collective-permute-start.34) | collective-permute-done | bytes 221216 | tf_op jit(solution)/shard_map/ppermute | solution.py:908
  (358 shorter events, 72.3 us)
Async XLA Ops:
  0.7 7.5 %copy-start.10 = (bf16[512,768]{1,0:T(8,128)(2,1)S(1)}, bf16[512,768]{1,0:T(8,128)(2,1)}, u32[]{:S(2)}) copy-start(bf16[512,768]{1,0:T(8,128)(2,1)} %refs_0_.2) | copy-start | bytes 2359300
  0.7 11.8 %copy-start.87 = (bf16[2,3072]{1,0:T(2,128)(2,1)S(1)}, bf16[2,3072]{1,0:T(2,128)(2,1)}, u32[]{:S(2)}) copy-start(bf16[2,3072]{1,0:T(2,128)(2,1)} %param.24) | copy-start | bytes 36868
  2.5 10.7 %collective-permute-start = (bf16[80,768]{1,0:T(8,128)(2,1)S(1)}, bf16[80,768]{1,0:T(8,128)(2,1)S(1)}, u32[]{:S(2)}, u32[]{:S(2)}) collective-permute-start(bf16[80,768]{1,0:T(8,128)(2,1)S(1)} %fusion.6), channel_id=1, source_target_pairs={{0,1},{1,0},{2,3},{3,2},{4,5},{5,4},{6,7},{7,6},{8,9},{9,8},{10,11... | collective-permute-start | bytes 368648 | tf_op jit(solution)/shard_map/ppermute | solution.py:27
  5.5 12.3 %collective-permute-start.1 = (bf16[80,768]{1,0:T(8,128)(2,1)S(1)}, bf16[80,768]{1,0:T(8,128)(2,1)S(1)}, u32[]{:S(2)}, u32[]{:S(2)}) collective-permute-start(bf16[80,768]{1,0:T(8,128)(2,1)S(1)} %fusion.6), channel_id=1, source_target_pairs={{0,2},{1,3},{2,0},{3,1},{4,6},{5,7},{6,4},{7,5},{8,10},{9,11},{10,... | collective-permute-start | bytes 368648 | tf_op jit(solution)/shard_map/ppermute | solution.py:27
  8.1 10.4 %collective-permute-start.2 = (bf16[80,768]{1,0:T(8,128)(2,1)S(1)}, bf16[80,768]{1,0:T(8,128)(2,1)S(1)}, u32[]{:S(2)}, u32[]{:S(2)}) collective-permute-start(bf16[80,768]{1,0:T(8,128)(2,1)S(1)} %fusion.6), channel_id=1, source_target_pairs={{0,3},{1,2},{2,1},{3,0},{4,7},{5,6},{6,5},{7,4},{8,11},{9,10},{10,... | collective-permute-start | bytes 368648 | tf_op jit(solution)/shard_map/ppermute | solution.py:27
  9.0 33.2 %collective-permute-start.8 = (bf16[384,768]{1,0:T(8,128)(2,1)}, bf16[384,768]{1,0:T(8,128)(2,1)}, u32[]{:S(2)}, u32[]{:S(2)}) collective-permute-start(bf16[384,768]{1,0:T(8,128)(2,1)} %constant_dynamic-slice_fusion.3), channel_id=1, source_target_pairs={{0,1},{1,0},{2,3},{3,2},{4,5},{5,4},{6,7},{7,6},{8,9},{9,8},{10,11... | collective-permute-start | bytes 1769480 | tf_op jit(solution)/shard_map/ppermute | solution.py:27
  19.2 5.4 %collective-permute-start.3 = (bf16[1,3,3,24,384]{4,3,2,1,0:T(8,128)(2,1)S(1)}, bf16[1,3,3,24,384]{4,3,2,1,0:T(8,128)(2,1)S(1)}, u32[]{:S(2)}, u32[]{:S(2)}) collective-permute-start(bf16[1,3,3,24,384]{4,3,2,1,0:T(8,128)(2,1)S(1)} %get-tuple-element.286), channel_id=1, source_target_pairs={{0,8},{4,12},{8,0},{12,4},{16,24},{20,28},{24,16},{28,20},{1,9},{5... | collective-permute-start | bytes 497672 | tf_op jit(solution)/shard_map/ppermute | solution.py:27
  20.8 7.1 %collective-permute-start.5 = (bf16[1,3,3,24,384]{4,3,2,1,0:T(8,128)(2,1)S(1)}, bf16[1,3,3,24,384]{4,3,2,1,0:T(8,128)(2,1)S(1)}, u32[]{:S(2)}, u32[]{:S(2)}) collective-permute-start(bf16[1,3,3,24,384]{4,3,2,1,0:T(8,128)(2,1)S(1)} %get-tuple-element.287), channel_id=1, source_target_pairs={{0,16},{4,20},{8,24},{12,28},{16,0},{20,4},{24,8},{28,12},{1,17},{... | collective-permute-start | bytes 497672 | tf_op jit(solution)/shard_map/ppermute | solution.py:27
  24.7 7.6 %collective-permute-start.4 = (bf16[2,3,3,24,384]{4,3,2,1,0:T(8,128)(2,1)S(1)}, bf16[2,3,3,24,384]{4,3,2,1,0:T(8,128)(2,1)S(1)}, u32[]{:S(2)}, u32[]{:S(2)}) collective-permute-start(bf16[2,3,3,24,384]{4,3,2,1,0:T(8,128)(2,1)S(1)} %pad_maximum_fusion.5), channel_id=1, source_target_pairs={{0,16},{4,20},{8,24},{12,28},{16,0},{20,4},{24,8},{28,12},{1,17},{... | collective-permute-start | bytes 995336 | tf_op jit(solution)/shard_map/ppermute | solution.py:27
  27.9 7.2 %collective-permute-start.6 = (bf16[2,3,3,24,384]{4,3,2,1,0:T(8,128)(2,1)S(1)}, bf16[2,3,3,24,384]{4,3,2,1,0:T(8,128)(2,1)S(1)}, u32[]{:S(2)}, u32[]{:S(2)}) collective-permute-start(bf16[2,3,3,24,384]{4,3,2,1,0:T(8,128)(2,1)S(1)} %pad_maximum_fusion.6), channel_id=1, source_target_pairs={{0,8},{4,12},{8,0},{12,4},{16,24},{20,28},{24,16},{28,20},{1,9},{5... | collective-permute-start | bytes 995336 | tf_op jit(solution)/shard_map/ppermute | solution.py:27
  37.4 8.1 %collective-permute-start.7 = (bf16[2,4,3,3,24,384]{5,4,3,2,1,0:T(8,128)(2,1)}, bf16[2,4,3,3,24,384]{5,4,3,2,1,0:T(8,128)(2,1)}, u32[]{:S(2)}, u32[]{:S(2)}) collective-permute-start(bf16[2,4,3,3,24,384]{5,4,3,2,1,0:T(8,128)(2,1)} %pad_maximum_fusion.1), channel_id=1, source_target_pairs={{0,4},{4,0},{8,12},{12,8},{16,20},{20,16},{24,28},{28,24},{1,5},{5... | collective-permute-start | bytes 3981320 | tf_op jit(solution)/shard_map/ppermute | solution.py:27
  48.3 23.1 %collective-permute-start.10 = (bf16[3,96,768]{2,1,0:T(8,128)(2,1)S(1)}, bf16[3,96,768]{2,1,0:T(8,128)(2,1)S(1)}, u32[]{:S(2)}, u32[]{:S(2)}) collective-permute-start(bf16[3,96,768]{2,1,0:T(8,128)(2,1)S(1)} %get-tuple-element.150), channel_id=1, source_target_pairs={{0,2},{1,3},{2,0},{3,1},{4,6},{5,7},{6,4},{7,5},{8,10},{9,11},{10,... | collective-permute-start | bytes 1327112 | tf_op jit(solution)/shard_map/ppermute | solution.py:27
  50.1 37.7 %collective-permute-start.9 = (bf16[3,96,768]{2,1,0:T(8,128)(2,1)S(1)}, bf16[3,96,768]{2,1,0:T(8,128)(2,1)S(1)}, u32[]{:S(2)}, u32[]{:S(2)}) collective-permute-start(bf16[3,96,768]{2,1,0:T(8,128)(2,1)S(1)} %get-tuple-element.150), channel_id=1, source_target_pairs={{0,1},{1,0},{2,3},{3,2},{4,5},{5,4},{6,7},{7,6},{8,9},{9,8},{10,11... | collective-permute-start | bytes 1327112 | tf_op jit(solution)/shard_map/ppermute | solution.py:27
  56.8 10.8 %copy-start.37 = (bf16[384,1536]{1,0:T(8,128)(2,1)}, bf16[384,1536]{1,0:T(8,128)(2,1)S(1)}, u32[]{:S(2)}) copy-start(bf16[384,1536]{1,0:T(8,128)(2,1)S(1)} %fusion.2.refs_4_) | copy-start | bytes 3538948
  56.8 14.7 %copy-start.11 = (bf16[2,768,768]{2,1,0:T(8,128)(2,1)S(1)}, bf16[2,768,768]{2,1,0:T(8,128)(2,1)}, u32[]{:S(2)}) copy-start(bf16[2,768,768]{2,1,0:T(8,128)(2,1)} %refs_8_.3) | copy-start | bytes 7077892
  71.4 16.3 %collective-permute-start.11 = (bf16[3,96,768]{2,1,0:T(8,128)(2,1)S(1)}, bf16[3,96,768]{2,1,0:T(8,128)(2,1)S(1)}, u32[]{:S(2)}, u32[]{:S(2)}) collective-permute-start(bf16[3,96,768]{2,1,0:T(8,128)(2,1)S(1)} %collective-permute-done.10.refs_1_), channel_id=1, source_target_pairs={{0,1},{1,0},{2,3},{3,2},{4,5},{5,4},{6,7},{7,6},{8,9},{9,8},{10,11... | collective-permute-start | bytes 1327112 | tf_op jit(solution)/shard_map/ppermute | solution.py:27
  87.9 3.1 collective-permute-start.12
  88.1 16.1 %collective-permute-start.13 = (bf16[384,768]{1,0:T(8,128)(2,1)S(1)}, bf16[384,768]{1,0:T(8,128)(2,1)S(1)}, u32[]{:S(2)}, u32[]{:S(2)}) collective-permute-start(bf16[384,768]{1,0:T(8,128)(2,1)S(1)} %constant_dynamic-slice_fusion.2), channel_id=1, source_target_pairs={{0,1},{1,0},{2,3},{3,2},{4,5},{5,4},{6,7},{7,6},{8,9},{9,8},{10,11... | collective-permute-start | bytes 1769480 | tf_op jit(solution)/shard_map/ppermute | solution.py:27
  92.0 12.2 %copy-start.79 = (bf16[2,4,2,96,768]{4,3,2,1,0:T(8,128)(2,1)}, bf16[2,4,2,96,768]{4,3,2,1,0:T(8,128)(2,1)S(1)}, u32[]{:S(2)}) copy-start(bf16[2,4,2,96,768]{4,3,2,1,0:T(8,128)(2,1)S(1)} %slice.183) | copy-start | bytes 7077892
  95.7 9.6 %copy-start.57 = (bf16[512,2304]{1,0:T(8,128)(2,1)}, bf16[512,2304]{1,0:T(8,128)(2,1)S(1)}, u32[]{:S(2)}) copy-start(bf16[512,2304]{1,0:T(8,128)(2,1)S(1)} %fusion.1.refs_3_) | copy-start | bytes 7077892
  105.3 10.3 %copy-start.39 = (bf16[384,1536]{1,0:T(8,128)(2,1)}, bf16[384,1536]{1,0:T(8,128)(2,1)S(1)}, u32[]{:S(2)}) copy-start(bf16[384,1536]{1,0:T(8,128)(2,1)S(1)} %fusion.3.refs_4_) | copy-start | bytes 3538948
  105.4 12.4 %copy-start.66 = (f32[512,768]{1,0:T(8,128)S(1)}, f32[512,768]{1,0:T(8,128)}, u32[]{:S(2)}) copy-start(f32[512,768]{1,0:T(8,128)} %copy-done.65) | copy-start | bytes 4718596
  117.7 12.3 %copy-start.16 = (bf16[512,768]{1,0:T(8,128)(2,1)S(1)}, bf16[512,768]{1,0:T(8,128)(2,1)}, u32[]{:S(2)}) copy-start(bf16[512,768]{1,0:T(8,128)(2,1)} %refs_0_.3) | copy-start | bytes 2359300
  149.3 4.9 %collective-permute-start.15 = (bf16[4,4,4,24,768]{4,3,2,1,0:T(8,128)(2,1)}, bf16[4,4,4,24,768]{4,3,2,1,0:T(8,128)(2,1)}, u32[]{:S(2)}, u32[]{:S(2)}) collective-permute-start(bf16[4,4,4,24,768]{4,3,2,1,0:T(8,128)(2,1)} %get-tuple-element.179), channel_id=1, source_target_pairs={{0,4},{4,0},{8,12},{12,8},{16,20},{20,16},{24,28},{28,24},{1,5},{5... | collective-permute-start | bytes 7077896 | tf_op jit(solution)/shard_map/ppermute | solution.py:27
  149.3 8.2 %collective-permute-start.14 = (bf16[4,4,4,24,768]{4,3,2,1,0:T(8,128)(2,1)}, bf16[4,4,4,24,768]{4,3,2,1,0:T(8,128)(2,1)}, u32[]{:S(2)}, u32[]{:S(2)}) collective-permute-start(bf16[4,4,4,24,768]{4,3,2,1,0:T(8,128)(2,1)} %get-tuple-element.178), channel_id=1, source_target_pairs={{0,4},{4,0},{8,12},{12,8},{16,20},{20,16},{24,28},{28,24},{1,5},{5... | collective-permute-start | bytes 7077896 | tf_op jit(solution)/shard_map/ppermute | solution.py:27
  159.2 7.2 %copy-start.40 = (bf16[384,1536]{1,0:T(8,128)(2,1)S(1)}, bf16[384,1536]{1,0:T(8,128)(2,1)}, u32[]{:S(2)}) copy-start(bf16[384,1536]{1,0:T(8,128)(2,1)} %copy-done.39) | copy-start | bytes 3538948
  159.2 7.2 %copy-start.58 = (bf16[512,2304]{1,0:T(8,128)(2,1)S(1)}, bf16[512,2304]{1,0:T(8,128)(2,1)}, u32[]{:S(2)}) copy-start(bf16[512,2304]{1,0:T(8,128)(2,1)} %copy-done.57) | copy-start | bytes 7077892
  159.2 7.2 %copy-start.62 = (bf16[512,768]{1,0:T(8,128)(2,1)S(1)}, bf16[512,768]{1,0:T(8,128)(2,1)}, u32[]{:S(2)}) copy-start(bf16[512,768]{1,0:T(8,128)(2,1)} %copy-done.61) | copy-start | bytes 2359300
  159.2 7.2 %copy-start.70 = (f32[768,512]{1,0:T(8,128)S(1)}, f32[768,512]{1,0:T(8,128)}, u32[]{:S(2)}) copy-start(f32[768,512]{1,0:T(8,128)} %copy-done.69) | copy-start | bytes 4718596
  165.7 29.2 %collective-permute-start.17 = (bf16[8,2,4,24,768]{4,3,2,1,0:T(8,128)(2,1)}, bf16[8,2,4,24,768]{4,3,2,1,0:T(8,128)(2,1)}, u32[]{:S(2)}, u32[]{:S(2)}) collective-permute-start(bf16[8,2,4,24,768]{4,3,2,1,0:T(8,128)(2,1)} %get-tuple-element.189), channel_id=1, source_target_pairs={{0,8},{4,20},{8,0},{12,28},{16,24},{20,4},{24,16},{28,12},{1,9},{5... | collective-permute-start | bytes 7077896 | tf_op jit(solution)/shard_map/ppermute | solution.py:908
  166.5 16.3 %copy-start.80 = (bf16[2,4,2,96,768]{4,3,2,1,0:T(8,128)(2,1)S(1)}, bf16[2,4,2,96,768]{4,3,2,1,0:T(8,128)(2,1)}, u32[]{:S(2)}) copy-start(bf16[2,4,2,96,768]{4,3,2,1,0:T(8,128)(2,1)} %copy-done.79) | copy-start | bytes 7077892
  182.8 7.9 %copy-start.51 = (bf16[512,2304]{1,0:T(8,128)(2,1)}, bf16[512,2304]{1,0:T(8,128)(2,1)S(1)}, u32[]{:S(2)}) copy-start(bf16[512,2304]{1,0:T(8,128)(2,1)S(1)} %get-tuple-element.182.refs_5_) | copy-start | bytes 7077892
  183.9 6.7 %copy-start.17 = (bf16[384,768]{1,0:T(8,128)(2,1)}, bf16[384,768]{1,0:T(8,128)(2,1)S(1)}, u32[]{:S(2)}) copy-start(bf16[384,768]{1,0:T(8,128)(2,1)S(1)} %convolution_convert_fusion.1.refs_8_) | copy-start | bytes 1769476
  190.6 28.7 %collective-permute-start.19 = (bf16[49,8,3072]{2,1,0:T(8,128)(2,1)}, bf16[49,8,3072]{2,1,0:T(8,128)(2,1)}, u32[]{:S(2)}, u32[]{:S(2)}) collective-permute-start(bf16[49,8,3072]{2,1,0:T(8,128)(2,1)} %get-tuple-element.205), channel_id=1, source_target_pairs={{0,4},{4,0},{8,12},{12,8},{16,20},{20,16},{24,28},{28,24},{1,5},{5... | collective-permute-start | bytes 7225352 | tf_op jit(solution)/shard_map/ppermute | solution.py:27
  191.2 15.6 %collective-permute-start.16 = (bf16[384,768]{1,0:T(8,128)(2,1)}, bf16[384,768]{1,0:T(8,128)(2,1)S(1)}, u32[]{:S(2)}, u32[]{:S(2)}) collective-permute-start(bf16[384,768]{1,0:T(8,128)(2,1)} %copy-done.17), channel_id=1, source_target_pairs={{0,1},{1,0},{2,3},{3,2},{4,5},{5,4},{6,7},{7,6},{8,9},{9,8},{10,11... | collective-permute-start | bytes 1769480 | tf_op jit(solution)/shard_map/ppermute | solution.py:27
  196.5 10.2 %slice-start = ((s8[6291456]{0:T(1024)(128)(4,1)}), s8[4194304]{0:T(1024)(128)(4,1)S(1)}, s32[]{:S(2)}) async-start(s8[6291456]{0:T(1024)(128)(4,1)} %bitcast.176), calls=%async_computation | async-start | bytes 8388608
  198.9 23.9 %collective-permute-start.18 = (bf16[4,2,4,24,768]{4,3,2,1,0:T(8,128)(2,1)S(1)}, bf16[4,2,4,24,768]{4,3,2,1,0:T(8,128)(2,1)S(1)}, u32[]{:S(2)}, u32[]{:S(2)}) collective-permute-start(bf16[4,2,4,24,768]{4,3,2,1,0:T(8,128)(2,1)S(1)} %get-tuple-element.203), channel_id=1, source_target_pairs={{0,16},{4,12},{8,24},{12,4},{16,0},{20,28},{24,8},{28,20},{1,17},{... | collective-permute-start | bytes 3538952 | tf_op jit(solution)/shard_map/ppermute | solution.py:908
  200.0 6.7 %slice-start.1 = ((s8[6291456]{0:T(1024)(128)(4,1)}), s8[2097152]{0:T(1024)(128)(4,1)S(1)}, s32[]{:S(2)}) async-start(s8[6291456]{0:T(1024)(128)(4,1)} %bitcast.176), calls=%async_computation.1 | async-start | bytes 4194304
  200.0 6.7 %copy-start.44 = (f32[512,768]{1,0:T(8,128)S(1)}, f32[512,768]{1,0:T(8,128)}, u32[]{:S(2)}) copy-start(f32[512,768]{1,0:T(8,128)} %copy-done.43) | copy-start | bytes 4718596
  200.0 6.7 %copy-start.46 = (f32[512,768]{1,0:T(8,128)S(1)}, f32[512,768]{1,0:T(8,128)}, u32[]{:S(2)}) copy-start(f32[512,768]{1,0:T(8,128)} %copy-done.45) | copy-start | bytes 4718596
  233.0 4.9 %collective-permute-start.21 = (bf16[4,4,4,24,768]{4,3,2,1,0:T(8,128)(2,1)}, bf16[4,4,4,24,768]{4,3,2,1,0:T(8,128)(2,1)}, u32[]{:S(2)}, u32[]{:S(2)}) collective-permute-start(bf16[4,4,4,24,768]{4,3,2,1,0:T(8,128)(2,1)} %get-tuple-element.215), channel_id=1, source_target_pairs={{0,4},{4,0},{8,12},{12,8},{16,20},{20,16},{24,28},{28,24},{1,5},{5... | collective-permute-start | bytes 7077896 | tf_op jit(solution)/shard_map/ppermute | solution.py:27
  233.0 8.2 %collective-permute-start.20 = (bf16[4,4,4,24,768]{4,3,2,1,0:T(8,128)(2,1)}, bf16[4,4,4,24,768]{4,3,2,1,0:T(8,128)(2,1)}, u32[]{:S(2)}, u32[]{:S(2)}) collective-permute-start(bf16[4,4,4,24,768]{4,3,2,1,0:T(8,128)(2,1)} %get-tuple-element.214), channel_id=1, source_target_pairs={{0,4},{4,0},{8,12},{12,8},{16,20},{20,16},{24,28},{28,24},{1,5},{5... | collective-permute-start | bytes 7077896 | tf_op jit(solution)/shard_map/ppermute | solution.py:27
  233.6 30.6 %collective-permute-start.24 = (bf16[25,8,3072]{2,1,0:T(8,128)(2,1)}, bf16[25,8,3072]{2,1,0:T(8,128)(2,1)S(1)}, u32[]{:S(2)}, u32[]{:S(2)}) collective-permute-start(bf16[25,8,3072]{2,1,0:T(8,128)(2,1)} %copy-done.15), channel_id=1, source_target_pairs={{0,8},{4,20},{8,0},{12,28},{16,24},{20,4},{24,16},{28,12},{1,9},{5... | collective-permute-start | bytes 3686408 | tf_op jit(solution)/shard_map/ppermute | solution.py:908
  234.9 33.8 %collective-permute-start.23 = (bf16[2,2,4,24,768]{4,3,2,1,0:T(8,128)(2,1)}, bf16[2,2,4,24,768]{4,3,2,1,0:T(8,128)(2,1)S(1)}, u32[]{:S(2)}, u32[]{:S(2)}) collective-permute-start(bf16[2,2,4,24,768]{4,3,2,1,0:T(8,128)(2,1)} %get-tuple-element.227), channel_id=1, source_target_pairs={{0,1},{1,0},{2,3},{3,2},{4,5},{5,4},{6,7},{7,6},{8,9},{9,8},{10,11... | collective-permute-start | bytes 1769480 | tf_op jit(solution)/shard_map/ppermute | solution.py:908
  246.6 29.2 %collective-permute-start.27 = (bf16[8,2,4,24,768]{4,3,2,1,0:T(8,128)(2,1)S(1)}, bf16[8,2,4,24,768]{4,3,2,1,0:T(8,128)(2,1)S(1)}, u32[]{:S(2)}, u32[]{:S(2)}) collective-permute-start(bf16[8,2,4,24,768]{4,3,2,1,0:T(8,128)(2,1)S(1)} %get-tuple-element.238), channel_id=1, source_target_pairs={{0,8},{4,20},{8,0},{12,28},{16,24},{20,4},{24,16},{28,12},{1,9},{5... | collective-permute-start | bytes 7077896 | tf_op jit(solution)/shard_map/ppermute | solution.py:908
  247.9 16.3 %copy-start.14 = (bf16[25,8,3072]{2,1,0:T(8,128)(2,1)S(1)}, bf16[25,8,3072]{2,1,0:T(8,128)(2,1)}, u32[]{:S(2)}) copy-start(bf16[25,8,3072]{2,1,0:T(8,128)(2,1)} %copy-done.13) | copy-start | bytes 3686404
  274.0 12.2 %collective-permute-start.25 = (bf16[49,8,3072]{2,1,0:T(8,128)(2,1)S(1)}, bf16[49,8,3072]{2,1,0:T(8,128)(2,1)S(1)}, u32[]{:S(2)}, u32[]{:S(2)}) collective-permute-start(bf16[49,8,3072]{2,1,0:T(8,128)(2,1)S(1)} %get-tuple-element.234), channel_id=1, source_target_pairs={{0,4},{4,0},{8,12},{12,8},{16,20},{20,16},{24,28},{28,24},{1,5},{5... | collective-permute-start | bytes 7225352 | tf_op jit(solution)/shard_map/ppermute | solution.py:27
  274.1 10.5 %collective-permute-start.26 = (bf16[13,8,3072]{2,1,0:T(8,128)(2,1)S(1)}, bf16[13,8,3072]{2,1,0:T(8,128)(2,1)S(1)}, u32[]{:S(2)}, u32[]{:S(2)}) collective-permute-start(bf16[13,8,3072]{2,1,0:T(8,128)(2,1)S(1)} %get-tuple-element.236), channel_id=1, source_target_pairs={{0,16},{4,12},{8,24},{12,4},{16,0},{20,28},{24,8},{28,20},{1,17},{... | collective-permute-start | bytes 1916936 | tf_op jit(solution)/shard_map/ppermute | solution.py:908
  276.9 26.7 %collective-permute-start.29 = (bf16[4,2,4,24,768]{4,3,2,1,0:T(8,128)(2,1)S(1)}, bf16[4,2,4,24,768]{4,3,2,1,0:T(8,128)(2,1)S(1)}, u32[]{:S(2)}, u32[]{:S(2)}) collective-permute-start(bf16[4,2,4,24,768]{4,3,2,1,0:T(8,128)(2,1)S(1)} %get-tuple-element.245), channel_id=1, source_target_pairs={{0,16},{4,12},{8,24},{12,4},{16,0},{20,28},{24,8},{28,20},{1,17},{... | collective-permute-start | bytes 3538952 | tf_op jit(solution)/shard_map/ppermute | solution.py:908
  288.4 21.5 %collective-permute-start.28 = (bf16[25,8,3072]{2,1,0:T(8,128)(2,1)}, bf16[25,8,3072]{2,1,0:T(8,128)(2,1)S(1)}, u32[]{:S(2)}, u32[]{:S(2)}) collective-permute-start(bf16[25,8,3072]{2,1,0:T(8,128)(2,1)} %get-tuple-element.243), channel_id=1, source_target_pairs={{0,8},{4,20},{8,0},{12,28},{16,24},{20,4},{24,16},{28,12},{1,9},{5... | collective-permute-start | bytes 3686408 | tf_op jit(solution)/shard_map/ppermute | solution.py:908
  289.1 18.7 %collective-permute-start.22 = (bf16[384,768]{1,0:T(8,128)(2,1)}, bf16[384,768]{1,0:T(8,128)(2,1)S(1)}, u32[]{:S(2)}, u32[]{:S(2)}) collective-permute-start(bf16[384,768]{1,0:T(8,128)(2,1)} %convolution_convert_fusion.refs_8_), channel_id=1, source_target_pairs={{0,1},{1,0},{2,3},{3,2},{4,5},{5,4},{6,7},{7,6},{8,9},{9,8},{10,11... | collective-permute-start | bytes 1769480 | tf_op jit(solution)/shard_map/ppermute | solution.py:27
  305.9 20.6 %collective-permute-start.31 = (bf16[2,2,4,24,768]{4,3,2,1,0:T(8,128)(2,1)}, bf16[2,2,4,24,768]{4,3,2,1,0:T(8,128)(2,1)}, u32[]{:S(2)}, u32[]{:S(2)}) collective-permute-start(bf16[2,2,4,24,768]{4,3,2,1,0:T(8,128)(2,1)} %get-tuple-element.251), channel_id=1, source_target_pairs={{0,1},{1,0},{2,3},{3,2},{4,5},{5,4},{6,7},{7,6},{8,9},{9,8},{10,11... | collective-permute-start | bytes 1769480 | tf_op jit(solution)/shard_map/ppermute | solution.py:908
  305.9 49.5 %collective-permute-start.37 = (bf16[1,2,4,24,768]{4,3,2,1,0:T(8,128)(2,1)}, bf16[1,2,4,24,768]{4,3,2,1,0:T(8,128)(2,1)}, u32[]{:S(2)}, u32[]{:S(2)}) collective-permute-start(bf16[1,2,4,24,768]{4,3,2,1,0:T(8,128)(2,1)} %get-tuple-element.269), channel_id=1, source_target_pairs={{0,2},{1,3},{2,0},{3,1},{4,6},{5,7},{6,4},{7,5},{8,10},{9,11},{10,... | collective-permute-start | bytes 884744 | tf_op jit(solution)/shard_map/ppermute | solution.py:908
  307.8 20.0 %copy-start.50 = (bf16[512,2304]{1,0:T(8,128)(2,1)S(1)}, bf16[512,2304]{1,0:T(8,128)(2,1)}, u32[]{:S(2)}) copy-start(bf16[512,2304]{1,0:T(8,128)(2,1)} %copy-done.49) | copy-start | bytes 7077892
  307.9 18.6 %copy-start.36 = (bf16[2,2,4,24,768]{4,3,2,1,0:T(8,128)(2,1)S(1)}, bf16[2,2,4,24,768]{4,3,2,1,0:T(8,128)(2,1)}, u32[]{:S(2)}) copy-start(bf16[2,2,4,24,768]{4,3,2,1,0:T(8,128)(2,1)} %copy-done.35) | copy-start | bytes 1769476
  308.0 33.7 %collective-permute-start.33 = (bf16[204,8,128]{2,1,0:T(8,128)(2,1)}, bf16[204,8,128]{2,1,0:T(8,128)(2,1)S(1)}, u32[]{:S(2)}, u32[]{:S(2)}) collective-permute-start(bf16[204,8,128]{2,1,0:T(8,128)(2,1)} %get-tuple-element.257), channel_id=1, source_target_pairs={{0,1},{1,0},{2,3},{3,2},{4,5},{5,4},{6,7},{7,6},{8,9},{9,8},{10,11... | collective-permute-start | bytes 1253384 | tf_op jit(solution)/shard_map/ppermute | solution.py:908
  309.9 18.0 %copy-start.7 = (bf16[3,4,8,24,768]{4,3,2,1,0:T(8,128)(2,1)S(1)}, bf16[3,4,8,24,768]{4,3,2,1,0:T(8,128)(2,1)}, u32[]{:S(2)}) copy-start(bf16[3,4,8,24,768]{4,3,2,1,0:T(8,128)(2,1)} %copy-done.6) | copy-start | bytes 10616836
  309.9 18.0 %copy-start.42 = (f32[512,768]{1,0:T(8,128)S(1)}, f32[512,768]{1,0:T(8,128)}, u32[]{:S(2)}) copy-start(f32[512,768]{1,0:T(8,128)} %copy-done.41) | copy-start | bytes 4718596
  310.7 20.3 %collective-permute-start.30 = (bf16[13,8,3072]{2,1,0:T(8,128)(2,1)S(1)}, bf16[13,8,3072]{2,1,0:T(8,128)(2,1)S(1)}, u32[]{:S(2)}, u32[]{:S(2)}) collective-permute-start(bf16[13,8,3072]{2,1,0:T(8,128)(2,1)S(1)} %get-tuple-element.249), channel_id=1, source_target_pairs={{0,16},{4,12},{8,24},{12,4},{16,0},{20,28},{24,8},{28,20},{1,17},{... | collective-permute-start | bytes 1916936 | tf_op jit(solution)/shard_map/ppermute | solution.py:908
  327.7 14.7 %collective-permute-start.36 = (bf16[1,2,4,24,768]{4,3,2,1,0:T(8,128)(2,1)S(1)}, bf16[1,2,4,24,768]{4,3,2,1,0:T(8,128)(2,1)S(1)}, u32[]{:S(2)}, u32[]{:S(2)}) collective-permute-start(bf16[1,2,4,24,768]{4,3,2,1,0:T(8,128)(2,1)S(1)} %get-tuple-element.267), channel_id=1, source_target_pairs={{0,2},{1,3},{2,0},{3,1},{4,6},{5,7},{6,4},{7,5},{8,10},{9,11},{10,... | collective-permute-start | bytes 884744 | tf_op jit(solution)/shard_map/ppermute | solution.py:908
  331.0 10.7 %copy-start.48 = (bf16[204,8,128]{2,1,0:T(8,128)(2,1)S(1)}, bf16[204,8,128]{2,1,0:T(8,128)(2,1)}, u32[]{:S(2)}) copy-start(bf16[204,8,128]{2,1,0:T(8,128)(2,1)} %copy-done.47) | copy-start | bytes 1253380
  331.9 22.4 %collective-permute-start.32 = (bf16[204,8,128]{2,1,0:T(8,128)(2,1)S(1)}, bf16[204,8,128]{2,1,0:T(8,128)(2,1)S(1)}, u32[]{:S(2)}, u32[]{:S(2)}) collective-permute-start(bf16[204,8,128]{2,1,0:T(8,128)(2,1)S(1)} %get-tuple-element.255), channel_id=1, source_target_pairs={{0,1},{1,0},{2,3},{3,2},{4,5},{5,4},{6,7},{7,6},{8,9},{9,8},{10,11... | collective-permute-start | bytes 1253384 | tf_op jit(solution)/shard_map/ppermute | solution.py:908
  342.3 15.4 %collective-permute-start.35 = (bf16[108,8,128]{2,1,0:T(8,128)(2,1)S(1)}, bf16[108,8,128]{2,1,0:T(8,128)(2,1)}, u32[]{:S(2)}, u32[]{:S(2)}) collective-permute-start(bf16[108,8,128]{2,1,0:T(8,128)(2,1)S(1)} %get-tuple-element.265), channel_id=1, source_target_pairs={{0,2},{1,3},{2,0},{3,1},{4,6},{5,7},{6,4},{7,5},{8,10},{9,11},{10,... | collective-permute-start | bytes 663560 | tf_op jit(solution)/shard_map/ppermute | solution.py:908
  356.5 11.1 %collective-permute-start.34 = (bf16[108,8,128]{2,1,0:T(8,128)(2,1)S(1)}, bf16[108,8,128]{2,1,0:T(8,128)(2,1)S(1)}, u32[]{:S(2)}, u32[]{:S(2)}) collective-permute-start(bf16[108,8,128]{2,1,0:T(8,128)(2,1)S(1)} %get-tuple-element.263), channel_id=1, source_target_pairs={{0,2},{1,3},{2,0},{3,1},{4,6},{5,7},{6,4},{7,5},{8,10},{9,11},{10,... | collective-permute-start | bytes 663560 | tf_op jit(solution)/shard_map/ppermute | solution.py:908
  (72 other events, 198.9 us)

commit v7 on v6

--- a/solution.py
+++ b/solution.py
@@ -292,7 +292,7 @@
             pltpu.VMEM((8, 2 * BLK), f32),
             pltpu.VMEM((pairs, BLK, BLK), f32),
         ],
-        compiler_params=pltpu.CompilerParams(vmem_limit_bytes=16 * 2**20),
+        compiler_params=pltpu.CompilerParams(vmem_limit_bytes=13 * 2**20),
         cost_estimate=cost(9),
         name="attend",
     )
@@ -324,7 +324,7 @@
             pltpu.VMEM((blocks * BLK, width), f32),
             pltpu.VMEM((blocks * BLK, width), f32),
         ],
-        compiler_params=pltpu.CompilerParams(vmem_limit_bytes=24 * 2**20),
+        compiler_params=pltpu.CompilerParams(vmem_limit_bytes=20 * 2**20),
         cost_estimate=cost(21),
         name="attend_back",
     )
@@ -596,7 +596,7 @@
         in_specs=[pl.BlockSpec(memory_space=pltpu.SMEM)] + vmem_specs(2),
         out_specs=tuple(vmem_specs(2)),
         scratch_shapes=[pltpu.VMEM((rows // 2, tokens), bf16)] if scratch else [],
-        compiler_params=pltpu.CompilerParams(vmem_limit_bytes=18 * 2**20),
+        compiler_params=pltpu.CompilerParams(vmem_limit_bytes=15 * 2**20),
         cost_estimate=cost(5),
         name="grad_up" if scratch else "grad_down",
     )
@@ -696,7 +696,7 @@
         out_shape=(jax.ShapeDtypeStruct((own.shape[0], head) + own.shape[1:], bf16),),
         in_specs=[pl.BlockSpec(memory_space=pltpu.SMEM)] + vmem_specs(1 + len(refs)),
         out_specs=vmem_specs(1),
-        compiler_params=pltpu.CompilerParams(vmem_limit_bytes=16 * 2**20),
+        compiler_params=pltpu.CompilerParams(vmem_limit_bytes=13 * 2**20),
         cost_estimate=cost(1.5),
         name="assemble",
     )

time: 378 us -> 376 us (level)
  starting transfers between devices: 30.4 us -> 45.7 us
  waiting for transfers between devices: 109 us -> 96.3 us
  Pallas kernels: 154 us -> 150 us
    ppermute x16, starting transfers between devices: 11.4 us -> 24 us  [step(): self.keeps, self.gots = ([keep], [lax.ppermute(send, axis_name, pairs)])]
    ppermute x16, waiting for transfers between devices: 70.2 us -> 58.6 us  [step(): self.keeps, self.gots = ([keep], [lax.ppermute(send, axis_name, pairs)])]
    pallas_call x34, Pallas kernels: 154 us -> 150 us  [ordered_call(): pl.pallas_call(body, out_shape=tuple(out_shape) + (jax.ShapeDtypeStruct((...]
  transfers between devices with their start and end apart: 38 -> 38, of which waited for: 22 -> 21; matrix products, arithmetic and copies ran while one was open for 10% -> 10% of each run, Pallas kernels for 27% -> 26%
where the time goes in v7:
time: 376 us; the launch traced here: 369 us
  Pallas kernels  150 us (40%)
  waiting for transfers between devices  96.3 us (26%)
  starting transfers between devices  45.7 us (12%)
  local copies, waits for them, and re-layouts  44.1 us (12%)
  matrix products  18.4 us (5%)
  other arithmetic  12.2 us (3%)
    pallas_call x34, Pallas kernels, ordered_call(): pl.pallas_call(body, out_shape=tuple(out_shape) + (jax.ShapeDtypeStruct((...  150 us
    ppermute x16, waiting for transfers between devices, step(): self.keeps, self.gots = ([keep], [lax.ppermute(send, axis_name, pairs)])  58.6 us
    ppermute x22, waiting for transfers between devices, swap(): return lax.ppermute(value, axis, [(i, i ^ bit) for i in range(size)])  37.7 us
    unnamed x200, local copies, waits for them, and re-layouts  30.3 us
    ppermute x16, starting transfers between devices, step(): self.keeps, self.gots = ([keep], [lax.ppermute(send, axis_name, pairs)])  24 us
    ppermute x22, starting transfers between devices, swap(): return lax.ppermute(value, axis, [(i, i ^ bit) for i in range(size)])  21.6 us
    dot_general x4, matrix products, nn(): lax.dot_general(left, right, (((1,), (0,)), ((), ())), preferred_element_...  10.5 us
    dot_general x4, matrix products, nt(): lax.dot_general(left, right, (((1,), (1,)), ((), ())), preferred_element_...  7.82 us
  transfers between devices with their start and end apart: 38, of which 21 were waited for; matrix products, arithmetic and copies ran while one was open for 10% of the time, Pallas kernels for 26%

profile of v7, /device:TPU:0, one launch (start us, length us, event | category | flops | bytes accessed | tf_op | source)
XLA Modules:
  0.0 368.9 jit_solution(1909670485601310225)
XLA Ops:
  2.5 3.1 collective-permute-start
  5.5 2.6 collective-permute-start.1
  13.8 4.1 %collective-permute-done.1 = bf16[80,768]{1,0:T(8,128)(2,1)S(1)} collective-permute-done((bf16[80,768]{1,0:T(8,128)(2,1)S(1)}, bf16[80,768]{1,0:T(8,128)(2,1)S(1)}, u32[]{:S(2)}, u32[]{:S(2)}) %collective-permute-start.1) | collective-permute-done | bytes 122912 | tf_op jit(solution)/shard_map/ppermute | solution.py:27
  22.3 2.3 collective-permute-done.3
  26.3 1.6 collective-permute-done.5
  28.9 3.4 collective-permute-done.4
  33.4 1.7 collective-permute-done.6
  45.5 1.6 pad_maximum_fusion
  48.3 1.8 collective-permute-start.10
  52.1 2.0 fusion.4.refs_3_
  54.1 2.6 fusion.2.refs_4_
  56.8 10.7 %attend.2 = (bf16[512,768]{1,0:T(8,128)(2,1)S(1)}, f32[768,512]{1,0:T(8,128)S(1)}, bf16[768,512]{1,0:T(8,128)(2,1)S(1)}, f32[4,8,256]{2,1,0:T(8,128)S(1)}, f32[8,128]{1,0:T(8,128)S(1)}) custom-call(s32[4,4]{1,0:T(4,128)S(1)} %pad_add_fusion.2.refs_0_, s32[4,1,256]{2,1,0:T(1,128)S(1)} %reshape.381.refs_1_, s32[896,1]{1,0:T(8,128)S(1)} %reshape.412.refs_2_, ...), custom_call_target="tpu_custom_call" | custom-call | flops 5175000064 | bytes 1000 | tf_op jit(solution)/shard_map/attend/pallas_call | solution.py:249
  71.5 11.4 %feed.2 = (f32[512,768]{1,0:T(8,128)S(1)}, bf16[768,512]{1,0:T(8,128)(2,1)S(1)}, bf16[3072,512]{1,0:T(8,128)(2,1)S(1)}, f32[512,3072]{1,0:T(8,128)S(1)}, f32[512...) custom-call(bf16[512,768]{1,0:T(8,128)(2,1)S(1)} %copy-done.10, ...), custom_call_target="tpu_custom_call" | custom-call | flops 8625000448 | bytes 1000 | tf_op jit(solution)/shard_map/feed/pallas_call | solution.py:249
  82.8 2.6 copy-done.32
  88.1 2.1 collective-permute-start.13
  93.7 2.0 fusion.1.refs_3_
  95.7 8.5 %collective-permute-done.13 = bf16[384,768]{1,0:T(8,128)(2,1)S(1)} collective-permute-done((bf16[384,768]{1,0:T(8,128)(2,1)S(1)}, bf16[384,768]{1,0:T(8,128)(2,1)S(1)}, u32[]{:S(2)}, u32[]{:S(2)}) %collective-permute-start.13) | collective-permute-done | bytes 589856 | tf_op jit(solution)/shard_map/ppermute | solution.py:27
  105.4 10.3 %attend.3 = (bf16[512,768]{1,0:T(8,128)(2,1)S(1)}, f32[768,512]{1,0:T(8,128)S(1)}, bf16[768,512]{1,0:T(8,128)(2,1)S(1)}, f32[4,8,256]{2,1,0:T(8,128)S(1)}, f32[8,128]{1,0:T(8,128)S(1)}) custom-call(s32[4,4]{1,0:T(4,128)S(1)} %pad_add_fusion.2.refs_0_, s32[4,1,256]{2,1,0:T(1,128)S(1)} %reshape.381.refs_1_, s32[896,1]{1,0:T(8,128)S(1)} %reshape.412.refs_2_, ...), custom_call_target="tpu_custom_call" | custom-call | flops 5175000064 | bytes 1000 | tf_op jit(solution)/shard_map/attend/pallas_call | solution.py:249
  117.7 12.2 %feed.3 = (f32[512,768]{1,0:T(8,128)S(1)}, bf16[768,512]{1,0:T(8,128)(2,1)S(1)}, bf16[3072,512]{1,0:T(8,128)(2,1)S(1)}, f32[512,3072]{1,0:T(8,128)S(1)}, f32[512...) custom-call(f32[512,768]{1,0:T(8,128)S(1)} %copy-done.66, ...), custom_call_target="tpu_custom_call" | custom-call | flops 8625000448 | bytes 1000 | tf_op jit(solution)/shard_map/feed/pallas_call | solution.py:249
  130.0 12.2 %feed_back.2 = (bf16[512,768]{1,0:T(8,128)(2,1)S(1)}, bf16[512,3072]{1,0:T(8,128)(2,1)S(1)}, bf16[512,768]{1,0:T(8,128)(2,1)S(1)}, f32[512,768]{1,0:T(8,128)S(1)...) custom-call(bf16[512,768]{1,0:T(8,128)(2,1)S(1)} %copy-done.16, ...), custom_call_target="tpu_custom_call" | custom-call | flops 9774999552 | bytes 1000 | tf_op jit(solution)/shard_map/feed_back/pallas_call | solution.py:249
  142.2 2.8 grad_down.2
  145.1 2.8 grad_up.2
  151.2 2.9 collective-permute-done.15
  154.2 3.4 collective-permute-done.14
  157.5 1.7 copy-done.5
  159.2 5.0 %advance.16 = (bf16[8,2,4,24,768]{4,3,2,1,0:T(8,128)(2,1)}, bf16[8,2,4,24,768]{4,3,2,1,0:T(8,128)(2,1)S(1)}, f32[8,128]{1,0:T(8,128)S(1)}) custom-call(s32[2]{0:T(128)S(1)} %pad_add_fusion.5.refs_0_, bf16[16,4,24,768]{3,2,1,0:T(8,128)(2,1)S(1)} %bitcast.157, bf16[16,4,24,768]{3,2,1,0:T(8,128)(2,1)S(1)} %bitcast.159, ...), custom_call_target="tpu_custom_call" | custom-call | flops 1931595264 | bytes 1000 | tf_op jit(solution)/shard_map/advance/pallas_call | solution.py:249
  165.0 14.0 %attend_back.2 = (bf16[512,2304]{1,0:T(8,128)(2,1)S(1)}, bf16[384,1536]{1,0:T(8,128)(2,1)S(1)}, f32[16,768]{1,0:T(8,128)S(1)}, f32[8,128]{1,0:T(8,128)S(1)}) custom-call(s32[4,4]{1,0:T(4,128)S(1)} %pad_add_fusion.2.refs_0_, s32[4,1,256]{2,1,0:T(1,128)S(1)} %reshape.381.refs_1_, s32[896,1]{1,0:T(8,128)S(1)} %reshape.412.refs_2_, ...), custom_call_target="tpu_custom_call" | custom-call | flops 12074999808 | bytes 1000 | tf_op jit(solution)/shard_map/attend_back/pallas_call | solution.py:249
  181.7 5.2 %grad_heads.2 = (bf16[49,8,3072]{2,1,0:T(8,128)(2,1)}, bf16[49,8,3072]{2,1,0:T(8,128)(2,1)S(1)}, f32[8,128]{1,0:T(8,128)S(1)}) custom-call(s32[1]{0:T(128)} %bitcast.36.refs_0_, bf16[8,96,512]{2,1,0:T(8,128)(2,1)S(1)} %bitcast.173, bf16[8,96,512]{2,1,0:T(8,128)(2,1)S(1)} %bitcast.172, bf16[8,96,384]{2,1,0:T(8,128)(2,1)S(1)} %bitcast.166, ...), custom_call_target="tpu_custom_call" | custom-call | flops 4600000000 | bytes 1000 | tf_op jit(solution)/shard_map/grad_heads/pallas_call | solution.py:249
  187.2 3.1 collective-permute-start.16
  190.4 3.0 collective-permute-done.17.refs_2_
  193.4 1.7 copy-done.1
  195.0 2.4 advance.17
  197.8 4.4 %convolution_add_fusion.3.refs_0_ = f32[512,768]{1,0:T(8,128)S(1)} fusion(f32[512,768]{1,0:T(8,128)} %copy-done.52, bf16[512,2304]{1,0:T(8,128)(2,1)} %copy-done.51, bf16[2304,768]{1,0:T(8,128)(2,1)S(1)} %bitcast.163), kind=kOutput, calls=%fused_computation.11 | convolution fusion | flops 1812332544 | bytes 9043968 | tf_op jit(solution)/shard_map/dot_general | solution.py:67
  202.2 2.4 collective-permute-done.16.refs_1_
  204.6 12.5 %feed_back.3 = (bf16[512,768]{1,0:T(8,128)(2,1)S(1)}, bf16[512,3072]{1,0:T(8,128)(2,1)S(1)}, bf16[512,768]{1,0:T(8,128)(2,1)S(1)}, f32[512,768]{1,0:T(8,128)S(1)...) custom-call(f32[512,768]{1,0:T(8,128)S(1)} %convolution_add_fusion.3.refs_, ...), custom_call_target="tpu_custom_call" | custom-call | flops 9774999552 | bytes 1000 | tf_op jit(solution)/shard_map/feed_back/pallas_call | solution.py:249
  217.1 3.4 advance.18
  223.7 2.8 grad_down.3
  226.6 2.8 grad_up.3
  231.4 2.0 collective-permute-start.24
  233.7 2.0 collective-permute-done.21
  235.7 3.4 collective-permute-done.20
  239.1 1.7 copy-done.3
  240.8 3.6 advance.20
  244.4 2.1 collective-permute-start.27
  246.5 14.0 %attend_back.3 = (bf16[512,2304]{1,0:T(8,128)(2,1)S(1)}, bf16[384,1536]{1,0:T(8,128)(2,1)S(1)}, f32[16,768]{1,0:T(8,128)S(1)}, f32[8,128]{1,0:T(8,128)S(1)}) custom-call(s32[4,4]{1,0:T(4,128)S(1)} %pad_add_fusion.2.refs_0_, s32[4,1,256]{2,1,0:T(1,128)S(1)} %reshape.381.refs_1_, s32[896,1]{1,0:T(8,128)S(1)} %reshape.412.refs_2_, ...), custom_call_target="tpu_custom_call" | custom-call | flops 12074999808 | bytes 1000 | tf_op jit(solution)/shard_map/attend_back/pallas_call | solution.py:249
  263.0 1.9 convolution_convert_fusion.refs_8_
  266.5 3.8 %grad_heads.3 = (bf16[49,8,3072]{2,1,0:T(8,128)(2,1)S(1)}, bf16[49,8,3072]{2,1,0:T(8,128)(2,1)S(1)}, f32[8,128]{1,0:T(8,128)S(1)}) custom-call(s32[1]{0:T(128)} %bitcast.36.refs_0_, bf16[8,96,512]{2,1,0:T(8,128)(2,1)S(1)} %bitcast.170, bf16[8,96,512]{2,1,0:T(8,128)(2,1)S(1)} %bitcast.169, bf16[8,96,384]{2,1,0:T(8,128)(2,1)S(1)} %bitcast.175, ...), custom_call_target="tpu_custom_call" | custom-call | flops 4600000000 | bytes 1000 | tf_op jit(solution)/shard_map/grad_heads/pallas_call | solution.py:249
  270.5 3.1 collective-permute-done.27.refs_2_
  275.2 5.7 %collective-permute-done.26.refs_2_ = bf16[13,8,3072]{2,1,0:T(8,128)(2,1)S(1)} collective-permute-done((bf16[13,8,3072]{2,1,0:T(8,128)(2,1)S(1)}, bf16[13,8,3072]{2,1,0:T(8,128)(2,1)S(1)}, u32[]{:S(2)}, u32[]{:S(2)}) %collective-permute-start.26) | collective-permute-done | bytes 639008 | tf_op jit(solution)/shard_map/ppermute | solution.py:908
  280.9 1.6 advance.24
  282.5 2.1 advance.25
  284.7 2.7 collective-permute-start.28
  287.4 11.6 %collective-permute-done.29.refs_2_ = bf16[4,2,4,24,768]{4,3,2,1,0:T(8,128)(2,1)S(1)} collective-permute-done((bf16[4,2,4,24,768]{4,3,2,1,0:T(8,128)(2,1)S(1)}, bf16[4,2,4,24,768]{4,3,2,1,0:T(8,128)(2,1)S(1)}, u32[]{:S(2)}, u32[]{:S(2)}) %collective-permute-start.29) | collective-permute-done | bytes 1179680 | tf_op jit(solution)/shard_map/ppermute | solution.py:908
  301.3 3.4 collective-permute-start.31
  304.8 2.8 collective-permute-start.37
  307.7 2.1 collective-permute-start.33
  310.7 15.0 %collective-permute-done.31.refs_2_ = bf16[2,2,4,24,768]{4,3,2,1,0:T(8,128)(2,1)} collective-permute-done((bf16[2,2,4,24,768]{4,3,2,1,0:T(8,128)(2,1)}, bf16[2,2,4,24,768]{4,3,2,1,0:T(8,128)(2,1)}, u32[]{:S(2)}, u32[]{:S(2)}) %collective-permute-start.31) | collective-permute-done | bytes 589856 | tf_op jit(solution)/shard_map/ppermute | solution.py:908
  326.9 1.8 collective-permute-start.36
  328.7 3.2 convert_add_fusion
  332.8 2.5 collective-permute-start.32
  335.4 7.3 %collective-permute-done.33.refs_2_ = bf16[204,8,128]{2,1,0:T(8,128)(2,1)S(1)} collective-permute-done((bf16[204,8,128]{2,1,0:T(8,128)(2,1)}, bf16[204,8,128]{2,1,0:T(8,128)(2,1)S(1)}, u32[]{:S(2)}, u32[]{:S(2)}) %collective-permute-start.33) | collective-permute-done | bytes 417824 | tf_op jit(solution)/shard_map/ppermute | solution.py:908
  343.9 7.1 %collective-permute-done.32.refs_2_ = bf16[204,8,128]{2,1,0:T(8,128)(2,1)S(1)} collective-permute-done((bf16[204,8,128]{2,1,0:T(8,128)(2,1)S(1)}, bf16[204,8,128]{2,1,0:T(8,128)(2,1)S(1)}, u32[]{:S(2)}, u32[]{:S(2)}) %collective-permute-start.32) | collective-permute-done | bytes 417824 | tf_op jit(solution)/shard_map/ppermute | solution.py:908
  353.1 2.7 collective-permute-start.34
  359.1 5.7 %collective-permute-done.34 = bf16[108,8,128]{2,1,0:T(8,128)(2,1)S(1)} collective-permute-done((bf16[108,8,128]{2,1,0:T(8,128)(2,1)S(1)}, bf16[108,8,128]{2,1,0:T(8,128)(2,1)S(1)}, u32[]{:S(2)}, u32[]{:S(2)}) %collective-permute-start.34) | collective-permute-done | bytes 221216 | tf_op jit(solution)/shard_map/ppermute | solution.py:908
  (358 shorter events, 76.3 us)
Async XLA Ops:
  0.7 7.5 %copy-start.10 = (bf16[512,768]{1,0:T(8,128)(2,1)S(1)}, bf16[512,768]{1,0:T(8,128)(2,1)}, u32[]{:S(2)}) copy-start(bf16[512,768]{1,0:T(8,128)(2,1)} %refs_0_.2) | copy-start | bytes 2359300
  0.7 11.8 %copy-start.87 = (bf16[2,3072]{1,0:T(2,128)(2,1)S(1)}, bf16[2,3072]{1,0:T(2,128)(2,1)}, u32[]{:S(2)}) copy-start(bf16[2,3072]{1,0:T(2,128)(2,1)} %param.24) | copy-start | bytes 36868
  2.5 10.7 %collective-permute-start = (bf16[80,768]{1,0:T(8,128)(2,1)S(1)}, bf16[80,768]{1,0:T(8,128)(2,1)S(1)}, u32[]{:S(2)}, u32[]{:S(2)}) collective-permute-start(bf16[80,768]{1,0:T(8,128)(2,1)S(1)} %fusion.6), channel_id=1, source_target_pairs={{0,1},{1,0},{2,3},{3,2},{4,5},{5,4},{6,7},{7,6},{8,9},{9,8},{10,11... | collective-permute-start | bytes 368648 | tf_op jit(solution)/shard_map/ppermute | solution.py:27
  5.5 12.3 %collective-permute-start.1 = (bf16[80,768]{1,0:T(8,128)(2,1)S(1)}, bf16[80,768]{1,0:T(8,128)(2,1)S(1)}, u32[]{:S(2)}, u32[]{:S(2)}) collective-permute-start(bf16[80,768]{1,0:T(8,128)(2,1)S(1)} %fusion.6), channel_id=1, source_target_pairs={{0,2},{1,3},{2,0},{3,1},{4,6},{5,7},{6,4},{7,5},{8,10},{9,11},{10,... | collective-permute-start | bytes 368648 | tf_op jit(solution)/shard_map/ppermute | solution.py:27
  8.1 10.4 %collective-permute-start.2 = (bf16[80,768]{1,0:T(8,128)(2,1)S(1)}, bf16[80,768]{1,0:T(8,128)(2,1)S(1)}, u32[]{:S(2)}, u32[]{:S(2)}) collective-permute-start(bf16[80,768]{1,0:T(8,128)(2,1)S(1)} %fusion.6), channel_id=1, source_target_pairs={{0,3},{1,2},{2,1},{3,0},{4,7},{5,6},{6,5},{7,4},{8,11},{9,10},{10,... | collective-permute-start | bytes 368648 | tf_op jit(solution)/shard_map/ppermute | solution.py:27
  9.0 33.2 %collective-permute-start.8 = (bf16[384,768]{1,0:T(8,128)(2,1)}, bf16[384,768]{1,0:T(8,128)(2,1)}, u32[]{:S(2)}, u32[]{:S(2)}) collective-permute-start(bf16[384,768]{1,0:T(8,128)(2,1)} %constant_dynamic-slice_fusion.3), channel_id=1, source_target_pairs={{0,1},{1,0},{2,3},{3,2},{4,5},{5,4},{6,7},{7,6},{8,9},{9,8},{10,11... | collective-permute-start | bytes 1769480 | tf_op jit(solution)/shard_map/ppermute | solution.py:27
  19.2 5.4 %collective-permute-start.3 = (bf16[1,3,3,24,384]{4,3,2,1,0:T(8,128)(2,1)S(1)}, bf16[1,3,3,24,384]{4,3,2,1,0:T(8,128)(2,1)S(1)}, u32[]{:S(2)}, u32[]{:S(2)}) collective-permute-start(bf16[1,3,3,24,384]{4,3,2,1,0:T(8,128)(2,1)S(1)} %get-tuple-element.286), channel_id=1, source_target_pairs={{0,8},{4,12},{8,0},{12,4},{16,24},{20,28},{24,16},{28,20},{1,9},{5... | collective-permute-start | bytes 497672 | tf_op jit(solution)/shard_map/ppermute | solution.py:27
  20.8 7.1 %collective-permute-start.5 = (bf16[1,3,3,24,384]{4,3,2,1,0:T(8,128)(2,1)S(1)}, bf16[1,3,3,24,384]{4,3,2,1,0:T(8,128)(2,1)S(1)}, u32[]{:S(2)}, u32[]{:S(2)}) collective-permute-start(bf16[1,3,3,24,384]{4,3,2,1,0:T(8,128)(2,1)S(1)} %get-tuple-element.287), channel_id=1, source_target_pairs={{0,16},{4,20},{8,24},{12,28},{16,0},{20,4},{24,8},{28,12},{1,17},{... | collective-permute-start | bytes 497672 | tf_op jit(solution)/shard_map/ppermute | solution.py:27
  24.7 7.6 %collective-permute-start.4 = (bf16[2,3,3,24,384]{4,3,2,1,0:T(8,128)(2,1)S(1)}, bf16[2,3,3,24,384]{4,3,2,1,0:T(8,128)(2,1)S(1)}, u32[]{:S(2)}, u32[]{:S(2)}) collective-permute-start(bf16[2,3,3,24,384]{4,3,2,1,0:T(8,128)(2,1)S(1)} %pad_maximum_fusion.5), channel_id=1, source_target_pairs={{0,16},{4,20},{8,24},{12,28},{16,0},{20,4},{24,8},{28,12},{1,17},{... | collective-permute-start | bytes 995336 | tf_op jit(solution)/shard_map/ppermute | solution.py:27
  27.9 7.2 %collective-permute-start.6 = (bf16[2,3,3,24,384]{4,3,2,1,0:T(8,128)(2,1)S(1)}, bf16[2,3,3,24,384]{4,3,2,1,0:T(8,128)(2,1)S(1)}, u32[]{:S(2)}, u32[]{:S(2)}) collective-permute-start(bf16[2,3,3,24,384]{4,3,2,1,0:T(8,128)(2,1)S(1)} %pad_maximum_fusion.6), channel_id=1, source_target_pairs={{0,8},{4,12},{8,0},{12,4},{16,24},{20,28},{24,16},{28,20},{1,9},{5... | collective-permute-start | bytes 995336 | tf_op jit(solution)/shard_map/ppermute | solution.py:27
  37.4 8.1 %collective-permute-start.7 = (bf16[2,4,3,3,24,384]{5,4,3,2,1,0:T(8,128)(2,1)}, bf16[2,4,3,3,24,384]{5,4,3,2,1,0:T(8,128)(2,1)}, u32[]{:S(2)}, u32[]{:S(2)}) collective-permute-start(bf16[2,4,3,3,24,384]{5,4,3,2,1,0:T(8,128)(2,1)} %pad_maximum_fusion.1), channel_id=1, source_target_pairs={{0,4},{4,0},{8,12},{12,8},{16,20},{20,16},{24,28},{28,24},{1,5},{5... | collective-permute-start | bytes 3981320 | tf_op jit(solution)/shard_map/ppermute | solution.py:27
  48.3 23.1 %collective-permute-start.10 = (bf16[3,96,768]{2,1,0:T(8,128)(2,1)S(1)}, bf16[3,96,768]{2,1,0:T(8,128)(2,1)S(1)}, u32[]{:S(2)}, u32[]{:S(2)}) collective-permute-start(bf16[3,96,768]{2,1,0:T(8,128)(2,1)S(1)} %get-tuple-element.150), channel_id=1, source_target_pairs={{0,2},{1,3},{2,0},{3,1},{4,6},{5,7},{6,4},{7,5},{8,10},{9,11},{10,... | collective-permute-start | bytes 1327112 | tf_op jit(solution)/shard_map/ppermute | solution.py:27
  50.1 37.7 %collective-permute-start.9 = (bf16[3,96,768]{2,1,0:T(8,128)(2,1)S(1)}, bf16[3,96,768]{2,1,0:T(8,128)(2,1)S(1)}, u32[]{:S(2)}, u32[]{:S(2)}) collective-permute-start(bf16[3,96,768]{2,1,0:T(8,128)(2,1)S(1)} %get-tuple-element.150), channel_id=1, source_target_pairs={{0,1},{1,0},{2,3},{3,2},{4,5},{5,4},{6,7},{7,6},{8,9},{9,8},{10,11... | collective-permute-start | bytes 1327112 | tf_op jit(solution)/shard_map/ppermute | solution.py:27
  56.8 10.8 %copy-start.37 = (bf16[384,1536]{1,0:T(8,128)(2,1)}, bf16[384,1536]{1,0:T(8,128)(2,1)S(1)}, u32[]{:S(2)}) copy-start(bf16[384,1536]{1,0:T(8,128)(2,1)S(1)} %fusion.2.refs_4_) | copy-start | bytes 3538948
  56.8 14.7 %copy-start.11 = (bf16[2,768,768]{2,1,0:T(8,128)(2,1)S(1)}, bf16[2,768,768]{2,1,0:T(8,128)(2,1)}, u32[]{:S(2)}) copy-start(bf16[2,768,768]{2,1,0:T(8,128)(2,1)} %refs_8_.3) | copy-start | bytes 7077892
  71.4 16.3 %collective-permute-start.11 = (bf16[3,96,768]{2,1,0:T(8,128)(2,1)S(1)}, bf16[3,96,768]{2,1,0:T(8,128)(2,1)S(1)}, u32[]{:S(2)}, u32[]{:S(2)}) collective-permute-start(bf16[3,96,768]{2,1,0:T(8,128)(2,1)S(1)} %collective-permute-done.10.refs_1_), channel_id=1, source_target_pairs={{0,1},{1,0},{2,3},{3,2},{4,5},{5,4},{6,7},{7,6},{8,9},{9,8},{10,11... | collective-permute-start | bytes 1327112 | tf_op jit(solution)/shard_map/ppermute | solution.py:27
  87.9 3.1 collective-permute-start.12
  88.1 16.1 %collective-permute-start.13 = (bf16[384,768]{1,0:T(8,128)(2,1)S(1)}, bf16[384,768]{1,0:T(8,128)(2,1)S(1)}, u32[]{:S(2)}, u32[]{:S(2)}) collective-permute-start(bf16[384,768]{1,0:T(8,128)(2,1)S(1)} %constant_dynamic-slice_fusion.2), channel_id=1, source_target_pairs={{0,1},{1,0},{2,3},{3,2},{4,5},{5,4},{6,7},{7,6},{8,9},{9,8},{10,11... | collective-permute-start | bytes 1769480 | tf_op jit(solution)/shard_map/ppermute | solution.py:27
  92.0 12.2 %copy-start.79 = (bf16[2,4,2,96,768]{4,3,2,1,0:T(8,128)(2,1)}, bf16[2,4,2,96,768]{4,3,2,1,0:T(8,128)(2,1)S(1)}, u32[]{:S(2)}) copy-start(bf16[2,4,2,96,768]{4,3,2,1,0:T(8,128)(2,1)S(1)} %slice.183) | copy-start | bytes 7077892
  95.7 9.6 %copy-start.57 = (bf16[512,2304]{1,0:T(8,128)(2,1)}, bf16[512,2304]{1,0:T(8,128)(2,1)S(1)}, u32[]{:S(2)}) copy-start(bf16[512,2304]{1,0:T(8,128)(2,1)S(1)} %fusion.1.refs_3_) | copy-start | bytes 7077892
  105.3 10.3 %copy-start.39 = (bf16[384,1536]{1,0:T(8,128)(2,1)}, bf16[384,1536]{1,0:T(8,128)(2,1)S(1)}, u32[]{:S(2)}) copy-start(bf16[384,1536]{1,0:T(8,128)(2,1)S(1)} %fusion.3.refs_4_) | copy-start | bytes 3538948
  105.3 12.4 %copy-start.66 = (f32[512,768]{1,0:T(8,128)S(1)}, f32[512,768]{1,0:T(8,128)}, u32[]{:S(2)}) copy-start(f32[512,768]{1,0:T(8,128)} %copy-done.65) | copy-start | bytes 4718596
  117.7 12.3 %copy-start.16 = (bf16[512,768]{1,0:T(8,128)(2,1)S(1)}, bf16[512,768]{1,0:T(8,128)(2,1)}, u32[]{:S(2)}) copy-start(bf16[512,768]{1,0:T(8,128)(2,1)} %refs_0_.3) | copy-start | bytes 2359300
  149.3 4.9 %collective-permute-start.15 = (bf16[4,4,4,24,768]{4,3,2,1,0:T(8,128)(2,1)}, bf16[4,4,4,24,768]{4,3,2,1,0:T(8,128)(2,1)}, u32[]{:S(2)}, u32[]{:S(2)}) collective-permute-start(bf16[4,4,4,24,768]{4,3,2,1,0:T(8,128)(2,1)} %get-tuple-element.179), channel_id=1, source_target_pairs={{0,4},{4,0},{8,12},{12,8},{16,20},{20,16},{24,28},{28,24},{1,5},{5... | collective-permute-start | bytes 7077896 | tf_op jit(solution)/shard_map/ppermute | solution.py:27
  149.3 8.2 %collective-permute-start.14 = (bf16[4,4,4,24,768]{4,3,2,1,0:T(8,128)(2,1)}, bf16[4,4,4,24,768]{4,3,2,1,0:T(8,128)(2,1)}, u32[]{:S(2)}, u32[]{:S(2)}) collective-permute-start(bf16[4,4,4,24,768]{4,3,2,1,0:T(8,128)(2,1)} %get-tuple-element.178), channel_id=1, source_target_pairs={{0,4},{4,0},{8,12},{12,8},{16,20},{20,16},{24,28},{28,24},{1,5},{5... | collective-permute-start | bytes 7077896 | tf_op jit(solution)/shard_map/ppermute | solution.py:27
  164.2 14.8 %copy-start = (bf16[8,2,4,24,768]{4,3,2,1,0:T(8,128)(2,1)}, bf16[8,2,4,24,768]{4,3,2,1,0:T(8,128)(2,1)S(1)}, u32[]{:S(2)}) copy-start(bf16[8,2,4,24,768]{4,3,2,1,0:T(8,128)(2,1)S(1)} %get-tuple-element.188.refs_1_) | copy-start | bytes 7077892
  164.2 29.2 %collective-permute-start.17 = (bf16[8,2,4,24,768]{4,3,2,1,0:T(8,128)(2,1)}, bf16[8,2,4,24,768]{4,3,2,1,0:T(8,128)(2,1)}, u32[]{:S(2)}, u32[]{:S(2)}) collective-permute-start(bf16[8,2,4,24,768]{4,3,2,1,0:T(8,128)(2,1)} %get-tuple-element.189), channel_id=1, source_target_pairs={{0,8},{4,20},{8,0},{12,28},{16,24},{20,4},{24,16},{28,12},{1,9},{5... | collective-permute-start | bytes 7077896 | tf_op jit(solution)/shard_map/ppermute | solution.py:908
  165.0 14.1 %copy-start.80 = (bf16[2,4,2,96,768]{4,3,2,1,0:T(8,128)(2,1)S(1)}, bf16[2,4,2,96,768]{4,3,2,1,0:T(8,128)(2,1)}, u32[]{:S(2)}) copy-start(bf16[2,4,2,96,768]{4,3,2,1,0:T(8,128)(2,1)} %copy-done.79) | copy-start | bytes 7077892
  179.0 7.9 %copy-start.51 = (bf16[512,2304]{1,0:T(8,128)(2,1)}, bf16[512,2304]{1,0:T(8,128)(2,1)S(1)}, u32[]{:S(2)}) copy-start(bf16[512,2304]{1,0:T(8,128)(2,1)S(1)} %get-tuple-element.182.refs_5_) | copy-start | bytes 7077892
  180.2 6.8 %copy-start.17 = (bf16[384,768]{1,0:T(8,128)(2,1)}, bf16[384,768]{1,0:T(8,128)(2,1)S(1)}, u32[]{:S(2)}) copy-start(bf16[384,768]{1,0:T(8,128)(2,1)S(1)} %convolution_convert_fusion.1.refs_8_) | copy-start | bytes 1769476
  186.9 30.2 %collective-permute-start.19 = (bf16[49,8,3072]{2,1,0:T(8,128)(2,1)}, bf16[49,8,3072]{2,1,0:T(8,128)(2,1)}, u32[]{:S(2)}, u32[]{:S(2)}) collective-permute-start(bf16[49,8,3072]{2,1,0:T(8,128)(2,1)} %get-tuple-element.205), channel_id=1, source_target_pairs={{0,4},{4,0},{8,12},{12,8},{16,20},{20,16},{24,28},{28,24},{1,5},{5... | collective-permute-start | bytes 7225352 | tf_op jit(solution)/shard_map/ppermute | solution.py:27
  187.2 17.3 %collective-permute-start.16 = (bf16[384,768]{1,0:T(8,128)(2,1)}, bf16[384,768]{1,0:T(8,128)(2,1)S(1)}, u32[]{:S(2)}, u32[]{:S(2)}) collective-permute-start(bf16[384,768]{1,0:T(8,128)(2,1)} %copy-done.17), channel_id=1, source_target_pairs={{0,1},{1,0},{2,3},{3,2},{4,5},{5,4},{6,7},{7,6},{8,9},{9,8},{10,11... | collective-permute-start | bytes 1769480 | tf_op jit(solution)/shard_map/ppermute | solution.py:27
  195.0 9.5 %slice-start = ((s8[6291456]{0:T(1024)(128)(4,1)}), s8[4194304]{0:T(1024)(128)(4,1)S(1)}, s32[]{:S(2)}) async-start(s8[6291456]{0:T(1024)(128)(4,1)} %bitcast.176), calls=%async_computation | async-start | bytes 8388608
  197.4 23.1 %collective-permute-start.18 = (bf16[4,2,4,24,768]{4,3,2,1,0:T(8,128)(2,1)S(1)}, bf16[4,2,4,24,768]{4,3,2,1,0:T(8,128)(2,1)S(1)}, u32[]{:S(2)}, u32[]{:S(2)}) collective-permute-start(bf16[4,2,4,24,768]{4,3,2,1,0:T(8,128)(2,1)S(1)} %get-tuple-element.203), channel_id=1, source_target_pairs={{0,16},{4,12},{8,24},{12,4},{16,0},{20,28},{24,8},{28,20},{1,17},{... | collective-permute-start | bytes 3538952 | tf_op jit(solution)/shard_map/ppermute | solution.py:908
  197.7 6.8 %copy-start.12 = (bf16[2,768,768]{2,1,0:T(8,128)(2,1)S(1)}, bf16[2,768,768]{2,1,0:T(8,128)(2,1)}, u32[]{:S(2)}) copy-start(bf16[2,768,768]{2,1,0:T(8,128)(2,1)} %refs_8_.3) | copy-start | bytes 7077892
  197.7 6.8 %slice-start.1 = ((s8[6291456]{0:T(1024)(128)(4,1)}), s8[2097152]{0:T(1024)(128)(4,1)S(1)}, s32[]{:S(2)}) async-start(s8[6291456]{0:T(1024)(128)(4,1)} %bitcast.176), calls=%async_computation.1 | async-start | bytes 4194304
  197.7 6.8 %copy-start.44 = (f32[512,768]{1,0:T(8,128)S(1)}, f32[512,768]{1,0:T(8,128)}, u32[]{:S(2)}) copy-start(f32[512,768]{1,0:T(8,128)} %copy-done.43) | copy-start | bytes 4718596
  197.7 6.8 %copy-start.46 = (f32[512,768]{1,0:T(8,128)S(1)}, f32[512,768]{1,0:T(8,128)}, u32[]{:S(2)}) copy-start(f32[512,768]{1,0:T(8,128)} %copy-done.45) | copy-start | bytes 4718596
  220.5 6.0 %copy-start.13 = (bf16[25,8,3072]{2,1,0:T(8,128)(2,1)}, bf16[25,8,3072]{2,1,0:T(8,128)(2,1)S(1)}, u32[]{:S(2)}) copy-start(bf16[25,8,3072]{2,1,0:T(8,128)(2,1)S(1)} %get-tuple-element.228.refs_1_) | copy-start | bytes 3686404
  220.5 8.8 %copy-start.15 = (bf16[25,8,3072]{2,1,0:T(8,128)(2,1)}, bf16[25,8,3072]{2,1,0:T(8,128)(2,1)S(1)}, u32[]{:S(2)}) copy-start(bf16[25,8,3072]{2,1,0:T(8,128)(2,1)S(1)} %get-tuple-element.229) | copy-start | bytes 3686404
  230.8 4.9 %collective-permute-start.21 = (bf16[4,4,4,24,768]{4,3,2,1,0:T(8,128)(2,1)}, bf16[4,4,4,24,768]{4,3,2,1,0:T(8,128)(2,1)}, u32[]{:S(2)}, u32[]{:S(2)}) collective-permute-start(bf16[4,4,4,24,768]{4,3,2,1,0:T(8,128)(2,1)} %get-tuple-element.215), channel_id=1, source_target_pairs={{0,4},{4,0},{8,12},{12,8},{16,20},{20,16},{24,28},{28,24},{1,5},{5... | collective-permute-start | bytes 7077896 | tf_op jit(solution)/shard_map/ppermute | solution.py:27
  230.8 8.2 %collective-permute-start.20 = (bf16[4,4,4,24,768]{4,3,2,1,0:T(8,128)(2,1)}, bf16[4,4,4,24,768]{4,3,2,1,0:T(8,128)(2,1)}, u32[]{:S(2)}, u32[]{:S(2)}) collective-permute-start(bf16[4,4,4,24,768]{4,3,2,1,0:T(8,128)(2,1)} %get-tuple-element.214), channel_id=1, source_target_pairs={{0,4},{4,0},{8,12},{12,8},{16,20},{20,16},{24,28},{28,24},{1,5},{5... | collective-permute-start | bytes 7077896 | tf_op jit(solution)/shard_map/ppermute | solution.py:27
  231.4 29.1 %collective-permute-start.24 = (bf16[25,8,3072]{2,1,0:T(8,128)(2,1)}, bf16[25,8,3072]{2,1,0:T(8,128)(2,1)S(1)}, u32[]{:S(2)}, u32[]{:S(2)}) collective-permute-start(bf16[25,8,3072]{2,1,0:T(8,128)(2,1)} %copy-done.15), channel_id=1, source_target_pairs={{0,8},{4,20},{8,0},{12,28},{16,24},{20,4},{24,16},{28,12},{1,9},{5... | collective-permute-start | bytes 3686408 | tf_op jit(solution)/shard_map/ppermute | solution.py:908
  233.4 31.5 %collective-permute-start.23 = (bf16[2,2,4,24,768]{4,3,2,1,0:T(8,128)(2,1)}, bf16[2,2,4,24,768]{4,3,2,1,0:T(8,128)(2,1)S(1)}, u32[]{:S(2)}, u32[]{:S(2)}) collective-permute-start(bf16[2,2,4,24,768]{4,3,2,1,0:T(8,128)(2,1)} %get-tuple-element.227), channel_id=1, source_target_pairs={{0,1},{1,0},{2,3},{3,2},{4,5},{5,4},{6,7},{7,6},{8,9},{9,8},{10,11... | collective-permute-start | bytes 1769480 | tf_op jit(solution)/shard_map/ppermute | solution.py:908
  244.4 29.2 %collective-permute-start.27 = (bf16[8,2,4,24,768]{4,3,2,1,0:T(8,128)(2,1)S(1)}, bf16[8,2,4,24,768]{4,3,2,1,0:T(8,128)(2,1)S(1)}, u32[]{:S(2)}, u32[]{:S(2)}) collective-permute-start(bf16[8,2,4,24,768]{4,3,2,1,0:T(8,128)(2,1)S(1)} %get-tuple-element.238), channel_id=1, source_target_pairs={{0,8},{4,20},{8,0},{12,28},{16,24},{20,4},{24,16},{28,12},{1,9},{5... | collective-permute-start | bytes 7077896 | tf_op jit(solution)/shard_map/ppermute | solution.py:908
  246.5 14.1 %copy-start.14 = (bf16[25,8,3072]{2,1,0:T(8,128)(2,1)S(1)}, bf16[25,8,3072]{2,1,0:T(8,128)(2,1)}, u32[]{:S(2)}) copy-start(bf16[25,8,3072]{2,1,0:T(8,128)(2,1)} %copy-done.13) | copy-start | bytes 3686404
  270.3 12.2 %collective-permute-start.25 = (bf16[49,8,3072]{2,1,0:T(8,128)(2,1)S(1)}, bf16[49,8,3072]{2,1,0:T(8,128)(2,1)S(1)}, u32[]{:S(2)}, u32[]{:S(2)}) collective-permute-start(bf16[49,8,3072]{2,1,0:T(8,128)(2,1)S(1)} %get-tuple-element.234), channel_id=1, source_target_pairs={{0,4},{4,0},{8,12},{12,8},{16,20},{20,16},{24,28},{28,24},{1,5},{5... | collective-permute-start | bytes 7225352 | tf_op jit(solution)/shard_map/ppermute | solution.py:27
  270.4 10.5 %collective-permute-start.26 = (bf16[13,8,3072]{2,1,0:T(8,128)(2,1)S(1)}, bf16[13,8,3072]{2,1,0:T(8,128)(2,1)S(1)}, u32[]{:S(2)}, u32[]{:S(2)}) collective-permute-start(bf16[13,8,3072]{2,1,0:T(8,128)(2,1)S(1)} %get-tuple-element.236), channel_id=1, source_target_pairs={{0,16},{4,12},{8,24},{12,4},{16,0},{20,28},{24,8},{28,20},{1,17},{... | collective-permute-start | bytes 1916936 | tf_op jit(solution)/shard_map/ppermute | solution.py:908
  274.7 24.3 %collective-permute-start.29 = (bf16[4,2,4,24,768]{4,3,2,1,0:T(8,128)(2,1)S(1)}, bf16[4,2,4,24,768]{4,3,2,1,0:T(8,128)(2,1)S(1)}, u32[]{:S(2)}, u32[]{:S(2)}) collective-permute-start(bf16[4,2,4,24,768]{4,3,2,1,0:T(8,128)(2,1)S(1)} %get-tuple-element.245), channel_id=1, source_target_pairs={{0,16},{4,12},{8,24},{12,4},{16,0},{20,28},{24,8},{28,20},{1,17},{... | collective-permute-start | bytes 3538952 | tf_op jit(solution)/shard_map/ppermute | solution.py:908
  284.7 25.1 %collective-permute-start.28 = (bf16[25,8,3072]{2,1,0:T(8,128)(2,1)}, bf16[25,8,3072]{2,1,0:T(8,128)(2,1)S(1)}, u32[]{:S(2)}, u32[]{:S(2)}) collective-permute-start(bf16[25,8,3072]{2,1,0:T(8,128)(2,1)} %get-tuple-element.243), channel_id=1, source_target_pairs={{0,8},{4,20},{8,0},{12,28},{16,24},{20,4},{24,16},{28,12},{1,9},{5... | collective-permute-start | bytes 3686408 | tf_op jit(solution)/shard_map/ppermute | solution.py:908
  287.4 20.2 %collective-permute-start.22 = (bf16[384,768]{1,0:T(8,128)(2,1)}, bf16[384,768]{1,0:T(8,128)(2,1)S(1)}, u32[]{:S(2)}, u32[]{:S(2)}) collective-permute-start(bf16[384,768]{1,0:T(8,128)(2,1)} %convolution_convert_fusion.refs_8_), channel_id=1, source_target_pairs={{0,1},{1,0},{2,3},{3,2},{4,5},{5,4},{6,7},{7,6},{8,9},{9,8},{10,11... | collective-permute-start | bytes 1769480 | tf_op jit(solution)/shard_map/ppermute | solution.py:27
  301.3 24.4 %collective-permute-start.31 = (bf16[2,2,4,24,768]{4,3,2,1,0:T(8,128)(2,1)}, bf16[2,2,4,24,768]{4,3,2,1,0:T(8,128)(2,1)}, u32[]{:S(2)}, u32[]{:S(2)}) collective-permute-start(bf16[2,2,4,24,768]{4,3,2,1,0:T(8,128)(2,1)} %get-tuple-element.251), channel_id=1, source_target_pairs={{0,1},{1,0},{2,3},{3,2},{4,5},{5,4},{6,7},{7,6},{8,9},{9,8},{10,11... | collective-permute-start | bytes 1769480 | tf_op jit(solution)/shard_map/ppermute | solution.py:908
  304.8 47.3 %collective-permute-start.37 = (bf16[1,2,4,24,768]{4,3,2,1,0:T(8,128)(2,1)}, bf16[1,2,4,24,768]{4,3,2,1,0:T(8,128)(2,1)}, u32[]{:S(2)}, u32[]{:S(2)}) collective-permute-start(bf16[1,2,4,24,768]{4,3,2,1,0:T(8,128)(2,1)} %get-tuple-element.269), channel_id=1, source_target_pairs={{0,2},{1,3},{2,0},{3,1},{4,6},{5,7},{6,4},{7,5},{8,10},{9,11},{10,... | collective-permute-start | bytes 884744 | tf_op jit(solution)/shard_map/ppermute | solution.py:908
  307.6 21.1 %copy-start.50 = (bf16[512,2304]{1,0:T(8,128)(2,1)S(1)}, bf16[512,2304]{1,0:T(8,128)(2,1)}, u32[]{:S(2)}) copy-start(bf16[512,2304]{1,0:T(8,128)(2,1)} %copy-done.49) | copy-start | bytes 7077892
  307.7 18.1 %copy-start.36 = (bf16[2,2,4,24,768]{4,3,2,1,0:T(8,128)(2,1)S(1)}, bf16[2,2,4,24,768]{4,3,2,1,0:T(8,128)(2,1)}, u32[]{:S(2)}) copy-start(bf16[2,2,4,24,768]{4,3,2,1,0:T(8,128)(2,1)} %copy-done.35) | copy-start | bytes 1769476
  307.7 34.9 %collective-permute-start.33 = (bf16[204,8,128]{2,1,0:T(8,128)(2,1)}, bf16[204,8,128]{2,1,0:T(8,128)(2,1)S(1)}, u32[]{:S(2)}, u32[]{:S(2)}) collective-permute-start(bf16[204,8,128]{2,1,0:T(8,128)(2,1)} %get-tuple-element.257), channel_id=1, source_target_pairs={{0,1},{1,0},{2,3},{3,2},{4,5},{5,4},{6,7},{7,6},{8,9},{9,8},{10,11... | collective-permute-start | bytes 1253384 | tf_op jit(solution)/shard_map/ppermute | solution.py:908
  309.8 18.9 %copy-start.7 = (bf16[3,4,8,24,768]{4,3,2,1,0:T(8,128)(2,1)S(1)}, bf16[3,4,8,24,768]{4,3,2,1,0:T(8,128)(2,1)}, u32[]{:S(2)}) copy-start(bf16[3,4,8,24,768]{4,3,2,1,0:T(8,128)(2,1)} %copy-done.6) | copy-start | bytes 10616836
  309.8 18.9 %copy-start.42 = (f32[512,768]{1,0:T(8,128)S(1)}, f32[512,768]{1,0:T(8,128)}, u32[]{:S(2)}) copy-start(f32[512,768]{1,0:T(8,128)} %copy-done.41) | copy-start | bytes 4718596
  310.7 21.2 %collective-permute-start.30 = (bf16[13,8,3072]{2,1,0:T(8,128)(2,1)S(1)}, bf16[13,8,3072]{2,1,0:T(8,128)(2,1)S(1)}, u32[]{:S(2)}, u32[]{:S(2)}) collective-permute-start(bf16[13,8,3072]{2,1,0:T(8,128)(2,1)S(1)} %get-tuple-element.249), channel_id=1, source_target_pairs={{0,16},{4,12},{8,24},{12,4},{16,0},{20,28},{24,8},{28,20},{1,17},{... | collective-permute-start | bytes 1916936 | tf_op jit(solution)/shard_map/ppermute | solution.py:908
  326.9 16.5 %collective-permute-start.36 = (bf16[1,2,4,24,768]{4,3,2,1,0:T(8,128)(2,1)S(1)}, bf16[1,2,4,24,768]{4,3,2,1,0:T(8,128)(2,1)S(1)}, u32[]{:S(2)}, u32[]{:S(2)}) collective-permute-start(bf16[1,2,4,24,768]{4,3,2,1,0:T(8,128)(2,1)S(1)} %get-tuple-element.267), channel_id=1, source_target_pairs={{0,2},{1,3},{2,0},{3,1},{4,6},{5,7},{6,4},{7,5},{8,10},{9,11},{10,... | collective-permute-start | bytes 884744 | tf_op jit(solution)/shard_map/ppermute | solution.py:908
  331.9 10.7 %copy-start.48 = (bf16[204,8,128]{2,1,0:T(8,128)(2,1)S(1)}, bf16[204,8,128]{2,1,0:T(8,128)(2,1)}, u32[]{:S(2)}) copy-start(bf16[204,8,128]{2,1,0:T(8,128)(2,1)} %copy-done.47) | copy-start | bytes 1253380
  332.8 18.1 %collective-permute-start.32 = (bf16[204,8,128]{2,1,0:T(8,128)(2,1)S(1)}, bf16[204,8,128]{2,1,0:T(8,128)(2,1)S(1)}, u32[]{:S(2)}, u32[]{:S(2)}) collective-permute-start(bf16[204,8,128]{2,1,0:T(8,128)(2,1)S(1)} %get-tuple-element.255), channel_id=1, source_target_pairs={{0,1},{1,0},{2,3},{3,2},{4,5},{5,4},{6,7},{7,6},{8,9},{9,8},{10,11... | collective-permute-start | bytes 1253384 | tf_op jit(solution)/shard_map/ppermute | solution.py:908
  343.3 13.7 %collective-permute-start.35 = (bf16[108,8,128]{2,1,0:T(8,128)(2,1)S(1)}, bf16[108,8,128]{2,1,0:T(8,128)(2,1)}, u32[]{:S(2)}, u32[]{:S(2)}) collective-permute-start(bf16[108,8,128]{2,1,0:T(8,128)(2,1)S(1)} %get-tuple-element.265), channel_id=1, source_target_pairs={{0,2},{1,3},{2,0},{3,1},{4,6},{5,7},{6,4},{7,5},{8,10},{9,11},{10,... | collective-permute-start | bytes 663560 | tf_op jit(solution)/shard_map/ppermute | solution.py:908
  353.1 11.7 %collective-permute-start.34 = (bf16[108,8,128]{2,1,0:T(8,128)(2,1)S(1)}, bf16[108,8,128]{2,1,0:T(8,128)(2,1)S(1)}, u32[]{:S(2)}, u32[]{:S(2)}) collective-permute-start(bf16[108,8,128]{2,1,0:T(8,128)(2,1)S(1)} %get-tuple-element.263), channel_id=1, source_target_pairs={{0,2},{1,3},{2,0},{3,1},{4,6},{5,7},{6,4},{7,5},{8,10},{9,11},{10,... | collective-permute-start | bytes 663560 | tf_op jit(solution)/shard_map/ppermute | solution.py:908
  (72 other events, 208.1 us)
